TPU v7x, 32 devices: a whole 2x2x4 slice. The times are simulated.
32 devices in a mesh: wide: 8 (over y, x, core), narrow: 4 (over z).
Axes of the slice: x: 2, y: 2, z: 4, core: 2. Of those that a mesh axis runs over, the one named last changes fastest.
Arguments:
- patches: bfloat16 [32, 256, 16], P('wide'), may hold values from -6 to 6
- target_noise: float32 [32, 256, 16], P('wide'), may hold values from -6 to 6
- kept_slots: int32 [32, 160], P('wide'), may hold values from 0 to 255, as said below
- kept_count: int32 [32], P('wide'), may hold values from 80 to 160, as said below
- time_step: int32 [32], P('wide'), may hold values from 0 to 999
- labels: int32 [32], P('wide'), may hold values from 0 to 999
- teacher: float32 [32, 1152], P('wide'), may hold values from -6 to 6
- attend_in: float32 [2, 1152, 3, 1152], P(None, 'wide', None, 'narrow'), may hold values from -0.1875 to 0.1875
- attend_out: float32 [2, 1152, 1152], P(None, 'narrow', 'wide'), may hold values from -0.5 to 0.5
- expand: float32 [2, 1152, 4608], P(None, 'wide', 'narrow'), may hold values from -0.1875 to 0.1875
- contract: float32 [2, 4608, 1152], P(None, 'narrow', 'wide'), may hold values from -0.09375 to 0.09375
- modulation: float32 [2, 1152, 6, 1152], P(None, 'wide', None, 'narrow'), may hold values from -0.1875 to 0.1875
- patch_table: float32 [33, 1152], P(None, 'narrow'), may hold values from -0.1875 to 0.1875
- condition: float32 [1256, 1152], P(None, 'narrow'), may hold values from -0.375 to 0.375
- moment_attend_in: float32 [2, 1152, 3, 1152], P(None, 'wide', None, 'narrow'), may hold values from -3.33786e-06 to 3.33786e-06
- moment_attend_out: float32 [2, 1152, 1152], P(None, 'narrow', 'wide'), may hold values from -3.33786e-06 to 3.33786e-06
- moment_expand: float32 [2, 1152, 4608], P(None, 'wide', 'narrow'), may hold values from -1.9073486e-06 to 1.9073486e-06
- moment_contract: float32 [2, 4608, 1152], P(None, 'narrow', 'wide'), may hold values from -3.33786e-06 to 3.33786e-06
- moment_modulation: float32 [2, 1152, 6, 1152], P(None, 'wide', None, 'narrow'), may hold values from -3.33786e-06 to 3.33786e-06
- moment_patch: float32 [33, 1152], P(None, 'narrow'), may hold values from -4.7683716e-06 to 4.7683716e-06
- moment_condition: float32 [1256, 1152], P(None, 'narrow'), may hold values from -4.7683716e-06 to 4.7683716e-06
- second_attend_in: float32 [2, 1152, 3, 1152], P(None, 'wide', None, 'narrow'), may hold values from 2.5375211e-14 to 1.01500846e-13
- second_attend_out: float32 [2, 1152, 1152], P(None, 'narrow', 'wide'), may hold values from 2.5375211e-14 to 1.01500846e-13
- second_expand: float32 [2, 1152, 4608], P(None, 'wide', 'narrow'), may hold values from 1.0150085e-14 to 4.060034e-14
- second_contract: float32 [2, 4608, 1152], P(None, 'narrow', 'wide'), may hold values from 2.5375211e-14 to 1.01500846e-13
- second_modulation: float32 [2, 1152, 6, 1152], P(None, 'wide', None, 'narrow'), may hold values from 2.5375211e-14 to 1.01500846e-13
- second_patch: float32 [33, 1152], P(None, 'narrow'), may hold values from 5.0750423e-14 to 2.0300169e-13
- second_condition: float32 [1256, 1152], P(None, 'narrow'), may hold values from 5.0750423e-14 to 2.0300169e-13
- average_attend_in: float32 [2, 1152, 3, 1152], P(None, 'wide', None, 'narrow'), may hold values from -0.1875 to 0.1875
- average_attend_out: float32 [2, 1152, 1152], P(None, 'narrow', 'wide'), may hold values from -0.5 to 0.5
- average_expand: float32 [2, 1152, 4608], P(None, 'wide', 'narrow'), may hold values from -0.1875 to 0.1875
- average_contract: float32 [2, 4608, 1152], P(None, 'narrow', 'wide'), may hold values from -0.09375 to 0.09375
- average_modulation: float32 [2, 1152, 6, 1152], P(None, 'wide', None, 'narrow'), may hold values from -0.1875 to 0.1875
- average_patch: float32 [33, 1152], P(None, 'narrow'), may hold values from -0.1875 to 0.1875
- average_condition: float32 [1256, 1152], P(None, 'narrow'), may hold values from -0.375 to 0.375
Outputs:
- loss_parts: float32 [2], replicated
- grad_norm: float32 [], replicated
- new_attend_in: float32 [2, 1152, 3, 1152], P(None, 'wide', None, 'narrow')
- new_attend_out: float32 [2, 1152, 1152], P(None, 'narrow', 'wide')
- new_expand: float32 [2, 1152, 4608], P(None, 'wide', 'narrow')
- new_contract: float32 [2, 4608, 1152], P(None, 'narrow', 'wide')
- new_modulation: float32 [2, 1152, 6, 1152], P(None, 'wide', None, 'narrow')
- new_patch: float32 [33, 1152], P(None, 'narrow')
- new_condition: float32 [1256, 1152], P(None, 'narrow')
- next_moment_attend_in: float32 [2, 1152, 3, 1152], P(None, 'wide', None, 'narrow')
- next_moment_attend_out: float32 [2, 1152, 1152], P(None, 'narrow', 'wide')
- next_moment_expand: float32 [2, 1152, 4608], P(None, 'wide', 'narrow')
- next_moment_contract: float32 [2, 4608, 1152], P(None, 'narrow', 'wide')
- next_moment_modulation: float32 [2, 1152, 6, 1152], P(None, 'wide', None, 'narrow')
- next_moment_patch: float32 [33, 1152], P(None, 'narrow')
- next_moment_condition: float32 [1256, 1152], P(None, 'narrow')
- next_second_attend_in: float32 [2, 1152, 3, 1152], P(None, 'wide', None, 'narrow')
- next_second_attend_out: float32 [2, 1152, 1152], P(None, 'narrow', 'wide')
- next_second_expand: float32 [2, 1152, 4608], P(None, 'wide', 'narrow')
- next_second_contract: float32 [2, 4608, 1152], P(None, 'narrow', 'wide')
- next_second_modulation: float32 [2, 1152, 6, 1152], P(None, 'wide', None, 'narrow')
- next_second_patch: float32 [33, 1152], P(None, 'narrow')
- next_second_condition: float32 [1256, 1152], P(None, 'narrow')
- next_average_attend_in: float32 [2, 1152, 3, 1152], P(None, 'wide', None, 'narrow')
- next_average_attend_out: float32 [2, 1152, 1152], P(None, 'narrow', 'wide')
- next_average_expand: float32 [2, 1152, 4608], P(None, 'wide', 'narrow')
- next_average_contract: float32 [2, 4608, 1152], P(None, 'narrow', 'wide')
- next_average_modulation: float32 [2, 1152, 6, 1152], P(None, 'wide', None, 'narrow')
- next_average_patch: float32 [33, 1152], P(None, 'narrow')
- next_average_condition: float32 [1256, 1152], P(None, 'narrow')
Inputs may be any that keep to these rules, and one draw needn't show every extreme that they name: `kept_slots`: within one image the 160 slots hold distinct positions. `kept_count`: some image holds exactly 160 kept tokens.
All inputs are finite; a program needn't handle non-finite values.
Results may differ from a plain program's by a relative error of at most 0.02.
Values may be sent and summed in bfloat16 or wider, within the bound.
A program may use at most 256 MiB of HBM per device.

v0:
```python
from functools import partial
import math

import jax
import jax.numpy as jnp
from jax import lax
from jax.sharding import PartitionSpec as P

HEAD_DIM = 72
CLASSES = 1000
FREQ = 256
PATCH_IN = 16
STEP = 10


highest_float_accuracy = lax.Precision.HIGHEST
norm_eps = 1e-06
contrast_sharpness_divisor = 0.02
nce_weight = 0.5
learn_rate = 0.05
beta_first = 0.9
beta_second = 0.999
adam_eps = 1e-08
weight_decay = 0.05
clip_norm = 0.05
ema_decay = 0.9999


def layer_norm(values):
    center = values - jnp.mean(values, -1, keepdims=True)
    return center * lax.rsqrt(jnp.mean(center * center, -1, keepdims=True) + norm_eps)


def modulate(values, shift, scale):
    return layer_norm(values) * (1.0 + scale[:, None, :]) + shift[:, None, :]


def sinusoid(places, width):
    half = width // 2
    freqs = jnp.exp(-math.log(10000.0) * jnp.arange(half, dtype=jnp.float32) / half)
    angle = places.astype(jnp.float32)[:, None] * freqs[None, :]
    return jnp.concatenate([jnp.cos(angle), jnp.sin(angle)], -1)


def narrow_sum(values):
    return lax.psum(values.astype(jnp.bfloat16), "narrow").astype(jnp.float32)


def fetch(stacks, lookup_index):
    return (
        lax.all_gather(stacks[0][lookup_index].astype(jnp.bfloat16), "wide", axis=0, tiled=True),
        lax.all_gather(stacks[1][lookup_index].astype(jnp.bfloat16), "wide", axis=1, tiled=True),
        lax.all_gather(stacks[2][lookup_index].astype(jnp.bfloat16), "wide", axis=0, tiled=True),
        lax.all_gather(stacks[3][lookup_index].astype(jnp.bfloat16), "wide", axis=1, tiled=True),
        lax.all_gather(stacks[4][lookup_index].astype(jnp.bfloat16), "wide", axis=0, tiled=True),
    )


def scores_of(query, key, key_valid):
    scale = 1.0 / math.sqrt(HEAD_DIM)
    scores = jnp.einsum("bqhe,bkhe->bhqk", query, key, preferred_element_type=jnp.float32) * scale
    return jnp.where(key_valid[:, None, None, :] > 0, scores, -1e30)


def attend_forward(query, key, value, key_valid):
    scores = scores_of(query, key, key_valid)
    peak = jnp.max(scores, -1, keepdims=True)
    expo = jnp.exp(scores - peak)
    total = jnp.sum(expo, -1, keepdims=True)
    probs = (expo / total).astype(jnp.bfloat16)
    context = jnp.einsum(
        "bhqk,bkhe->bqhe", probs, value, preferred_element_type=jnp.float32
    ).astype(jnp.bfloat16)
    return (context, peak + jnp.log(total))


def attend_backward(query, key, value, log_total, grad_context, key_valid):
    scale = 1.0 / math.sqrt(HEAD_DIM)
    probs = jnp.exp(scores_of(query, key, key_valid) - log_total)
    grad_value = jnp.einsum(
        "bhqk,bqhe->bkhe",
        probs.astype(jnp.bfloat16),
        grad_context,
        preferred_element_type=jnp.float32,
    ).astype(jnp.bfloat16)
    grad_probs = jnp.einsum(
        "bqhe,bkhe->bhqk", grad_context, value, preferred_element_type=jnp.float32
    )
    grad_scores = (probs * (grad_probs - jnp.sum(grad_probs * probs, -1, keepdims=True))).astype(
        jnp.bfloat16
    )
    grad_query = (
        jnp.einsum("bhqk,bkhe->bqhe", grad_scores, key, preferred_element_type=jnp.float32) * scale
    ).astype(jnp.bfloat16)
    grad_key = (
        jnp.einsum("bhqk,bqhe->bkhe", grad_scores, query, preferred_element_type=jnp.float32)
        * scale
    ).astype(jnp.bfloat16)
    return (grad_query, grad_key, grad_value)


def split_heads(triple, lookup_index):
    batch, length = (triple.shape[0], triple.shape[1])
    return triple[:, :, lookup_index].reshape(batch, length, triple.shape[3] // HEAD_DIM, HEAD_DIM)


def block_forward(values, mod, key_valid, weight_tensors):
    attend_in, attend_out, expand, contract = weight_tensors
    shift_a, scale_a, gate_a, shift_m, scale_m, gate_m = [
        mod[:, lookup_index] for lookup_index in range(6)
    ]
    batch, length = (values.shape[0], values.shape[1])
    local = attend_in.shape[2]
    normed = modulate(values, shift_a, scale_a).astype(jnp.bfloat16)
    triple = jnp.einsum(
        "bld,dce->blce", normed, attend_in, preferred_element_type=jnp.float32
    ).astype(jnp.bfloat16)
    context, log_total = attend_forward(
        split_heads(triple, 0), split_heads(triple, 1), split_heads(triple, 2), key_valid
    )
    flat_context = context.reshape(batch, length, local)
    partial_attn = jnp.einsum(
        "ble,ed->bld", flat_context, attend_out, preferred_element_type=jnp.float32
    )
    attn = narrow_sum(partial_attn)
    middle = values + gate_a[:, None, :] * attn
    normed_m = modulate(middle, shift_m, scale_m).astype(jnp.bfloat16)
    inner = jnp.einsum("bld,df->blf", normed_m, expand, preferred_element_type=jnp.float32)
    active = jax.nn.gelu(inner, approximate=True).astype(jnp.bfloat16)
    branch = narrow_sum(
        jnp.einsum("blf,fd->bld", active, contract, preferred_element_type=jnp.float32)
    )
    result = middle + gate_m[:, None, :] * branch
    return (result, (values, middle, triple, flat_context, log_total, attn, inner, active, branch))


def block_backward(grad, mod, key_valid, weight_tensors, saved):
    attend_in, attend_out, expand, contract = weight_tensors
    values, middle, triple, flat_context, log_total, attn, inner, active, branch = saved
    shift_a, scale_a, gate_a, shift_m, scale_m, gate_m = [
        mod[:, lookup_index] for lookup_index in range(6)
    ]
    batch, length, local = (triple.shape[0], triple.shape[1], triple.shape[3])
    grad_branch = (gate_m[:, None, :] * grad).astype(jnp.bfloat16)
    grad_gate_m = jnp.sum(grad * branch, 1)
    derivative_live_entries = jnp.einsum(
        "bld,fd->blf", grad_branch, contract, preferred_element_type=jnp.float32
    )
    gelu_back = jax.vjp(partial(jax.nn.gelu, approximate=True), inner)[1]
    grad_inner = gelu_back(derivative_live_entries)[0].astype(jnp.bfloat16)
    grad_contract = jnp.einsum(
        "blf,bld->fd", active, grad_branch, preferred_element_type=jnp.float32
    )
    normed_m, modulate_back = jax.vjp(modulate, middle, shift_m, scale_m)
    grad_expand = jnp.einsum(
        "bld,blf->df", normed_m.astype(jnp.bfloat16), grad_inner, preferred_element_type=jnp.float32
    )
    grad_normed = narrow_sum(
        jnp.einsum("blf,df->bld", grad_inner, expand, preferred_element_type=jnp.float32)
    )
    grad_mid, grad_shift_m, grad_scale_m = modulate_back(grad_normed)
    grad_mid = grad + grad_mid
    grad_attn = (gate_a[:, None, :] * grad_mid).astype(jnp.bfloat16)
    grad_gate_a = jnp.sum(grad_mid * attn, 1)
    grad_flat = jnp.einsum(
        "bld,ed->ble", grad_attn, attend_out, preferred_element_type=jnp.float32
    ).astype(jnp.bfloat16)
    grad_attend_out = jnp.einsum(
        "ble,bld->ed", flat_context, grad_attn, preferred_element_type=jnp.float32
    )
    grad_context = grad_flat.reshape(batch, length, local // HEAD_DIM, HEAD_DIM)
    grad_query, grad_key, grad_value = attend_backward(
        split_heads(triple, 0),
        split_heads(triple, 1),
        split_heads(triple, 2),
        log_total,
        grad_context,
        key_valid,
    )
    grad_triple = jnp.stack([grad_query, grad_key, grad_value], 2).reshape(batch, length, 3, local)
    normed_a, modulate_back = jax.vjp(modulate, values, shift_a, scale_a)
    grad_attend_in = jnp.einsum(
        "bld,blce->dce",
        normed_a.astype(jnp.bfloat16),
        grad_triple,
        preferred_element_type=jnp.float32,
    )
    grad_normed = narrow_sum(
        jnp.einsum("blce,dce->bld", grad_triple, attend_in, preferred_element_type=jnp.float32)
    )
    grad_values, grad_shift_a, grad_scale_a = modulate_back(grad_normed)
    grad_mod = jnp.stack(
        [grad_shift_a, grad_scale_a, grad_gate_a, grad_shift_m, grad_scale_m, grad_gate_m], 1
    )
    return (
        grad_mid + grad_values,
        grad_mod,
        (grad_attend_in, grad_attend_out, grad_expand, grad_contract),
    )


def adam(weight, grad, moment, second, average, factor):
    grad = grad * factor
    moment = beta_first * moment + (1.0 - beta_first) * grad
    second = beta_second * second + (1.0 - beta_second) * grad * grad
    update = (
        moment
        / (1.0 - beta_first**STEP)
        / (jnp.sqrt(second / (1.0 - beta_second**STEP)) + adam_eps)
    )
    fresh = weight - learn_rate * (update + weight_decay * weight)
    average_decay = min(ema_decay, (1.0 + STEP) / (10.0 + STEP))
    average = average_decay * average + (1.0 - average_decay) * fresh
    return (fresh, moment, second, average)


def shards(
    patches,
    target_noise,
    kept_slots,
    kept_count,
    time_step,
    labels,
    teacher,
    attend_in,
    attend_out,
    expand,
    contract,
    modulation,
    patch_table,
    condition,
    moment_attend_in,
    moment_attend_out,
    moment_expand,
    moment_contract,
    moment_modulation,
    moment_patch,
    moment_condition,
    second_attend_in,
    second_attend_out,
    second_expand,
    second_contract,
    second_modulation,
    second_patch,
    second_condition,
    average_attend_in,
    average_attend_out,
    average_expand,
    average_contract,
    average_modulation,
    average_patch,
    average_condition,
):
    batch, length = (patches.shape[0], patches.shape[1])
    capacity = kept_slots.shape[1]
    local = attend_in.shape[3]
    wide_index = lax.axis_index("wide")
    narrow_index = lax.axis_index("narrow")
    images = batch * lax.axis_size("wide")
    leader = (narrow_index == 0).astype(jnp.float32)
    stacks = (attend_in, attend_out, expand, contract, modulation)
    patch_full, cond_full = (
        lax.all_gather(patch_table.astype(jnp.bfloat16), "narrow", axis=1, tiled=True),
        lax.all_gather(condition.astype(jnp.bfloat16), "narrow", axis=1, tiled=True),
    )
    width = patch_full.shape[1]
    slot_valid = (jnp.arange(capacity)[None, :] < kept_count[:, None]).astype(jnp.float32)
    select = (kept_slots[:, :, None] == jnp.arange(length)[None, None, :]).astype(
        jnp.float32
    ) * slot_valid[:, :, None]
    kept_place = jnp.sum(select, 1)
    places = sinusoid(jnp.arange(length), width)
    features = sinusoid(time_step, FREQ)
    onehot = (labels[:, None] == jnp.arange(CLASSES)[None, :]).astype(jnp.float32)
    cond_sum = jnp.dot(
        features, cond_full[:FREQ].astype(jnp.float32), precision=highest_float_accuracy
    )
    cond_sum = cond_sum + jnp.dot(
        onehot.astype(jnp.bfloat16), cond_full[FREQ:], preferred_element_type=jnp.float32
    )
    silu_back = jax.vjp(jax.nn.silu, cond_sum)[1]
    sigmoid_linear_narrow = jax.nn.silu(cond_sum).astype(jnp.bfloat16)
    collected_rows = [fetch(stacks, 0), fetch(stacks, 1)]
    shift_scale_gate_factors = []
    for lookup_index in range(2):
        slice_part = jnp.einsum(
            "ip,pkc->ikc",
            sigmoid_linear_narrow,
            collected_rows[lookup_index][4],
            preferred_element_type=jnp.float32,
        )
        shift_scale_gate_factors.append(lax.all_gather(slice_part, "narrow", axis=2, tiled=True))
    kept_patches = jnp.einsum(
        "bcl,blp->bcp", select.astype(jnp.bfloat16), patches, preferred_element_type=jnp.float32
    )
    embed = jnp.einsum(
        "bcp,pd->bcd",
        kept_patches.astype(jnp.bfloat16),
        patch_full[:PATCH_IN],
        preferred_element_type=jnp.float32,
    )
    embed = embed + jnp.einsum("bcl,ld->bcd", select, places, precision=highest_float_accuracy)
    encoded, saved_enc = block_forward(
        embed, shift_scale_gate_factors[0], slot_valid, collected_rows[0][:4]
    )
    counts = kept_count.astype(jnp.float32)[:, None]

    def pool_unit(values):
        pooled = jnp.sum(values * slot_valid[:, :, None], 1) / counts
        return pooled * lax.rsqrt(jnp.sum(pooled * pooled, -1, keepdims=True) + 1e-06)

    normalised_direction, pool_back = jax.vjp(pool_unit, encoded)
    negatives = lax.all_gather(teacher, "wide", axis=0, tiled=True)
    frozen_target_direction = negatives * lax.rsqrt(
        jnp.sum(negatives * negatives, -1, keepdims=True) + 1e-06
    )
    cosine_match_scores = (
        jnp.dot(normalised_direction, frozen_target_direction.T, precision=highest_float_accuracy)
        / contrast_sharpness_divisor
    )
    peak = jnp.max(cosine_match_scores, -1, keepdims=True)
    expo = jnp.exp(cosine_match_scores - peak)
    total = jnp.sum(expo, -1, keepdims=True)
    positive = (
        (wide_index * batch + jnp.arange(batch))[:, None] == jnp.arange(images)[None, :]
    ).astype(jnp.float32)
    nce_local = jnp.sum(
        peak[:, 0] + jnp.log(total[:, 0]) - jnp.sum(cosine_match_scores * positive, -1)
    )
    derivative_of_raw_scores = (expo / total - positive) * (nce_weight / images)
    unit_vector_gradient = (
        jnp.dot(derivative_of_raw_scores, frozen_target_direction, precision=highest_float_accuracy)
        / contrast_sharpness_divisor
    )
    grad_pool = pool_back(unit_vector_gradient)[0]
    mask_token = patch_full[2 * PATCH_IN].astype(jnp.float32)
    decode_in = jnp.einsum("bcl,bcd->bld", select, encoded, precision=highest_float_accuracy)
    decode_in = decode_in + (1.0 - kept_place)[:, :, None] * mask_token + places[None]
    all_keys = jnp.ones((batch, length), jnp.float32)
    decoded, saved_dec = block_forward(
        decode_in, shift_scale_gate_factors[1], all_keys, collected_rows[1][:4]
    )
    final, final_back = jax.vjp(layer_norm, decoded)
    final_low = final.astype(jnp.bfloat16)
    head = patch_full[PATCH_IN : 2 * PATCH_IN]
    predict = jnp.einsum("bld,pd->blp", final_low, head, preferred_element_type=jnp.float32)
    error_map = predict - target_noise
    count_all = images * length * PATCH_IN
    mse_local = jnp.sum(error_map * error_map)
    loss_terms = (mse_local * leader, nce_local * leader)
    loss_sums = lax.psum((loss_terms[0], loss_terms[1]), ("wide", "narrow"))
    grad_predict = (error_map * (2.0 / count_all)).astype(jnp.bfloat16)
    grad_head = jnp.einsum(
        "blp,bld->pd", grad_predict, final_low, preferred_element_type=jnp.float32
    )
    grad_final = jnp.einsum("blp,pd->bld", grad_predict, head, preferred_element_type=jnp.float32)
    grad_decoded = final_back(grad_final)[0]
    weights_dec = collected_rows[1]
    grad_dec_in, grad_mod_dec, grads_dec = block_backward(
        grad_decoded, shift_scale_gate_factors[1], all_keys, weights_dec[:4], saved_dec
    )
    grad_mask = jnp.sum((1.0 - kept_place)[:, :, None] * grad_dec_in, (0, 1))
    grad_encoded = (
        jnp.einsum("bcl,bld->bcd", select, grad_dec_in, precision=highest_float_accuracy)
        + grad_pool
    )
    weights_enc = collected_rows[0]
    grad_embed, grad_mod_enc, grads_enc = block_backward(
        grad_encoded, shift_scale_gate_factors[0], slot_valid, weights_enc[:4], saved_enc
    )
    grad_patch = jnp.einsum(
        "bcp,bcd->pd", kept_patches, grad_embed, precision=highest_float_accuracy
    )
    sigmoid_linear_broad = sigmoid_linear_narrow.astype(jnp.float32)
    grad_silu = jnp.zeros_like(cond_sum)
    block_grads = []
    for grad_mod, weight_tensors, grads in (
        (grad_mod_enc, weights_enc, grads_enc),
        (grad_mod_dec, weights_dec, grads_dec),
    ):
        slice_part = lax.dynamic_slice_in_dim(grad_mod, narrow_index * local, local, 2)
        table_gradient = jnp.einsum(
            "kt,kyg->tyg", sigmoid_linear_broad, slice_part, precision=highest_float_accuracy
        )
        grad_silu = grad_silu + jnp.einsum(
            "jwy,vwy->jv",
            slice_part,
            weight_tensors[4].astype(jnp.float32),
            precision=highest_float_accuracy,
        )
        block_grads.append(
            (
                lax.psum_scatter(
                    grads[0].astype(jnp.bfloat16), "wide", scatter_dimension=0, tiled=True
                ).astype(jnp.float32),
                lax.psum_scatter(
                    grads[1].astype(jnp.bfloat16), "wide", scatter_dimension=1, tiled=True
                ).astype(jnp.float32),
                lax.psum_scatter(
                    grads[2].astype(jnp.bfloat16), "wide", scatter_dimension=0, tiled=True
                ).astype(jnp.float32),
                lax.psum_scatter(
                    grads[3].astype(jnp.bfloat16), "wide", scatter_dimension=1, tiled=True
                ).astype(jnp.float32),
                lax.psum_scatter(
                    table_gradient.astype(jnp.bfloat16), "wide", scatter_dimension=0, tiled=True
                ).astype(jnp.float32),
            )
        )
    grad_silu = narrow_sum(grad_silu)
    grad_cond = silu_back(grad_silu)[0]
    grad_condition = jnp.concatenate(
        [
            jnp.dot(features.T, grad_cond, precision=highest_float_accuracy),
            jnp.dot(onehot.T, grad_cond, precision=highest_float_accuracy),
        ],
        0,
    )
    grad_table_all = jnp.concatenate([grad_patch, grad_head, grad_mask[None, :]], 0)
    small_pieces = (
        lax.dynamic_slice_in_dim(grad_table_all, narrow_index * local, local, 1),
        lax.dynamic_slice_in_dim(grad_condition, narrow_index * local, local, 1),
    )
    grad_patch_table, grad_cond_table = (
        lax.psum(small_pieces[0].astype(jnp.bfloat16), "wide").astype(jnp.float32),
        lax.psum(small_pieces[1].astype(jnp.bfloat16), "wide").astype(jnp.float32),
    )
    grads = [
        jnp.stack([block_grads[0][lookup_index], block_grads[1][lookup_index]])
        for lookup_index in range(5)
    ]
    grads = grads + [grad_patch_table, grad_cond_table]
    square_big = jnp.float32(0.0)
    for grad in grads[:5]:
        square_big = square_big + jnp.sum(grad * grad)
    square_small = jnp.sum(grad_patch_table * grad_patch_table) + jnp.sum(
        grad_cond_table * grad_cond_table
    )
    square_local = square_big + (wide_index == 0).astype(jnp.float32) * square_small
    squares = lax.psum(square_local, ("wide", "narrow"))
    grad_norm = jnp.sqrt(squares)
    factor = clip_norm / jnp.maximum(grad_norm, clip_norm)
    params = (attend_in, attend_out, expand, contract, modulation, patch_table, condition)
    moments = (
        moment_attend_in,
        moment_attend_out,
        moment_expand,
        moment_contract,
        moment_modulation,
        moment_patch,
        moment_condition,
    )
    seconds = (
        second_attend_in,
        second_attend_out,
        second_expand,
        second_contract,
        second_modulation,
        second_patch,
        second_condition,
    )
    averages = (
        average_attend_in,
        average_attend_out,
        average_expand,
        average_contract,
        average_modulation,
        average_patch,
        average_condition,
    )
    fresh = [
        adam(
            params[lookup_index],
            grads[lookup_index],
            moments[lookup_index],
            seconds[lookup_index],
            averages[lookup_index],
            factor,
        )
        for lookup_index in range(7)
    ]
    loss_parts = jnp.stack([loss_sums[0] / count_all, loss_sums[1] / images])
    return (
        loss_parts,
        grad_norm,
        fresh[0][0],
        fresh[1][0],
        fresh[2][0],
        fresh[3][0],
        fresh[4][0],
        fresh[5][0],
        fresh[6][0],
        fresh[0][1],
        fresh[1][1],
        fresh[2][1],
        fresh[3][1],
        fresh[4][1],
        fresh[5][1],
        fresh[6][1],
        fresh[0][2],
        fresh[1][2],
        fresh[2][2],
        fresh[3][2],
        fresh[4][2],
        fresh[5][2],
        fresh[6][2],
        fresh[0][3],
        fresh[1][3],
        fresh[2][3],
        fresh[3][3],
        fresh[4][3],
        fresh[5][3],
        fresh[6][3],
    )


def solution(mesh):
    in_specs = (
        P("wide", None, None),
        P("wide", None, None),
        P("wide", None),
        P("wide"),
        P("wide"),
        P("wide"),
        P("wide", None),
        P(None, "wide", None, "narrow"),
        P(None, "narrow", "wide"),
        P(None, "wide", "narrow"),
        P(None, "narrow", "wide"),
        P(None, "wide", None, "narrow"),
        P(None, "narrow"),
        P(None, "narrow"),
        P(None, "wide", None, "narrow"),
        P(None, "narrow", "wide"),
        P(None, "wide", "narrow"),
        P(None, "narrow", "wide"),
        P(None, "wide", None, "narrow"),
        P(None, "narrow"),
        P(None, "narrow"),
        P(None, "wide", None, "narrow"),
        P(None, "narrow", "wide"),
        P(None, "wide", "narrow"),
        P(None, "narrow", "wide"),
        P(None, "wide", None, "narrow"),
        P(None, "narrow"),
        P(None, "narrow"),
        P(None, "wide", None, "narrow"),
        P(None, "narrow", "wide"),
        P(None, "wide", "narrow"),
        P(None, "narrow", "wide"),
        P(None, "wide", None, "narrow"),
        P(None, "narrow"),
        P(None, "narrow"),
    )
    out_specs = (
        P(),
        P(),
        P(None, "wide", None, "narrow"),
        P(None, "narrow", "wide"),
        P(None, "wide", "narrow"),
        P(None, "narrow", "wide"),
        P(None, "wide", None, "narrow"),
        P(None, "narrow"),
        P(None, "narrow"),
        P(None, "wide", None, "narrow"),
        P(None, "narrow", "wide"),
        P(None, "wide", "narrow"),
        P(None, "narrow", "wide"),
        P(None, "wide", None, "narrow"),
        P(None, "narrow"),
        P(None, "narrow"),
        P(None, "wide", None, "narrow"),
        P(None, "narrow", "wide"),
        P(None, "wide", "narrow"),
        P(None, "narrow", "wide"),
        P(None, "wide", None, "narrow"),
        P(None, "narrow"),
        P(None, "narrow"),
        P(None, "wide", None, "narrow"),
        P(None, "narrow", "wide"),
        P(None, "wide", "narrow"),
        P(None, "narrow", "wide"),
        P(None, "wide", None, "narrow"),
        P(None, "narrow"),
        P(None, "narrow"),
    )
    return jax.shard_map(shards, mesh=mesh, in_specs=in_specs, out_specs=out_specs, check_vma=False)
```

profile of v0, /device:TPU:0, one launch (start us, length us, event | category | flops | bytes accessed | tf_op | source)
XLA Modules:
  0.0 1823.3 jit_solution(16808277263575324066)
XLA Ops:
  13.5 15.7 all-gather.10
  30.1 11.8 all-gather.2
  49.9 24.1 %all-gather.22.cloned.1.call-done = bf16[1256,1152]{0,1:T(8,128)(2,1)} async-done(((bf16[1256,288]{0,1:T(8,128)(2,1)}), bf16[1256,1152]{0,1:T(8,128)(2,1)}) %all-gather.22.cloned.1.call-update) | async-done | bytes 2893840 | tf_op jit(solution)/shard_map/all_gather | solution.py:264
  78.7 38.0 %all-gather.24.cloned.1.call-done = bf16[1,1152,6,288]{3,1,2,0:T(8,128)(2,1)} async-done(((bf16[1,144,6,288]{3,1,2,0:T(8,128)(2,1)}), bf16[1,1152,6,288]{3,1,2,0:T(8,128)(2,1)}) %all-gather.24.cloned.1.call-update) | async-done | bytes 3981328 | tf_op jit(solution)/shard_map/all_gather | solution.py:55
  120.3 42.6 %all_gather.48 = f32[4,6,1152]{1,0,2:T(4,128)S(1)} all-gather(f32[4,6,288]{1,0,2:T(4,128)S(1)} %copy.265), channel_id=1, replica_groups=mesh['wide'=8,'narrow'=4] {'narrow'}, dimensions={2}, use_global_device_ids=true | all-gather | bytes 138240 | tf_op jit(solution)/shard_map/all_gather | solution.py:292
  162.9 9.2 fusion.264
  199.5 57.4 %all-reduce.11.cloned.1.call-done = bf16[4,160,1152]{2,1,0:T(8,128)(2,1)} async-done(((bf16[4,160,1152]{2,1,0:T(8,128)(2,1)}), bf16[4,160,1152]{2,1,0:T(8,128)(2,1)}) %all-reduce.11.cloned.1.call-update) | async-done | bytes 1474576 | tf_op jit(solution)/shard_map/psum | solution.py:46
  260.1 28.6 %all-gather.28.cloned.1.call-done = bf16[1,1152,1152]{2,1,0:T(8,128)(2,1)} async-done(((bf16[1,144,1152]{2,1,0:T(8,128)(2,1)}), bf16[1,1152,1152]{2,1,0:T(8,128)(2,1)}) %all-gather.28.cloned.1.call-update) | async-done | bytes 2654224 | tf_op jit(solution)/shard_map/all_gather | solution.py:53
  288.7 5.7 fusion.77
  294.5 27.0 %all-gather.30.cloned.1.call-done = bf16[1,1152,1152]{1,2,0:T(8,128)(2,1)} async-done(((bf16[1,1152,144]{1,2,0:T(8,128)(2,1)}), bf16[1,1152,1152]{1,2,0:T(8,128)(2,1)}) %all-gather.30.cloned.1.call-update) | async-done | bytes 2654224 | tf_op jit(solution)/shard_map/all_gather | solution.py:54
  321.5 6.5 convolution_convert_fusion.6
  330.3 16.1 all-gather.7
  347.0 22.0 %all-gather.32.cloned.1.call-done = bf16[1,1152,6,288]{3,1,2,0:T(8,128)(2,1)} async-done(((bf16[1,144,6,288]{3,1,2,0:T(8,128)(2,1)}), bf16[1,1152,6,288]{3,1,2,0:T(8,128)(2,1)}) %all-gather.32.cloned.1.call-update) | async-done | bytes 3981328 | tf_op jit(solution)/shard_map/all_gather | solution.py:55
  374.0 69.8 %all_gather.54 = f32[4,6,1152]{1,0,2:T(4,128)S(1)} all-gather(f32[4,6,288]{1,0,2:T(4,128)S(1)} %copy.281), channel_id=1, replica_groups=mesh['wide'=8,'narrow'=4] {'narrow'}, dimensions={2}, use_global_device_ids=true | all-gather | bytes 138240 | tf_op jit(solution)/shard_map/all_gather | solution.py:292
  443.8 9.1 fusion.263
  459.6 5.4 all-reduce.13.cloned.1.call-done
  465.1 7.3 fusion.275
  475.8 20.5 %all-gather.34.cloned.1.call-done = bf16[1,1152,3,288]{3,1,2,0:T(8,128)(2,1)} async-done(((bf16[1,144,3,288]{3,1,2,0:T(8,128)(2,1)}), bf16[1,1152,3,288]{3,1,2,0:T(8,128)(2,1)}) %all-gather.34.cloned.1.call-update) | async-done | bytes 1990672 | tf_op jit(solution)/shard_map/all_gather | solution.py:51
  496.3 6.1 fusion.110
  521.0 84.9 %all-reduce.15.cloned.1.call-done = bf16[4,256,1152]{2,1,0:T(8,128)(2,1)} async-done(((bf16[4,256,1152]{2,1,0:T(8,128)(2,1)}), bf16[4,256,1152]{2,1,0:T(8,128)(2,1)}) %all-reduce.15.cloned.1.call-update) | async-done | bytes 2359312 | tf_op jit(solution)/shard_map/psum | solution.py:46
  613.1 24.7 %all-gather.36.cloned.1.call-done = bf16[1,1152,1152]{2,1,0:T(8,128)(2,1)} async-done(((bf16[1,144,1152]{2,1,0:T(8,128)(2,1)}), bf16[1,1152,1152]{2,1,0:T(8,128)(2,1)}) %all-gather.36.cloned.1.call-update) | async-done | bytes 2654224 | tf_op jit(solution)/shard_map/all_gather | solution.py:53
  637.7 9.0 fusion.74
  646.7 23.6 %all-gather.38.cloned.1.call-done = bf16[1,1152,1152]{1,2,0:T(8,128)(2,1)} async-done(((bf16[1,1152,144]{1,2,0:T(8,128)(2,1)}), bf16[1,1152,1152]{1,2,0:T(8,128)(2,1)}) %all-gather.38.cloned.1.call-update) | async-done | bytes 2654224 | tf_op jit(solution)/shard_map/all_gather | solution.py:54
  670.3 8.8 convolution_convert_fusion.4
  682.3 92.6 %all-reduce.17.cloned.1.call-done = bf16[4,256,1152]{2,1,0:T(8,128)(2,1)} async-done(((bf16[4,256,1152]{2,1,0:T(8,128)(2,1)}), bf16[4,256,1152]{2,1,0:T(8,128)(2,1)}) %all-reduce.17.cloned.1.call-update) | async-done | bytes 2359312 | tf_op jit(solution)/shard_map/psum | solution.py:46
  784.7 5.2 fusion.29
  791.3 4.8 convolution_convert_fusion.3
  797.5 93.5 %all-reduce.19.cloned.1.call-done = bf16[4,256,1152]{2,1,0:T(8,128)(2,1)} async-done(((bf16[4,256,1152]{2,1,0:T(8,128)(2,1)}), bf16[4,256,1152]{2,1,0:T(8,128)(2,1)}) %all-reduce.19.cloned.1.call-update) | async-done | bytes 2359312 | tf_op jit(solution)/shard_map/psum | solution.py:46
  895.2 4.9 fusion.30
  900.1 5.3 fusion.22
  914.7 5.0 bitcast_convert_fusion.2
  919.8 9.2 all-gather.11
  933.2 81.3 %all-reduce.21.cloned.1.call-done = bf16[4,256,1152]{2,1,0:T(8,128)(2,1)} async-done(((bf16[4,256,1152]{2,1,0:T(8,128)(2,1)}), bf16[4,256,1152]{2,1,0:T(8,128)(2,1)}) %all-reduce.21.cloned.1.call-update) | async-done | bytes 2359312 | tf_op jit(solution)/shard_map/psum | solution.py:46
  1022.3 7.5 convolution_add_fusion.1
  1037.9 64.9 %all-reduce.23.cloned.1.call-done = bf16[4,160,1152]{2,1,0:T(8,128)(2,1)} async-done(((bf16[4,160,1152]{2,1,0:T(8,128)(2,1)}), bf16[4,160,1152]{2,1,0:T(8,128)(2,1)}) %all-reduce.23.cloned.1.call-update) | async-done | bytes 1474576 | tf_op jit(solution)/shard_map/psum | solution.py:46
  1126.6 5.7 fusion.37
  1132.4 4.7 fusion.58
  1137.3 7.9 multiply_reduce_fusion
  1151.3 46.1 %all-reduce.25.cloned.1.call-done = bf16[4,160,1152]{2,1,0:T(8,128)(2,1)} async-done(((bf16[4,160,1152]{2,1,0:T(8,128)(2,1)}), bf16[4,160,1152]{2,1,0:T(8,128)(2,1)}) %all-reduce.25.cloned.1.call-update) | async-done | bytes 1474576 | tf_op jit(solution)/shard_map/psum | solution.py:46
  1204.3 6.8 fusion.89
  1211.2 5.0 fusion.98
  1216.2 10.4 psum.109
  1231.0 8.9 fusion.3
  1240.0 6.8 fusion.2
  1247.3 8.3 fusion.1
  1255.7 5.6 fusion
  1261.4 8.1 bitcast_convert_fusion
  1269.7 5.5 bitcast_convert_fusion.1
  1275.4 7.0 convolution_convert_fusion
  1282.5 7.0 convolution_convert_fusion.1
  1297.0 4.2 fusion.83
  1301.5 22.6 %psum.108 = bf16[33,288]{1,0:T(8,128)(2,1)S(1)} all-reduce(bf16[33,288]{1,0:T(8,128)(2,1)S(1)} %fusion.188), channel_id=1, replica_groups=mesh['wide'=8,'narrow'=4] {'wide'}, use_global_device_ids=true, to_apply=%region_74.75 | all-reduce | flops 9504 | bytes 38016 | tf_op jit(solution)/shard_map/psum | solution.py:425
  1324.6 8.2 all-reduce.27.cloned.1.call-done
  1336.2 44.1 %reduce-scatter.25.cloned.1.call-done = bf16[1152,144]{0,1:T(8,128)(2,1)} async-done(((bf16[1152,1152]{0,1:T(8,128)(2,1)}), bf16[1152,144]{0,1:T(8,128)(2,1)}) %reduce-scatter.25.cloned.1.call-update) | async-done | bytes 331792 | tf_op jit(solution)/shard_map/reduce_scatter | solution.py:402
  1380.3 47.7 %reduce-scatter.23.cloned.1.call-done = bf16[1152,144]{0,1:T(8,128)(2,1)} async-done(((bf16[1152,1152]{0,1:T(8,128)(2,1)}), bf16[1152,144]{0,1:T(8,128)(2,1)}) %reduce-scatter.23.cloned.1.call-update) | async-done | bytes 331792 | tf_op jit(solution)/shard_map/reduce_scatter | solution.py:402
  1430.0 45.8 %reduce-scatter.21.cloned.1.call-done = bf16[144,1152]{1,0:T(8,128)(2,1)} async-done(((bf16[1152,1152]{1,0:T(8,128)(2,1)}), bf16[144,1152]{1,0:T(8,128)(2,1)}) %reduce-scatter.21.cloned.1.call-update) | async-done | bytes 331792 | tf_op jit(solution)/shard_map/reduce_scatter | solution.py:399
  1475.9 48.1 %reduce-scatter.19.cloned.1.call-done = bf16[144,1152]{1,0:T(8,128)(2,1)} async-done(((bf16[1152,1152]{1,0:T(8,128)(2,1)}), bf16[144,1152]{1,0:T(8,128)(2,1)}) %reduce-scatter.19.cloned.1.call-update) | async-done | bytes 331792 | tf_op jit(solution)/shard_map/reduce_scatter | solution.py:399
  1526.0 45.8 %reduce-scatter.13.cloned.1.call-done = bf16[144,3,288]{2,0,1:T(8,128)(2,1)} async-done(((bf16[1152,3,288]{2,0,1:T(8,128)(2,1)}), bf16[144,3,288]{2,0,1:T(8,128)(2,1)}) %reduce-scatter.13.cloned.1.call-update) | async-done | bytes 248848 | tf_op jit(solution)/shard_map/reduce_scatter | solution.py:393
  1571.8 48.1 %reduce-scatter.11.cloned.1.call-done = bf16[144,3,288]{2,0,1:T(8,128)(2,1)} async-done(((bf16[1152,3,288]{2,0,1:T(8,128)(2,1)}), bf16[144,3,288]{2,0,1:T(8,128)(2,1)}) %reduce-scatter.11.cloned.1.call-update) | async-done | bytes 248848 | tf_op jit(solution)/shard_map/reduce_scatter | solution.py:393
  1624.7 55.9 %reduce-scatter.29.cloned.1.call-done = bf16[144,6,288]{2,0,1:T(8,128)(2,1)} async-done(((bf16[1152,6,288]{2,0,1:T(8,128)(2,1)}), bf16[144,6,288]{2,0,1:T(8,128)(2,1)}) %reduce-scatter.29.cloned.1.call-update) | async-done | bytes 497680 | tf_op jit(solution)/shard_map/reduce_scatter | solution.py:405
  1680.6 60.8 %reduce-scatter.27.cloned.1.call-done = bf16[144,6,288]{2,0,1:T(8,128)(2,1)} async-done(((bf16[1152,6,288]{2,0,1:T(8,128)(2,1)}), bf16[144,6,288]{2,0,1:T(8,128)(2,1)}) %reduce-scatter.27.cloned.1.call-update) | async-done | bytes 497680 | tf_op jit(solution)/shard_map/reduce_scatter | solution.py:405
  1744.6 39.6 %all-reduce = (f32[]{:T(128)}, f32[]{:T(128)}, f32[]{:T(128)}) all-reduce(f32[]{:T(128)S(6)} %mul.1137, f32[]{:T(128)S(6)} %mul.1126, f32[]{:T(128)S(6)} %add.500), channel_id=1, replica_groups=mesh['wide'=8,'narrow'=4] {'wide','narrow'}, use_global_device_ids=true, to_apply=%region_28.29 | all-reduce | flops 3 | bytes 24 | tf_op jit(solution)/shard_map/psum | solution.py:351
  1790.1 5.5 multiply_add_fusion.2
  1806.1 5.4 multiply_add_fusion
  (669 shorter events, 223.0 us)
Async XLA Ops:
  7.2 37.3 %copy-start = (bf16[4,256,16]{1,2,0:T(8,128)(2,1)S(1)}, bf16[4,256,16]{1,2,0:T(8,128)(2,1)}, u32[]{:S(2)}) copy-start(bf16[4,256,16]{1,2,0:T(8,128)(2,1)} %param.35) | copy-start | bytes 98308
  7.2 66.8 %all-gather.22.cloned.1.call-start = ((), (), s32[]{:S(2)}) async-start(), calls=%async_computation.10 | async-start | bytes 3686400 | tf_op jit(solution)/shard_map/all_gather | solution.py:264
  9.8 106.9 %all-gather.24.cloned.1.call-start = ((), (), s32[]{:S(2)}) async-start(), calls=%async_computation.30 | async-start | bytes 5971968 | tf_op jit(solution)/shard_map/all_gather | solution.py:55
  11.2 165.3 %all-gather.26.cloned.1.call-start = ((), (), s32[]{:S(2)}) async-start(), calls=%async_computation.31 | async-start | bytes 2985984 | tf_op jit(solution)/shard_map/all_gather | solution.py:51
  12.8 244.0 %all-reduce.11.cloned.1.call-start = ((), (), s32[]{:S(2)}) async-start(), calls=%async_computation.11 | async-start | bytes 2949120 | tf_op jit(solution)/shard_map/psum | solution.py:46
  13.5 451.5 %copy-start.113 = (f32[4,160]{1,0:T(4,128)}, f32[4,160]{1,0:T(4,128)S(1)}, u32[]{:S(2)}) copy-start(f32[4,160]{1,0:T(4,128)S(1)} %get-tuple-element.246) | copy-start | bytes 7684
  49.4 127.2 %copy-start.126 = (f32[4,160]{1,0:T(4,128)}, f32[4,160]{1,0:T(4,128)S(1)}, u32[]{:S(2)}) copy-start(f32[4,160]{1,0:T(4,128)S(1)} %broadcast_multiply_fusion.4) | copy-start | bytes 7684
  49.8 126.7 %copy-start.166 = (f32[4,160]{1,0:T(4,128)}, f32[4,160]{1,0:T(4,128)S(1)}, u32[]{:S(2)}) copy-start(f32[4,160]{1,0:T(4,128)S(1)} %fusion.207) | copy-start | bytes 7684
  78.7 290.3 %copy-start.105 = (bf16[4,1152,1]{1,0,2:T(4,128)(2,1)}, bf16[4,1152,1]{1,0,2:T(4,128)(2,1)S(1)}, u32[]{:S(2)}) copy-start(bf16[4,1152,1]{1,0,2:T(4,128)(2,1)S(1)} %fusion.201) | copy-start | bytes 27652
  190.0 98.7 %all-gather.28.cloned.1.call-start = ((), (), s32[]{:S(2)}) async-start(), calls=%async_computation.32 | async-start | bytes 2985984 | tf_op jit(solution)/shard_map/all_gather | solution.py:53
  191.0 130.4 %all-gather.30.cloned.1.call-start = ((), (), s32[]{:S(2)}) async-start(), calls=%async_computation.33 | async-start | bytes 2985984 | tf_op jit(solution)/shard_map/all_gather | solution.py:54
  192.5 176.5 %all-gather.32.cloned.1.call-start = ((), (), s32[]{:S(2)}) async-start(), calls=%async_computation.34 | async-start | bytes 5971968 | tf_op jit(solution)/shard_map/all_gather | solution.py:55
  193.2 271.8 %all-reduce.13.cloned.1.call-start = ((), (), s32[]{:S(2)}) async-start(), calls=%async_computation.12 | async-start | bytes 2949120 | tf_op jit(solution)/shard_map/psum | solution.py:46
  195.8 92.9 %copy-start.187 = (f32[4,1,1152]{2,0,1:T(4,128)}, f32[4,1,1152]{2,0,1:T(4,128)S(1)}, u32[]{:S(2)}) copy-start(f32[4,1,1152]{2,0,1:T(4,128)S(1)} %copy.278) | copy-start | bytes 55300
  199.4 60.1 %copy-start.110 = (f32[4,1,1152]{2,0,1:T(4,128)}, f32[4,1,1152]{2,0,1:T(4,128)S(1)}, u32[]{:S(2)}) copy-start(f32[4,1,1152]{2,0,1:T(4,128)S(1)} %copy.266) | copy-start | bytes 55300
  199.5 89.2 %copy-start.99 = (f32[4,1152]{1,0:T(4,128)}, f32[4,1152]{1,0:T(4,128)S(1)}, u32[]{:S(2)}) copy-start(f32[4,1152]{1,0:T(4,128)S(1)} %add_bitcast_fusion.2) | copy-start | bytes 55300
  294.5 35.6 %copy-start.142 = (s32[4,160]{1,0:T(4,128)S(1)}, s32[4,160]{1,0:T(4,128)}, u32[]{:S(2)}) copy-start(s32[4,160]{1,0:T(4,128)} %param.37) | copy-start | bytes 7684
  294.5 35.8 %copy-start.86 = (bf16[1,288,144]{1,2,0:T(8,128)(2,1)S(1)}, bf16[1,288,144]{1,2,0:T(8,128)(2,1)}, u32[]{:S(2)}) copy-start(bf16[1,288,144]{1,2,0:T(8,128)(2,1)} %get-tuple-element.237) | copy-start | bytes 248836
  327.9 168.4 %all-gather.34.cloned.1.call-start = ((), (), s32[]{:S(2)}) async-start(), calls=%async_computation.35 | async-start | bytes 2985984 | tf_op jit(solution)/shard_map/all_gather | solution.py:51
  328.7 277.3 %all-reduce.15.cloned.1.call-start = ((), (), s32[]{:S(2)}) async-start(), calls=%async_computation.13 | async-start | bytes 4718592 | tf_op jit(solution)/shard_map/psum | solution.py:46
  457.2 39.1 %copy-start.188 = (f32[4,1,1152]{2,0,1:T(4,128)}, f32[4,1,1152]{2,0,1:T(4,128)S(1)}, u32[]{:S(2)}) copy-start(f32[4,1,1152]{2,0,1:T(4,128)S(1)} %copy.284) | copy-start | bytes 55300
  459.6 36.7 %copy-start.84 = (f32[4,1152]{1,0:T(4,128)}, f32[4,1152]{1,0:T(4,128)S(1)}, u32[]{:S(2)}) copy-start(f32[4,1152]{1,0:T(4,128)S(1)} %add_bitcast_fusion.1) | copy-start | bytes 55300
  510.1 127.6 %all-gather.36.cloned.1.call-start = ((), (), s32[]{:S(2)}) async-start(), calls=%async_computation.36 | async-start | bytes 2985984 | tf_op jit(solution)/shard_map/all_gather | solution.py:53
  510.9 159.4 %all-gather.38.cloned.1.call-start = ((), (), s32[]{:S(2)}) async-start(), calls=%async_computation.37 | async-start | bytes 2985984 | tf_op jit(solution)/shard_map/all_gather | solution.py:54
  511.5 263.4 %all-reduce.17.cloned.1.call-start = ((), (), s32[]{:S(2)}) async-start(), calls=%async_computation.14 | async-start | bytes 4718592 | tf_op jit(solution)/shard_map/psum | solution.py:46
  609.7 37.0 %copy-start.123 = (f32[4,256]{1,0:T(4,128)}, f32[4,256]{1,0:T(4,128)S(1)}, u32[]{:S(2)}) copy-start(f32[4,256]{1,0:T(4,128)S(1)} %broadcast_multiply_fusion.1) | copy-start | bytes 12292
  679.1 211.9 %all-reduce.19.cloned.1.call-start = ((), (), s32[]{:S(2)}) async-start(), calls=%async_computation.15 | async-start | bytes 4718592 | tf_op jit(solution)/shard_map/psum | solution.py:46
  796.2 218.4 %all-reduce.21.cloned.1.call-start = ((), (), s32[]{:S(2)}) async-start(), calls=%async_computation.16 | async-start | bytes 4718592 | tf_op jit(solution)/shard_map/psum | solution.py:46
  919.7 94.8 %copy-start.85 = (f32[4,1152]{1,0:T(4,128)S(1)}, f32[4,1152]{1,0:T(4,128)}, u32[]{:S(2)}) copy-start(f32[4,1152]{1,0:T(4,128)} %copy-done.84) | copy-start | bytes 55300
  919.7 94.8 %copy-start.116 = (f32[4,256]{1,0:T(4,128)S(1)}, f32[4,256]{1,0:T(4,128)}, u32[]{:S(2)}) copy-start(f32[4,256]{1,0:T(4,128)} %copy-done.115) | copy-start | bytes 12292
  919.8 183.1 %all-reduce.23.cloned.1.call-start = ((), (), s32[]{:S(2)}) async-start(), calls=%async_computation.17 | async-start | bytes 2949120 | tf_op jit(solution)/shard_map/psum | solution.py:46
  933.2 85.5 %copy-start.177 = (f32[4,256]{1,0:T(4,128)S(1)}, f32[4,256]{1,0:T(4,128)}, u32[]{:S(2)}) copy-start(f32[4,256]{1,0:T(4,128)} %copy-done.176) | copy-start | bytes 12292
  933.2 85.5 %copy-start.149 = (f32[4,256]{1,0:T(4,128)S(1)}, f32[4,256]{1,0:T(4,128)}, u32[]{:S(2)}) copy-start(f32[4,256]{1,0:T(4,128)} %copy-done.148) | copy-start | bytes 12292
  1034.4 68.5 %copy-start.100 = (f32[4,1152]{1,0:T(4,128)S(1)}, f32[4,1152]{1,0:T(4,128)}, u32[]{:S(2)}) copy-start(f32[4,1152]{1,0:T(4,128)} %copy-done.99) | copy-start | bytes 55300
  1034.4 68.5 %copy-start.129 = (f32[4,160]{1,0:T(4,128)S(1)}, f32[4,160]{1,0:T(4,128)}, u32[]{:S(2)}) copy-start(f32[4,160]{1,0:T(4,128)} %copy-done.128) | copy-start | bytes 7684
  1037.8 67.2 %copy-start.175 = (f32[4,160]{1,0:T(4,128)S(1)}, f32[4,160]{1,0:T(4,128)}, u32[]{:S(2)}) copy-start(f32[4,160]{1,0:T(4,128)} %copy-done.174) | copy-start | bytes 7684
  1037.8 67.3 %copy-start.170 = (f32[4,160]{1,0:T(4,128)S(1)}, f32[4,160]{1,0:T(4,128)}, u32[]{:S(2)}) copy-start(f32[4,160]{1,0:T(4,128)} %copy-done.169) | copy-start | bytes 7684
  1037.8 159.6 %all-reduce.25.cloned.1.call-start = ((), (), s32[]{:S(2)}) async-start(), calls=%async_computation.26 | async-start | bytes 2949120 | tf_op jit(solution)/shard_map/psum | solution.py:46
  1132.2 163.0 %reduce-scatter.17.cloned.1.call-start = ((), (), s32[]{:S(2)}) async-start(), calls=%async_computation.21 | async-start | bytes 995328 | tf_op jit(solution)/shard_map/reduce_scatter | solution.py:396
  1137.1 158.2 %reduce-scatter.15.cloned.1.call-start = ((), (), s32[]{:S(2)}) async-start(), calls=%async_computation.20 | async-start | bytes 995328 | tf_op jit(solution)/shard_map/reduce_scatter | solution.py:396
  1148.8 48.6 %copy-start.127 = (f32[4,160]{1,0:T(4,128)S(1)}, f32[4,160]{1,0:T(4,128)}, u32[]{:S(2)}) copy-start(f32[4,160]{1,0:T(4,128)} %copy-done.126) | copy-start | bytes 7684
  1151.2 49.2 %copy-start.173 = (f32[4,160]{1,0:T(4,128)S(1)}, f32[4,160]{1,0:T(4,128)}, u32[]{:S(2)}) copy-start(f32[4,160]{1,0:T(4,128)} %copy-done.172) | copy-start | bytes 7684
  1151.2 49.2 %copy-start.97 = (f32[4,1152]{1,0:T(4,128)S(1)}, f32[4,1152]{1,0:T(4,128)}, u32[]{:S(2)}) copy-start(f32[4,1152]{1,0:T(4,128)} %copy-done.96) | copy-start | bytes 55300
  1151.2 49.2 %copy-start.167 = (f32[4,160]{1,0:T(4,128)S(1)}, f32[4,160]{1,0:T(4,128)}, u32[]{:S(2)}) copy-start(f32[4,160]{1,0:T(4,128)} %copy-done.166) | copy-start | bytes 7684
  1151.3 181.6 %all-reduce.27.cloned.1.call-start = ((), (), s32[]{:S(2)}) async-start(), calls=%async_computation.29 | async-start | bytes 1474560 | tf_op jit(solution)/shard_map/psum | solution.py:426
  1230.9 149.4 %reduce-scatter.25.cloned.1.call-start = ((), (), s32[]{:S(2)}) async-start(), calls=%async_computation.25 | async-start | bytes 2985984 | tf_op jit(solution)/shard_map/reduce_scatter | solution.py:402
  1239.9 188.1 %reduce-scatter.23.cloned.1.call-start = ((), (), s32[]{:S(2)}) async-start(), calls=%async_computation.24 | async-start | bytes 2985984 | tf_op jit(solution)/shard_map/reduce_scatter | solution.py:402
  1246.8 229.0 %reduce-scatter.21.cloned.1.call-start = ((), (), s32[]{:S(2)}) async-start(), calls=%async_computation.23 | async-start | bytes 2985984 | tf_op jit(solution)/shard_map/reduce_scatter | solution.py:399
  1255.7 268.3 %reduce-scatter.19.cloned.1.call-start = ((), (), s32[]{:S(2)}) async-start(), calls=%async_computation.22 | async-start | bytes 2985984 | tf_op jit(solution)/shard_map/reduce_scatter | solution.py:399
  1261.4 310.4 %reduce-scatter.13.cloned.1.call-start = ((), (), s32[]{:S(2)}) async-start(), calls=%async_computation.19 | async-start | bytes 2985984 | tf_op jit(solution)/shard_map/reduce_scatter | solution.py:393
  1269.5 350.4 %reduce-scatter.11.cloned.1.call-start = ((), (), s32[]{:S(2)}) async-start(), calls=%async_computation.18 | async-start | bytes 2985984 | tf_op jit(solution)/shard_map/reduce_scatter | solution.py:393
  1275.3 405.3 %reduce-scatter.29.cloned.1.call-start = ((), (), s32[]{:S(2)}) async-start(), calls=%async_computation.28 | async-start | bytes 5971968 | tf_op jit(solution)/shard_map/reduce_scatter | solution.py:405
  1282.4 458.9 %reduce-scatter.27.cloned.1.call-start = ((), (), s32[]{:S(2)}) async-start(), calls=%async_computation.27 | async-start | bytes 5971968 | tf_op jit(solution)/shard_map/reduce_scatter | solution.py:405
  1301.3 485.5 %copy-start.104 = (f32[33,288]{1,0:T(8,128)S(1)}, f32[33,288]{1,0:T(8,128)}, u32[]{:S(2)}) copy-start(f32[33,288]{1,0:T(8,128)} %param.47) | copy-start | bytes 114052
  1301.3 485.5 %copy-start.156 = (f32[33,288]{1,0:T(8,128)S(1)}, f32[33,288]{1,0:T(8,128)}, u32[]{:S(2)}) copy-start(f32[33,288]{1,0:T(8,128)} %param.68) | copy-start | bytes 114052
  1301.3 485.5 %copy-start.157 = (f32[33,288]{1,0:T(8,128)S(1)}, f32[33,288]{1,0:T(8,128)}, u32[]{:S(2)}) copy-start(f32[33,288]{1,0:T(8,128)} %param.54) | copy-start | bytes 114052
  1301.3 485.5 %copy-start.158 = (f32[33,288]{1,0:T(8,128)S(1)}, f32[33,288]{1,0:T(8,128)}, u32[]{:S(2)}) copy-start(f32[33,288]{1,0:T(8,128)} %param.61) | copy-start | bytes 114052
  1301.3 486.2 %copy-start.57 = (f32[2,288,144]{1,2,0:T(8,128)S(1)}, f32[2,288,144]{1,2,0:T(8,128)}, u32[]{:S(2)}) copy-start(f32[2,288,144]{1,2,0:T(8,128)} %param.43) | copy-start | bytes 995332
  1301.3 486.2 %copy-start.87 = (bf16[288,144]{0,1:T(8,128)(2,1)S(1)}, bf16[288,144]{0,1:T(8,128)(2,1)}, u32[]{:S(2)}) copy-start(bf16[288,144]{0,1:T(8,128)(2,1)} %reduce-scatter.17.cloned.1.call-done) | copy-start | bytes 248836
  1301.3 486.2 %copy-start.88 = (bf16[288,144]{0,1:T(8,128)(2,1)S(1)}, bf16[288,144]{0,1:T(8,128)(2,1)}, u32[]{:S(2)}) copy-start(bf16[288,144]{0,1:T(8,128)(2,1)} %reduce-scatter.15.cloned.1.call-done) | copy-start | bytes 248836
  1301.3 486.1 %copy-start.89 = (f32[2,288,144]{1,2,0:T(8,128)S(1)}, f32[2,288,144]{1,2,0:T(8,128)}, u32[]{:S(2)}) copy-start(f32[2,288,144]{1,2,0:T(8,128)} %param.64) | copy-start | bytes 995332
  1301.3 486.1 %copy-start.90 = (f32[2,288,144]{1,2,0:T(8,128)S(1)}, f32[2,288,144]{1,2,0:T(8,128)}, u32[]{:S(2)}) copy-start(f32[2,288,144]{1,2,0:T(8,128)} %param.50) | copy-start | bytes 995332
  1621.9 168.1 %copy-start.34 = (f32[2,1152,144]{1,2,0:T(8,128)S(1)}, f32[2,1152,144]{1,2,0:T(8,128)}, u32[]{:S(2)}) copy-start(f32[2,1152,144]{1,2,0:T(8,128)} %param.45) | copy-start | bytes 3981316
  1621.9 168.1 %copy-start.61 = (bf16[1152,144]{0,1:T(8,128)(2,1)S(1)}, bf16[1152,144]{0,1:T(8,128)(2,1)}, u32[]{:S(2)}) copy-start(bf16[1152,144]{0,1:T(8,128)(2,1)} %reduce-scatter.25.cloned.1.call-done) | copy-start | bytes 995332
  (183 other events, 1162.2 us)
Sparse Core Ops, SparseCore 0:
  10.2 63.7 all-gather.21
  76.5 40.2 all-gather.23
  119.2 30.2 all-gather.25
  190.1 66.6 all-reduce.10
  259.3 29.3 all-gather.27
  291.2 30.2 all-gather.29
  324.1 44.8 all-gather.31
  372.1 92.8 all-reduce.12
  467.5 28.7 all-gather.33
  510.3 95.6 all-reduce.14
  608.4 29.2 all-gather.35
  640.0 30.2 all-gather.37
  679.2 95.6 all-reduce.16
  796.3 94.6 all-reduce.18
  919.8 94.6 all-reduce.20
  1037.9 64.8 all-reduce.22
  1132.4 64.9 all-reduce.24
  1201.0 34.2 reduce-scatter.16
  1239.5 35.0 reduce-scatter.14
  1278.2 54.6 all-reduce.26
  1336.3 43.9 reduce-scatter.24
  1384.2 43.7 reduce-scatter.22
  1432.1 43.7 reduce-scatter.20
  1480.2 43.7 reduce-scatter.18
  1528.0 43.7 reduce-scatter.12
  1576.1 43.7 reduce-scatter.10
  1623.3 57.2 reduce-scatter.28
  1684.1 57.2 reduce-scatter.26
where the time goes:
time: 1830 us; the launch traced here: 1820 us
  waiting for transfers between devices  1140 us (62%)
  blocking collectives  238 us (13%)
  matrix products  210 us (11%)
  other arithmetic  114 us (6%)
  local copies, waits for them, and re-layouts  90.7 us (5%)
  between operations  26.6 us (1%)
    psum x8, waiting for transfers between devices, narrow_sum(): return lax.psum(values.astype(jnp.bfloat16), 'narrow').astype(jnp.float32)  526 us
    reduce_scatter x2, waiting for transfers between devices, shards(): lax.psum_scatter(table_gradient.astype(jnp.bfloat16), 'wide', scatter_dim...  117 us
    all_gather x2, blocking collectives, shards(): lax.all_gather(slice_part, 'narrow', axis=2, tiled=True)  112 us
    reduce_scatter x2, waiting for transfers between devices, shards(): lax.psum_scatter(grads[2].astype(jnp.bfloat16), 'wide', scatter_dimension...  93.9 us
    reduce_scatter x2, waiting for transfers between devices, shards(): lax.psum_scatter(grads[0].astype(jnp.bfloat16), 'wide', scatter_dimension...  93.9 us
    reduce_scatter x2, waiting for transfers between devices, shards(): lax.psum_scatter(grads[3].astype(jnp.bfloat16), 'wide', scatter_dimension...  91.8 us
    all_gather x2, waiting for transfers between devices, fetch(): lax.all_gather(stacks[4][lookup_index].astype(jnp.bfloat16), 'wide', axis...  60 us
    all_gather x2, waiting for transfers between devices, fetch(): lax.all_gather(stacks[2][lookup_index].astype(jnp.bfloat16), 'wide', axis...  53.3 us
  transfers between devices with their start and end apart: 28, of which 25 were waited for; matrix products, arithmetic and copies ran while one was open for 13% of the time, Pallas kernels for 0%

commit v1 on v0

v1 whole, which is shorter than its diff:
```python
from functools import partial
import math

import jax
import jax.numpy as jnp
from jax import lax
from jax.experimental import pallas as pl
from jax.experimental.pallas import tpu as pltpu
from jax.sharding import Mesh
from jax.sharding import PartitionSpec as P

HEAD_DIM = 72
CLASSES = 1000
FREQ = 256
PATCH_IN = 16
STEP = 10

MESH = pl.DeviceIdType.MESH
WIDE = ("plane", "core")
NARROW = ("zh", "zl")
ALL = WIDE + NARROW

highest_float_accuracy = lax.Precision.HIGHEST
norm_eps = 1e-06
contrast_sharpness_divisor = 0.02
nce_weight = 0.5
learn_rate = 0.05
beta_first = 0.9
beta_second = 0.999
adam_eps = 1e-08
weight_decay = 0.05
clip_norm = 0.05
ema_decay = 0.9999


def layer_norm(values):
    center = values - jnp.mean(values, -1, keepdims=True)
    return center * lax.rsqrt(jnp.mean(center * center, -1, keepdims=True) + norm_eps)


def modulate(values, shift, scale):
    return layer_norm(values) * (1.0 + scale[None, :]) + shift[None, :]


def sinusoid(places, width):
    half = width // 2
    freqs = jnp.exp(-math.log(10000.0) * jnp.arange(half, dtype=jnp.float32) / half)
    angle = places.astype(jnp.float32)[:, None] * freqs[None, :]
    return jnp.concatenate([jnp.cos(angle), jnp.sin(angle)], -1)


def flat_place(axes):
    place = 0
    for axis in axes:
        place = place * lax.axis_size(axis) + lax.axis_index(axis)
    return place


def group_size(axes):
    size = 1
    for axis in axes:
        size = size * lax.axis_size(axis)
    return size


def device_at(axes, place):
    where = {}
    for axis in reversed(axes):
        where[axis] = lax.rem(place, lax.axis_size(axis))
        place = place // lax.axis_size(axis)
    return where


def exchange_kernel(specs, *refs):
    count = len(specs)
    sources, results, sems = refs[:count], refs[count : 2 * count], refs[2 * count :]
    barrier = pltpu.get_barrier_semaphore()
    greeted = 0
    for axes, _ in specs:
        size, me = group_size(axes), flat_place(axes)
        greeted += size - 1

        def greet(offset, carry, axes=axes, size=size, me=me):
            target = lax.rem(me + offset, size)
            pl.semaphore_signal(
                barrier, inc=1, device_id=device_at(axes, target), device_id_type=MESH
            )
            return carry

        lax.fori_loop(1, size, greet, 0)
    pl.semaphore_wait(barrier, greeted)

    def copy_to(index, offset, arriving):
        axes, mode = specs[index]
        size, me = group_size(axes), flat_place(axes)
        target = lax.rem(me + offset, size)
        source = sources[index].at[target] if mode == "each" else sources[index]
        return pltpu.make_async_remote_copy(
            src_ref=source,
            dst_ref=results[index].at[target if arriving else me],
            send_sem=sems[2 * index].at[target],
            recv_sem=sems[2 * index + 1].at[target if arriving else me],
            device_id=device_at(axes, target),
            device_id_type=MESH,
        )

    for index, (axes, mode) in enumerate(specs):

        def start(offset, carry, index=index):
            copy_to(index, offset, False).start()
            return carry

        lax.fori_loop(1, group_size(axes), start, 0)
    for index, (axes, mode) in enumerate(specs):
        me = flat_place(axes)
        own = sources[index][me] if mode == "each" else sources[index][...]
        results[index][me] = own
    for index, (axes, mode) in enumerate(specs):

        def finish(offset, carry, index=index):
            copy_to(index, offset, True).wait_recv()
            copy_to(index, offset, False).wait_send()
            return carry

        lax.fori_loop(1, group_size(axes), finish, 0)


def exchange(arrays, specs, collective_id):
    shapes, scratch = [], []
    for array, (axes, mode) in zip(arrays, specs):
        size = group_size(axes)
        piece = array.shape[1:] if mode == "each" else array.shape
        shapes.append(jax.ShapeDtypeStruct((size,) + piece, array.dtype))
        scratch += [pltpu.SemaphoreType.DMA((size,)), pltpu.SemaphoreType.DMA((size,))]
    return pl.pallas_call(
        partial(exchange_kernel, specs),
        out_shape=shapes,
        in_specs=[pl.BlockSpec(memory_space=pltpu.VMEM)] * len(arrays),
        out_specs=[pl.BlockSpec(memory_space=pltpu.VMEM)] * len(arrays),
        scratch_shapes=scratch,
        compiler_params=pltpu.CompilerParams(
            collective_id=collective_id, has_side_effects=True, vmem_limit_bytes=40 * 2**20
        ),
        cost_estimate=pl.CostEstimate(flops=0, bytes_accessed=16 * 2**20, transcendentals=0),
    )(*arrays)


def group_places():
    core, low = lax.axis_index("core"), lax.axis_index("zl")
    return {
        "me": core * 2 + low,
        "mate": (1 - core) * 2 + low,
        "far": core * 2 + (1 - low),
        "far_mate": (1 - core) * 2 + (1 - low),
        "mate_id": {"core": 1 - core},
        "far_id": {"zl": 1 - low},
    }


def greet_group(at):
    barrier = pltpu.get_barrier_semaphore()
    for name in ("mate_id", "far_id"):
        pl.semaphore_signal(barrier, inc=1, device_id=at[name], device_id_type=MESH)
    pl.semaphore_wait(barrier, 2)


def own_sum_kernel(chunk, part_ref, sum_ref, near, home, stage, far, sends, recvs):
    length = part_ref.shape[1]
    steps = length // chunk
    at = group_places()
    greet_group(at)

    def copy(source, target, kind, step, to):
        return pltpu.make_async_remote_copy(
            src_ref=source,
            dst_ref=target,
            send_sem=sends.at[kind, step],
            recv_sem=recvs.at[kind, step],
            device_id=at[to],
            device_id_type=MESH,
        )

    rows = [pl.ds(step * chunk, chunk) for step in range(steps)]
    to_near = [
        copy(part_ref.at[at["far_mate"], rows[s]], near.at[rows[s]], 0, s, "mate_id")
        for s in range(steps)
    ]
    to_home = [
        copy(part_ref.at[at["mate"], rows[s]], home.at[rows[s]], 1, s, "mate_id")
        for s in range(steps)
    ]
    to_far = [copy(stage.at[rows[s]], far.at[rows[s]], 2, s, "far_id") for s in range(steps)]
    for s in range(steps):
        to_near[s].start()
    for s in range(steps):
        to_home[s].start()
    for s in range(steps):
        to_near[s].wait_recv()
        both = part_ref[at["far"], rows[s]].astype(jnp.float32) + near[rows[s]].astype(jnp.float32)
        stage[rows[s]] = both.astype(jnp.bfloat16)
        to_far[s].start()
    for s in range(steps):
        to_home[s].wait_recv()
        sum_ref[rows[s]] = part_ref[at["me"], rows[s]].astype(jnp.float32) + home[rows[s]].astype(
            jnp.float32
        )
    for s in range(steps):
        to_far[s].wait_recv()
        sum_ref[rows[s]] = sum_ref[rows[s]] + far[rows[s]].astype(jnp.float32)
    for s in range(steps):
        to_near[s].wait_send()
        to_home[s].wait_send()
        to_far[s].wait_send()


def chunk_of(length):
    return 64 if length % 64 == 0 else 32


def own_sum(parts, collective_id):
    _, length, width = parts.shape
    chunk = chunk_of(length)
    steps = length // chunk
    buffer = pltpu.VMEM((length, width), jnp.bfloat16)
    return pl.pallas_call(
        partial(own_sum_kernel, chunk),
        out_shape=jax.ShapeDtypeStruct((length, width), jnp.float32),
        in_specs=[pl.BlockSpec(memory_space=pltpu.VMEM)],
        out_specs=pl.BlockSpec(memory_space=pltpu.VMEM),
        scratch_shapes=[buffer] * 4
        + [pltpu.SemaphoreType.DMA((3, steps)), pltpu.SemaphoreType.DMA((3, steps))],
        compiler_params=pltpu.CompilerParams(
            collective_id=collective_id, has_side_effects=True, vmem_limit_bytes=40 * 2**20
        ),
        cost_estimate=pl.CostEstimate(
            flops=0, bytes_accessed=length * 256 * 1024, transcendentals=0
        ),
    )(parts)


def group_copy_kernel(chunk, own_ref, all_ref, sends, recvs):
    length = own_ref.shape[0]
    steps = length // chunk
    at = group_places()
    greet_group(at)

    def copy(source, target, kind, step, to):
        return pltpu.make_async_remote_copy(
            src_ref=source,
            dst_ref=target,
            send_sem=sends.at[kind, step],
            recv_sem=recvs.at[kind, step],
            device_id=at[to],
            device_id_type=MESH,
        )

    rows = [pl.ds(step * chunk, chunk) for step in range(steps)]
    out = [copy(own_ref.at[rows[s]], all_ref.at[at["me"], rows[s]], 0, s, "far_id") for s in range(steps)]
    arrive = [copy(own_ref.at[rows[s]], all_ref.at[at["far"], rows[s]], 0, s, "far_id") for s in range(steps)]
    mate_out = [copy(own_ref.at[rows[s]], all_ref.at[at["me"], rows[s]], 1, s, "mate_id") for s in range(steps)]
    mate_in = [copy(own_ref.at[rows[s]], all_ref.at[at["mate"], rows[s]], 1, s, "mate_id") for s in range(steps)]
    pass_out = [
        copy(all_ref.at[at["far"], rows[s]], all_ref.at[at["far"], rows[s]], 2, s, "mate_id")
        for s in range(steps)
    ]
    pass_in = [
        copy(all_ref.at[at["far"], rows[s]], all_ref.at[at["far_mate"], rows[s]], 2, s, "mate_id")
        for s in range(steps)
    ]
    for s in range(steps):
        out[s].start()
    for s in range(steps):
        mate_out[s].start()
    all_ref[at["me"]] = own_ref[...]
    for s in range(steps):
        arrive[s].wait_recv()
        pass_out[s].start()
    for s in range(steps):
        mate_in[s].wait_recv()
        pass_in[s].wait_recv()
    for s in range(steps):
        out[s].wait_send()
        mate_out[s].wait_send()
        pass_out[s].wait_send()


def group_copy(own, collective_id):
    length, width = own.shape
    chunk = chunk_of(length)
    steps = length // chunk
    return pl.pallas_call(
        partial(group_copy_kernel, chunk),
        out_shape=jax.ShapeDtypeStruct((4, length, width), jnp.bfloat16),
        in_specs=[pl.BlockSpec(memory_space=pltpu.VMEM)],
        out_specs=pl.BlockSpec(memory_space=pltpu.VMEM),
        scratch_shapes=[pltpu.SemaphoreType.DMA((3, steps)), pltpu.SemaphoreType.DMA((3, steps))],
        compiler_params=pltpu.CompilerParams(
            collective_id=collective_id, has_side_effects=True, vmem_limit_bytes=40 * 2**20
        ),
        cost_estimate=pl.CostEstimate(
            flops=0, bytes_accessed=length * 256 * 1024, transcendentals=0
        ),
    )(own)


def swap_pairs():
    forth, straight = [], []
    half, low = lax.axis_size("zh"), lax.axis_size("zl")
    for h in range(half):
        for z in range(low):
            zero, one = h * low + z, half * low + h * low + z
            other_one = half * low + (half - 1 - h) * low + z
            forth += [(zero, other_one), (one, zero)]
            straight += [(one, other_one)]
    return forth, straight


SWAP = ("core", "zh", "zl")


def gather_rows(shard):
    forth, straight = swap_pairs()
    first = lax.ppermute(shard, SWAP, forth)
    second = lax.ppermute(shard, SWAP, straight)
    on_zero = lax.axis_index("core") == 0
    pair = jnp.stack([jnp.where(on_zero, shard, first), jnp.where(on_zero, first, second)])
    full = lax.all_gather(pair, "plane", axis=0, tiled=True)
    return full.reshape(full.shape[0] * full.shape[1], full.shape[2])


def scatter_rows(grad):
    planes = lax.axis_size("plane")
    rows = grad.shape[0] // planes
    mine = lax.psum_scatter(grad, "plane", scatter_dimension=0, tiled=True)
    low, high = mine[: rows // 2], mine[rows // 2 :]
    forth, straight = swap_pairs()
    back = [(to, at) for at, to in forth]
    onward = [(to, at) for at, to in straight]
    on_zero = lax.axis_index("core") == 0
    first = lax.ppermute(jnp.where(on_zero, high, low), SWAP, back)
    second = lax.ppermute(high, SWAP, onward)
    return jnp.where(on_zero, low, second).astype(jnp.float32) + first.astype(jnp.float32)


def scores_of(query, key, key_valid):
    scale = 1.0 / math.sqrt(HEAD_DIM)
    scores = jnp.einsum("bqhe,bkhe->bhqk", query, key, preferred_element_type=jnp.float32) * scale
    if key_valid is None:
        return scores
    return jnp.where(key_valid[:, None, None, :] > 0, scores, -1e30)


def attend_forward(query, key, value, key_valid):
    scores = scores_of(query, key, key_valid)
    peak = jnp.max(scores, -1, keepdims=True)
    expo = jnp.exp(scores - peak)
    total = jnp.sum(expo, -1, keepdims=True)
    probs = (expo / total).astype(jnp.bfloat16)
    context = jnp.einsum(
        "bhqk,bkhe->bqhe", probs, value, preferred_element_type=jnp.float32
    ).astype(jnp.bfloat16)
    return (context, peak + jnp.log(total))


def attend_backward(query, key, value, log_total, grad_context, key_valid):
    scale = 1.0 / math.sqrt(HEAD_DIM)
    probs = jnp.exp(scores_of(query, key, key_valid) - log_total)
    grad_value = jnp.einsum(
        "bhqk,bqhe->bkhe",
        probs.astype(jnp.bfloat16),
        grad_context,
        preferred_element_type=jnp.float32,
    ).astype(jnp.bfloat16)
    grad_probs = jnp.einsum(
        "bqhe,bkhe->bhqk", grad_context, value, preferred_element_type=jnp.float32
    )
    grad_scores = (probs * (grad_probs - jnp.sum(grad_probs * probs, -1, keepdims=True))).astype(
        jnp.bfloat16
    )
    grad_query = (
        jnp.einsum("bhqk,bkhe->bqhe", grad_scores, key, preferred_element_type=jnp.float32) * scale
    ).astype(jnp.bfloat16)
    grad_key = (
        jnp.einsum("bhqk,bqhe->bkhe", grad_scores, query, preferred_element_type=jnp.float32)
        * scale
    ).astype(jnp.bfloat16)
    return (grad_query, grad_key, grad_value)


def split_heads(triple):
    batch, length, three = triple.shape
    local = three // 3
    return [
        triple[:, :, i * local : (i + 1) * local].reshape(
            batch, length, local // HEAD_DIM, HEAD_DIM
        )
        for i in range(3)
    ]


def weight_parts(attend, feed):
    local = attend.shape[1] // 4
    hidden = feed.shape[1] // 2
    return attend[:, : 3 * local], attend[:, 3 * local :], feed[:, :hidden], feed[:, hidden:]


def low_dot(spec, left, right):
    return jnp.einsum(spec, left, right, preferred_element_type=jnp.float32)


def block_forward(values, mod, key_valid, weight_tensors, ids):
    attend_in, attend_out, expand, contract = weight_tensors
    shift_a, scale_a, gate_a, shift_m, scale_m, gate_m = [mod[i] for i in range(6)]
    sum_id, copy_id = ids
    normed = group_copy(modulate(values, shift_a, scale_a).astype(jnp.bfloat16), copy_id)
    triple = low_dot("bld,dc->blc", normed, attend_in).astype(jnp.bfloat16)
    context, log_total = attend_forward(*split_heads(triple), key_valid)
    flat_context = context.reshape(triple.shape[0], triple.shape[1], triple.shape[2] // 3)
    attn = own_sum(low_dot("ble,de->bld", flat_context, attend_out).astype(jnp.bfloat16), sum_id)
    middle = values + gate_a[None, :] * attn
    normed_m = group_copy(modulate(middle, shift_m, scale_m).astype(jnp.bfloat16), copy_id)
    inner = low_dot("bld,df->blf", normed_m, expand)
    active = jax.nn.gelu(inner, approximate=True).astype(jnp.bfloat16)
    branch = own_sum(low_dot("blf,df->bld", active, contract).astype(jnp.bfloat16), sum_id)
    result = middle + gate_m[None, :] * branch
    saved = (values, middle, normed, normed_m, triple, flat_context, log_total, attn, inner, active, branch)
    return (result, saved)


def block_backward(grad, mod, key_valid, weight_tensors, saved, ids):
    attend_in, attend_out, expand, contract = weight_tensors
    values, middle, normed, normed_m, triple, flat_context, log_total, attn, inner, active, branch = saved
    shift_a, scale_a, gate_a, shift_m, scale_m, gate_m = [mod[i] for i in range(6)]
    sum_id, copy_id = ids
    grad_branch = group_copy((gate_m[None, :] * grad).astype(jnp.bfloat16), copy_id)
    grad_gate_m = jnp.sum(grad * branch, 0)
    grad_active = low_dot("bld,df->blf", grad_branch, contract)
    gelu_back = jax.vjp(partial(jax.nn.gelu, approximate=True), inner)[1]
    grad_inner = gelu_back(grad_active)[0].astype(jnp.bfloat16)
    grad_normed = own_sum(
        low_dot("blf,df->bld", grad_inner, expand).astype(jnp.bfloat16), sum_id
    )
    grad_contract = low_dot("bld,blf->df", grad_branch, active)
    grad_expand = low_dot("bld,blf->df", normed_m, grad_inner)
    grad_feed = jnp.concatenate([grad_expand, grad_contract], 1).astype(jnp.bfloat16)
    _, modulate_back = jax.vjp(modulate, middle, shift_m, scale_m)
    grad_mid, grad_shift_m, grad_scale_m = modulate_back(grad_normed)
    grad_mid = grad + grad_mid
    grad_attn = group_copy((gate_a[None, :] * grad_mid).astype(jnp.bfloat16), copy_id)
    grad_gate_a = jnp.sum(grad_mid * attn, 0)
    grad_flat = low_dot("bld,de->ble", grad_attn, attend_out).astype(jnp.bfloat16)
    grad_attend_out = low_dot("bld,ble->de", grad_attn, flat_context)
    query, key, value = split_heads(triple)
    grad_context = grad_flat.reshape(query.shape)
    grad_parts = attend_backward(query, key, value, log_total, grad_context, key_valid)
    grad_triple = jnp.concatenate([g.reshape(flat_context.shape) for g in grad_parts], 2)
    grad_normed = own_sum(
        low_dot("blc,dc->bld", grad_triple, attend_in).astype(jnp.bfloat16), sum_id
    )
    grad_attend_in = low_dot("bld,blc->dc", normed, grad_triple)
    grad_attend = jnp.concatenate([grad_attend_in, grad_attend_out], 1).astype(jnp.bfloat16)
    _, modulate_back = jax.vjp(modulate, values, shift_a, scale_a)
    grad_values, grad_shift_a, grad_scale_a = modulate_back(grad_normed)
    grad_mod = jnp.stack(
        [grad_shift_a, grad_scale_a, grad_gate_a, grad_shift_m, grad_scale_m, grad_gate_m], 0
    )
    return (grad_mid + grad_values, grad_mod, grad_attend, grad_feed)


def adam(weight, grad, moment, second, average, factor):
    grad = grad * factor
    moment = beta_first * moment + (1.0 - beta_first) * grad
    second = beta_second * second + (1.0 - beta_second) * grad * grad
    update = (
        moment
        / (1.0 - beta_first**STEP)
        / (jnp.sqrt(second / (1.0 - beta_second**STEP)) + adam_eps)
    )
    fresh = weight - learn_rate * (update + weight_decay * weight)
    average_decay = min(ema_decay, (1.0 + STEP) / (10.0 + STEP))
    average = average_decay * average + (1.0 - average_decay) * fresh
    return (fresh, moment, second, average)


def shards(
    patches,
    target_noise,
    kept_slots,
    kept_count,
    time_step,
    labels,
    teacher,
    *tables,
):
    params, moments, seconds, averages = tables[:7], tables[7:14], tables[14:21], tables[21:]
    attend_in, attend_out, expand, contract, modulation, patch_table, condition = params
    batch, length = (patches.shape[0], patches.shape[1])
    capacity = kept_slots.shape[1]
    rows, local = (attend_in.shape[1], attend_in.shape[3])
    wides, narrows = (group_size(WIDE), group_size(NARROW))
    wide_index, narrow_index = (flat_place(WIDE), flat_place(NARROW))
    images = batch * wides
    width = local * narrows
    assert batch == narrows

    attend_rows, feed_rows = [], []
    for i in range(2):
        attend_shard = jnp.concatenate(
            [attend_in[i].reshape(rows, 3 * local), attend_out[i].T], 1
        ).astype(jnp.bfloat16)
        feed_shard = jnp.concatenate([expand[i], contract[i].T], 1).astype(jnp.bfloat16)
        attend_rows.append(gather_rows(attend_shard))
        feed_rows.append(gather_rows(feed_shard))
    weights = [weight_parts(attend_rows[i], feed_rows[i]) for i in range(2)]

    def own(array):
        return lax.dynamic_index_in_dim(array, narrow_index, 0, keepdims=False)

    condition_low = condition.astype(jnp.bfloat16)
    features = sinusoid(time_step, FREQ)
    onehot = (labels[:, None] == jnp.arange(CLASSES)[None, :]).astype(jnp.bfloat16)
    cond_part = jnp.dot(
        features, condition_low[:FREQ].astype(jnp.float32), precision=highest_float_accuracy
    ) + low_dot("bc,cd->bd", onehot, condition_low[FREQ:])
    facts = jnp.stack([kept_count, time_step, labels], 1).astype(jnp.float32)
    facts = jnp.pad(own(facts)[None, :], ((0, 7), (0, local - 3)))
    payload = jnp.concatenate([cond_part, own(teacher).reshape(narrows, local), facts], 0)
    table_pad = jnp.pad(patch_table.astype(jnp.bfloat16), ((0, 15), (0, 0)))
    everyone, tables_near = exchange(
        [payload, table_pad], [(ALL, "same"), (NARROW, "same")], 0
    )
    everyone = everyone.reshape(wides, narrows, batch + narrows + 8, local)
    cond_sum = jnp.transpose(everyone[:, :, :batch], (0, 2, 1, 3)).reshape(images, width)
    negatives = everyone[:, :, batch : batch + narrows].reshape(images, width)
    facts_all = everyone[:, :, batch + narrows, :3]
    time_all = facts_all[:, :, 1].reshape(images).astype(jnp.int32)
    labels_all = facts_all[:, :, 2].reshape(images).astype(jnp.int32)
    patch_full = jnp.transpose(tables_near, (1, 0, 2)).reshape(48, width)[:33]
    silu_low = jax.nn.silu(cond_sum).astype(jnp.bfloat16)
    silu_rows = lax.dynamic_slice_in_dim(silu_low, wide_index * rows, rows, 1)
    modulation_low = modulation.astype(jnp.bfloat16)
    mod_part = low_dot("ip,npkc->inkc", silu_rows, modulation_low)
    mod_part = mod_part.reshape(wides, batch, 12, local)
    (mod_wide,) = exchange([mod_part], [(WIDE, "each")], 1)
    (mod_near,) = exchange([jnp.sum(mod_wide, 0)], [(NARROW, "each")], 2)
    mods = jnp.transpose(mod_near, (1, 0, 2)).reshape(2, 6, width)

    count_own = own(kept_count).astype(jnp.float32)
    slot_valid = (jnp.arange(capacity) < own(kept_count)).astype(jnp.float32)
    select = (own(kept_slots)[:, None] == jnp.arange(length)[None, :]).astype(
        jnp.float32
    ) * slot_valid[:, None]
    kept_place = jnp.sum(select, 0)
    places = sinusoid(jnp.arange(length), width)
    group_counts = lax.dynamic_slice(
        facts_all[:, :, 0],
        (lax.axis_index("plane") * 2, lax.axis_index("zh") * 2),
        (2, 2),
    ).reshape(4)
    group_valid = (jnp.arange(capacity)[None, :] < group_counts[:, None]).astype(jnp.float32)
    kept_patches = low_dot("cl,lp->cp", select.astype(jnp.bfloat16), own(patches))
    embed = low_dot("cp,pd->cd", kept_patches.astype(jnp.bfloat16), patch_full[:PATCH_IN])
    embed = embed + jnp.dot(select, places, precision=highest_float_accuracy)
    encoded, saved_enc = block_forward(embed, mods[0], group_valid, weights[0], (3, 4))

    def pool_unit(values):
        pooled = jnp.sum(values * slot_valid[:, None], 0) / count_own
        return pooled * lax.rsqrt(jnp.sum(pooled * pooled, -1, keepdims=True) + 1e-06)

    normalised_direction, pool_back = jax.vjp(pool_unit, encoded)
    frozen_target_direction = negatives * lax.rsqrt(
        jnp.sum(negatives * negatives, -1, keepdims=True) + 1e-06
    )
    cosine_match_scores = (
        jnp.sum(normalised_direction[None, :] * frozen_target_direction, -1)
        / contrast_sharpness_divisor
    )
    peak = jnp.max(cosine_match_scores)
    expo = jnp.exp(cosine_match_scores - peak)
    total = jnp.sum(expo)
    positive = ((wide_index * batch + narrow_index) == jnp.arange(images)).astype(jnp.float32)
    nce_local = peak + jnp.log(total) - jnp.sum(cosine_match_scores * positive)
    derivative_of_raw_scores = (expo / total - positive) * (nce_weight / images)
    unit_vector_gradient = (
        jnp.sum(derivative_of_raw_scores[:, None] * frozen_target_direction, 0)
        / contrast_sharpness_divisor
    )
    grad_pool = pool_back(unit_vector_gradient)[0]
    mask_token = patch_full[2 * PATCH_IN].astype(jnp.float32)
    decode_in = jnp.einsum("cl,cd->ld", select, encoded, precision=highest_float_accuracy)
    decode_in = decode_in + (1.0 - kept_place)[:, None] * mask_token + places
    decoded, saved_dec = block_forward(decode_in, mods[1], None, weights[1], (5, 6))
    final, final_back = jax.vjp(layer_norm, decoded)
    final_low = final.astype(jnp.bfloat16)
    head = patch_full[PATCH_IN : 2 * PATCH_IN]
    predict = low_dot("ld,pd->lp", final_low, head)
    error_map = predict - own(target_noise)
    count_all = images * length * PATCH_IN
    mse_local = jnp.sum(error_map * error_map)
    grad_predict = (error_map * (2.0 / count_all)).astype(jnp.bfloat16)
    grad_head = low_dot("lp,ld->pd", grad_predict, final_low)
    grad_final = low_dot("lp,pd->ld", grad_predict, head)
    grad_decoded = final_back(grad_final)[0]
    grad_dec_in, grad_mod_dec, attend_dec, feed_dec = block_backward(
        grad_decoded, mods[1], None, weights[1], saved_dec, (5, 6)
    )
    grad_mask = jnp.sum((1.0 - kept_place)[:, None] * grad_dec_in, 0)
    grad_encoded = jnp.dot(select, grad_dec_in, precision=highest_float_accuracy) + grad_pool
    grad_embed, grad_mod_enc, attend_enc, feed_enc = block_backward(
        grad_encoded, mods[0], group_valid, weights[0], saved_enc, (3, 4)
    )
    grad_patch = jnp.einsum(
        "cp,cd->pd", kept_patches, grad_embed, precision=highest_float_accuracy
    )

    attend_sums = [scatter_rows(g) for g in (attend_enc, attend_dec)]
    feed_sums = [scatter_rows(g) for g in (feed_enc, feed_dec)]

    grad_mods = jnp.stack([grad_mod_enc, grad_mod_dec]).reshape(12, narrows, local)
    grad_mods = jnp.transpose(grad_mods, (1, 0, 2))
    grad_table = jnp.concatenate([grad_patch, grad_head, grad_mask[None, :]], 0)
    grad_table = jnp.transpose(grad_table.reshape(33, narrows, local), (1, 0, 2))
    mods_near, table_near = exchange(
        [grad_mods, jnp.pad(grad_table, ((0, 0), (0, 7), (0, 0)))],
        [(NARROW, "each"), (NARROW, "each")],
        7,
    )
    table_sum = jnp.pad(jnp.sum(table_near, 0), ((0, 8), (0, 0))).astype(jnp.bfloat16)
    mods_all, table_all = exchange(
        [mods_near, table_sum], [(WIDE, "same"), (WIDE, "same")], 8
    )
    grad_patch_table = jnp.sum(table_all.astype(jnp.float32), 0)[:33]
    mods_all = mods_all.reshape(images, 2, 6, local)
    silu_broad = silu_rows.astype(jnp.float32)
    grad_modulation = jnp.einsum(
        "ip,inkc->npkc", silu_broad, mods_all, precision=highest_float_accuracy
    )
    grad_silu = jnp.einsum(
        "inkc,npkc->ip",
        mods_all,
        modulation_low.astype(jnp.float32),
        precision=highest_float_accuracy,
    )
    (silu_near,) = exchange([grad_silu], [(NARROW, "same")], 9)
    (silu_wide,) = exchange([jnp.sum(silu_near, 0)], [(WIDE, "same")], 10)
    grad_silu = jnp.transpose(silu_wide, (1, 0, 2)).reshape(images, width)
    grad_silu = lax.dynamic_slice_in_dim(grad_silu, narrow_index * local, local, 1)
    cond_cols = lax.dynamic_slice_in_dim(cond_sum, narrow_index * local, local, 1)
    grad_cond = jax.vjp(jax.nn.silu, cond_cols)[1](grad_silu)[0]
    features_all = sinusoid(time_all, FREQ)
    onehot_all = (labels_all[:, None] == jnp.arange(CLASSES)[None, :]).astype(jnp.float32)
    grad_condition = jnp.dot(
        jnp.concatenate([features_all, onehot_all], 1).T, grad_cond, precision=highest_float_accuracy
    )

    grads = [
        jnp.stack([g[:, : 3 * local].reshape(rows, 3, local) for g in attend_sums]),
        jnp.stack([g[:, 3 * local :].T for g in attend_sums]),
        jnp.stack([g[:, : expand.shape[2]] for g in feed_sums]),
        jnp.stack([g[:, expand.shape[2] :].T for g in feed_sums]),
        grad_modulation,
        grad_patch_table,
        grad_condition,
    ]
    square_big = jnp.sum(grad_modulation * grad_modulation)
    for g in attend_sums + feed_sums:
        square_big = square_big + jnp.sum(g * g)
    square_small = jnp.sum(grad_patch_table * grad_patch_table) + jnp.sum(
        grad_condition * grad_condition
    )
    square_local = square_big + (wide_index == 0).astype(jnp.float32) * square_small
    scalars = jnp.stack([mse_local, nce_local, square_local])
    scalars = jnp.pad(scalars[None, :], ((0, 7), (0, 125)))
    (scalars_all,) = exchange([scalars], [(ALL, "same")], 11)
    sums = jnp.sum(scalars_all[:, 0], 0)
    grad_norm = jnp.sqrt(sums[2])
    factor = clip_norm / jnp.maximum(grad_norm, clip_norm)
    fresh = [
        adam(params[i], grads[i], moments[i], seconds[i], averages[i], factor) for i in range(7)
    ]
    loss_parts = jnp.stack([sums[0] / count_all, sums[1] / images])
    return (loss_parts, grad_norm) + tuple(fresh[i][k] for k in range(4) for i in range(7))


def solution(mesh):
    wide, narrow = mesh.devices.shape
    grid = Mesh(mesh.devices.reshape(wide // 2, 2, narrow // 2, 2), ALL)
    image_specs = (
        P(WIDE, None, None),
        P(WIDE, None, None),
        P(WIDE, None),
        P(WIDE),
        P(WIDE),
        P(WIDE),
        P(WIDE, None),
    )
    table_specs = (
        P(None, WIDE, None, NARROW),
        P(None, NARROW, WIDE),
        P(None, WIDE, NARROW),
        P(None, NARROW, WIDE),
        P(None, WIDE, None, NARROW),
        P(None, NARROW),
        P(None, NARROW),
    )
    return jax.shard_map(
        shards,
        mesh=grid,
        in_specs=image_specs + table_specs * 4,
        out_specs=(P(), P()) + table_specs * 4,
        check_vma=False,
    )
```

time: 1830 us -> 861 us (0.47)
  waiting for transfers between devices: 1140 us -> 88.6 us
  Pallas kernels: 0 us -> 360 us
  blocking collectives: 238 us -> 0 us
  matrix products: 210 us -> 130 us
  starting transfers between devices: 2.13 us -> 64.5 us
  other arithmetic: 114 us -> 87 us
    psum x9 -> x0, waiting for transfers between devices: 534 us -> none  [the longest x8 526 us: narrow_sum(): return lax.psum(values.astype(jnp.bfloat16), 'narrow').astype(jnp.float32)]
    reduce_scatter x10 -> x4, waiting for transfers between devices: 396 us -> 0.03 us  [scatter_rows(): mine = lax.psum_scatter(grad, 'plane', scatter_dimension=0, tiled=True)]
    pallas_call x0 -> x24, Pallas kernels: none -> 360 us  [the longest x8 129 us: exchange(): pl.pallas_call(partial(exchange_kernel, specs), out_shape=shapes, in_spec...]
    all_gather x9 -> x4, waiting for transfers between devices: 209 us -> 0.06 us  [gather_rows(): full = lax.all_gather(pair, 'plane', axis=0, tiled=True)]
    all_gather x6 -> x0, blocking collectives: 165 us -> none  [the longest x2 112 us: shards(): lax.all_gather(slice_part, 'narrow', axis=2, tiled=True)]
    ppermute x0 -> x16, waiting for transfers between devices: none -> 88.4 us  [the longest x4 66.2 us: scatter_rows(): first = lax.ppermute(jnp.where(on_zero, high, low), SWAP, back)]
    dot_general x45 -> x39, matrix products: 196 us -> 113 us  [the longest x31 97.4 us: low_dot(): return jnp.einsum(spec, left, right, preferred_element_type=jnp.float32)]
    psum x3 -> x0, blocking collectives: 72.5 us -> none  [the longest x1 39.6 us: shards(): loss_sums = lax.psum((loss_terms[0], loss_terms[1]), ('wide', 'narrow'))]
  transfers between devices with their start and end apart: 28 -> 24, of which waited for: 25 -> 7; matrix products, arithmetic and copies ran while one was open for 13% -> 23% of each run, Pallas kernels for 0% -> 31%
where the time goes in v1:
time: 861 us; the launch traced here: 850 us
  Pallas kernels  360 us (42%)
  matrix products  130 us (15%)
  local copies, waits for them, and re-layouts  90.7 us (11%)
  waiting for transfers between devices  88.6 us (10%)
  other arithmetic  87 us (10%)
  starting transfers between devices  64.5 us (7%)
  between operations  28.9 us (3%)
    pallas_call x8, Pallas kernels, exchange(): pl.pallas_call(partial(exchange_kernel, specs), out_shape=shapes, in_spec...  129 us
    pallas_call x8, Pallas kernels, own_sum(): pl.pallas_call(partial(own_sum_kernel, chunk), out_shape=jax.ShapeDtypeSt...  119 us
    pallas_call x8, Pallas kernels, group_copy(): pl.pallas_call(partial(group_copy_kernel, chunk), out_shape=jax.ShapeDtyp...  112 us
    dot_general x31, matrix products, low_dot(): return jnp.einsum(spec, left, right, preferred_element_type=jnp.float32)  97.4 us
    ppermute x4, waiting for transfers between devices, scatter_rows(): first = lax.ppermute(jnp.where(on_zero, high, low), SWAP, back)  66.2 us
    unnamed x339, local copies, waits for them, and re-layouts  54 us
    ppermute x4, starting transfers between devices, gather_rows(): first = lax.ppermute(shard, SWAP, forth)  46.6 us
    add x7, other arithmetic, adam(): average = average_decay * average + (1.0 - average_decay) * fresh  23.8 us
  transfers between devices with their start and end apart: 24, of which 7 were waited for; matrix products, arithmetic and copies ran while one was open for 23% of the time, Pallas kernels for 31%

profile of v1, /device:TPU:0, one launch (start us, length us, event | category | flops | bytes accessed | tf_op | source)
XLA Modules:
  0.0 849.7 jit_solution(8828623901728396576)
XLA Ops:
  11.1 4.8 collective-permute-start
  17.1 3.6 collective-permute-start.4
  20.7 3.3 collective-permute-done
  24.0 6.5 collective-permute-done.4
  35.9 18.4 %collective-permute-start.2 = (bf16[144,2304]{1,0:T(8,128)(2,1)S(1)}, bf16[144,2304]{1,0:T(8,128)(2,1)S(1)}, u32[]{:S(2)}, u32[]{:S(2)}) collective-permute-start(bf16[144,2304]{1,0:T(8,128)(2,1)S(1)} %pad_maximum_fusion.13), channel_id=1, source_target_pairs={{0,6},{4,0},{1,7},{5,1},{2,4},{6,2},{3,5},{7,3},{8,14},{12,8},{9,1... | collective-permute-start | bytes 1990664 | tf_op jit(solution)/shard_map/ppermute | solution.py:323
  54.2 12.3 %collective-permute-done.2 = bf16[144,2304]{1,0:T(8,128)(2,1)S(1)} collective-permute-done((bf16[144,2304]{1,0:T(8,128)(2,1)S(1)}, bf16[144,2304]{1,0:T(8,128)(2,1)S(1)}, u32[]{:S(2)}, u32[]{:S(2)}) %collective-permute-start.2) | collective-permute-done | bytes 663584 | tf_op jit(solution)/shard_map/ppermute | solution.py:323
  70.5 19.8 %collective-permute-start.6 = (bf16[144,2304]{1,0:T(8,128)(2,1)}, bf16[144,2304]{1,0:T(8,128)(2,1)}, u32[]{:S(2)}, u32[]{:S(2)}) collective-permute-start(bf16[144,2304]{1,0:T(8,128)(2,1)} %pad_maximum_fusion.15), channel_id=1, source_target_pairs={{0,6},{4,0},{1,7},{5,1},{2,4},{6,2},{3,5},{7,3},{8,14},{12,8},{9,1... | collective-permute-start | bytes 1990664 | tf_op jit(solution)/shard_map/ppermute | solution.py:323
  93.7 44.9 %shard_map.562 = (f32[32,16,288]{2,1,0:T(8,128)S(1)}, bf16[4,48,288]{2,1,0:T(8,128)(2,1)S(1)}) custom-call(f32[16,288]{1,0:T(8,128)S(1)} %select_maximum_fusion.refs_0_, bf16[48,288]{1,0:T(8,128)(2,1)S(1)} %pad.22.refs_1_), custom_call_target="tpu_custom_call" | custom-call | bytes 16777216 | tf_op jit(solution)/shard_map/pallas_call | solution.py:135
  143.8 20.4 %shard_map.563 = f32[8,4,12,288]{3,2,1,0:T(8,128)S(1)} custom-call(f32[8,4,12,288]{3,2,1,0:T(8,128)S(1)} %copy.395.refs_0_), custom_call_target="tpu_custom_call" | custom-call | bytes 16777216 | tf_op jit(solution)/shard_map/pallas_call | solution.py:135
  164.3 7.1 shard_map.564
  182.6 11.8 %shard_map.565 = bf16[4,160,1152]{2,1,0:T(8,128)(2,1)S(1)} custom-call(bf16[160,1152]{1,0:T(8,128)(2,1)S(1)} %add_convert_fusion.3.own_ref), custom_call_target="tpu_custom_call" | custom-call | bytes 41943040 | tf_op jit(solution)/shard_map/pallas_call | solution.py:291
  198.3 3.4 fusion.35
  208.1 12.4 %shard_map.566 = f32[160,1152]{1,0:T(8,128)S(1)} custom-call(bf16[4,160,1152]{2,1,0:T(8,128)(2,1)S(1)} %convolution_convert_fusion.6.part_ref), custom_call_target="tpu_custom_call" | custom-call | bytes 41943040 | tf_op jit(solution)/shard_map/pallas_call | solution.py:225
  221.7 11.6 %shard_map.567 = bf16[4,160,1152]{2,1,0:T(8,128)(2,1)S(1)} custom-call(bf16[160,1152]{1,0:T(8,128)(2,1)S(1)} %add_convert_fusion.2.own_ref), custom_call_target="tpu_custom_call" | custom-call | bytes 41943040 | tf_op jit(solution)/shard_map/pallas_call | solution.py:291
  233.4 4.5 fusion.31
  242.2 12.4 %shard_map.568 = f32[160,1152]{1,0:T(8,128)S(1)} custom-call(bf16[4,160,1152]{2,1,0:T(8,128)(2,1)S(1)} %convolution_convert_fusion.5.part_ref), custom_call_target="tpu_custom_call" | custom-call | bytes 41943040 | tf_op jit(solution)/shard_map/pallas_call | solution.py:225
  258.0 16.5 %shard_map.569 = bf16[4,256,1152]{2,1,0:T(8,128)(2,1)S(1)} custom-call(bf16[256,1152]{1,0:T(8,128)(2,1)S(1)} %add_convert_fusion.1.own_ref), custom_call_target="tpu_custom_call" | custom-call | bytes 67108864 | tf_op jit(solution)/shard_map/pallas_call | solution.py:291
  275.9 4.8 convolution_convert_fusion.8
  288.6 17.2 %shard_map.570 = f32[256,1152]{1,0:T(8,128)S(1)} custom-call(bf16[4,256,1152]{2,1,0:T(8,128)(2,1)S(1)} %convolution_convert_fusion.1.part_ref), custom_call_target="tpu_custom_call" | custom-call | bytes 67108864 | tf_op jit(solution)/shard_map/pallas_call | solution.py:225
  307.2 16.3 %shard_map.571 = bf16[4,256,1152]{2,1,0:T(8,128)(2,1)S(1)} custom-call(bf16[256,1152]{1,0:T(8,128)(2,1)S(1)} %add_convert_fusion.own_ref), custom_call_target="tpu_custom_call" | custom-call | bytes 67108864 | tf_op jit(solution)/shard_map/pallas_call | solution.py:291
  325.1 6.3 fusion.32
  331.4 4.4 convolution_convert_fusion.3.part_ref
  335.9 17.2 %shard_map.572 = f32[256,1152]{1,0:T(8,128)S(1)} custom-call(bf16[4,256,1152]{2,1,0:T(8,128)(2,1)S(1)} %convolution_convert_fusion.3.part_ref), custom_call_target="tpu_custom_call" | custom-call | bytes 67108864 | tf_op jit(solution)/shard_map/pallas_call | solution.py:225
  356.7 16.4 %shard_map.573 = bf16[4,256,1152]{2,1,0:T(8,128)(2,1)S(1)} custom-call(bf16[256,1152]{1,0:T(8,128)(2,1)S(1)} %get-tuple-element.258.own_ref), custom_call_target="tpu_custom_call" | custom-call | bytes 67108864 | tf_op jit(solution)/shard_map/pallas_call | solution.py:291
  373.1 6.7 fusion.10
  379.8 4.0 convolution_convert_fusion.2.part_ref
  383.8 17.2 %shard_map.574 = f32[256,1152]{1,0:T(8,128)S(1)} custom-call(bf16[4,256,1152]{2,1,0:T(8,128)(2,1)S(1)} %convolution_convert_fusion.2.part_ref), custom_call_target="tpu_custom_call" | custom-call | bytes 67108864 | tf_op jit(solution)/shard_map/pallas_call | solution.py:225
  403.8 16.3 %shard_map.575 = bf16[4,256,1152]{2,1,0:T(8,128)(2,1)S(1)} custom-call(bf16[256,1152]{1,0:T(8,128)(2,1)S(1)} %get-tuple-element.234.own_ref), custom_call_target="tpu_custom_call" | custom-call | bytes 67108864 | tf_op jit(solution)/shard_map/pallas_call | solution.py:291
  430.2 3.7 bitcast_convert_fusion
  434.0 4.2 convolution_convert_fusion.part_ref
  445.7 17.2 %shard_map.576 = f32[256,1152]{1,0:T(8,128)S(1)} custom-call(bf16[4,256,1152]{2,1,0:T(8,128)(2,1)S(1)} %copy-done.9), custom_call_target="tpu_custom_call" | custom-call | bytes 67108864 | tf_op jit(solution)/shard_map/pallas_call | solution.py:225
  464.6 5.2 copy.459
  474.7 11.6 %shard_map.577 = bf16[4,160,1152]{2,1,0:T(8,128)(2,1)S(1)} custom-call(bf16[160,1152]{1,0:T(8,128)(2,1)S(1)} %get-tuple-element.313.own_ref), custom_call_target="tpu_custom_call" | custom-call | bytes 41943040 | tf_op jit(solution)/shard_map/pallas_call | solution.py:291
  486.3 5.4 fusion.18
  494.1 12.4 %shard_map.578 = f32[160,1152]{1,0:T(8,128)S(1)} custom-call(bf16[4,160,1152]{2,1,0:T(8,128)(2,1)S(1)} %convolution_convert_fusion.4.part_ref), custom_call_target="tpu_custom_call" | custom-call | bytes 41943040 | tf_op jit(solution)/shard_map/pallas_call | solution.py:225
  508.8 11.7 %shard_map.579 = bf16[4,160,1152]{2,1,0:T(8,128)(2,1)S(1)} custom-call(bf16[160,1152]{1,0:T(8,128)(2,1)S(1)} %multiply_convert_fusion.7.own_ref), custom_call_target="tpu_custom_call" | custom-call | bytes 41943040 | tf_op jit(solution)/shard_map/pallas_call | solution.py:291
  520.5 3.0 convolution_convert_fusion.12
  525.6 3.3 convolution_convert_fusion.9
  531.0 3.0 multiply_reduce_fusion.3
  539.1 2.9 fusion.46
  550.1 5.2 copy.457
  555.4 5.8 fusion.2
  561.2 6.2 fusion.3
  570.2 8.6 %copy.463 = bf16[1152,2304]{1,0:T(8,128)(2,1)} copy(bf16[1152,2304]{0,1:T(8,128)(2,1)} %pad_maximum_fusion.1) | data formatting | bytes 10616832
  580.2 3.9 fusion
  589.6 8.6 %copy.461 = bf16[1152,2304]{1,0:T(8,128)(2,1)} copy(bf16[1152,2304]{0,1:T(8,128)(2,1)} %pad_maximum_fusion) | data formatting | bytes 10616832
  604.6 4.0 convolution_convert_fusion.7.part_ref
  608.6 12.4 %shard_map.580 = f32[160,1152]{1,0:T(8,128)S(1)} custom-call(bf16[4,160,1152]{2,1,0:T(8,128)(2,1)S(1)} %convolution_convert_fusion.7.part_ref), custom_call_target="tpu_custom_call" | custom-call | bytes 41943040 | tf_op jit(solution)/shard_map/pallas_call | solution.py:225
  623.0 11.2 %shard_map.581 = (f32[4,12,288]{2,1,0:T(8,128)S(1)}, f32[4,40,288]{2,1,0:T(8,128)S(1)}) custom-call(f32[4,12,288]{2,1,0:T(8,128)S(1)} %bitcast.295, f32[4,40,288]{2,1,0:T(8,128)S(1)} %pad.23.refs_1_), custom_call_target="tpu_custom_call" | custom-call | bytes 16777216 | tf_op jit(solution)/shard_map/pallas_call | solution.py:135
  634.2 21.8 %shard_map.582 = (f32[8,4,12,288]{3,2,1,0:T(8,128)S(1)}, bf16[8,48,288]{2,1,0:T(8,128)(2,1)S(1)}) custom-call(f32[4,12,288]{2,1,0:T(8,128)S(1)} %get-tuple-element.38.refs_0_, bf16[48,288]{1,0:T(8,128)(2,1)S(1)} %pad.24.refs_1_), custom_call_target="tpu_custom_call" | custom-call | bytes 16777216 | tf_op jit(solution)/shard_map/pallas_call | solution.py:135
  661.6 7.8 shard_map.583
  669.4 6.3 shard_map.584
  677.4 4.1 multiply_reduce_fusion.4
  681.5 4.5 multiply_reduce_fusion.2
  698.6 16.6 %collective-permute-done.11 = bf16[144,1152]{1,0:T(8,128)(2,1)} collective-permute-done((bf16[144,1152]{1,0:T(8,128)(2,1)}, bf16[144,1152]{1,0:T(8,128)(2,1)}, u32[]{:S(2)}, u32[]{:S(2)}) %collective-permute-start.11) | collective-permute-done | bytes 331808 | tf_op jit(solution)/shard_map/ppermute | solution.py:340
  738.7 4.0 collective-permute-start.13
  742.7 37.8 %collective-permute-done.15 = bf16[144,2304]{1,0:T(8,128)(2,1)} collective-permute-done((bf16[144,2304]{1,0:T(8,128)(2,1)}, bf16[144,2304]{1,0:T(8,128)(2,1)}, u32[]{:S(2)}, u32[]{:S(2)}) %collective-permute-start.15) | collective-permute-done | bytes 663584 | tf_op jit(solution)/shard_map/ppermute | solution.py:340
  783.7 10.9 %collective-permute-done.13 = bf16[144,2304]{1,0:T(8,128)(2,1)S(1)} collective-permute-done((bf16[144,2304]{1,0:T(8,128)(2,1)S(1)}, bf16[144,2304]{1,0:T(8,128)(2,1)S(1)}, u32[]{:S(2)}, u32[]{:S(2)}) %collective-permute-start.13) | collective-permute-done | bytes 663584 | tf_op jit(solution)/shard_map/ppermute | solution.py:340
  798.8 9.7 %shard_map.585 = f32[32,8,128]{2,1,0:T(8,128)S(1)} custom-call(f32[8,128]{1,0:T(8,128)S(1)} %pad.25.refs_0_), custom_call_target="tpu_custom_call" | custom-call | bytes 16777216 | tf_op jit(solution)/shard_map/pallas_call | solution.py:135
  812.5 6.8 multiply_add_fusion.1
  820.9 4.9 multiply_add_fusion
  828.6 3.3 multiply_add_fusion.3
  833.5 3.3 multiply_add_fusion.4
  838.3 3.2 multiply_add_fusion.5
  (635 shorter events, 185.3 us)
Async XLA Ops:
  7.2 169.8 %copy-start = (bf16[4,256,16]{1,2,0:T(8,128)(2,1)S(1)}, bf16[4,256,16]{1,2,0:T(8,128)(2,1)}, u32[]{:S(2)}) copy-start(bf16[4,256,16]{1,2,0:T(8,128)(2,1)} %param.35) | copy-start | bytes 98308
  7.2 191.0 %all-gather.5.cloned.1.call-start = ((), (), s32[]{:S(2)}) async-start(), calls=%async_computation.4 | async-start | bytes 3317760 | tf_op jit(solution)/shard_map/all_gather | solution.py:327
  10.4 10.3 %collective-permute-start.1 = (bf16[144,1152]{1,0:T(8,128)(2,1)S(1)}, bf16[144,1152]{1,0:T(8,128)(2,1)S(1)}, u32[]{:S(2)}, u32[]{:S(2)}) collective-permute-start(bf16[144,1152]{1,0:T(8,128)(2,1)S(1)} %pad_maximum_fusion.16), channel_id=1, source_target_pairs={{4,6},{5,7},{6,4},{7,5},{12,14},{13,15},{14,12},{15,13},{20,22},{2... | collective-permute-start | bytes 995336 | tf_op jit(solution)/shard_map/ppermute | solution.py:324
  11.1 12.9 %collective-permute-start = (bf16[144,1152]{1,0:T(8,128)(2,1)S(1)}, bf16[144,1152]{1,0:T(8,128)(2,1)S(1)}, u32[]{:S(2)}, u32[]{:S(2)}) collective-permute-start(bf16[144,1152]{1,0:T(8,128)(2,1)S(1)} %pad_maximum_fusion.16), channel_id=1, source_target_pairs={{0,6},{4,0},{1,7},{5,1},{2,4},{6,2},{3,5},{7,3},{8,14},{12,8},{9,1... | collective-permute-start | bytes 995336 | tf_op jit(solution)/shard_map/ppermute | solution.py:323
  16.4 7.6 collective-permute-start.5
  17.1 13.4 %collective-permute-start.4 = (bf16[144,1152]{1,0:T(8,128)(2,1)S(1)}, bf16[144,1152]{1,0:T(8,128)(2,1)}, u32[]{:S(2)}, u32[]{:S(2)}) collective-permute-start(bf16[144,1152]{1,0:T(8,128)(2,1)S(1)} %pad_maximum_fusion.17), channel_id=1, source_target_pairs={{0,6},{4,0},{1,7},{5,1},{2,4},{6,2},{3,5},{7,3},{8,14},{12,8},{9,1... | collective-permute-start | bytes 995336 | tf_op jit(solution)/shard_map/ppermute | solution.py:323
  33.5 199.8 %all-gather.7.cloned.1.call-start = ((), (), s32[]{:S(2)}) async-start(), calls=%async_computation.5 | async-start | bytes 6635520 | tf_op jit(solution)/shard_map/all_gather | solution.py:327
  35.2 19.1 %collective-permute-start.3 = (bf16[144,2304]{1,0:T(8,128)(2,1)S(1)}, bf16[144,2304]{1,0:T(8,128)(2,1)S(1)}, u32[]{:S(2)}, u32[]{:S(2)}) collective-permute-start(bf16[144,2304]{1,0:T(8,128)(2,1)S(1)} %pad_maximum_fusion.13), channel_id=1, source_target_pairs={{4,6},{5,7},{6,4},{7,5},{12,14},{13,15},{14,12},{15,13},{20,22},{2... | collective-permute-start | bytes 1990664 | tf_op jit(solution)/shard_map/ppermute | solution.py:324
  35.9 30.7 %collective-permute-start.2 = (bf16[144,2304]{1,0:T(8,128)(2,1)S(1)}, bf16[144,2304]{1,0:T(8,128)(2,1)S(1)}, u32[]{:S(2)}, u32[]{:S(2)}) collective-permute-start(bf16[144,2304]{1,0:T(8,128)(2,1)S(1)} %pad_maximum_fusion.13), channel_id=1, source_target_pairs={{0,6},{4,0},{1,7},{5,1},{2,4},{6,2},{3,5},{7,3},{8,14},{12,8},{9,1... | collective-permute-start | bytes 1990664 | tf_op jit(solution)/shard_map/ppermute | solution.py:323
  68.0 22.3 %copy-start.151 = (s32[4]{0:T(128)S(1)}, s32[4]{0:T(128)}, u32[]{:S(2)}) copy-start(s32[4]{0:T(128)} %param.38) | copy-start | bytes 52
  68.0 23.6 %copy-start.150 = (s32[4]{0:T(128)S(1)}, s32[4]{0:T(128)}, u32[]{:S(2)}) copy-start(s32[4]{0:T(128)} %param.39) | copy-start | bytes 52
  68.0 23.6 %copy-start.152 = (s32[4]{0:T(128)S(1)}, s32[4]{0:T(128)}, u32[]{:S(2)}) copy-start(s32[4]{0:T(128)} %param.40) | copy-start | bytes 52
  68.0 24.7 %copy-start.91 = (f32[33,288]{1,0:T(8,128)S(1)}, f32[33,288]{1,0:T(8,128)}, u32[]{:S(2)}) copy-start(f32[33,288]{1,0:T(8,128)} %param.47) | copy-start | bytes 114052
  68.0 24.7 %copy-start.36 = (f32[1256,288]{0,1:T(8,128)S(1)}, f32[1256,288]{0,1:T(8,128)}, u32[]{:S(2)}) copy-start(f32[1256,288]{0,1:T(8,128)} %param.48) | copy-start | bytes 4340740
  68.1 207.8 %all-gather.9.cloned.1.call-start = ((), (), s32[]{:S(2)}) async-start(), calls=%async_computation.6 | async-start | bytes 3317760 | tf_op jit(solution)/shard_map/all_gather | solution.py:327
  69.0 126.4 %collective-permute-start.7 = (bf16[144,2304]{1,0:T(8,128)(2,1)}, bf16[144,2304]{1,0:T(8,128)(2,1)}, u32[]{:S(2)}, u32[]{:S(2)}) collective-permute-start(bf16[144,2304]{1,0:T(8,128)(2,1)} %pad_maximum_fusion.15), channel_id=1, source_target_pairs={{4,6},{5,7},{6,4},{7,5},{12,14},{13,15},{14,12},{15,13},{20,22},{2... | collective-permute-start | bytes 1990664 | tf_op jit(solution)/shard_map/ppermute | solution.py:324
  70.5 124.9 %collective-permute-start.6 = (bf16[144,2304]{1,0:T(8,128)(2,1)}, bf16[144,2304]{1,0:T(8,128)(2,1)}, u32[]{:S(2)}, u32[]{:S(2)}) collective-permute-start(bf16[144,2304]{1,0:T(8,128)(2,1)} %pad_maximum_fusion.15), channel_id=1, source_target_pairs={{0,6},{4,0},{1,7},{5,1},{2,4},{6,2},{3,5},{7,3},{8,14},{12,8},{9,1... | collective-permute-start | bytes 1990664 | tf_op jit(solution)/shard_map/ppermute | solution.py:323
  143.8 33.4 %copy-start.82 = (bf16[1,144,1152]{2,1,0:T(8,128)(2,1)S(1)}, bf16[1,144,1152]{2,1,0:T(8,128)(2,1)}, u32[]{:S(2)}) copy-start(bf16[1,144,1152]{2,1,0:T(8,128)(2,1)} %get-tuple-element.282) | copy-start | bytes 995332
  173.1 84.0 %copy-start.95 = (f32[1152]{0:T(1024)}, f32[1152]{0:T(1024)S(1)}, u32[]{:S(2)}) copy-start(f32[1152]{0:T(1024)S(1)} %add.485) | copy-start | bytes 13828
  174.1 46.5 %copy-start.98 = (f32[1152]{0:T(1024)}, f32[1152]{0:T(1024)S(1)}, u32[]{:S(2)}) copy-start(f32[1152]{0:T(1024)S(1)} %mul.1105) | copy-start | bytes 13828
  176.3 18.2 %copy-start.113 = (f32[160]{0:T(256)}, f32[160]{0:T(256)S(1)}, u32[]{:S(2)}) copy-start(f32[160]{0:T(256)S(1)} %compare_convert_fusion) | copy-start | bytes 1924
  177.0 17.5 %copy-start.117 = (s32[1,160]{1,0:T(1,128)}, s32[1,160]{1,0:T(1,128)S(1)}, u32[]{:S(2)}) copy-start(s32[1,160]{1,0:T(1,128)S(1)} %constant_dynamic-slice_fusion.2) | copy-start | bytes 1924
  178.2 146.9 %all-gather.11.cloned.1.call-start = ((), (), s32[]{:S(2)}) async-start(), calls=%async_computation.7 | async-start | bytes 6635520 | tf_op jit(solution)/shard_map/all_gather | solution.py:327
  198.0 488.0 %reduce-scatter.15.cloned.1.call-start = ((), (), s32[]{:S(2)}) async-start(), calls=%async_computation.9 | async-start | bytes 3317760 | tf_op jit(solution)/shard_map/reduce_scatter | solution.py:334
  220.8 102.7 %copy-start.25 = (f32[160,1152]{1,0:T(8,128)}, f32[160,1152]{1,0:T(8,128)S(1)}, u32[]{:S(2)}) copy-start(f32[160,1152]{1,0:T(8,128)S(1)} %get-tuple-element.245) | copy-start | bytes 2211844
  242.2 12.5 %copy-start.38 = (f32[256,576]{1,0:T(8,128)S(1)}, f32[256,576]{1,0:T(8,128)}, u32[]{:S(2)}) copy-start(f32[256,576]{1,0:T(8,128)} %copy-done.37) | copy-start | bytes 1769476
  242.2 12.5 %copy-start.40 = (f32[256,576]{1,0:T(8,128)S(1)}, f32[256,576]{1,0:T(8,128)}, u32[]{:S(2)}) copy-start(f32[256,576]{1,0:T(8,128)} %copy-done.39) | copy-start | bytes 1769476
  242.2 12.5 %copy-start.109 = (f32[1152]{0:T(1024)S(1)}, f32[1152]{0:T(1024)}, u32[]{:S(2)}) copy-start(f32[1152]{0:T(1024)} %reshape.599) | copy-start | bytes 13828
  242.2 12.5 %copy-start.114 = (f32[160]{0:T(256)S(1)}, f32[160]{0:T(256)}, u32[]{:S(2)}) copy-start(f32[160]{0:T(256)} %copy-done.113) | copy-start | bytes 1924
  257.0 17.5 %copy-start.142 = (f32[256]{0:T(256)}, f32[256]{0:T(256)S(1)}, u32[]{:S(2)}) copy-start(f32[256]{0:T(256)S(1)} %multiply_reduce_fusion.17) | copy-start | bytes 3076
  257.7 16.8 %copy-start.132 = (f32[256]{0:T(256)}, f32[256]{0:T(256)S(1)}, u32[]{:S(2)}) copy-start(f32[256]{0:T(256)S(1)} %fusion.126) | copy-start | bytes 3076
  288.6 17.3 %copy-start.21 = (f32[256,1152]{1,0:T(8,128)S(1)}, f32[256,1152]{1,0:T(8,128)}, u32[]{:S(2)}) copy-start(f32[256,1152]{1,0:T(8,128)} %copy-done.20) | copy-start | bytes 3538948
  288.6 17.3 %copy-start.100 = (f32[1152]{0:T(1024)S(1)}, f32[1152]{0:T(1024)}, u32[]{:S(2)}) copy-start(f32[1152]{0:T(1024)} %mul.1129) | copy-start | bytes 13828
  306.4 17.1 %copy-start.144 = (f32[256]{0:T(256)}, f32[256]{0:T(256)S(1)}, u32[]{:S(2)}) copy-start(f32[256]{0:T(256)S(1)} %multiply_reduce_fusion.16) | copy-start | bytes 3076
  306.8 16.7 %copy-start.134 = (f32[256]{0:T(256)}, f32[256]{0:T(256)S(1)}, u32[]{:S(2)}) copy-start(f32[256]{0:T(256)S(1)} %fusion.127) | copy-start | bytes 3076
  307.2 17.8 %copy-start.115 = (f32[160]{0:T(256)S(1)}, f32[160]{0:T(256)}, u32[]{:S(2)}) copy-start(f32[160]{0:T(256)} %copy-done.113) | copy-start | bytes 1924
  331.4 41.6 %copy-start.162 = (f32[4,256,1152]{2,1,0:T(8,128)}, f32[4,256,1152]{2,1,0:T(8,128)S(1)}, u32[]{:S(2)}) copy-start(f32[4,256,1152]{2,1,0:T(8,128)S(1)} %fusion.32) | copy-start | bytes 14155780
  335.9 17.3 %copy-start.24 = (f32[256,1152]{1,0:T(8,128)S(1)}, f32[256,1152]{1,0:T(8,128)}, u32[]{:S(2)}) copy-start(f32[256,1152]{1,0:T(8,128)} %copy-done.23) | copy-start | bytes 3538948
  335.9 17.3 %copy-start.101 = (f32[1152]{0:T(1024)S(1)}, f32[1152]{0:T(1024)}, u32[]{:S(2)}) copy-start(f32[1152]{0:T(1024)} %mul.1138) | copy-start | bytes 13828
  383.8 17.3 %copy-start.127 = (f32[256]{0:T(256)S(1)}, f32[256]{0:T(256)}, u32[]{:S(2)}) copy-start(f32[256]{0:T(256)} %copy-done.126) | copy-start | bytes 3076
  383.8 17.3 %copy-start.135 = (f32[256]{0:T(256)S(1)}, f32[256]{0:T(256)}, u32[]{:S(2)}) copy-start(f32[256]{0:T(256)} %copy-done.134) | copy-start | bytes 3076
  403.8 16.3 %copy-start.158 = (bf16[4,4,72,256]{3,2,1,0:T(8,128)(2,1)S(1)}, bf16[4,4,72,256]{3,2,1,0:T(8,128)(2,1)}, u32[]{:S(2)}) copy-start(bf16[4,4,72,256]{3,2,1,0:T(8,128)(2,1)} %copy-done.157) | copy-start | bytes 1769476
  445.7 17.2 %copy-start.70 = (bf16[1152,864]{0,1:T(8,128)(2,1)S(1)}, bf16[1152,864]{0,1:T(8,128)(2,1)}, u32[]{:S(2)}) copy-start(bf16[1152,864]{0,1:T(8,128)(2,1)} %bitcast_convert_fusion) | copy-start | bytes 5971972
  445.7 17.2 %copy-start.83 = (bf16[1152,288]{0,1:T(8,128)(2,1)S(1)}, bf16[1152,288]{0,1:T(8,128)(2,1)}, u32[]{:S(2)}) copy-start(bf16[1152,288]{0,1:T(8,128)(2,1)} %fusion.23) | copy-start | bytes 1990660
  469.9 221.7 %reduce-scatter.13.cloned.1.call-start = ((), (), s32[]{:S(2)}) async-start(), calls=%async_computation.8 | async-start | bytes 3317760 | tf_op jit(solution)/shard_map/reduce_scatter | solution.py:334
  473.6 12.7 %copy-start.160 = (f32[4,160,1152]{2,1,0:T(8,128)S(1)}, f32[4,160,1152]{2,1,0:T(8,128)}, u32[]{:S(2)}) copy-start(f32[4,160,1152]{2,1,0:T(8,128)} %copy-done.159) | copy-start | bytes 8847364
  473.6 18.1 %slice-start = ((s8[5308416]{0:T(1024)(128)(4,1)}), s8[1114112]{0:T(1024)(128)(4,1)S(1)}, s32[]{:S(2)}) async-start(s8[5308416]{0:T(1024)(128)(4,1)} %bitcast.348), calls=%async_computation.12 | async-start | bytes 2228224
  494.1 12.9 %copy-start.141 = (f32[160]{0:T(256)S(1)}, f32[160]{0:T(256)}, u32[]{:S(2)}) copy-start(f32[160]{0:T(256)} %copy-done.140) | copy-start | bytes 1924
  555.3 177.2 %reduce-scatter.19.cloned.1.call-start = ((), (), s32[]{:S(2)}) async-start(), calls=%async_computation.11 | async-start | bytes 6635520 | tf_op jit(solution)/shard_map/reduce_scatter | solution.py:334
  578.8 157.7 %reduce-scatter.17.cloned.1.call-start = ((), (), s32[]{:S(2)}) async-start(), calls=%async_computation.10 | async-start | bytes 6635520 | tf_op jit(solution)/shard_map/reduce_scatter | solution.py:334
  634.2 25.0 %copy-start.30 = (f32[2,144,6,288]{3,1,2,0:T(8,128)S(1)}, f32[2,144,6,288]{3,1,2,0:T(8,128)}, u32[]{:S(2)}) copy-start(f32[2,144,6,288]{3,1,2,0:T(8,128)} %param.46) | copy-start | bytes 5971972
  688.1 10.5 %collective-permute-start.10 = (bf16[144,1152]{1,0:T(8,128)(2,1)}, bf16[144,1152]{1,0:T(8,128)(2,1)S(1)}, u32[]{:S(2)}, u32[]{:S(2)}) collective-permute-start(bf16[144,1152]{1,0:T(8,128)(2,1)} %get-tuple-element.265), channel_id=1, source_target_pairs={{6,4},{7,5},{4,6},{5,7},{14,12},{15,13},{12,14},{13,15},{22,20},{2... | collective-permute-start | bytes 995336 | tf_op jit(solution)/shard_map/ppermute | solution.py:341
  688.8 26.5 %collective-permute-start.11 = (bf16[144,1152]{1,0:T(8,128)(2,1)}, bf16[144,1152]{1,0:T(8,128)(2,1)}, u32[]{:S(2)}, u32[]{:S(2)}) collective-permute-start(bf16[144,1152]{1,0:T(8,128)(2,1)} %get-tuple-element.266), channel_id=1, source_target_pairs={{6,0},{0,4},{7,1},{1,5},{4,2},{2,6},{5,3},{3,7},{14,8},{8,12},{15,... | collective-permute-start | bytes 995336 | tf_op jit(solution)/shard_map/ppermute | solution.py:340
  693.5 28.0 %collective-permute-start.8 = (bf16[144,1152]{1,0:T(8,128)(2,1)}, bf16[144,1152]{1,0:T(8,128)(2,1)}, u32[]{:S(2)}, u32[]{:S(2)}) collective-permute-start(bf16[144,1152]{1,0:T(8,128)(2,1)} %get-tuple-element.267), channel_id=1, source_target_pairs={{6,4},{7,5},{4,6},{5,7},{14,12},{15,13},{12,14},{13,15},{22,20},{2... | collective-permute-start | bytes 995336 | tf_op jit(solution)/shard_map/ppermute | solution.py:341
  694.9 27.5 %collective-permute-start.9 = (bf16[144,1152]{1,0:T(8,128)(2,1)}, bf16[144,1152]{1,0:T(8,128)(2,1)}, u32[]{:S(2)}, u32[]{:S(2)}) collective-permute-start(bf16[144,1152]{1,0:T(8,128)(2,1)} %get-tuple-element.268), channel_id=1, source_target_pairs={{6,0},{0,4},{7,1},{1,5},{4,2},{2,6},{5,3},{3,7},{14,8},{8,12},{15,... | collective-permute-start | bytes 995336 | tf_op jit(solution)/shard_map/ppermute | solution.py:340
  735.0 7.7 collective-permute-start.14
  736.5 44.0 %collective-permute-start.15 = (bf16[144,2304]{1,0:T(8,128)(2,1)}, bf16[144,2304]{1,0:T(8,128)(2,1)}, u32[]{:S(2)}, u32[]{:S(2)}) collective-permute-start(bf16[144,2304]{1,0:T(8,128)(2,1)} %get-tuple-element.254), channel_id=1, source_target_pairs={{6,0},{0,4},{7,1},{1,5},{4,2},{2,6},{5,3},{3,7},{14,8},{8,12},{15,... | collective-permute-start | bytes 1990664 | tf_op jit(solution)/shard_map/ppermute | solution.py:340
  736.5 44.0 %copy-start.54 = (bf16[288,2304]{1,0:T(8,128)(2,1)S(1)}, bf16[288,2304]{1,0:T(8,128)(2,1)}, u32[]{:S(2)}) copy-start(bf16[288,2304]{1,0:T(8,128)(2,1)} %reduce-scatter.19.cloned.1.call-done) | copy-start | bytes 3981316
  738.0 45.8 %collective-permute-start.12 = (bf16[144,2304]{1,0:T(8,128)(2,1)S(1)}, bf16[144,2304]{1,0:T(8,128)(2,1)S(1)}, u32[]{:S(2)}, u32[]{:S(2)}) collective-permute-start(bf16[144,2304]{1,0:T(8,128)(2,1)S(1)} %get-tuple-element.255), channel_id=1, source_target_pairs={{6,4},{7,5},{4,6},{5,7},{14,12},{15,13},{12,14},{13,15},{22,20},{2... | collective-permute-start | bytes 1990664 | tf_op jit(solution)/shard_map/ppermute | solution.py:341
  738.7 55.9 %collective-permute-start.13 = (bf16[144,2304]{1,0:T(8,128)(2,1)S(1)}, bf16[144,2304]{1,0:T(8,128)(2,1)S(1)}, u32[]{:S(2)}, u32[]{:S(2)}) collective-permute-start(bf16[144,2304]{1,0:T(8,128)(2,1)S(1)} %get-tuple-element.256), channel_id=1, source_target_pairs={{6,0},{0,4},{7,1},{1,5},{4,2},{2,6},{5,3},{3,7},{14,8},{8,12},{15,... | collective-permute-start | bytes 1990664 | tf_op jit(solution)/shard_map/ppermute | solution.py:340
  795.6 16.2 %copy-start.92 = (f32[33,288]{1,0:T(8,128)S(1)}, f32[33,288]{1,0:T(8,128)}, u32[]{:S(2)}) copy-start(f32[33,288]{1,0:T(8,128)} %param.47) | copy-start | bytes 114052
  795.6 16.2 %copy-start.106 = (f32[33,288]{1,0:T(8,128)S(1)}, f32[33,288]{1,0:T(8,128)}, u32[]{:S(2)}) copy-start(f32[33,288]{1,0:T(8,128)} %param.68) | copy-start | bytes 114052
  795.6 16.2 %copy-start.107 = (f32[33,288]{1,0:T(8,128)S(1)}, f32[33,288]{1,0:T(8,128)}, u32[]{:S(2)}) copy-start(f32[33,288]{1,0:T(8,128)} %param.54) | copy-start | bytes 114052
  795.6 16.2 %copy-start.108 = (f32[33,288]{1,0:T(8,128)S(1)}, f32[33,288]{1,0:T(8,128)}, u32[]{:S(2)}) copy-start(f32[33,288]{1,0:T(8,128)} %param.61) | copy-start | bytes 114052
  (127 other events, 519.2 us)
Sparse Core Ops, SparseCore 0:
  33.6 55.5 all-gather.4
  91.7 75.7 all-gather.6
  178.3 39.4 all-gather.8
  220.0 61.9 all-gather.10
  470.0 39.0 reduce-scatter.14
  555.4 39.0 reduce-scatter.12
  597.6 68.3 reduce-scatter.18
  669.0 62.0 reduce-scatter.16

commit v2 on v1

v2 whole, which is shorter than its diff:
```python
from functools import partial
import math

import jax
import jax.numpy as jnp
from jax import lax
from jax.experimental import pallas as pl
from jax.experimental.pallas import tpu as pltpu
from jax.sharding import Mesh
from jax.sharding import PartitionSpec as P

HEAD_DIM = 72
CLASSES = 1000
FREQ = 256
PATCH_IN = 16
STEP = 10

MESH = pl.DeviceIdType.MESH
WIDE = ("py", "px", "core")
NARROW = ("zh", "zl")
ALL = WIDE + NARROW

highest_float_accuracy = lax.Precision.HIGHEST
norm_eps = 1e-06
contrast_sharpness_divisor = 0.02
nce_weight = 0.5
learn_rate = 0.05
beta_first = 0.9
beta_second = 0.999
adam_eps = 1e-08
weight_decay = 0.05
clip_norm = 0.05
ema_decay = 0.9999


def layer_norm(values):
    center = values - jnp.mean(values, -1, keepdims=True)
    return center * lax.rsqrt(jnp.mean(center * center, -1, keepdims=True) + norm_eps)


def modulate(values, shift, scale):
    return layer_norm(values) * (1.0 + scale[None, :]) + shift[None, :]


def sinusoid(places, width):
    half = width // 2
    freqs = jnp.exp(-math.log(10000.0) * jnp.arange(half, dtype=jnp.float32) / half)
    angle = places.astype(jnp.float32)[:, None] * freqs[None, :]
    return jnp.concatenate([jnp.cos(angle), jnp.sin(angle)], -1)


def flat_place(axes):
    place = 0
    for axis in axes:
        place = place * lax.axis_size(axis) + lax.axis_index(axis)
    return place


def group_size(axes):
    size = 1
    for axis in axes:
        size = size * lax.axis_size(axis)
    return size


def device_at(axes, place):
    where = {}
    for axis in reversed(axes):
        where[axis] = lax.rem(place, lax.axis_size(axis))
        place = place // lax.axis_size(axis)
    return where


def turned(axis, offset):
    size = lax.axis_size(axis)
    return lax.rem(lax.axis_index(axis) + (offset % size), size)


def other(axis):
    return 1 - lax.axis_index(axis)


class Part:
    def __init__(self):
        self.arrays, self.in_spaces = [], []
        self.shapes, self.out_spaces = [], []
        self.aliases = {}
        self.scratch = []
        self.peers = []

    def take(self, array, space=pltpu.HBM):
        self.arrays.append(array)
        self.in_spaces.append(space)
        return len(self.arrays) - 1

    def give(self, shape, dtype=jnp.bfloat16, space=pltpu.HBM, source=None):
        self.shapes.append(jax.ShapeDtypeStruct(shape, dtype))
        self.out_spaces.append(space)
        if source is not None:
            self.aliases[source] = len(self.shapes) - 1
        return len(self.shapes) - 1

    def greet(self, barrier):
        for peer in self.peers:
            pl.semaphore_signal(barrier, inc=1, device_id=peer(), device_id_type=MESH)
        return len(self.peers)

    def begin(self, ins, outs, scratch):
        pass

    def finish(self, ins, outs, scratch):
        pass


class Exchange(Part):
    def __init__(self, arrays, specs):
        super().__init__()
        self.specs = specs
        for array, (axes, mode) in zip(arrays, specs):
            size = group_size(axes)
            piece = array.shape[1:] if mode == "each" else array.shape
            self.take(array, pltpu.VMEM)
            self.give((size,) + piece, array.dtype, pltpu.VMEM)
            self.scratch += [pltpu.SemaphoreType.DMA((size,)), pltpu.SemaphoreType.DMA((size,))]

    def greet(self, barrier):
        greeted = 0
        for axes, _ in self.specs:
            size, me = group_size(axes), flat_place(axes)
            greeted += size - 1

            def signal(offset, carry, axes=axes, size=size, me=me):
                target = lax.rem(me + offset, size)
                pl.semaphore_signal(
                    barrier, inc=1, device_id=device_at(axes, target), device_id_type=MESH
                )
                return carry

            lax.fori_loop(1, size, signal, 0)
        return greeted

    def begin(self, ins, outs, scratch):
        def copy_to(index, offset, arriving):
            axes, mode = self.specs[index]
            size, me = group_size(axes), flat_place(axes)
            target = lax.rem(me + offset, size)
            return pltpu.make_async_remote_copy(
                src_ref=ins[index].at[target] if mode == "each" else ins[index],
                dst_ref=outs[index].at[target if arriving else me],
                send_sem=scratch[2 * index].at[target],
                recv_sem=scratch[2 * index + 1].at[target if arriving else me],
                device_id=device_at(axes, target),
                device_id_type=MESH,
            )

        for index, (axes, mode) in enumerate(self.specs):

            def start(offset, carry, index=index):
                copy_to(index, offset, False).start()
                return carry

            lax.fori_loop(1, group_size(axes), start, 0)
        for index, (axes, mode) in enumerate(self.specs):
            me = flat_place(axes)
            outs[index][me] = ins[index][me] if mode == "each" else ins[index][...]
        for index, (axes, mode) in enumerate(self.specs):

            def end(offset, carry, index=index):
                copy_to(index, offset, True).wait_recv()
                copy_to(index, offset, False).wait_send()
                return carry

            lax.fori_loop(1, group_size(axes), end, 0)


def chunk_of(length):
    return 64 if length % 64 == 0 else 32


class GroupPart(Part):
    def __init__(self, length):
        super().__init__()
        self.chunk = chunk_of(length)
        self.steps = length // self.chunk
        self.peers = [lambda: {"core": other("core")}, lambda: {"zl": other("zl")}]

    def ranks(self):
        core, low = lax.axis_index("core"), lax.axis_index("zl")
        return core * 2 + low, (1 - core) * 2 + low, core * 2 + 1 - low, (1 - core) * 2 + 1 - low

    def copy(self, source, target, sems, kind, step):
        peer = {"zl": other("zl")} if kind == "far" else {"core": other("core")}
        row = {"far": 0, "mate": 1, "relay": 2}[kind]
        return pltpu.make_async_remote_copy(
            src_ref=source,
            dst_ref=target,
            send_sem=sems[0].at[row, step],
            recv_sem=sems[1].at[row, step],
            device_id=peer,
            device_id_type=MESH,
        )

    def sems(self):
        return [pltpu.SemaphoreType.DMA((3, self.steps)), pltpu.SemaphoreType.DMA((3, self.steps))]


class OwnSum(GroupPart):
    def __init__(self, parts):
        _, length, width = parts.shape
        super().__init__(length)
        self.take(parts, pltpu.VMEM)
        self.give((length, width), jnp.float32, pltpu.VMEM)
        self.scratch = [pltpu.VMEM((length, width), jnp.bfloat16)] * 4 + self.sems()

    def begin(self, ins, outs, scratch):
        (part_ref,), (sum_ref,) = ins, outs
        near, home, stage, far = scratch[:4]
        sems = scratch[4:]
        me, mate, away, away_mate = self.ranks()
        rows = [pl.ds(s * self.chunk, self.chunk) for s in range(self.steps)]
        every = range(self.steps)
        to_near = [self.copy(part_ref.at[away_mate, rows[s]], near.at[rows[s]], sems, "mate", s) for s in every]
        to_home = [self.copy(part_ref.at[mate, rows[s]], home.at[rows[s]], sems, "relay", s) for s in every]
        to_far = [self.copy(stage.at[rows[s]], far.at[rows[s]], sems, "far", s) for s in every]
        for s in every:
            to_near[s].start()
        for s in every:
            to_home[s].start()
        for s in every:
            to_near[s].wait_recv()
            both = part_ref[away, rows[s]].astype(jnp.float32) + near[rows[s]].astype(jnp.float32)
            stage[rows[s]] = both.astype(jnp.bfloat16)
            to_far[s].start()
        for s in every:
            to_home[s].wait_recv()
            sum_ref[rows[s]] = part_ref[me, rows[s]].astype(jnp.float32) + home[rows[s]].astype(
                jnp.float32
            )
        for s in every:
            to_far[s].wait_recv()
            sum_ref[rows[s]] = sum_ref[rows[s]] + far[rows[s]].astype(jnp.float32)
        for s in every:
            to_near[s].wait_send()
            to_home[s].wait_send()
            to_far[s].wait_send()


class GroupCopy(GroupPart):
    def __init__(self, own):
        length, width = own.shape
        super().__init__(length)
        self.take(own, pltpu.VMEM)
        self.give((4, length, width), jnp.bfloat16, pltpu.VMEM)
        self.scratch = self.sems()

    def begin(self, ins, outs, scratch):
        (own_ref,), (all_ref,) = ins, outs
        me, mate, away, away_mate = self.ranks()
        rows = [pl.ds(s * self.chunk, self.chunk) for s in range(self.steps)]
        every = range(self.steps)

        def move(kind, source, slot, s):
            return self.copy(source.at[rows[s]], all_ref.at[slot, rows[s]], scratch, kind, s)

        out = [move("far", own_ref, me, s) for s in every]
        arrive = [move("far", own_ref, away, s) for s in every]
        mate_out = [move("mate", own_ref, me, s) for s in every]
        mate_in = [move("mate", own_ref, mate, s) for s in every]
        relay_out = [move("relay", all_ref.at[away], away, s) for s in every]
        relay_in = [move("relay", all_ref.at[away], away_mate, s) for s in every]
        for s in every:
            out[s].start()
        for s in every:
            mate_out[s].start()
        all_ref[me] = own_ref[...]
        for s in every:
            arrive[s].wait_recv()
            relay_out[s].start()
        for s in every:
            mate_in[s].wait_recv()
            relay_in[s].wait_recv()
        for s in every:
            out[s].wait_send()
            mate_out[s].wait_send()
            relay_out[s].wait_send()


class Errand(Part):
    def plan(self, ins, outs):
        raise NotImplementedError

    def local(self, ins, outs):
        return []

    def reserve(self, count, local=0):
        self.scratch = [pltpu.SemaphoreType.DMA((count,)), pltpu.SemaphoreType.DMA((count,))]
        if local:
            self.scratch.append(pltpu.SemaphoreType.DMA((local,)))

    def run(self, ins, outs, scratch, ending):
        for i, (source, target, landing, device, when) in enumerate(self.plan(ins, outs)):

            def remote(place, i=i, source=source, device=device):
                return pltpu.make_async_remote_copy(
                    src_ref=source,
                    dst_ref=place,
                    send_sem=scratch[0].at[i],
                    recv_sem=scratch[1].at[i],
                    device_id=device,
                    device_id_type=MESH,
                )

            def act(remote=remote, target=target, landing=landing):
                if ending:
                    remote(landing).wait_recv()
                    remote(target).wait_send()
                else:
                    remote(target).start()

            if when is None:
                act()
            else:
                pl.when(when)(act)
        for i, (source, target, when) in enumerate(self.local(ins, outs)):

            def act_local(i=i, source=source, target=target):
                copy = pltpu.make_async_copy(source, target, scratch[2].at[i])
                if ending:
                    copy.wait()
                else:
                    copy.start()

            pl.when(when)(act_local)

    def begin(self, ins, outs, scratch):
        self.run(ins, outs, scratch, False)

    def finish(self, ins, outs, scratch):
        self.run(ins, outs, scratch, True)


def plane_peers():
    peers = []
    for axis in ("py", "px"):
        for offset in range(1, lax.axis_size(axis)):
            peers.append(lambda axis=axis, offset=offset: {axis: turned(axis, offset)})
    return peers


SWAP_PEERS = [
    lambda: {"core": other("core")},
    lambda: {"zh": other("zh")},
    lambda: {"core": other("core"), "zh": other("zh")},
]


class SwapIn(Errand):
    def __init__(self, shard):
        super().__init__()
        self.take(shard)
        self.give((lax.axis_size("py"), lax.axis_size("px"), 2) + shard.shape)
        self.peers = SWAP_PEERS
        self.reserve(2, 1)

    def plan(self, ins, outs):
        core, half = lax.axis_index("core"), lax.axis_index("zh")
        home = outs[0].at[lax.axis_index("py"), lax.axis_index("px")]
        crossed = jnp.where(core == 0, 1 - half, half)
        return [
            (ins[0], home.at[core], home.at[1 - core], {"core": 1 - core, "zh": crossed}, None),
            (ins[0], home.at[1], home.at[1], {"zh": 1 - half}, core == 1),
        ]

    def local(self, ins, outs):
        home = outs[0].at[lax.axis_index("py"), lax.axis_index("px")]
        return [(ins[0], home.at[0], lax.axis_index("core") == 0)]


class Spread(Errand):
    def __init__(self, rows, stages):
        super().__init__()
        self.stages = stages
        self.give(rows.shape, rows.dtype, pltpu.HBM, self.take(rows))
        self.peers = plane_peers()
        ny, nx = rows.shape[:2]
        straight = nx + ny - 2
        self.reserve(
            sum({"a": straight, "b": straight, "c": 2 * (nx - 1) * (ny - 1)}[s] for s in stages)
        )

    def plan(self, ins, outs):
        rows = outs[0]
        ny, nx = rows.shape[:2]
        y, x = lax.axis_index("py"), lax.axis_index("px")
        moves = []

        def along(axis, offset, at, core):
            to = {axis: turned(axis, offset)}
            back = turned(axis, -offset)
            here = rows.at[at["py"], at["px"], core]
            land = dict(at)
            land[axis] = back
            moves.append((here, here, rows.at[land["py"], land["px"], core], to, None))

        own = {"py": y, "px": x}
        sides = [("px", nx), ("py", ny)]
        for stage in self.stages:
            if stage in "ab":
                for core, (axis, size) in enumerate(sides if stage == "a" else sides[::-1]):
                    for offset in range(1, size):
                        along(axis, offset, own, core)
            else:
                for e in range(1, nx):
                    for offset in range(1, ny):
                        along("py", offset, {"py": y, "px": turned("px", e)}, 0)
                for e in range(1, ny):
                    for offset in range(1, nx):
                        along("px", offset, {"py": turned("py", e), "px": x}, 1)
        return moves


class FoldFar(Errand):
    def __init__(self, grad):
        super().__init__()
        self.take(grad)
        ny, nx, _, rows, columns = grad.shape
        self.give((ny - 1, nx - 1, rows, columns))
        self.give((nx - 1, ny - 1, rows, columns))
        self.peers = plane_peers()
        self.reserve(2 * (nx - 1) * (ny - 1))

    def plan(self, ins, outs):
        grad = ins[0]
        ny, nx = grad.shape[:2]
        moves = []
        for e in range(1, nx):
            for d in range(1, ny):
                slot = outs[0].at[d - 1, e - 1]
                to = turned("py", d)
                moves.append((grad.at[to, turned("px", e), 0], slot, slot, {"py": to}, None))
        for e in range(1, ny):
            for d in range(1, nx):
                slot = outs[1].at[d - 1, e - 1]
                to = turned("px", d)
                moves.append((grad.at[turned("py", e), to, 1], slot, slot, {"px": to}, None))
        return moves


class FoldNear(Errand):
    def __init__(self, grad):
        super().__init__()
        self.take(grad)
        ny, nx, _, rows, columns = grad.shape
        self.give((ny - 1, rows, columns))
        self.give((nx - 1, rows, columns))
        self.peers = plane_peers()
        self.reserve(nx + ny - 2)

    def plan(self, ins, outs):
        grad = ins[0]
        ny, nx = grad.shape[:2]
        y, x = lax.axis_index("py"), lax.axis_index("px")
        moves = []
        for d in range(1, ny):
            to, slot = turned("py", d), outs[0].at[d - 1]
            moves.append((grad.at[to, x, 0], slot, slot, {"py": to}, None))
        for d in range(1, nx):
            to, slot = turned("px", d), outs[1].at[d - 1]
            moves.append((grad.at[y, to, 1], slot, slot, {"px": to}, None))
        return moves


class FoldRelay(Errand):
    def __init__(self, sums):
        super().__init__()
        for each in sums:
            self.take(each)
            self.give(each.shape)
        self.peers = plane_peers()
        self.reserve(sums[0].shape[0] + sums[1].shape[0])

    def plan(self, ins, outs):
        moves = []
        for i, axis in enumerate(("px", "py")):
            for e in range(1, lax.axis_size(axis)):
                slot = outs[i].at[e - 1]
                moves.append((ins[i].at[e - 1], slot, slot, {axis: turned(axis, e)}, None))
        return moves


class SwapOut(Errand):
    def __init__(self, pair):
        super().__init__()
        self.take(pair)
        self.give(pair.shape)
        self.peers = SWAP_PEERS
        self.reserve(2, 1)

    def plan(self, ins, outs):
        core, half = lax.axis_index("core"), lax.axis_index("zh")
        crossed = jnp.where(core == 0, half, 1 - half)
        pair, met = ins[0], outs[0]
        return [
            (pair.at[1 - core], met.at[0], met.at[0], {"core": 1 - core, "zh": crossed}, None),
            (pair.at[1], met.at[1], met.at[1], {"zh": 1 - half}, core == 1),
        ]

    def local(self, ins, outs):
        return [(ins[0].at[0], outs[0].at[1], lax.axis_index("core") == 0)]


def take_counts(refs, parts, name):
    taken, rest = [], list(refs)
    for part in parts:
        size = len(getattr(part, name))
        taken.append(rest[:size])
        rest = rest[size:]
    return taken, rest


def kernel(parts, *refs):
    ins, refs = take_counts(refs, parts, "arrays")
    outs, refs = take_counts(refs, parts, "shapes")
    scratch, _ = take_counts(refs, parts, "scratch")
    barrier = pltpu.get_barrier_semaphore()
    greeted = sum(part.greet(barrier) for part in parts)
    pl.semaphore_wait(barrier, greeted)
    for i in range(1, len(parts)):
        parts[i].begin(ins[i], outs[i], scratch[i])
    parts[0].begin(ins[0], outs[0], scratch[0])
    for i in range(1, len(parts)):
        parts[i].finish(ins[i], outs[i], scratch[i])


def travel(collective_id, *parts):
    aliases, first_in, first_out = {}, 0, 0
    for part in parts:
        for source, result in part.aliases.items():
            aliases[first_in + source] = first_out + result
        first_in += len(part.arrays)
        first_out += len(part.shapes)
    results = pl.pallas_call(
        partial(kernel, parts),
        out_shape=[shape for part in parts for shape in part.shapes],
        in_specs=[pl.BlockSpec(memory_space=space) for part in parts for space in part.in_spaces],
        out_specs=[pl.BlockSpec(memory_space=space) for part in parts for space in part.out_spaces],
        scratch_shapes=[each for part in parts for each in part.scratch],
        input_output_aliases=aliases,
        compiler_params=pltpu.CompilerParams(
            collective_id=collective_id, has_side_effects=True, vmem_limit_bytes=40 * 2**20
        ),
        cost_estimate=pl.CostEstimate(flops=0, bytes_accessed=16 * 2**20, transcendentals=0),
    )(*[array for part in parts for array in part.arrays])
    split, _ = take_counts(results, parts, "shapes")
    return split


class Route:
    def __init__(self, shards, errands):
        self.shards = shards
        self.errands = iter(errands)
        self.rows, self.grads, self.far, self.near = {}, {}, {}, {}
        self.relayed, self.met = {}, {}
        self.count = 0

    def step(self, main):
        errands, parts = next(self.errands), [main]
        for name, what in errands:
            if what == "in":
                parts.append(SwapIn(self.shards[name]))
            elif what in ("a", "b", "c", "ab", "bc"):
                parts.append(Spread(self.rows[name], what))
            elif what == "far":
                parts.append(FoldFar(self.grads[name]))
            elif what == "near":
                parts.append(FoldNear(self.grads[name]))
            elif what == "relay":
                parts.append(FoldRelay(self.far_sums(name)))
            elif what == "out":
                parts.append(SwapOut(self.pair(name)))
        results = travel(self.count, *parts)
        self.count += 1
        for (name, what), got in zip(errands, results[1:]):
            if what in ("in", "a", "b", "c", "ab", "bc"):
                self.rows[name] = got[0]
            else:
                {"far": self.far, "near": self.near, "relay": self.relayed, "out": self.met}[what][
                    name
                ] = got
        return results[0]

    def weight(self, name):
        rows = self.rows[name]
        return rows.reshape(-1, rows.shape[-1])

    def give_grad(self, name, grad):
        self.grads[name] = grad.astype(jnp.bfloat16).reshape(self.rows[name].shape)

    def own_rows(self, name, py, px, core):
        grad = self.grads[name]
        at = lax.dynamic_slice(grad, (py, px, core, 0, 0), (1, 1, 1) + grad.shape[3:])
        return at[0, 0, 0].astype(jnp.float32)

    def far_sums(self, name):
        y, x = lax.axis_index("py"), lax.axis_index("px")
        along_y, along_x = self.far[name]
        first = [
            self.own_rows(name, y, turned("px", e), 0) + jnp.sum(along_y[:, e - 1].astype(jnp.float32), 0)
            for e in range(1, lax.axis_size("px"))
        ]
        last = [
            self.own_rows(name, turned("py", e), x, 1) + jnp.sum(along_x[:, e - 1].astype(jnp.float32), 0)
            for e in range(1, lax.axis_size("py"))
        ]
        return jnp.stack(first).astype(jnp.bfloat16), jnp.stack(last).astype(jnp.bfloat16)

    def pair(self, name):
        y, x = lax.axis_index("py"), lax.axis_index("px")
        halves = []
        for core in range(2):
            near = jnp.sum(self.near[name][core].astype(jnp.float32), 0)
            relayed = jnp.sum(self.relayed[name][core].astype(jnp.float32), 0)
            halves.append(self.own_rows(name, y, x, core) + near + relayed)
        return jnp.stack(halves).astype(jnp.bfloat16)

    def total(self, name):
        met = self.met[name][0].astype(jnp.float32)
        return met[0] + met[1]


def scores_of(query, key, key_valid):
    scale = 1.0 / math.sqrt(HEAD_DIM)
    scores = jnp.einsum("bqhe,bkhe->bhqk", query, key, preferred_element_type=jnp.float32) * scale
    if key_valid is None:
        return scores
    return jnp.where(key_valid[:, None, None, :] > 0, scores, -1e30)


def attend_forward(query, key, value, key_valid):
    scores = scores_of(query, key, key_valid)
    peak = jnp.max(scores, -1, keepdims=True)
    expo = jnp.exp(scores - peak)
    total = jnp.sum(expo, -1, keepdims=True)
    probs = (expo / total).astype(jnp.bfloat16)
    context = jnp.einsum(
        "bhqk,bkhe->bqhe", probs, value, preferred_element_type=jnp.float32
    ).astype(jnp.bfloat16)
    return (context, peak + jnp.log(total))


def attend_backward(query, key, value, log_total, grad_context, key_valid):
    scale = 1.0 / math.sqrt(HEAD_DIM)
    probs = jnp.exp(scores_of(query, key, key_valid) - log_total)
    grad_value = jnp.einsum(
        "bhqk,bqhe->bkhe",
        probs.astype(jnp.bfloat16),
        grad_context,
        preferred_element_type=jnp.float32,
    ).astype(jnp.bfloat16)
    grad_probs = jnp.einsum(
        "bqhe,bkhe->bhqk", grad_context, value, preferred_element_type=jnp.float32
    )
    grad_scores = (probs * (grad_probs - jnp.sum(grad_probs * probs, -1, keepdims=True))).astype(
        jnp.bfloat16
    )
    grad_query = (
        jnp.einsum("bhqk,bkhe->bqhe", grad_scores, key, preferred_element_type=jnp.float32) * scale
    ).astype(jnp.bfloat16)
    grad_key = (
        jnp.einsum("bhqk,bqhe->bkhe", grad_scores, query, preferred_element_type=jnp.float32)
        * scale
    ).astype(jnp.bfloat16)
    return (grad_query, grad_key, grad_value)


def split_heads(triple):
    batch, length, three = triple.shape
    local = three // 3
    return [
        triple[:, :, i * local : (i + 1) * local].reshape(
            batch, length, local // HEAD_DIM, HEAD_DIM
        )
        for i in range(3)
    ]


def low_dot(spec, left, right):
    return jnp.einsum(spec, left, right, preferred_element_type=jnp.float32)


def block_forward(values, mod, key_valid, block, route):
    shift_a, scale_a, gate_a, shift_m, scale_m, gate_m = [mod[i] for i in range(6)]
    (normed,) = route.step(GroupCopy(modulate(values, shift_a, scale_a).astype(jnp.bfloat16)))
    triple = low_dot("bld,dc->blc", normed, route.weight(f"in{block}")).astype(jnp.bfloat16)
    context, log_total = attend_forward(*split_heads(triple), key_valid)
    flat_context = context.reshape(triple.shape[0], triple.shape[1], triple.shape[2] // 3)
    partial_attn = low_dot("ble,de->bld", flat_context, route.weight(f"out{block}"))
    (attn,) = route.step(OwnSum(partial_attn.astype(jnp.bfloat16)))
    middle = values + gate_a[None, :] * attn
    (normed_m,) = route.step(GroupCopy(modulate(middle, shift_m, scale_m).astype(jnp.bfloat16)))
    inner = low_dot("bld,df->blf", normed_m, route.weight(f"expand{block}"))
    active = jax.nn.gelu(inner, approximate=True).astype(jnp.bfloat16)
    partial_branch = low_dot("blf,df->bld", active, route.weight(f"contract{block}"))
    (branch,) = route.step(OwnSum(partial_branch.astype(jnp.bfloat16)))
    result = middle + gate_m[None, :] * branch
    saved = (values, middle, normed, normed_m, triple, flat_context)
    return (result, saved + (log_total, attn, inner, active, branch))


def block_backward(grad, mod, key_valid, block, saved, route):
    values, middle, normed, normed_m, triple, flat_context = saved[:6]
    log_total, attn, inner, active, branch = saved[6:]
    shift_a, scale_a, gate_a, shift_m, scale_m, gate_m = [mod[i] for i in range(6)]
    (grad_branch,) = route.step(GroupCopy((gate_m[None, :] * grad).astype(jnp.bfloat16)))
    grad_gate_m = jnp.sum(grad * branch, 0)
    grad_active = low_dot("bld,df->blf", grad_branch, route.weight(f"contract{block}"))
    gelu_back = jax.vjp(partial(jax.nn.gelu, approximate=True), inner)[1]
    grad_inner = gelu_back(grad_active)[0].astype(jnp.bfloat16)
    partial_normed = low_dot("blf,df->bld", grad_inner, route.weight(f"expand{block}"))
    route.give_grad(f"contract{block}", low_dot("bld,blf->df", grad_branch, active))
    route.give_grad(f"expand{block}", low_dot("bld,blf->df", normed_m, grad_inner))
    (grad_normed,) = route.step(OwnSum(partial_normed.astype(jnp.bfloat16)))
    _, modulate_back = jax.vjp(modulate, middle, shift_m, scale_m)
    grad_mid, grad_shift_m, grad_scale_m = modulate_back(grad_normed)
    grad_mid = grad + grad_mid
    (grad_attn,) = route.step(GroupCopy((gate_a[None, :] * grad_mid).astype(jnp.bfloat16)))
    grad_gate_a = jnp.sum(grad_mid * attn, 0)
    grad_flat = low_dot("bld,de->ble", grad_attn, route.weight(f"out{block}")).astype(jnp.bfloat16)
    route.give_grad(f"out{block}", low_dot("bld,ble->de", grad_attn, flat_context))
    query, key, value = split_heads(triple)
    grad_context = grad_flat.reshape(query.shape)
    grad_parts = attend_backward(query, key, value, log_total, grad_context, key_valid)
    grad_triple = jnp.concatenate([g.reshape(flat_context.shape) for g in grad_parts], 2)
    partial_normed = low_dot("blc,dc->bld", grad_triple, route.weight(f"in{block}"))
    route.give_grad(f"in{block}", low_dot("bld,blc->dc", normed, grad_triple))
    (grad_normed,) = route.step(OwnSum(partial_normed.astype(jnp.bfloat16)))
    _, modulate_back = jax.vjp(modulate, values, shift_a, scale_a)
    grad_values, grad_shift_a, grad_scale_a = modulate_back(grad_normed)
    grad_mod = jnp.stack(
        [grad_shift_a, grad_scale_a, grad_gate_a, grad_shift_m, grad_scale_m, grad_gate_m], 0
    )
    return (grad_mid + grad_values, grad_mod)


def both(what, block):
    return [(f"in{block}", what), (f"out{block}", what)]


def errands_in_turn():
    return [
        both("in", 0),
        both("ab", 0) + [("expand0", "in")],
        both("c", 0) + [("contract0", "in")],
        [("expand0", "ab")] + both("in", 1),
        [("expand0", "c"), ("contract0", "a"), ("expand1", "in")],
        [("contract0", "bc"), ("contract1", "in")],
        both("ab", 1),
        both("c", 1) + [("expand1", "a")],
        [("expand1", "bc"), ("contract1", "a")],
        [("contract1", "bc")],
        [],
        [],
        [("expand1", "far"), ("contract1", "far")],
        [("expand1", "near"), ("expand1", "relay")],
        [("contract1", "near"), ("contract1", "relay")],
        both("far", 1) + both("near", 1),
        both("relay", 1) + [("expand0", "far"), ("expand1", "out")],
        [("contract0", "far"), ("expand0", "near"), ("contract1", "out")],
        [("contract0", "near"), ("expand0", "relay")] + both("out", 1),
        [("contract0", "relay"), ("expand0", "out")] + both("far", 0),
        both("near", 0) + both("relay", 0) + [("contract0", "out")],
        both("out", 0),
        [],
        [],
    ]


def adam(weight, grad, moment, second, average, factor):
    grad = grad * factor
    moment = beta_first * moment + (1.0 - beta_first) * grad
    second = beta_second * second + (1.0 - beta_second) * grad * grad
    update = (
        moment
        / (1.0 - beta_first**STEP)
        / (jnp.sqrt(second / (1.0 - beta_second**STEP)) + adam_eps)
    )
    fresh = weight - learn_rate * (update + weight_decay * weight)
    average_decay = min(ema_decay, (1.0 + STEP) / (10.0 + STEP))
    average = average_decay * average + (1.0 - average_decay) * fresh
    return (fresh, moment, second, average)


def shards(
    patches,
    target_noise,
    kept_slots,
    kept_count,
    time_step,
    labels,
    teacher,
    *tables,
):
    params, moments, seconds, averages = tables[:7], tables[7:14], tables[14:21], tables[21:]
    attend_in, attend_out, expand, contract, modulation, patch_table, condition = params
    batch, length = (patches.shape[0], patches.shape[1])
    capacity = kept_slots.shape[1]
    rows, local = (attend_in.shape[1], attend_in.shape[3])
    wides, narrows = (group_size(WIDE), group_size(NARROW))
    wide_index, narrow_index = (flat_place(WIDE), flat_place(NARROW))
    images = batch * wides
    width = local * narrows
    assert batch == narrows

    shards_low = {}
    for i in range(2):
        shards_low[f"in{i}"] = attend_in[i].reshape(rows, 3 * local).astype(jnp.bfloat16)
        shards_low[f"out{i}"] = attend_out[i].T.astype(jnp.bfloat16)
        shards_low[f"expand{i}"] = expand[i].astype(jnp.bfloat16)
        shards_low[f"contract{i}"] = contract[i].T.astype(jnp.bfloat16)
    route = Route(shards_low, errands_in_turn())

    def own(array):
        return lax.dynamic_index_in_dim(array, narrow_index, 0, keepdims=False)

    condition_low = condition.astype(jnp.bfloat16)
    features = sinusoid(time_step, FREQ)
    onehot = (labels[:, None] == jnp.arange(CLASSES)[None, :]).astype(jnp.bfloat16)
    cond_part = jnp.dot(
        features, condition_low[:FREQ].astype(jnp.float32), precision=highest_float_accuracy
    ) + low_dot("bc,cd->bd", onehot, condition_low[FREQ:])
    facts = jnp.stack([kept_count, time_step, labels], 1).astype(jnp.float32)
    facts = jnp.pad(own(facts)[None, :], ((0, 7), (0, local - 3)))
    payload = jnp.concatenate([cond_part, own(teacher).reshape(narrows, local), facts], 0)
    table_pad = jnp.pad(patch_table.astype(jnp.bfloat16), ((0, 15), (0, 0)))
    everyone, tables_near = route.step(
        Exchange([payload, table_pad], [(ALL, "same"), (NARROW, "same")])
    )
    everyone = everyone.reshape(wides, narrows, batch + narrows + 8, local)
    cond_sum = jnp.transpose(everyone[:, :, :batch], (0, 2, 1, 3)).reshape(images, width)
    negatives = everyone[:, :, batch : batch + narrows].reshape(images, width)
    facts_all = everyone[:, :, batch + narrows, :3]
    time_all = facts_all[:, :, 1].reshape(images).astype(jnp.int32)
    labels_all = facts_all[:, :, 2].reshape(images).astype(jnp.int32)
    patch_full = jnp.transpose(tables_near, (1, 0, 2)).reshape(48, width)[:33]
    silu_low = jax.nn.silu(cond_sum).astype(jnp.bfloat16)
    silu_rows = lax.dynamic_slice_in_dim(silu_low, wide_index * rows, rows, 1)
    modulation_low = modulation.astype(jnp.bfloat16)
    mod_part = low_dot("ip,npkc->inkc", silu_rows, modulation_low)
    mod_part = mod_part.reshape(wides, batch, 12, local)
    (mod_wide,) = route.step(Exchange([mod_part], [(WIDE, "each")]))
    (mod_near,) = route.step(Exchange([jnp.sum(mod_wide, 0)], [(NARROW, "each")]))
    mods = jnp.transpose(mod_near, (1, 0, 2)).reshape(2, 6, width)

    count_own = own(kept_count).astype(jnp.float32)
    slot_valid = (jnp.arange(capacity) < own(kept_count)).astype(jnp.float32)
    select = (own(kept_slots)[:, None] == jnp.arange(length)[None, :]).astype(
        jnp.float32
    ) * slot_valid[:, None]
    kept_place = jnp.sum(select, 0)
    places = sinusoid(jnp.arange(length), width)
    group_counts = lax.dynamic_slice(
        facts_all[:, :, 0],
        (flat_place(("py", "px")) * 2, lax.axis_index("zh") * 2),
        (2, 2),
    ).reshape(4)
    group_valid = (jnp.arange(capacity)[None, :] < group_counts[:, None]).astype(jnp.float32)
    kept_patches = low_dot("cl,lp->cp", select.astype(jnp.bfloat16), own(patches))
    embed = low_dot("cp,pd->cd", kept_patches.astype(jnp.bfloat16), patch_full[:PATCH_IN])
    embed = embed + jnp.dot(select, places, precision=highest_float_accuracy)
    encoded, saved_enc = block_forward(embed, mods[0], group_valid, 0, route)

    def pool_unit(values):
        pooled = jnp.sum(values * slot_valid[:, None], 0) / count_own
        return pooled * lax.rsqrt(jnp.sum(pooled * pooled, -1, keepdims=True) + 1e-06)

    normalised_direction, pool_back = jax.vjp(pool_unit, encoded)
    frozen_target_direction = negatives * lax.rsqrt(
        jnp.sum(negatives * negatives, -1, keepdims=True) + 1e-06
    )
    cosine_match_scores = (
        jnp.sum(normalised_direction[None, :] * frozen_target_direction, -1)
        / contrast_sharpness_divisor
    )
    peak = jnp.max(cosine_match_scores)
    expo = jnp.exp(cosine_match_scores - peak)
    total = jnp.sum(expo)
    positive = ((wide_index * batch + narrow_index) == jnp.arange(images)).astype(jnp.float32)
    nce_local = peak + jnp.log(total) - jnp.sum(cosine_match_scores * positive)
    derivative_of_raw_scores = (expo / total - positive) * (nce_weight / images)
    unit_vector_gradient = (
        jnp.sum(derivative_of_raw_scores[:, None] * frozen_target_direction, 0)
        / contrast_sharpness_divisor
    )
    grad_pool = pool_back(unit_vector_gradient)[0]
    mask_token = patch_full[2 * PATCH_IN].astype(jnp.float32)
    decode_in = jnp.einsum("cl,cd->ld", select, encoded, precision=highest_float_accuracy)
    decode_in = decode_in + (1.0 - kept_place)[:, None] * mask_token + places
    decoded, saved_dec = block_forward(decode_in, mods[1], None, 1, route)
    final, final_back = jax.vjp(layer_norm, decoded)
    final_low = final.astype(jnp.bfloat16)
    head = patch_full[PATCH_IN : 2 * PATCH_IN]
    predict = low_dot("ld,pd->lp", final_low, head)
    error_map = predict - own(target_noise)
    count_all = images * length * PATCH_IN
    mse_local = jnp.sum(error_map * error_map)
    grad_predict = (error_map * (2.0 / count_all)).astype(jnp.bfloat16)
    grad_head = low_dot("lp,ld->pd", grad_predict, final_low)
    grad_final = low_dot("lp,pd->ld", grad_predict, head)
    grad_decoded = final_back(grad_final)[0]
    grad_dec_in, grad_mod_dec = block_backward(grad_decoded, mods[1], None, 1, saved_dec, route)
    grad_mask = jnp.sum((1.0 - kept_place)[:, None] * grad_dec_in, 0)
    grad_encoded = jnp.dot(select, grad_dec_in, precision=highest_float_accuracy) + grad_pool
    grad_embed, grad_mod_enc = block_backward(
        grad_encoded, mods[0], group_valid, 0, saved_enc, route
    )
    grad_patch = jnp.einsum(
        "cp,cd->pd", kept_patches, grad_embed, precision=highest_float_accuracy
    )

    grad_mods = jnp.stack([grad_mod_enc, grad_mod_dec]).reshape(12, narrows, local)
    grad_mods = jnp.transpose(grad_mods, (1, 0, 2))
    grad_table = jnp.concatenate([grad_patch, grad_head, grad_mask[None, :]], 0)
    grad_table = jnp.transpose(grad_table.reshape(33, narrows, local), (1, 0, 2))
    grad_table = jnp.pad(grad_table, ((0, 0), (0, 7), (0, 0)))
    mods_near, table_near = route.step(
        Exchange([grad_mods, grad_table], [(NARROW, "each"), (NARROW, "each")])
    )
    table_sum = jnp.pad(jnp.sum(table_near, 0), ((0, 8), (0, 0))).astype(jnp.bfloat16)
    mods_all, table_all = route.step(
        Exchange([mods_near, table_sum], [(WIDE, "same"), (WIDE, "same")])
    )
    grad_patch_table = jnp.sum(table_all.astype(jnp.float32), 0)[:33]
    mods_all = mods_all.reshape(images, 2, 6, local)
    silu_broad = silu_rows.astype(jnp.float32)
    grad_modulation = jnp.einsum(
        "ip,inkc->npkc", silu_broad, mods_all, precision=highest_float_accuracy
    )
    grad_silu = jnp.einsum(
        "inkc,npkc->ip",
        mods_all,
        modulation_low.astype(jnp.float32),
        precision=highest_float_accuracy,
    )
    (silu_near,) = route.step(Exchange([grad_silu], [(NARROW, "same")]))
    (silu_wide,) = route.step(Exchange([jnp.sum(silu_near, 0)], [(WIDE, "same")]))
    grad_silu = jnp.transpose(silu_wide, (1, 0, 2)).reshape(images, width)
    grad_silu = lax.dynamic_slice_in_dim(grad_silu, narrow_index * local, local, 1)
    cond_cols = lax.dynamic_slice_in_dim(cond_sum, narrow_index * local, local, 1)
    grad_cond = jax.vjp(jax.nn.silu, cond_cols)[1](grad_silu)[0]
    features_all = sinusoid(time_all, FREQ)
    onehot_all = (labels_all[:, None] == jnp.arange(CLASSES)[None, :]).astype(jnp.float32)
    grad_condition = jnp.dot(
        jnp.concatenate([features_all, onehot_all], 1).T, grad_cond, precision=highest_float_accuracy
    )

    totals = {name: route.total(name) for name in shards_low}

    def stacked(name, shape):
        return jnp.stack([shape(totals[f"{name}{i}"]) for i in range(2)])

    grads = [
        stacked("in", lambda g: g.reshape(rows, 3, local)),
        stacked("out", lambda g: g.T),
        stacked("expand", lambda g: g),
        stacked("contract", lambda g: g.T),
        grad_modulation,
        grad_patch_table,
        grad_condition,
    ]
    square_big = jnp.sum(grad_modulation * grad_modulation)
    for g in totals.values():
        square_big = square_big + jnp.sum(g * g)
    square_small = jnp.sum(grad_patch_table * grad_patch_table) + jnp.sum(
        grad_condition * grad_condition
    )
    square_local = square_big + (wide_index == 0).astype(jnp.float32) * square_small
    scalars = jnp.stack([mse_local, nce_local, square_local])
    scalars = jnp.pad(scalars[None, :], ((0, 7), (0, 125)))
    (scalars_all,) = route.step(Exchange([scalars], [(ALL, "same")]))
    sums = jnp.sum(scalars_all[:, 0], 0)
    grad_norm = jnp.sqrt(sums[2])
    factor = clip_norm / jnp.maximum(grad_norm, clip_norm)
    fresh = [
        adam(params[i], grads[i], moments[i], seconds[i], averages[i], factor) for i in range(7)
    ]
    loss_parts = jnp.stack([sums[0] / count_all, sums[1] / images])
    return (loss_parts, grad_norm) + tuple(fresh[i][k] for k in range(4) for i in range(7))


def solution(mesh):
    wide, narrow = mesh.devices.shape
    planes = wide // 2
    across = max(n for n in range(1, math.isqrt(planes) + 1) if planes % n == 0)
    grid = Mesh(mesh.devices.reshape(across, planes // across, 2, narrow // 2, 2), ALL)
    image_specs = (
        P(WIDE, None, None),
        P(WIDE, None, None),
        P(WIDE, None),
        P(WIDE),
        P(WIDE),
        P(WIDE),
        P(WIDE, None),
    )
    table_specs = (
        P(None, WIDE, None, NARROW),
        P(None, NARROW, WIDE),
        P(None, WIDE, NARROW),
        P(None, NARROW, WIDE),
        P(None, WIDE, None, NARROW),
        P(None, NARROW),
        P(None, NARROW),
    )
    return jax.shard_map(
        shards,
        mesh=grid,
        in_specs=image_specs + table_specs * 4,
        out_specs=(P(), P()) + table_specs * 4,
        check_vma=False,
    )
```

time: 861 us -> 836 us (0.971)
  Pallas kernels: 360 us -> 491 us
  waiting for transfers between devices: 88.6 us -> 0 us
  starting transfers between devices: 64.5 us -> 0 us
  matrix products: 130 us -> 106 us
  local copies, waits for them, and re-layouts: 90.7 us -> 113 us
  between operations: 28.9 us -> 18.5 us
  other arithmetic: 87 us -> 97 us
    pallas_call x24, Pallas kernels: 360 us -> 491 us  [travel(): pl.pallas_call(partial(kernel, parts), out_shape=[shape for part in parts...]
    ppermute x16 -> x0, waiting for transfers between devices: 88.4 us -> none  [the longest x4 66.2 us: scatter_rows(): first = lax.ppermute(jnp.where(on_zero, high, low), SWAP, back)]
    ppermute x16 -> x0, starting transfers between devices: 63.1 us -> none  [the longest x4 46.6 us: gather_rows(): first = lax.ppermute(shard, SWAP, forth)]
    dot_general x31, matrix products: 97.4 us -> 73.6 us  [low_dot(): return jnp.einsum(spec, left, right, preferred_element_type=jnp.float32)]
    another operation x10 -> x0, local copies, waits for them, and re-layouts: 11.8 us -> none  [the longest x4 6.91 us: shards(): jnp.stack([g[:, :3 * local].reshape(rows, 3, local) for g in attend_sums])]
    concatenate x8 -> x0, other arithmetic: 10.1 us -> none  [the longest x2 5.51 us: block_backward(): jnp.concatenate([grad_expand, grad_contract], 1).astype(jnp.bfloat16)]
    convert_element_type x1 -> x10, local copies, waits for them, and re-layouts: 2.12 us -> 11.6 us  [the longest x4 7.67 us: give_grad(): self.grads[name] = grad.astype(jnp.bfloat16).reshape(self.rows[name].shape)]
    unnamed x339 -> x483, local copies, waits for them, and re-layouts: 54 us -> 44.7 us
  transfers between devices with their start and end apart: 24 -> 0, of which waited for: 7 -> 0; matrix products, arithmetic and copies ran while one was open for 23% -> 0% of each run, Pallas kernels for 31% -> 0%
where the time goes in v2:
time: 836 us; the launch traced here: 826 us
  Pallas kernels  491 us (59%)
  local copies, waits for them, and re-layouts  113 us (14%)
  matrix products  106 us (13%)
  other arithmetic  97 us (12%)
  between operations  18.5 us (2%)
    pallas_call x24, Pallas kernels, travel(): pl.pallas_call(partial(kernel, parts), out_shape=[shape for part in parts...  491 us
    dot_general x31, matrix products, low_dot(): return jnp.einsum(spec, left, right, preferred_element_type=jnp.float32)  73.6 us
    unnamed x483, local copies, waits for them, and re-layouts  44.7 us
    add x7, other arithmetic, adam(): average = average_decay * average + (1.0 - average_decay) * fresh  25 us

profile of v2, /device:TPU:0, one launch (start us, length us, event | category | flops | bytes accessed | tf_op | source)
XLA Modules:
  0.0 825.6 jit_solution(16041609819262610109)
XLA Ops:
  18.2 2.3 multiply_cosine_fusion
  23.5 44.6 %shard_map.562 = (f32[32,16,288]{2,1,0:T(8,128)S(1)}, bf16[4,48,288]{2,1,0:T(8,128)(2,1)S(1)}, bf16[2,2,2,144,864]{4,3,2,1,0:T(8,128)(2,1)S(1)}, bf16[2,2,2,144,288]{4,3,2,1,0:T(8,128)(2,1)S(1)}) custom-call(f32[16,288]{1,0:T(8,128)S(1)} %select_maximum_fusion.refs_0_, bf16[48,288]{1,0:T(8,128)(2,1)S(1)} %copy-done.84, ...), custom_call_target="tpu_custom_call" | custom-call | bytes 16777216 | tf_op jit(solution)/shard_map/pallas_call | solution.py:542
  80.8 3.0 fusion.155
  83.8 2.0 reshape.1466
  87.3 27.2 %shard_map.563 = (f32[8,4,12,288]{3,2,1,0:T(8,128)S(1)}, bf16[2,2,2,144,864]{4,3,2,1,0:T(8,128)(2,1)S(1)}, bf16[2,2,2,144,288]{4,3,2,1,0:T(8,128)(2,1)S(1)}, bf16[2,2,2,144,1152]{4,3,2,1,0:T(8,128)(2,1)S(1)}) custom-call(f32[8,4,12,288]{3,2,1,0:T(8,128)S(1)} %copy.258.refs_0_, ...), custom_call_target="tpu_custom_call", output_to_operand_aliasing={{1}: (1, {}), {2}: (2, {})} | custom-call | bytes 16777216 | tf_op jit(solution)/shard_map/pallas_call | solution.py:542
  123.4 21.6 %shard_map.564 = (f32[4,12,288]{2,1,0:T(8,128)S(1)}, bf16[2,2,2,144,864]{4,3,2,1,0:T(8,128)(2,1)S(1)}, bf16[2,2,2,144,288]{4,3,2,1,0:T(8,128)(2,1)S(1)}, bf16[2,2,2,144,1152]{4,3,2,1,0:T(8,128)(2,1)S(1)}) custom-call(f32[4,12,288]{2,1,0:T(8,128)S(1)} %copy-done.69, ...), custom_call_target="tpu_custom_call", output_to_operand_aliasing={{1}: (1, {}), {2}: (2, {})} | custom-call | bytes 16777216 | tf_op jit(solution)/shard_map/pallas_call | solution.py:542
  166.0 18.5 %shard_map.565 = (bf16[4,160,1152]{2,1,0:T(8,128)(2,1)S(1)}, bf16[2,2,2,144,1152]{4,3,2,1,0:T(8,128)(2,1)S(1)}, bf16[2,2,2,144,864]{4,3,2,1,0:T(8,128)(2,1)S(1)}, bf16[2,2,2,144,288]{4,3,2,1,0:T(8,128)(2,1)S(1)}) custom-call(bf16[160,1152]{1,0:T(8,128)(2,1)S(1)} %add_convert_fusion.3.refs_0_, ...), custom_call_target="tpu_custom_call", output_to_operand_aliasing={{1}: (1, {})} | custom-call | bytes 16777216 | tf_op jit(solution)/shard_map/pallas_call | solution.py:542
  189.0 2.1 copy.265
  191.1 2.1 copy.264
  193.3 2.1 copy.261
  202.2 21.5 %shard_map.566 = (f32[160,1152]{1,0:T(8,128)S(1)}, bf16[2,2,2,144,1152]{4,3,2,1,0:T(8,128)(2,1)S(1)}, bf16[2,2,2,144,1152]{4,3,2,1,0:T(8,128)(2,1)S(1)}, bf16[2,2,2,144,1152]{4,3,2,1,0:T(8,128)(2,1)S(1)}) custom-call(bf16[4,160,1152]{2,1,0:T(8,128)(2,1)S(1)} %convolution_convert_fusion.6.refs_0_, ...), custom_call_target="tpu_custom_call", output_to_operand_aliasing={{1}: (1, {}), {2}: (2, {})} | custom-call | bytes 16777216 | tf_op jit(solution)/shard_map/pallas_call | solution.py:542
  226.6 20.3 %shard_map.567 = (bf16[4,160,1152]{2,1,0:T(8,128)(2,1)S(1)}, bf16[2,2,2,144,1152]{4,3,2,1,0:T(8,128)(2,1)S(1)}, bf16[2,2,2,144,1152]{4,3,2,1,0:T(8,128)(2,1)S(1)}) custom-call(bf16[160,1152]{1,0:T(8,128)(2,1)S(1)} %add_convert_fusion.2.refs_0_, bf16[2,2,2,144,1152]{4,3,2,1,0:T(8,128)(2,1)S(1)} %get-tuple-element.148.refs_1_, ...), custom_call_target="tpu_custom_call", output_to_operand_aliasing={{1}: (1, {})} | custom-call | bytes 16777216 | tf_op jit(solution)/shard_map/pallas_call | solution.py:542
  248.0 2.3 fusion.221
  250.4 2.7 convolution_convert_fusion.5.refs_0_
  253.2 19.3 %shard_map.568 = (f32[160,1152]{1,0:T(8,128)S(1)}, bf16[2,2,2,144,864]{4,3,2,1,0:T(8,128)(2,1)S(1)}, bf16[2,2,2,144,288]{4,3,2,1,0:T(8,128)(2,1)S(1)}) custom-call(bf16[4,160,1152]{2,1,0:T(8,128)(2,1)S(1)} %convolution_convert_fusion.5.refs_0_, bf16[2,2,2,144,864]{4,3,2,1,0:T(8,128)(2,1)S(1)} %copy-done.27, ...), custom_call_target="tpu_custom_call", output_to_operand_aliasing={{1}: (1, {}), {2}: (2, {})} | custom-call | bytes 16777216 | tf_op jit(solution)/shard_map/pallas_call | solution.py:542
  296.7 17.6 %shard_map.569 = (bf16[4,256,1152]{2,1,0:T(8,128)(2,1)S(1)}, bf16[2,2,2,144,864]{4,3,2,1,0:T(8,128)(2,1)S(1)}, bf16[2,2,2,144,288]{4,3,2,1,0:T(8,128)(2,1)S(1)}, bf16[2,2,2,144,1152]{4,3,2,1,0:T(8,128)(2,1)S(1)}) custom-call(bf16[256,1152]{1,0:T(8,128)(2,1)S(1)} %add_convert_fusion.1.refs_0_, ...), custom_call_target="tpu_custom_call", output_to_operand_aliasing={{1}: (1, {}), {2}: (2, {}), {3}: (3, {})} | custom-call | bytes 16777216 | tf_op jit(solution)/shard_map/pallas_call | solution.py:542
  314.3 2.5 convolution_convert_fusion.8
  323.8 24.1 %shard_map.570 = (f32[256,1152]{1,0:T(8,128)S(1)}, bf16[2,2,2,144,1152]{4,3,2,1,0:T(8,128)(2,1)S(1)}, bf16[2,2,2,144,1152]{4,3,2,1,0:T(8,128)(2,1)S(1)}) custom-call(bf16[4,256,1152]{2,1,0:T(8,128)(2,1)S(1)} %convolution_convert_fusion.1.refs_0_, ...), custom_call_target="tpu_custom_call", output_to_operand_aliasing={{1}: (1, {}), {2}: (2, {})} | custom-call | bytes 16777216 | tf_op jit(solution)/shard_map/pallas_call | solution.py:542
  349.4 16.8 %shard_map.571 = (bf16[4,256,1152]{2,1,0:T(8,128)(2,1)S(1)}, bf16[2,2,2,144,1152]{4,3,2,1,0:T(8,128)(2,1)S(1)}) custom-call(bf16[256,1152]{1,0:T(8,128)(2,1)S(1)} %add_convert_fusion.refs_0_, bf16[2,2,2,144,1152]{4,3,2,1,0:T(8,128)(2,1)S(1)} %get-tuple-element.164.refs_1_), custom_call_target="tpu_custom_call", output_to_operand_aliasing={{1}: (1, {})} | custom-call | bytes 16777216 | tf_op jit(solution)/shard_map/pallas_call | solution.py:542
  367.6 3.5 fusion.222
  371.1 4.4 convolution_convert_fusion.3.refs_0_
  375.6 16.7 %shard_map.572 = f32[256,1152]{1,0:T(8,128)S(1)} custom-call(bf16[4,256,1152]{2,1,0:T(8,128)(2,1)S(1)} %convolution_convert_fusion.3.refs_0_), custom_call_target="tpu_custom_call" | custom-call | bytes 16777216 | tf_op jit(solution)/shard_map/pallas_call | solution.py:542
  397.6 16.6 %shard_map.573 = bf16[4,256,1152]{2,1,0:T(8,128)(2,1)S(1)} custom-call(bf16[256,1152]{1,0:T(8,128)(2,1)S(1)} %get-tuple-element.408.refs_0_), custom_call_target="tpu_custom_call" | custom-call | bytes 16777216 | tf_op jit(solution)/shard_map/pallas_call | solution.py:542
  414.2 5.0 fusion.10
  419.2 3.3 fusion.1
  422.6 4.2 convolution_convert_fusion.2.refs_0_
  426.7 3.3 fusion
  430.0 17.7 %shard_map.574 = (f32[256,1152]{1,0:T(8,128)S(1)}, bf16[1,1,144,1152]{3,2,1,0:T(8,128)(2,1)S(1)}, bf16[1,1,144,1152]{3,2,1,0:T(8,128)(2,1)S(1)}, bf16[1,1,144,11...) custom-call(bf16[4,256,1152]{2,1,0:T(8,128)(2,1)S(1)} %convolution_convert_fusion.2.refs_0_, ...), custom_call_target="tpu_custom_call" | custom-call | bytes 16777216 | tf_op jit(solution)/shard_map/pallas_call | solution.py:542
  452.6 16.9 %shard_map.575 = (bf16[4,256,1152]{2,1,0:T(8,128)(2,1)S(1)}, bf16[1,144,1152]{2,1,0:T(8,128)(2,1)S(1)}, bf16[1,144,1152]{2,1,0:T(8,128)(2,1)S(1)}, bf16[1,144,11...) custom-call(bf16[256,1152]{1,0:T(8,128)(2,1)S(1)} %get-tuple-element.368.refs_0_, ...), custom_call_target="tpu_custom_call" | custom-call | bytes 16777216 | tf_op jit(solution)/shard_map/pallas_call | solution.py:542
  475.8 3.4 fusion.43
  484.7 3.9 bitcast_convert_fusion.1
  488.6 3.3 convolution_convert_fusion.refs_0_
  491.9 17.1 %shard_map.576 = (f32[256,1152]{1,0:T(8,128)S(1)}, bf16[1,144,1152]{2,1,0:T(8,128)(2,1)S(1)}, bf16[1,144,1152]{2,1,0:T(8,128)(2,1)S(1)}, bf16[1,144,1152]{2,1,0:T(8,128)(2,1)S(1)}, bf16[1,144,1152]{2,1,0:T(8,128)(2,1)S(1)}) custom-call(bf16[4,256,1152]{2,1,0:T(8,128)(2,1)S(1)} %convolution_convert_fusion.refs_0_, ...), custom_call_target="tpu_custom_call" | custom-call | bytes 16777216 | tf_op jit(solution)/shard_map/pallas_call | solution.py:542
  516.1 2.9 copy.280
  519.0 19.1 %shard_map.577 = (bf16[4,160,1152]{2,1,0:T(8,128)(2,1)S(1)}, bf16[1,1,144,864]{3,2,1,0:T(8,128)(2,1)S(1)}, bf16[1,1,144,864]{3,2,1,0:T(8,128)(2,1)S(1)}, bf16[1,...) custom-call(bf16[160,1152]{1,0:T(8,128)(2,1)S(1)} %get-tuple-element, ...), custom_call_target="tpu_custom_call" | custom-call | bytes 16777216 | tf_op jit(solution)/shard_map/pallas_call | solution.py:542
  538.1 3.2 fusion.18
  541.3 2.3 convolution_convert_fusion.4.refs_0_
  543.7 2.4 fusion.2
  546.1 2.5 fusion.3
  550.3 20.0 %shard_map.578 = (f32[160,1152]{1,0:T(8,128)S(1)}, bf16[1,144,864]{2,1,0:T(8,128)(2,1)S(1)}, bf16[1,144,864]{2,1,0:T(8,128)(2,1)S(1)}, bf16[1,144,288]{2,1,0:T(8...) custom-call(bf16[4,160,1152]{2,1,0:T(8,128)(2,1)S(1)} %convolution_c, ...), custom_call_target="tpu_custom_call" | custom-call | bytes 16777216 | tf_op jit(solution)/shard_map/pallas_call | solution.py:542
  577.1 19.9 %shard_map.579 = (bf16[4,160,1152]{2,1,0:T(8,128)(2,1)S(1)}, bf16[1,1,144,1152]{3,2,1,0:T(8,128)(2,1)S(1)}, bf16[1,1,144,1152]{3,2,1,0:T(8,128)(2,1)S(1)}, bf16[...) custom-call(bf16[160,1152]{1,0:T(8,128)(2,1)S(1)} %multiply_convert_fusion.7.refs_, ...), custom_call_target="tpu_custom_call" | custom-call | bytes 16777216 | tf_op jit(solution)/shard_map/pallas_call | solution.py:542
  602.3 2.3 convolution_convert_fusion.10
  612.3 2.3 copy.287
  614.6 2.1 copy.288
  616.7 3.3 convolution_convert_fusion.7.refs_0_
  620.2 3.4 bitcast_convert_fusion
  623.6 21.2 %shard_map.580 = (f32[160,1152]{1,0:T(8,128)S(1)}, bf16[1,144,1152]{2,1,0:T(8,128)(2,1)S(1)}, bf16[1,144,1152]{2,1,0:T(8,128)(2,1)S(1)}, bf16[1,144,1152]{2,1,0:...) custom-call(bf16[4,160,1152]{2,1,0:T(8,128)(2,1)S(1)} %convolution_c, ...), custom_call_target="tpu_custom_call" | custom-call | bytes 16777216 | tf_op jit(solution)/shard_map/pallas_call | solution.py:542
  650.3 2.9 copy.294
  654.7 20.7 %shard_map.581 = (f32[4,12,288]{2,1,0:T(8,128)S(1)}, f32[4,40,288]{2,1,0:T(8,128)S(1)}, bf16[1,144,1152]{2,1,0:T(8,128)(2,1)S(1)}, bf16[1,144,1152]{2,1,0:T(8,12...) custom-call(f32[4,12,288]{2,1,0:T(8,128)S(1)} %bitcast.489, ...), custom_call_target="tpu_custom_call" | custom-call | bytes 16777216 | tf_op jit(solution)/shard_map/pallas_call | solution.py:542
  683.7 2.4 add.1031
  686.1 2.1 copy.304
  689.9 35.7 %shard_map.582 = (f32[8,4,12,288]{3,2,1,0:T(8,128)S(1)}, bf16[8,48,288]{2,1,0:T(8,128)(2,1)S(1)}, bf16[1,144,864]{2,1,0:T(8,128)(2,1)S(1)}, bf16[1,144,864]{2,1,...) custom-call(f32[4,12,288]{2,1,0:T(8,128)S(1)} %copy-done.88, ...), custom_call_target="tpu_custom_call" | custom-call | bytes 16777216 | tf_op jit(solution)/shard_map/pallas_call | solution.py:542
  727.1 3.1 fusion.48.refs_0_
  730.9 21.0 %shard_map.583 = (f32[4,32,144]{2,1,0:T(8,128)S(1)}, bf16[2,144,864]{2,1,0:T(8,128)(2,1)S(1)}, bf16[2,144,288]{2,1,0:T(8,128)(2,1)S(1)}) custom-call(f32[32,144]{1,0:T(8,128)S(1)} %fusion.48.refs_0_, bf16[2,144,864]{2,1,0:T(8,128)(2,1)S(1)} %pad_maximum_fusion.11.refs_1_, bf16[2,144,288]{2,1,0:T(8,128)(2,1)S(1)} %pad_maximum_fusion.15.refs_2_), custom_call_target="tpu_custom_call" | custom-call | bytes 16777216 | tf_op jit(solution)/shard_map/pallas_call | solution.py:542
  751.9 7.4 shard_map.584
  763.2 4.0 multiply_reduce_fusion.4
  770.3 3.1 multiply_reduce_fusion.2
  780.0 10.0 %shard_map.585 = f32[32,8,128]{2,1,0:T(8,128)S(1)} custom-call(f32[8,128]{1,0:T(8,128)S(1)} %pad.25.refs_0_), custom_call_target="tpu_custom_call" | custom-call | bytes 16777216 | tf_op jit(solution)/shard_map/pallas_call | solution.py:542
  794.9 3.1 multiply_add_fusion.13
  798.1 5.1 multiply_add_fusion.3
  803.3 3.3 multiply_add_fusion.4
  808.1 3.3 multiply_add_fusion.5
  813.2 3.7 multiply_add_fusion.1
  819.4 4.9 multiply_add_fusion
  (740 shorter events, 192.4 us)
Async XLA Ops:
  0.7 8.6 %copy-start = (bf16[4,256,16]{1,2,0:T(8,128)(2,1)S(1)}, bf16[4,256,16]{1,2,0:T(8,128)(2,1)}, u32[]{:S(2)}) copy-start(bf16[4,256,16]{1,2,0:T(8,128)(2,1)} %param.35) | copy-start | bytes 98308
  0.7 12.0 %copy-start.126 = (f32[2,144,3,288]{3,1,2,0:T(8,128)S(1)}, f32[2,144,3,288]{3,1,2,0:T(8,128)}, u32[]{:S(2)}) copy-start(f32[2,144,3,288]{3,1,2,0:T(8,128)} %param.42) | copy-start | bytes 2985988
  3.4 17.2 %copy-start.199 = (f32[160]{0:T(256)}, f32[160]{0:T(256)S(1)}, u32[]{:S(2)}) copy-start(f32[160]{0:T(256)S(1)} %compare_convert_fusion) | copy-start | bytes 1924
  3.4 9.4 %copy-start.233 = (f32[128]{0:T(128)}, f32[128]{0:T(128)S(1)}, u32[]{:S(2)}) copy-start(f32[128]{0:T(128)S(1)} %multiply_exponential_fusion.1) | copy-start | bytes 1540
  4.8 15.8 %copy-start.202 = (s32[1,160]{1,0:T(1,128)}, s32[1,160]{1,0:T(1,128)S(1)}, u32[]{:S(2)}) copy-start(s32[1,160]{1,0:T(1,128)S(1)} %constant_dynamic-slice_fusion.4) | copy-start | bytes 1924
  9.5 65.5 %copy-start.192 = (f32[160,16]{0,1:T(8,128)}, f32[160,16]{0,1:T(8,128)S(1)}, u32[]{:S(2)}) copy-start(f32[160,16]{0,1:T(8,128)S(1)} %fusion.125) | copy-start | bytes 30724
  18.2 5.3 copy-start.67
  18.2 5.3 copy-start.84
  146.4 53.2 %copy-start.32 = (bf16[2,2,2,144,288]{4,3,2,1,0:T(8,128)(2,1)}, bf16[2,2,2,144,288]{4,3,2,1,0:T(8,128)(2,1)S(1)}, u32[]{:S(2)}) copy-start(bf16[2,2,2,144,288]{4,3,2,1,0:T(8,128)(2,1)S(1)} %get-tuple-element.144) | copy-start | bytes 1990660
  151.4 74.8 %copy-start.177 = (f32[1152]{0:T(1024)}, f32[1152]{0:T(1024)S(1)}, u32[]{:S(2)}) copy-start(f32[1152]{0:T(1024)S(1)} %add.913) | copy-start | bytes 13828
  152.9 31.7 %copy-start.175 = (f32[1152]{0:T(1024)}, f32[1152]{0:T(1024)S(1)}, u32[]{:S(2)}) copy-start(f32[1152]{0:T(1024)S(1)} %add.904) | copy-start | bytes 13828
  166.0 18.6 %copy-start.24 = (bf16[2,2,2,144,864]{4,3,2,1,0:T(8,128)(2,1)S(1)}, bf16[2,2,2,144,864]{4,3,2,1,0:T(8,128)(2,1)}, u32[]{:S(2)}) copy-start(bf16[2,2,2,144,864]{4,3,2,1,0:T(8,128)(2,1)} %copy-done.23) | copy-start | bytes 5971972
  189.0 6.4 copy-start.232
  202.2 23.1 %copy-start.109 = (f32[160,1152]{1,0:T(8,128)S(1)}, f32[160,1152]{1,0:T(8,128)}, u32[]{:S(2)}) copy-start(f32[160,1152]{1,0:T(8,128)} %copy-done.108) | copy-start | bytes 2211844
  202.2 23.1 %copy-start.185 = (f32[1152]{0:T(1024)S(1)}, f32[1152]{0:T(1024)}, u32[]{:S(2)}) copy-start(f32[1152]{0:T(1024)} %mul.1126) | copy-start | bytes 13828
  225.2 21.7 %copy-start.11 = (bf16[2,2,2,144,1152]{4,3,2,1,0:T(8,128)(2,1)}, bf16[2,2,2,144,1152]{4,3,2,1,0:T(8,128)(2,1)S(1)}, u32[]{:S(2)}) copy-start(bf16[2,2,2,144,1152]{4,3,2,1,0:T(8,128)(2,1)S(1)} %get-tuple-element.150) | copy-start | bytes 7962628
  225.4 49.7 %copy-start.106 = (f32[160,1152]{1,0:T(8,128)}, f32[160,1152]{1,0:T(8,128)S(1)}, u32[]{:S(2)}) copy-start(f32[160,1152]{1,0:T(8,128)S(1)} %get-tuple-element.379) | copy-start | bytes 2211844
  225.4 21.5 %copy-start.207 = (f32[160]{0:T(256)}, f32[160]{0:T(256)S(1)}, u32[]{:S(2)}) copy-start(f32[160]{0:T(256)S(1)} %broadcast_multiply_fusion.6) | copy-start | bytes 1924
  226.2 20.7 %copy-start.217 = (f32[160]{0:T(256)}, f32[160]{0:T(256)S(1)}, u32[]{:S(2)}) copy-start(f32[160]{0:T(256)S(1)} %fusion.177) | copy-start | bytes 1924
  253.2 19.4 %copy-start.119 = (f32[256,576]{1,0:T(8,128)S(1)}, f32[256,576]{1,0:T(8,128)}, u32[]{:S(2)}) copy-start(f32[256,576]{1,0:T(8,128)} %copy-done.118) | copy-start | bytes 1769476
  253.2 19.4 %copy-start.121 = (f32[256,576]{1,0:T(8,128)S(1)}, f32[256,576]{1,0:T(8,128)}, u32[]{:S(2)}) copy-start(f32[256,576]{1,0:T(8,128)} %copy-done.120) | copy-start | bytes 1769476
  253.2 19.4 %copy-start.179 = (f32[1152]{0:T(1024)S(1)}, f32[1152]{0:T(1024)}, u32[]{:S(2)}) copy-start(f32[1152]{0:T(1024)} %mul.1135) | copy-start | bytes 13828
  253.2 19.4 %copy-start.196 = (f32[1152]{0:T(1024)S(1)}, f32[1152]{0:T(1024)}, u32[]{:S(2)}) copy-start(f32[1152]{0:T(1024)} %reshape.1511) | copy-start | bytes 13828
  253.2 19.4 %copy-start.200 = (f32[160]{0:T(256)S(1)}, f32[160]{0:T(256)}, u32[]{:S(2)}) copy-start(f32[160]{0:T(256)} %copy-done.199) | copy-start | bytes 1924
  253.2 19.4 %copy-start.203 = (s32[1,160]{1,0:T(1,128)S(1)}, s32[1,160]{1,0:T(1,128)}, u32[]{:S(2)}) copy-start(s32[1,160]{1,0:T(1,128)} %copy-done.202) | copy-start | bytes 1924
  253.2 19.4 %copy-start.222 = (f32[256]{0:T(256)S(1)}, f32[256]{0:T(256)}, u32[]{:S(2)}) copy-start(f32[256]{0:T(256)} %broadcast_subtract_fusion) | copy-start | bytes 3076
  274.2 19.3 %copy-start.181 = (f32[1152]{0:T(1024)S(1)}, f32[1152]{0:T(1024)}, u32[]{:S(2)}) copy-start(f32[1152]{0:T(1024)} %add.924) | copy-start | bytes 13828
  275.1 20.0 %copy-start.18 = (bf16[2,2,2,144,1152]{4,3,2,1,0:T(8,128)(2,1)S(1)}, bf16[2,2,2,144,1152]{4,3,2,1,0:T(8,128)(2,1)}, u32[]{:S(2)}) copy-start(bf16[2,2,2,144,1152]{4,3,2,1,0:T(8,128)(2,1)} %copy-done.17) | copy-start | bytes 7962628
  323.8 24.2 %copy-start.102 = (f32[256,1152]{1,0:T(8,128)S(1)}, f32[256,1152]{1,0:T(8,128)}, u32[]{:S(2)}) copy-start(f32[256,1152]{1,0:T(8,128)} %copy-done.101) | copy-start | bytes 3538948
  323.8 24.2 %copy-start.187 = (f32[1152]{0:T(1024)S(1)}, f32[1152]{0:T(1024)}, u32[]{:S(2)}) copy-start(f32[1152]{0:T(1024)} %mul.1150) | copy-start | bytes 13828
  347.9 18.2 %copy-start.36 = (f32[256,1152]{1,0:T(8,128)}, f32[256,1152]{1,0:T(8,128)S(1)}, u32[]{:S(2)}) copy-start(f32[256,1152]{1,0:T(8,128)S(1)} %get-tuple-element.163) | copy-start | bytes 3538948
  348.0 18.3 %copy-start.19 = (bf16[2,2,2,144,1152]{4,3,2,1,0:T(8,128)(2,1)}, bf16[2,2,2,144,1152]{4,3,2,1,0:T(8,128)(2,1)S(1)}, u32[]{:S(2)}) copy-start(bf16[2,2,2,144,1152]{4,3,2,1,0:T(8,128)(2,1)S(1)} %get-tuple-element.166) | copy-start | bytes 7962628
  348.2 44.0 %copy-start.104 = (f32[256,1152]{1,0:T(8,128)}, f32[256,1152]{1,0:T(8,128)S(1)}, u32[]{:S(2)}) copy-start(f32[256,1152]{1,0:T(8,128)S(1)} %get-tuple-element.377) | copy-start | bytes 3538948
  348.5 17.7 %copy-start.230 = (f32[256]{0:T(256)}, f32[256]{0:T(256)S(1)}, u32[]{:S(2)}) copy-start(f32[256]{0:T(256)S(1)} %multiply_reduce_fusion.14) | copy-start | bytes 3076
  348.8 17.4 %copy-start.220 = (f32[256]{0:T(256)}, f32[256]{0:T(256)S(1)}, u32[]{:S(2)}) copy-start(f32[256]{0:T(256)S(1)} %fusion.179) | copy-start | bytes 3076
  366.2 4.9 copy-start.15
  375.6 16.7 %copy-start.189 = (f32[1152]{0:T(1024)S(1)}, f32[1152]{0:T(1024)}, u32[]{:S(2)}) copy-start(f32[1152]{0:T(1024)} %mul.1159) | copy-start | bytes 13828
  396.3 17.8 %copy-start.240 = (f32[4,256,1152]{2,1,0:T(8,128)S(1)}, f32[4,256,1152]{2,1,0:T(8,128)}, u32[]{:S(2)}) copy-start(f32[4,256,1152]{2,1,0:T(8,128)} %copy-done.239) | copy-start | bytes 14155780
  397.6 16.6 %copy-start.16 = (bf16[2,2,2,144,1152]{4,3,2,1,0:T(8,128)(2,1)S(1)}, bf16[2,2,2,144,1152]{4,3,2,1,0:T(8,128)(2,1)}, u32[]{:S(2)}) copy-start(bf16[2,2,2,144,1152]{4,3,2,1,0:T(8,128)(2,1)} %copy-done.15) | copy-start | bytes 7962628
  519.0 19.1 %copy-start.6 = (bf16[2,2,2,144,1152]{4,3,2,1,0:T(8,128)(2,1)S(1)}, bf16[2,2,2,144,1152]{4,3,2,1,0:T(8,128)(2,1)}, u32[]{:S(2)}) copy-start(bf16[2,2,2,144,1152]{4,3,2,1,0:T(8,128)(2,1)} %copy-done.5) | copy-start | bytes 7962628
  519.0 19.1 %copy-start.238 = (f32[4,160,1152]{2,1,0:T(8,128)S(1)}, f32[4,160,1152]{2,1,0:T(8,128)}, u32[]{:S(2)}) copy-start(f32[4,160,1152]{2,1,0:T(8,128)} %copy-done.237) | copy-start | bytes 8847364
  546.1 31.0 %copy-start.4 = (bf16[1152,1152]{1,0:T(8,128)(2,1)}, bf16[1152,1152]{1,0:T(8,128)(2,1)S(1)}, u32[]{:S(2)}) copy-start(bf16[1152,1152]{1,0:T(8,128)(2,1)S(1)} %fusion.2) | copy-start | bytes 7962628
  548.6 49.4 %copy-start.2 = (bf16[1152,1152]{1,0:T(8,128)(2,1)}, bf16[1152,1152]{1,0:T(8,128)(2,1)S(1)}, u32[]{:S(2)}) copy-start(bf16[1152,1152]{1,0:T(8,128)(2,1)S(1)} %fusion.3) | copy-start | bytes 7962628
  577.1 19.9 %copy-start.33 = (bf16[2,2,2,144,288]{4,3,2,1,0:T(8,128)(2,1)S(1)}, bf16[2,2,2,144,288]{4,3,2,1,0:T(8,128)(2,1)}, u32[]{:S(2)}) copy-start(bf16[2,2,2,144,288]{4,3,2,1,0:T(8,128)(2,1)} %copy-done.32) | copy-start | bytes 1990660
  623.6 21.2 %copy-start.75 = (bf16[1,144,1152]{2,1,0:T(8,128)(2,1)S(1)}, bf16[1,144,1152]{2,1,0:T(8,128)(2,1)}, u32[]{:S(2)}) copy-start(bf16[1,144,1152]{2,1,0:T(8,128)(2,1)} %copy-done.74) | copy-start | bytes 995332
  623.6 21.2 %copy-start.77 = (bf16[1,144,1152]{2,1,0:T(8,128)(2,1)S(1)}, bf16[1,144,1152]{2,1,0:T(8,128)(2,1)}, u32[]{:S(2)}) copy-start(bf16[1,144,1152]{2,1,0:T(8,128)(2,1)} %copy-done.76) | copy-start | bytes 995332
  644.8 5.0 copy-start.64
  654.6 20.8 %copy-start.71 = (bf16[1,144,1152]{2,1,0:T(8,128)(2,1)S(1)}, bf16[1,144,1152]{2,1,0:T(8,128)(2,1)}, u32[]{:S(2)}) copy-start(bf16[1,144,1152]{2,1,0:T(8,128)(2,1)} %copy-done.70) | copy-start | bytes 995332
  654.7 20.8 %copy-start.73 = (bf16[1,144,1152]{2,1,0:T(8,128)(2,1)S(1)}, bf16[1,144,1152]{2,1,0:T(8,128)(2,1)}, u32[]{:S(2)}) copy-start(bf16[1,144,1152]{2,1,0:T(8,128)(2,1)} %copy-done.72) | copy-start | bytes 995332
  730.3 30.1 %copy-start.166 = (f32[48,288]{1,0:T(8,128)}, f32[48,288]{1,0:T(8,128)S(1)}, u32[]{:S(2)}) copy-start(f32[48,288]{1,0:T(8,128)S(1)} %convert_reduce_fusion) | copy-start | bytes 165892
  762.3 6.2 copy-start.61
  770.3 24.6 %copy-start.161 = (f32[1,288,144]{1,2,0:T(8,128)S(1)}, f32[1,288,144]{1,2,0:T(8,128)}, u32[]{:S(2)}) copy-start(f32[1,288,144]{1,2,0:T(8,128)} %fusion.139) | copy-start | bytes 497668
  798.1 5.2 copy-start.125
  798.1 5.2 copy-start.140
  798.1 5.1 copy-start.143
  798.1 5.1 copy-start.155
  798.1 5.1 copy-start.156
  798.1 5.1 copy-start.157
  803.3 4.8 copy-start.160
  808.1 5.0 copy-start.153
  813.2 4.7 copy-start.137
  813.2 5.5 copy-start.138
  813.2 6.2 copy-start.139
  819.4 4.9 copy-start.1
  (177 other events, 350.1 us)

commit v3 on v2

v3 whole, which is shorter than its diff:
```python
from functools import partial
import math

import jax
import jax.numpy as jnp
from jax import lax
from jax.experimental import pallas as pl
from jax.experimental.pallas import tpu as pltpu
from jax.sharding import Mesh
from jax.sharding import PartitionSpec as P

HEAD_DIM = 72
CLASSES = 1000
FREQ = 256
PATCH_IN = 16
STEP = 10

MESH = pl.DeviceIdType.MESH
PY, PX, CORE, ZH, ZL = "py", "px", "core", "zh", "zl"
WIDE = (PY, PX, CORE)
NARROW = (ZH, ZL)
ALL = WIDE + NARROW
EACH, SAME = range(2)
IN, OUT, EXPAND, CONTRACT = range(4)
TERM_SQUARE, TERM_HEAD, TERM_GATE, TERM_SHIFT, TERM_SCALE, TERM_MASK, TERM_PATCH = range(7)
ENTER, STRAIGHT, CROSS, RELAY, FAR, NEAR, PASS, LEAVE = range(8)

highest_float_accuracy = lax.Precision.HIGHEST
norm_eps = 1e-06
contrast_sharpness_divisor = 0.02
nce_weight = 0.5
learn_rate = 0.05
beta_first = 0.9
beta_second = 0.999
adam_eps = 1e-08
weight_decay = 0.05
clip_norm = 0.05
ema_decay = 0.9999


def layer_norm(values):
    center = values - jnp.mean(values, -1, keepdims=True)
    return center * lax.rsqrt(jnp.mean(center * center, -1, keepdims=True) + norm_eps)


def modulate(values, shift, scale):
    return layer_norm(values) * (1.0 + scale[None, :]) + shift[None, :]


def sinusoid(places, width):
    half = width // 2
    freqs = jnp.exp(-math.log(10000.0) * jnp.arange(half, dtype=jnp.float32) / half)
    angle = places.astype(jnp.float32)[:, None] * freqs[None, :]
    return jnp.concatenate([jnp.cos(angle), jnp.sin(angle)], -1)


def flat_place(axes):
    place = 0
    for axis in axes:
        place = place * lax.axis_size(axis) + lax.axis_index(axis)
    return place


def group_size(axes):
    size = 1
    for axis in axes:
        size = size * lax.axis_size(axis)
    return size


def device_at(axes, place):
    where = {}
    for axis in reversed(axes):
        where[axis] = lax.rem(place, lax.axis_size(axis))
        place = place // lax.axis_size(axis)
    return where


def turned(axis, offset):
    size = lax.axis_size(axis)
    return lax.rem(lax.axis_index(axis) + (offset % size), size)


def other(axis):
    return 1 - lax.axis_index(axis)


class Part:
    def __init__(self):
        self.arrays, self.in_spaces = [], []
        self.shapes, self.out_spaces = [], []
        self.aliases = {}
        self.scratch = []
        self.peers = []

    def take(self, array, space=pltpu.HBM):
        self.arrays.append(array)
        self.in_spaces.append(space)
        return len(self.arrays) - 1

    def give(self, shape, dtype=jnp.bfloat16, space=pltpu.HBM, source=None):
        held = pltpu.HBM if space == pltpu.HBM else jax.ShapeDtypeStruct
        self.shapes.append(held(shape, dtype))
        self.out_spaces.append(space)
        if source is not None:
            self.aliases[source] = len(self.shapes) - 1
        return len(self.shapes) - 1

    def greet(self, barrier):
        for peer in self.peers:
            pl.semaphore_signal(barrier, inc=1, device_id=peer(), device_id_type=MESH)
        return len(self.peers)

    def begin(self, ins, outs, scratch, halfway):
        pass

    def go(self, step, ins, outs, scratch):
        pass


class Exchange(Part):
    def __init__(self, arrays, specs):
        super().__init__()
        self.specs = specs
        for array, (axes, mode) in zip(arrays, specs):
            size = group_size(axes)
            piece = array.shape[1:] if mode == EACH else array.shape
            self.take(array, pltpu.VMEM)
            self.give((size,) + piece, array.dtype, pltpu.VMEM)
            self.scratch += [pltpu.SemaphoreType.DMA((size,)), pltpu.SemaphoreType.DMA((size,))]

    def greet(self, barrier):
        greeted = 0
        for axes, _ in self.specs:
            size, me = group_size(axes), flat_place(axes)
            greeted += size - 1

            def signal(offset, carry, axes=axes, size=size, me=me):
                target = lax.rem(me + offset, size)
                pl.semaphore_signal(
                    barrier, inc=1, device_id=device_at(axes, target), device_id_type=MESH
                )
                return carry

            lax.fori_loop(1, size, signal, 0)
        return greeted

    def begin(self, ins, outs, scratch, halfway):
        def copy_to(index, offset, arriving):
            axes, mode = self.specs[index]
            size, me = group_size(axes), flat_place(axes)
            target = lax.rem(me + offset, size)
            return pltpu.make_async_remote_copy(
                src_ref=ins[index].at[target] if mode == EACH else ins[index],
                dst_ref=outs[index].at[target if arriving else me],
                send_sem=scratch[2 * index].at[target],
                recv_sem=scratch[2 * index + 1].at[target if arriving else me],
                device_id=device_at(axes, target),
                device_id_type=MESH,
            )

        for index, (axes, mode) in enumerate(self.specs):

            def start(offset, carry, index=index):
                copy_to(index, offset, False).start()
                return carry

            lax.fori_loop(1, group_size(axes), start, 0)
        for index, (axes, mode) in enumerate(self.specs):
            me = flat_place(axes)
            outs[index][me] = ins[index][me] if mode == EACH else ins[index][...]
        for index, (axes, mode) in enumerate(self.specs):

            def end(offset, carry, index=index):
                copy_to(index, offset, True).wait_recv()
                copy_to(index, offset, False).wait_send()
                return carry

            lax.fori_loop(1, group_size(axes), end, 0)
        halfway()


class Norm(Exchange):
    def __init__(self, scalars, mets):
        super().__init__([scalars], [(ALL, SAME)])
        for met in mets:
            self.take(met, pltpu.VMEM)
        self.scratch.append(pltpu.VMEM(scalars.shape, jnp.float32))

    def begin(self, ins, outs, scratch, halfway):
        square = jnp.zeros((8, 128), jnp.float32)
        for met in ins[1:]:
            total = met[0].astype(jnp.float32) + met[1].astype(jnp.float32)
            columns = total.shape[1]
            squares = total * total
            if squares.shape[0] % 8:
                squares = jnp.pad(fold(squares), ((0, 7), (0, 0)))
            eights = jnp.sum(squares.reshape(-1, 8, columns), 0)
            for start in range(0, columns, 128):
                lanes = eights[:, start : start + 128]
                if lanes.shape[1] < 128:
                    lanes = jnp.pad(lanes, ((0, 0), (0, 128 - lanes.shape[1])))
                square = square + lanes
        lane = lax.broadcasted_iota(jnp.int32, (8, 128), 1)
        scratch[2][...] = ins[0][...] + jnp.where(lane == 2, jnp.sum(square), 0.0)
        super().begin([scratch[2]], outs, scratch[:2], halfway)


class RowPieces(Part):
    def __init__(self, pieces):
        super().__init__()
        self.each = pieces.shape[0]
        wides, narrows = group_size(WIDE), group_size(NARROW)
        self.take(pieces, pltpu.VMEM)
        self.give((wides,) + pieces.shape[1:], pieces.dtype, pltpu.VMEM)
        self.scratch = [
            pltpu.SemaphoreType.DMA((self.each * narrows,)),
            pltpu.SemaphoreType.DMA((wides,)),
        ]

    def sends(self):
        narrows, me = group_size(NARROW), flat_place(WIDE) * group_size(NARROW) + flat_place(NARROW)
        for j in range(self.each):
            for z in range(narrows):
                wide = flat_place(NARROW) * self.each + j
                to = {**device_at(WIDE, wide), **device_at(NARROW, jnp.int32(z))}
                yield j, z, to, wide * narrows + z != me

    def receives(self):
        narrows, me = group_size(NARROW), flat_place(WIDE) * group_size(NARROW) + flat_place(NARROW)
        z = flat_place(WIDE) // self.each
        for w in range(group_size(WIDE)):
            to = {**device_at(WIDE, jnp.int32(w)), **device_at(NARROW, z)}
            yield w, to, w * narrows + z != me

    def greet(self, barrier):
        for _, _, to, remote in self.sends():

            @pl.when(remote)
            def _(to=to):
                pl.semaphore_signal(barrier, inc=1, device_id=to, device_id_type=MESH)

        for _, to, remote in self.receives():

            @pl.when(remote)
            def _(to=to):
                pl.semaphore_signal(barrier, inc=1, device_id=to, device_id_type=MESH)

        counts = [r.astype(jnp.int32) for _, _, _, r in self.sends()]
        counts += [r.astype(jnp.int32) for _, _, r in self.receives()]
        return sum(counts)

    def begin(self, ins, outs, scratch, halfway):
        me = flat_place(WIDE)
        z = flat_place(WIDE) // self.each
        narrows = group_size(NARROW)

        def copy(j, slot, sem, to):
            return pltpu.make_async_remote_copy(
                src_ref=ins[0].at[j],
                dst_ref=outs[0].at[slot],
                send_sem=scratch[0].at[sem],
                recv_sem=scratch[1].at[slot],
                device_id=to,
                device_id_type=MESH,
            )

        for j, t, to, remote in self.sends():

            @pl.when(remote)
            def _(j=j, t=t, to=to):
                copy(j, me, j * narrows + t, to).start()

            @pl.when(jnp.logical_not(remote))
            def _(j=j):
                outs[0][me] = ins[0][j]

        for w, to, remote in self.receives():

            @pl.when(remote)
            def _(w=w, to=to):
                copy(0, w, 0, to).wait_recv()

        for j, t, to, remote in self.sends():

            @pl.when(remote)
            def _(j=j, t=t, to=to):
                copy(j, me, j * narrows + t, to).wait_send()

        halfway()


def chunk_of(length):
    return 64 if length % 64 == 0 else 32


def normal(values):
    center = values - jnp.mean(values, -1, keepdims=True)
    scale = lax.rsqrt(jnp.mean(center * center, -1, keepdims=True) + norm_eps)
    return center * scale, scale


def normal_back(grad, unit, scale):
    flat = jnp.mean(grad, -1, keepdims=True)
    tilt = jnp.mean(grad * unit, -1, keepdims=True)
    return scale * (grad - flat - unit * tilt)


def fold(values):
    return jnp.sum(values, 0, keepdims=True)


def full_dot(left, right):
    return jnp.dot(
        left, right, precision=highest_float_accuracy, preferred_element_type=jnp.float32
    )


SHIFT_A, SCALE_A, GATE_A, SHIFT_M, SCALE_M, GATE_M = range(6)


class Bridge(Part):
    whole = False
    sends_on = True

    def __init__(self, terms, more, width, length_in, length_out):
        super().__init__()
        self.length_in, self.length_out, self.width = length_in, length_out, width
        self.sums = terms is not None
        self.first = 0
        if self.sums:
            self.take(terms, pltpu.VMEM)
            self.first = 1
        for array in more:
            self.take(array, pltpu.VMEM)
        if self.sends_on:
            self.give((4, length_out, width), jnp.bfloat16, pltpu.VMEM)
        self.peers = [lambda: {CORE: other(CORE)}, lambda: {ZL: other(ZL)}]
        self.scratch = []
        if self.sums:
            self.scratch += [pltpu.VMEM((length_in, width), jnp.bfloat16)] * 4
            self.scratch += self.sems(length_in)
        if self.sends_on:
            self.scratch += self.sems(length_out)

    def result(self, shape, dtype=jnp.float32):
        self.give(shape, dtype, pltpu.VMEM)

    def sems(self, length):
        steps = length // chunk_of(length)
        return [pltpu.SemaphoreType.DMA((3, steps)), pltpu.SemaphoreType.DMA((3, steps))]

    def ranks(self):
        core, low = lax.axis_index(CORE), lax.axis_index(ZL)
        return core * 2 + low, (1 - core) * 2 + low, core * 2 + 1 - low, (1 - core) * 2 + 1 - low

    def copy(self, source, target, sems, kind, step):
        return pltpu.make_async_remote_copy(
            src_ref=source,
            dst_ref=target,
            send_sem=sems[0].at[kind, step],
            recv_sem=sems[1].at[kind, step],
            device_id={ZL: other(ZL)} if kind == 0 else {CORE: other(CORE)},
            device_id_type=MESH,
        )

    def rows(self, length):
        chunk = chunk_of(length)
        return [pl.ds(s * chunk, chunk) for s in range(length // chunk)]

    def begin(self, ins, outs, scratch, halfway):
        me, mate, away, away_mate = self.ranks()
        given = ins[self.first :]
        made = outs[1:] if self.sends_on else outs
        state = self.start(given, made)
        sends = []
        rows_in, rows_out = self.rows(self.length_in), self.rows(self.length_out)
        if self.sums:
            terms = ins[0]
            near, home, stage, far = scratch[:4]
            sems = scratch[4:6]
            to_near = [
                self.copy(terms.at[away_mate, r], near.at[r], sems, 1, s)
                for s, r in enumerate(rows_in)
            ]
            to_home = [
                self.copy(terms.at[mate, r], home.at[r], sems, 2, s) for s, r in enumerate(rows_in)
            ]
            to_far = [self.copy(stage.at[r], far.at[r], sems, 0, s) for s, r in enumerate(rows_in)]
            for each in to_near:
                each.start()
            for each in to_home:
                each.start()
            for s, r in enumerate(rows_in):
                to_near[s].wait_recv()
                both = terms[away, r].astype(jnp.float32) + near[r].astype(jnp.float32)
                stage[r] = both.astype(jnp.bfloat16)
                to_far[s].start()
            sends += to_near + to_home + to_far

            def total(s, r):
                to_home[s].wait_recv()
                own = terms[me, r].astype(jnp.float32) + home[r].astype(jnp.float32)
                to_far[s].wait_recv()
                return own + far[r].astype(jnp.float32)

        else:

            def total(s, r):
                return None

        if self.sends_on:
            every = outs[0]
            sems_out = scratch[-2:]

            def move(kind, here, there, s, r):
                return self.copy(every.at[here, r], every.at[there, r], sems_out, kind, s)

            def pass_on(s, r, fresh):
                every[me, r] = fresh
                for kind in (0, 1):
                    each = move(kind, me, me, s, r)
                    each.start()
                    sends.append(each)

        if self.whole:
            for s, r in enumerate(rows_in):
                self.collect(r, total(s, r), given, made, state)
            self.turn(given, made, state)
            for s, r in enumerate(rows_out):
                pass_on(s, r, self.work(r, None, given, made, state))
        else:
            for s, r in enumerate(rows_in):
                fresh = self.work(r, total(s, r), given, made, state)
                if self.sends_on:
                    pass_on(s, r, fresh)
        self.end(given, made, state)
        self.aside(given, made)
        if self.sums:
            halfway()
        if self.sends_on:
            for s, r in enumerate(rows_out):
                move(0, me, away, s, r).wait_recv()
                each = move(2, away, away, s, r)
                each.start()
                sends.append(each)
            for s, r in enumerate(rows_out):
                move(1, me, mate, s, r).wait_recv()
                move(2, away, away_mate, s, r).wait_recv()
        for each in sends:
            each.wait_send()
        if not self.sums:
            halfway()

    def start(self, given, made):
        return {}

    def add(self, state, name, value):
        state[name] = value if name not in state else state[name] + value

    def end(self, given, made, state):
        pass

    def aside(self, given, made):
        pass


def outer(left, right, result):
    step = 384 if left.shape[2] % 384 == 0 else 128

    def tile(i, carry):
        columns = pl.ds(pl.multiple_of(i * step, step), step)
        value = lax.dot_general(
            left[:, :, columns].reshape(-1, step),
            right[...].reshape(-1, right.shape[2]),
            (((0,), (0,)), ((), ())),
            preferred_element_type=jnp.float32,
        )
        result[columns] = value.astype(jnp.bfloat16)
        return carry

    lax.fori_loop(0, left.shape[2] // step, tile, 0)


class Enter(Bridge):
    def __init__(self, values, mod):
        length, width = values.shape
        super().__init__(None, [values, mod], width, length, length)

    def work(self, r, total, given, made, state):
        values, mod = given
        unit, _ = normal(values[r])
        return (unit * (1.0 + mod[SCALE_A : SCALE_A + 1]) + mod[SHIFT_A : SHIFT_A + 1]).astype(
            jnp.bfloat16
        )


class Middle(Bridge):
    def __init__(self, terms, values, mod):
        length, width = values.shape
        super().__init__(terms, [values, mod], width, length, length)
        self.result((length, width))
        self.result((length, width))

    def work(self, r, total, given, made, state):
        values, mod = given
        attn, middle = made
        attn[r] = total
        fresh = values[r] + mod[GATE_A : GATE_A + 1] * total
        middle[r] = fresh
        unit, _ = normal(fresh)
        return (unit * (1.0 + mod[SCALE_M : SCALE_M + 1]) + mod[SHIFT_M : SHIFT_M + 1]).astype(
            jnp.bfloat16
        )


class Decode(Bridge):
    whole = True

    def __init__(self, terms, middle, mod, mod_next, place, base):
        (length, width), (length_next, _) = middle.shape, base.shape
        super().__init__(terms, [middle, mod, mod_next, place, base], width, length, length_next)
        self.result((length, width))
        self.result((length, width))
        self.result((length_next, width))

    def collect(self, r, total, given, made, state):
        middle, mod = given[:2]
        branch, encoded = made[:2]
        branch[r] = total
        encoded[r] = middle[r] + mod[GATE_M : GATE_M + 1] * total

    def turn(self, given, made, state):
        place, base = given[3:]
        made[2][...] = full_dot(place[...], made[1][...]) + base[...]

    def work(self, r, total, given, made, state):
        mod = given[2]
        unit, _ = normal(made[2][r])
        return (unit * (1.0 + mod[SCALE_A : SCALE_A + 1]) + mod[SHIFT_A : SHIFT_A + 1]).astype(
            jnp.bfloat16
        )


class Turn(Bridge):
    def __init__(self, terms, middle, mod, head, noise, count_all):
        length, width = middle.shape
        super().__init__(terms, [middle, mod, head, noise], width, length, length)
        self.scale = 2.0 / count_all
        self.result((length, width))
        self.result((1, width))
        self.result(head.shape)
        self.result((1, 1))

    def work(self, r, total, given, made, state):
        middle, mod, head, noise = given
        gate = mod[GATE_M : GATE_M + 1]
        unit, scale = normal(middle[r] + gate * total)
        low = unit.astype(jnp.bfloat16)
        rows_by_rows = (((1,), (1,)), ((), ()))
        predict = lax.dot_general(low, head[...], rows_by_rows, preferred_element_type=jnp.float32)
        error = predict - noise[r]
        self.add(state, TERM_SQUARE, jnp.sum(error * error, keepdims=True))
        grad_predict = (error * self.scale).astype(jnp.bfloat16)
        columns_by_columns = (((0,), (0,)), ((), ()))
        self.add(
            state,
            TERM_HEAD,
            lax.dot_general(
                grad_predict, low, columns_by_columns, preferred_element_type=jnp.float32
            ),
        )
        grad_final = jnp.dot(grad_predict, head[...], preferred_element_type=jnp.float32)
        grad = normal_back(grad_final, unit, scale)
        made[0][r] = grad
        self.add(state, TERM_GATE, fold(grad * total))
        return (gate * grad).astype(jnp.bfloat16)

    def end(self, given, made, state):
        made[1][...] = state[TERM_GATE]
        made[2][...] = state[TERM_HEAD]
        made[3][...] = state[TERM_SQUARE]


class MiddleBack(Bridge):
    def __init__(self, terms, middle, attn, grad, mod):
        length, width = middle.shape
        super().__init__(terms, [middle, attn, grad, mod], width, length, length)
        self.result((length, width))
        self.result((3, width))

    def work(self, r, total, given, made, state):
        middle, attn, grad, mod = given
        unit, scale = normal(middle[r])
        self.add(state, TERM_SHIFT, fold(total))
        self.add(state, TERM_SCALE, fold(total * unit))
        back = normal_back(total * (1.0 + mod[SCALE_M : SCALE_M + 1]), unit, scale)
        fresh = grad[r] + back
        made[0][r] = fresh
        self.add(state, TERM_GATE, fold(fresh * attn[r]))
        return (mod[GATE_A : GATE_A + 1] * fresh).astype(jnp.bfloat16)

    def end(self, given, made, state):
        made[1][0:1] = state[TERM_SHIFT]
        made[1][1:2] = state[TERM_SCALE]
        made[1][2:3] = state[TERM_GATE]


class Encode(Bridge):
    whole = True

    def __init__(self, terms, values, grad, mod, open_place, select, pool, branch, mod_next, pairs):
        (length, width), (length_next, _) = values.shape, branch.shape
        super().__init__(
            terms,
            [values, grad, mod, open_place, select, pool, branch, mod_next, *pairs],
            width,
            length,
            length_next,
        )
        self.result((length_next, width))
        self.result((4, width))
        self.result((width, pairs[1].shape[2]), jnp.bfloat16)
        self.result((width, pairs[3].shape[2]), jnp.bfloat16)
        self.scratch = [pltpu.VMEM((length, width), jnp.float32)] + self.scratch

    def begin(self, ins, outs, scratch, halfway):
        self.held = scratch[0]
        super().begin(ins, outs, scratch[1:], halfway)

    def collect(self, r, total, given, made, state):
        values, grad, mod, open_place = given[:4]
        unit, scale = normal(values[r])
        self.add(state, TERM_SHIFT, fold(total))
        self.add(state, TERM_SCALE, fold(total * unit))
        back = normal_back(total * (1.0 + mod[SCALE_A : SCALE_A + 1]), unit, scale)
        fresh = grad[r] + back
        self.held[r] = fresh
        self.add(state, TERM_MASK, fold(open_place[r] * fresh))

    def turn(self, given, made, state):
        select, pool = given[4:6]
        made[0][...] = full_dot(select[...], self.held[...]) + pool[...]

    def work(self, r, total, given, made, state):
        branch, mod_next = given[6:8]
        fresh = made[0][r]
        self.add(state, TERM_GATE, fold(fresh * branch[r]))
        return (mod_next[GATE_M : GATE_M + 1] * fresh).astype(jnp.bfloat16)

    def end(self, given, made, state):
        made[1][0:1] = state[TERM_SHIFT]
        made[1][1:2] = state[TERM_SCALE]
        made[1][2:3] = state[TERM_GATE]
        made[1][3:4] = state[TERM_MASK]

    def aside(self, given, made):
        outer(given[8], given[9], made[2])
        outer(given[10], given[11], made[3])


class Leave(Bridge):
    sends_on = False

    def __init__(self, terms, values, grad, mod, kept, sums, pairs):
        length, width = values.shape
        super().__init__(terms, [values, grad, mod, kept, *sums, *pairs], width, length, length)
        narrows = group_size(NARROW)
        piece = jax.ShapeDtypeStruct((narrows, 48, width // narrows), jnp.float32)
        self.tell = Exchange([piece], [(NARROW, EACH)])
        self.result(piece.shape)
        self.result((width, pairs[1].shape[2]), jnp.bfloat16)
        self.result((width, pairs[3].shape[2]), jnp.bfloat16)
        self.scratch = (
            [pltpu.VMEM((48, width), jnp.float32), pltpu.VMEM(piece.shape, jnp.float32)]
            + self.tell.scratch
            + self.scratch
        )

    def greet(self, barrier):
        return super().greet(barrier) + self.tell.greet(barrier)

    def begin(self, ins, outs, scratch, halfway):
        self.table, self.piece = scratch[:2]
        self.tell_sems = scratch[2:4]
        super().begin(ins, outs, scratch[4:], halfway)

    def work(self, r, total, given, made, state):
        values, grad, mod, kept = given[:4]
        unit, scale = normal(values[r])
        self.add(state, TERM_SHIFT, fold(total))
        self.add(state, TERM_SCALE, fold(total * unit))
        back = normal_back(total * (1.0 + mod[SCALE_A : SCALE_A + 1]), unit, scale)
        columns_by_columns = (((0,), (0,)), ((), ()))
        self.add(
            state,
            TERM_PATCH,
            lax.dot_general(
                kept[r],
                grad[r] + back,
                columns_by_columns,
                precision=highest_float_accuracy,
                preferred_element_type=jnp.float32,
            ),
        )

    def end(self, given, made, state):
        sums_m0, sums_a1, sums_m1, gate_m1, head = given[4:9]
        table = self.table
        table[...] = jnp.zeros(table.shape, jnp.float32)
        table[0:1] = state[TERM_SHIFT]
        table[1:2] = state[TERM_SCALE]
        table[2:3] = sums_m0[2:3]
        table[3:5] = sums_m0[0:2]
        table[5:6] = sums_a1[2:3]
        table[6:8] = sums_a1[0:2]
        table[8:9] = sums_m1[2:3]
        table[9:11] = sums_m1[0:2]
        table[11:12] = gate_m1[...]
        table[12:28] = state[TERM_PATCH]
        table[28:44] = head[...]
        table[44:45] = sums_a1[3:4]
        local = self.piece.shape[2]
        for z in range(self.piece.shape[0]):
            self.piece[z] = table[:, z * local : (z + 1) * local]
        self.tell.begin([self.piece], made[:1], self.tell_sems, lambda: None)

    def aside(self, given, made):
        outer(given[9], given[10], made[1])
        outer(given[11], given[12], made[2])


class Errand(Part):
    def plan(self, ins, outs):
        raise NotImplementedError

    def local(self, ins, outs):
        return []

    def reserve(self, count, local=0):
        self.scratch = [pltpu.SemaphoreType.DMA((count,)), pltpu.SemaphoreType.DMA((count,))]
        if local:
            self.scratch.append(pltpu.SemaphoreType.DMA((local,)))

    def go(self, step, ins, outs, scratch):
        first = 0
        plans = self.plan(ins, outs)
        if step == 1 and len(plans) == 1:
            return
        for turn, moves in enumerate(plans):
            last = turn == len(plans) - 1
            if step == (2 if last else turn + 1):
                self.run(moves, first, scratch, True)
            if step == turn:
                self.run(moves, first, scratch, False)
            first += len(moves)
        if step != 1:
            for i, (source, target, when) in enumerate(self.local(ins, outs)):

                def act_local(i=i, source=source, target=target):
                    copy = pltpu.make_async_copy(source, target, scratch[2].at[i])
                    if step:
                        copy.wait()
                    else:
                        copy.start()

                pl.when(when)(act_local)

    def run(self, moves, first, scratch, ending):
        for i, (source, target, landing, device, when) in enumerate(moves):

            def remote(place, i=first + i, source=source, device=device):
                return pltpu.make_async_remote_copy(
                    src_ref=source,
                    dst_ref=place,
                    send_sem=scratch[0].at[i],
                    recv_sem=scratch[1].at[i],
                    device_id=device,
                    device_id_type=MESH,
                )

            def act(remote=remote, target=target, landing=landing):
                if ending:
                    remote(landing).wait_recv()
                    remote(target).wait_send()
                else:
                    remote(target).start()

            if when is None:
                act()
            else:
                pl.when(when)(act)


def plane_peers():
    peers = []
    for axis in (PY, PX):
        for offset in range(1, lax.axis_size(axis)):
            peers.append(lambda axis=axis, offset=offset: {axis: turned(axis, offset)})
    return peers


SWAP_PEERS = [
    lambda: {CORE: other(CORE)},
    lambda: {ZH: other(ZH)},
    lambda: {CORE: other(CORE), ZH: other(ZH)},
]


class SwapIn(Errand):
    def __init__(self, shard):
        super().__init__()
        self.take(shard)
        self.give((lax.axis_size(PY), lax.axis_size(PX), 2) + shard.shape)
        self.peers = SWAP_PEERS
        self.reserve(2, 1)

    def plan(self, ins, outs):
        core, half = lax.axis_index(CORE), lax.axis_index(ZH)
        home = outs[0].at[lax.axis_index(PY), lax.axis_index(PX)]
        crossed = jnp.where(core == 0, 1 - half, half)
        return [
            [
                (ins[0], home.at[core], home.at[1 - core], {CORE: 1 - core, ZH: crossed}, None),
                (ins[0], home.at[1], home.at[1], {ZH: 1 - half}, core == 1),
            ]
        ]

    def local(self, ins, outs):
        home = outs[0].at[lax.axis_index(PY), lax.axis_index(PX)]
        return [(ins[0], home.at[0], lax.axis_index(CORE) == 0)]


class Spread(Errand):
    def __init__(self, rows, stages):
        super().__init__()
        self.stages = stages
        self.give(rows.shape, rows.dtype, pltpu.HBM, self.take(rows))
        self.peers = plane_peers()
        ny, nx = rows.shape[:2]
        straight, relayed = nx + ny - 2, 2 * (nx - 1) * (ny - 1)
        self.reserve(sum(relayed if stage == RELAY else straight for stage in stages))

    def plan(self, ins, outs):
        rows = outs[0]
        ny, nx = rows.shape[:2]
        first, then = [], []
        own = {PY: lax.axis_index(PY), PX: lax.axis_index(PX)}
        sides = [(PX, nx), (PY, ny)]

        def along(moves, axis, offset, at, core):
            land = dict(at)
            land[axis] = turned(axis, -offset)
            here = rows.at[at[PY], at[PX], core]
            there = rows.at[land[PY], land[PX], core]
            moves.append((here, here, there, {axis: turned(axis, offset)}, None))

        for stage in self.stages:
            if stage == RELAY:
                for e in range(1, nx):
                    for offset in range(1, ny):
                        along(then, PY, offset, {**own, PX: turned(PX, e)}, 0)
                for e in range(1, ny):
                    for offset in range(1, nx):
                        along(then, PX, offset, {**own, PY: turned(PY, e)}, 1)
            else:
                for core, (axis, size) in enumerate(sides if stage == STRAIGHT else sides[::-1]):
                    for offset in range(1, size):
                        along(first, axis, offset, own, core)
        if STRAIGHT in self.stages:
            return [first, then] if then else [first]
        return [first + then]


class FoldFar(Errand):
    def __init__(self, grad):
        super().__init__()
        self.take(grad)
        ny, nx, _, rows, columns = grad.shape
        self.give((ny - 1, nx - 1, rows, columns))
        self.give((nx - 1, ny - 1, rows, columns))
        self.peers = plane_peers()
        self.reserve(2 * (nx - 1) * (ny - 1))

    def plan(self, ins, outs):
        grad = ins[0]
        ny, nx = grad.shape[:2]
        moves = []
        for e in range(1, nx):
            for d in range(1, ny):
                slot = outs[0].at[d - 1, e - 1]
                to = turned(PY, d)
                moves.append((grad.at[to, turned(PX, e), 0], slot, slot, {PY: to}, None))
        for e in range(1, ny):
            for d in range(1, nx):
                slot = outs[1].at[d - 1, e - 1]
                to = turned(PX, d)
                moves.append((grad.at[turned(PY, e), to, 1], slot, slot, {PX: to}, None))
        return [moves]


class FoldNear(Errand):
    def __init__(self, grad):
        super().__init__()
        self.take(grad)
        ny, nx, _, rows, columns = grad.shape
        self.give((ny - 1, rows, columns))
        self.give((nx - 1, rows, columns))
        self.peers = plane_peers()
        self.reserve(nx + ny - 2)

    def plan(self, ins, outs):
        grad = ins[0]
        ny, nx = grad.shape[:2]
        y, x = lax.axis_index(PY), lax.axis_index(PX)
        moves = []
        for d in range(1, ny):
            to, slot = turned(PY, d), outs[0].at[d - 1]
            moves.append((grad.at[to, x, 0], slot, slot, {PY: to}, None))
        for d in range(1, nx):
            to, slot = turned(PX, d), outs[1].at[d - 1]
            moves.append((grad.at[y, to, 1], slot, slot, {PX: to}, None))
        return [moves]


class FoldRelay(Errand):
    def __init__(self, sums):
        super().__init__()
        for each in sums:
            self.take(each)
            self.give(each.shape)
        self.peers = plane_peers()
        self.reserve(sums[0].shape[0] + sums[1].shape[0])

    def plan(self, ins, outs):
        moves = []
        for i, axis in enumerate((PX, PY)):
            for e in range(1, lax.axis_size(axis)):
                slot = outs[i].at[e - 1]
                moves.append((ins[i].at[e - 1], slot, slot, {axis: turned(axis, e)}, None))
        return [moves]


class SwapOut(Errand):
    def __init__(self, pair):
        super().__init__()
        self.take(pair)
        self.give(pair.shape)
        self.peers = SWAP_PEERS
        self.reserve(2, 1)

    def plan(self, ins, outs):
        core, half = lax.axis_index(CORE), lax.axis_index(ZH)
        crossed = jnp.where(core == 0, half, 1 - half)
        pair, met = ins[0], outs[0]
        return [
            [
                (pair.at[1 - core], met.at[0], met.at[0], {CORE: 1 - core, ZH: crossed}, None),
                (pair.at[1], met.at[1], met.at[1], {ZH: 1 - half}, core == 1),
            ]
        ]

    def local(self, ins, outs):
        return [(ins[0].at[0], outs[0].at[1], lax.axis_index(CORE) == 0)]


def take_counts(refs, sizes):
    taken, rest = [], list(refs)
    for size in sizes:
        taken.append(rest[:size])
        rest = rest[size:]
    return taken, rest


def kernel(parts, *refs):
    ins, refs = take_counts(refs, [len(part.arrays) for part in parts])
    outs, refs = take_counts(refs, [len(part.shapes) for part in parts])
    scratch, _ = take_counts(refs, [len(part.scratch) for part in parts])
    barrier = pltpu.get_barrier_semaphore()
    greeted = sum(part.greet(barrier) for part in parts)
    pl.semaphore_wait(barrier, greeted)

    def errands(step):
        for i in range(1, len(parts)):
            parts[i].go(step, ins[i], outs[i], scratch[i])

    errands(0)
    parts[0].begin(ins[0], outs[0], scratch[0], partial(errands, 1))
    errands(2)


def travel(collective_id, *parts):
    aliases, first_in, first_out = {}, 0, 0
    for part in parts:
        for source, result in part.aliases.items():
            aliases[first_in + source] = first_out + result
        first_in += len(part.arrays)
        first_out += len(part.shapes)
    results = pl.pallas_call(
        partial(kernel, parts),
        out_shape=[shape for part in parts for shape in part.shapes],
        in_specs=[pl.BlockSpec(memory_space=space) for part in parts for space in part.in_spaces],
        out_specs=[pl.BlockSpec(memory_space=space) for part in parts for space in part.out_spaces],
        scratch_shapes=[each for part in parts for each in part.scratch],
        input_output_aliases=aliases,
        compiler_params=pltpu.CompilerParams(
            collective_id=collective_id, has_side_effects=True, vmem_limit_bytes=24 * 2**20
        ),
        cost_estimate=pl.CostEstimate(flops=2 * 10**10, bytes_accessed=1024, transcendentals=0),
    )(*[array for part in parts for array in part.arrays])
    split, _ = take_counts(results, [len(part.shapes) for part in parts])
    return split


class Route:
    def __init__(self, shards, errands):
        self.shards = shards
        self.errands = iter(errands)
        self.rows, self.grads, self.got = {}, {}, {FAR: {}, NEAR: {}, PASS: {}, LEAVE: {}}
        self.count = 0

    def step(self, main):
        errands, parts = next(self.errands), [main]
        for name, what in errands:
            if what == (ENTER,):
                parts.append(SwapIn(self.shards[name]))
            elif what == (FAR,):
                parts.append(FoldFar(self.grads[name]))
            elif what == (NEAR,):
                parts.append(FoldNear(self.grads[name]))
            elif what == (PASS,):
                parts.append(FoldRelay(self.far_sums(name)))
            elif what == (LEAVE,):
                parts.append(SwapOut(self.pair(name)))
            else:
                parts.append(Spread(self.rows[name], what))
        results = travel(self.count, *parts)
        self.count += 1
        for (name, what), got in zip(errands, results[1:]):
            if what[0] in self.got:
                self.got[what[0]][name] = got
            else:
                self.rows[name] = got[0]
        return results[0]

    def weight(self, kind, block):
        rows = self.rows[kind, block]
        return rows.reshape(-1, rows.shape[-1])

    def give_grad(self, kind, block, grad):
        name = (kind, block)
        self.grads[name] = grad.astype(jnp.bfloat16).reshape(self.rows[name].shape)

    def own_rows(self, name, py, px, core):
        grad = self.grads[name]
        at = lax.dynamic_slice(grad, (py, px, core, 0, 0), (1, 1, 1) + grad.shape[3:])
        return at[0, 0, 0].astype(jnp.float32)

    def far_sums(self, name):
        y, x = lax.axis_index(PY), lax.axis_index(PX)
        along_y, along_x = self.got[FAR][name]
        first = [
            self.own_rows(name, y, turned(PX, e), 0)
            + jnp.sum(along_y[:, e - 1].astype(jnp.float32), 0)
            for e in range(1, lax.axis_size(PX))
        ]
        last = [
            self.own_rows(name, turned(PY, e), x, 1)
            + jnp.sum(along_x[:, e - 1].astype(jnp.float32), 0)
            for e in range(1, lax.axis_size(PY))
        ]
        return jnp.stack(first).astype(jnp.bfloat16), jnp.stack(last).astype(jnp.bfloat16)

    def pair(self, name):
        y, x = lax.axis_index(PY), lax.axis_index(PX)
        halves = []
        for core in range(2):
            near = jnp.sum(self.got[NEAR][name][core].astype(jnp.float32), 0)
            relayed = jnp.sum(self.got[PASS][name][core].astype(jnp.float32), 0)
            halves.append(self.own_rows(name, y, x, core) + near + relayed)
        return jnp.stack(halves).astype(jnp.bfloat16)

    def met(self, kind, block):
        return self.got[LEAVE][kind, block][0]


def scores_of(query, key, key_valid):
    scale = 1.0 / math.sqrt(HEAD_DIM)
    scores = jnp.einsum("bqhe,bkhe->bhqk", query, key, preferred_element_type=jnp.float32) * scale
    if key_valid is None:
        return scores
    return jnp.where(key_valid[:, None, None, :] > 0, scores, -1e30)


def attend_forward(query, key, value, key_valid):
    scores = scores_of(query, key, key_valid)
    peak = jnp.max(scores, -1, keepdims=True)
    expo = jnp.exp(scores - peak)
    total = jnp.sum(expo, -1, keepdims=True)
    probs = (expo / total).astype(jnp.bfloat16)
    context = jnp.einsum(
        "bhqk,bkhe->bqhe", probs, value, preferred_element_type=jnp.float32
    ).astype(jnp.bfloat16)
    return (context, peak + jnp.log(total))


def attend_backward(query, key, value, log_total, grad_context, key_valid):
    scale = 1.0 / math.sqrt(HEAD_DIM)
    probs = jnp.exp(scores_of(query, key, key_valid) - log_total)
    grad_value = jnp.einsum(
        "bhqk,bqhe->bkhe",
        probs.astype(jnp.bfloat16),
        grad_context,
        preferred_element_type=jnp.float32,
    ).astype(jnp.bfloat16)
    grad_probs = jnp.einsum(
        "bqhe,bkhe->bhqk", grad_context, value, preferred_element_type=jnp.float32
    )
    grad_scores = (probs * (grad_probs - jnp.sum(grad_probs * probs, -1, keepdims=True))).astype(
        jnp.bfloat16
    )
    grad_query = (
        jnp.einsum("bhqk,bkhe->bqhe", grad_scores, key, preferred_element_type=jnp.float32) * scale
    ).astype(jnp.bfloat16)
    grad_key = (
        jnp.einsum("bhqk,bqhe->bkhe", grad_scores, query, preferred_element_type=jnp.float32)
        * scale
    ).astype(jnp.bfloat16)
    return (grad_query, grad_key, grad_value)


def split_heads(triple):
    batch, length, three = triple.shape
    local = three // 3
    return [
        triple[:, :, i * local : (i + 1) * local].reshape(
            batch, length, local // HEAD_DIM, HEAD_DIM
        )
        for i in range(3)
    ]


def low_dot(spec, left, right):
    return jnp.einsum(spec, left, right, preferred_element_type=jnp.float32)


def attend(normed, key_valid, block, route):
    triple = low_dot("bld,dc->blc", normed, route.weight(IN, block)).astype(jnp.bfloat16)
    context, log_total = attend_forward(*split_heads(triple), key_valid)
    flat_context = context.reshape(triple.shape[0], triple.shape[1], triple.shape[2] // 3)
    terms = low_dot("ble,de->bld", flat_context, route.weight(OUT, block)).astype(jnp.bfloat16)
    return terms, (triple, flat_context, log_total)


def feed(normed, block, route):
    inner = low_dot("bld,df->blf", normed, route.weight(EXPAND, block))
    active = jax.nn.gelu(inner, approximate=True).astype(jnp.bfloat16)
    terms = low_dot("blf,df->bld", active, route.weight(CONTRACT, block)).astype(jnp.bfloat16)
    return terms, (inner, active)


def feed_back(grad_branch, normed, saved, block, route):
    inner, active = saved
    grad_active = low_dot("bld,df->blf", grad_branch, route.weight(CONTRACT, block))
    gelu_back = jax.vjp(partial(jax.nn.gelu, approximate=True), inner)[1]
    grad_inner = gelu_back(grad_active)[0].astype(jnp.bfloat16)
    terms = low_dot("blf,df->bld", grad_inner, route.weight(EXPAND, block)).astype(jnp.bfloat16)
    route.give_grad(CONTRACT, block, low_dot("bld,blf->df", grad_branch, active))
    route.give_grad(EXPAND, block, low_dot("bld,blf->df", normed, grad_inner))
    return terms


def attend_back(grad_attn, normed, saved, key_valid, block, route):
    triple, flat_context, log_total = saved
    grad_flat = low_dot("bld,de->ble", grad_attn, route.weight(OUT, block)).astype(jnp.bfloat16)
    query, key, value = split_heads(triple)
    grad_context = grad_flat.reshape(query.shape)
    grad_parts = attend_backward(query, key, value, log_total, grad_context, key_valid)
    grad_triple = jnp.concatenate([g.reshape(flat_context.shape) for g in grad_parts], 2)
    terms = low_dot("blc,dc->bld", grad_triple, route.weight(IN, block)).astype(jnp.bfloat16)
    return terms, (normed, grad_triple, grad_attn, flat_context)


def errands_in_turn():
    def attend(block, *what):
        return [((IN, block), what), ((OUT, block), what)]

    def expand(block, *what):
        return [((EXPAND, block), what)]

    def contract(block, *what):
        return [((CONTRACT, block), what)]

    def feed(block, *what):
        return expand(block, *what) + contract(block, *what)

    return [
        attend(0, ENTER),
        attend(0, STRAIGHT) + expand(0, ENTER),
        attend(0, CROSS, RELAY) + contract(0, ENTER),
        expand(0, STRAIGHT, CROSS, RELAY) + attend(1, ENTER),
        contract(0, STRAIGHT, CROSS, RELAY) + expand(1, ENTER),
        attend(1, STRAIGHT, CROSS, RELAY) + expand(1, STRAIGHT) + contract(1, ENTER),
        contract(1, STRAIGHT, CROSS, RELAY) + expand(1, CROSS, RELAY),
        [],
        feed(1, FAR) + feed(1, NEAR),
        feed(1, PASS),
        feed(0, FAR) + attend(1, FAR) + attend(1, NEAR) + expand(1, LEAVE),
        feed(0, NEAR) + feed(0, PASS) + attend(1, PASS) + contract(1, LEAVE),
        attend(0, FAR) + feed(0, LEAVE),
        attend(0, NEAR) + attend(0, PASS) + attend(1, LEAVE),
        attend(0, LEAVE),
        [],
    ]


def adam(weight, grad, moment, second, average, factor):
    grad = grad * factor
    moment = beta_first * moment + (1.0 - beta_first) * grad
    second = beta_second * second + (1.0 - beta_second) * grad * grad
    update = (
        moment
        / (1.0 - beta_first**STEP)
        / (jnp.sqrt(second / (1.0 - beta_second**STEP)) + adam_eps)
    )
    fresh = weight - learn_rate * (update + weight_decay * weight)
    average_decay = min(ema_decay, (1.0 + STEP) / (10.0 + STEP))
    average = average_decay * average + (1.0 - average_decay) * fresh
    return (fresh, moment, second, average)


def shards(
    patches,
    target_noise,
    kept_slots,
    kept_count,
    time_step,
    labels,
    teacher,
    *tables,
):
    params, moments, seconds, averages = tables[:7], tables[7:14], tables[14:21], tables[21:]
    attend_in, attend_out, expand, contract, modulation, patch_table, condition = params
    batch, length = (patches.shape[0], patches.shape[1])
    capacity = kept_slots.shape[1]
    rows, local = (attend_in.shape[1], attend_in.shape[3])
    wides, narrows = (group_size(WIDE), group_size(NARROW))
    wide_index, narrow_index = (flat_place(WIDE), flat_place(NARROW))
    images = batch * wides
    width = local * narrows
    assert batch == narrows

    shards_low = {}
    for i in range(2):
        shards_low[IN, i] = attend_in[i].reshape(rows, 3 * local).astype(jnp.bfloat16)
        shards_low[OUT, i] = attend_out[i].T.astype(jnp.bfloat16)
        shards_low[EXPAND, i] = expand[i].astype(jnp.bfloat16)
        shards_low[CONTRACT, i] = contract[i].T.astype(jnp.bfloat16)
    route = Route(shards_low, errands_in_turn())

    def own(array):
        return lax.dynamic_index_in_dim(array, narrow_index, 0, keepdims=False)

    condition_low = condition.astype(jnp.bfloat16)
    features = sinusoid(time_step, FREQ)
    onehot = (labels[:, None] == jnp.arange(CLASSES)[None, :]).astype(jnp.bfloat16)
    cond_part = jnp.dot(
        features, condition_low[:FREQ].astype(jnp.float32), precision=highest_float_accuracy
    ) + low_dot("bc,cd->bd", onehot, condition_low[FREQ:])
    pieces = jax.nn.silu(cond_part).reshape(batch, local // rows, rows)
    pieces = jnp.pad(jnp.transpose(pieces, (1, 0, 2)), ((0, 0), (0, 8 - batch), (0, 0)))
    (silu_wide,) = route.step(RowPieces(pieces))
    silu_rows = silu_wide[:, :batch].reshape(images, rows).astype(jnp.bfloat16)
    modulation_low = modulation.astype(jnp.bfloat16)
    mod_part = low_dot("ip,npkc->inkc", silu_rows, modulation_low)
    mod_part = mod_part.reshape(wides, batch, 12 * local)
    (mod_wide,) = route.step(Exchange([mod_part], [(WIDE, EACH)]))
    facts = jnp.stack([kept_count, time_step, labels], 1).astype(jnp.float32)
    facts = jnp.pad(facts, ((0, 4), (0, local - 3)))
    teacher_rows = teacher.reshape(batch * narrows, local)
    payload = jnp.concatenate([cond_part, facts[:batch], teacher_rows], 0)
    table_pad = jnp.pad(patch_table.astype(jnp.bfloat16), ((0, 15), (0, 0)))
    mod_near, everyone, tables_near = route.step(
        Exchange(
            [jnp.sum(mod_wide, 0).reshape(batch, 12, local), payload, table_pad],
            [(NARROW, EACH), (WIDE, SAME), (NARROW, SAME)],
        )
    )
    mods = jnp.transpose(mod_near, (1, 0, 2)).reshape(12, width)
    mod_enc, mod_dec = mods[:6], mods[6:]
    cond_cols = everyone[:, :batch].reshape(images, local)
    facts_all = everyone[:, batch : 2 * batch, :3]
    negatives = everyone[:, 2 * batch :].reshape(images, width)
    time_all = facts_all[:, :, 1].reshape(images).astype(jnp.int32)
    labels_all = facts_all[:, :, 2].reshape(images).astype(jnp.int32)
    patch_full = jnp.transpose(tables_near, (1, 0, 2)).reshape(48, width)

    count_own = own(kept_count).astype(jnp.float32)
    slot_valid = (jnp.arange(capacity) < own(kept_count)).astype(jnp.float32)[:, None]
    select = (own(kept_slots)[:, None] == jnp.arange(length)[None, :]).astype(
        jnp.float32
    ) * slot_valid
    open_place = 1.0 - jnp.sum(select, 0)[:, None]
    places = sinusoid(jnp.arange(length), width)
    group_counts = lax.dynamic_slice(
        facts_all[:, :, 0],
        (flat_place((PY, PX)) * 2, lax.axis_index(ZH) * 2),
        (2, 2),
    ).reshape(4)
    group_valid = (jnp.arange(capacity)[None, :] < group_counts[:, None]).astype(jnp.float32)
    kept_patches = low_dot("cl,lp->cp", select.astype(jnp.bfloat16), own(patches))
    embed = low_dot("cp,pd->cd", kept_patches.astype(jnp.bfloat16), patch_full[:PATCH_IN])
    embed = embed + jnp.dot(select, places, precision=highest_float_accuracy)
    mask_token = patch_full[2 * PATCH_IN : 2 * PATCH_IN + 1].astype(jnp.float32)
    base = open_place * mask_token + places
    head = patch_full[PATCH_IN : 2 * PATCH_IN]
    count_all = images * length * PATCH_IN

    (normed_a0,) = route.step(Enter(embed, mod_enc))
    terms, saved_a0 = attend(normed_a0, group_valid, 0, route)
    normed_m0, attn0, middle0 = route.step(Middle(terms, embed, mod_enc))
    terms, saved_m0 = feed(normed_m0, 0, route)
    normed_a1, branch0, encoded, decode_in = route.step(
        Decode(terms, middle0, mod_enc, mod_dec, select.T, base)
    )
    terms, saved_a1 = attend(normed_a1, None, 1, route)
    normed_m1, attn1, middle1 = route.step(Middle(terms, decode_in, mod_dec))
    terms, saved_m1 = feed(normed_m1, 1, route)
    grad_branch, grad_decoded, gate_m1, grad_head, square = route.step(
        Turn(terms, middle1, mod_dec, head, own(target_noise), count_all)
    )

    def pool_unit(values):
        pooled = jnp.sum(values * slot_valid, 0, keepdims=True) / count_own
        return pooled * lax.rsqrt(jnp.sum(pooled * pooled, -1, keepdims=True) + 1e-06)

    normalised_direction, pool_back = jax.vjp(pool_unit, encoded)
    frozen_target_direction = negatives * lax.rsqrt(
        jnp.sum(negatives * negatives, -1, keepdims=True) + 1e-06
    )
    cosine_match_scores = (
        jnp.sum(normalised_direction * frozen_target_direction, -1, keepdims=True)
        / contrast_sharpness_divisor
    )
    peak = jnp.max(cosine_match_scores)
    expo = jnp.exp(cosine_match_scores - peak)
    total = jnp.sum(expo)
    positive = ((wide_index * batch + narrow_index) == jnp.arange(images)).astype(jnp.float32)
    positive = positive[:, None]
    nce_local = peak + jnp.log(total) - jnp.sum(cosine_match_scores * positive)
    derivative_of_raw_scores = (expo / total - positive) * (nce_weight / images)
    unit_vector_gradient = (
        jnp.sum(derivative_of_raw_scores * frozen_target_direction, 0, keepdims=True)
        / contrast_sharpness_divisor
    )
    grad_pool = pool_back(unit_vector_gradient)[0]

    terms = feed_back(grad_branch, normed_m1, saved_m1, 1, route)
    grad_attn, grad_mid, sums_m1 = route.step(
        MiddleBack(terms, middle1, attn1, grad_decoded, mod_dec)
    )
    terms, pairs = attend_back(grad_attn, normed_a1, saved_a1, None, 1, route)
    back_to = (open_place, select, grad_pool, branch0, mod_enc)
    grad_branch, grad_encoded, sums_a1, grad_in, grad_out = route.step(
        Encode(terms, decode_in, grad_mid, mod_dec, *back_to, pairs)
    )
    route.give_grad(IN, 1, grad_in)
    route.give_grad(OUT, 1, grad_out)
    terms = feed_back(grad_branch, normed_m0, saved_m0, 0, route)
    grad_attn, grad_mid, sums_m0 = route.step(
        MiddleBack(terms, middle0, attn0, grad_encoded, mod_enc)
    )
    terms, pairs = attend_back(grad_attn, normed_a0, saved_a0, group_valid, 0, route)
    sums = (sums_m0, sums_a1, sums_m1, gate_m1, grad_head)
    rows_near, grad_in, grad_out = route.step(
        Leave(terms, embed, grad_mid, mod_enc, kept_patches, sums, pairs)
    )
    route.give_grad(IN, 0, grad_in)
    route.give_grad(OUT, 0, grad_out)

    mods_near = rows_near[:, :12].reshape(narrows, 12 * local)
    table_near = rows_near[:, 12:45]
    table_sum = jnp.pad(jnp.sum(table_near, 0), ((0, 15), (0, 0))).astype(jnp.bfloat16)
    mods_all, table_all = route.step(
        Exchange([mods_near, table_sum], [(WIDE, SAME), (WIDE, SAME)])
    )
    grad_patch_table = jnp.sum(table_all.astype(jnp.float32), 0)[:33]
    mods_all = mods_all.reshape(images, 2, 6, local)
    silu_broad = silu_rows.astype(jnp.float32)
    grad_modulation = jnp.einsum(
        "ip,inkc->npkc", silu_broad, mods_all, precision=highest_float_accuracy
    )
    grad_silu = jnp.einsum(
        "inkc,npkc->ip",
        mods_all,
        modulation_low.astype(jnp.float32),
        precision=highest_float_accuracy,
    )
    (silu_near,) = route.step(Exchange([grad_silu], [(NARROW, SAME)]))
    (silu_wide,) = route.step(Exchange([jnp.sum(silu_near, 0)], [(WIDE, SAME)]))
    grad_silu = jnp.transpose(silu_wide, (1, 0, 2)).reshape(images, width)
    grad_silu = lax.dynamic_slice_in_dim(grad_silu, narrow_index * local, local, 1)
    grad_cond = jax.vjp(jax.nn.silu, cond_cols)[1](grad_silu)[0]
    features_all = sinusoid(time_all, FREQ)
    onehot_all = (labels_all[:, None] == jnp.arange(CLASSES)[None, :]).astype(jnp.float32)
    grad_condition = jnp.dot(
        jnp.concatenate([features_all, onehot_all], 1).T, grad_cond, precision=highest_float_accuracy
    )


    def totals(kind, shape):
        both = [route.met(kind, i).astype(jnp.float32) for i in range(2)]
        return jnp.stack([shape(each[0] + each[1]) for each in both])

    def by_third(g):
        thirds = [g[:, i * local : (i + 1) * local] for i in range(3)]
        return jnp.transpose(jnp.stack(thirds), (1, 0, 2))

    grads = [
        totals(IN, by_third),
        totals(OUT, lambda g: g.T),
        totals(EXPAND, lambda g: g),
        totals(CONTRACT, lambda g: g.T),
        grad_modulation,
        grad_patch_table,
        grad_condition,
    ]
    square_small = jnp.sum(grad_patch_table * grad_patch_table) + jnp.sum(
        grad_condition * grad_condition
    )
    square_local = jnp.sum(grad_modulation * grad_modulation)
    square_local = square_local + (wide_index == 0).astype(jnp.float32) * square_small
    scalars = jnp.stack([square[0, 0], nce_local, square_local])
    scalars = jnp.pad(scalars[None, :], ((0, 7), (0, 125)))
    mets = [route.met(kind, i) for i in range(2) for kind in (IN, OUT, EXPAND, CONTRACT)]
    (scalars_all,) = route.step(Norm(scalars, mets))
    sums = jnp.sum(scalars_all[:, 0], 0)
    grad_norm = jnp.sqrt(sums[2])
    factor = clip_norm / jnp.maximum(grad_norm, clip_norm)
    fresh = [
        adam(params[i], grads[i], moments[i], seconds[i], averages[i], factor) for i in range(7)
    ]
    loss_parts = jnp.stack([sums[0] / count_all, sums[1] / images])
    return (loss_parts, grad_norm) + tuple(fresh[i][k] for k in range(4) for i in range(7))


def solution(mesh):
    wide, narrow = mesh.devices.shape
    planes = wide // 2
    across = max(n for n in range(1, math.isqrt(planes) + 1) if planes % n == 0)
    grid = Mesh(mesh.devices.reshape(across, planes // across, 2, narrow // 2, 2), ALL)
    image_specs = (
        P(WIDE, None, None),
        P(WIDE, None, None),
        P(WIDE, None),
        P(WIDE),
        P(WIDE),
        P(WIDE),
        P(WIDE, None),
    )
    table_specs = (
        P(None, WIDE, None, NARROW),
        P(None, NARROW, WIDE),
        P(None, WIDE, NARROW),
        P(None, NARROW, WIDE),
        P(None, WIDE, None, NARROW),
        P(None, NARROW),
        P(None, NARROW),
    )
    return jax.shard_map(
        shards,
        mesh=grid,
        in_specs=image_specs + table_specs * 4,
        out_specs=(P(), P()) + table_specs * 4,
        check_vma=False,
    )
```

time: 836 us -> 723 us (0.86)
  local copies, waits for them, and re-layouts: 113 us -> 71.9 us
  Pallas kernels: 491 us -> 458 us
  other arithmetic: 97 us -> 70.7 us
    pallas_call x24 -> x16, Pallas kernels: 491 us -> 458 us  [travel(): pl.pallas_call(partial(kernel, parts), out_shape=[shape for part in parts...]
    reduce_sum x34 -> x6, other arithmetic: 18.9 us -> 0.62 us  [the longest x2 0.29 us: shards(): jnp.sum(normalised_direction * frozen_target_direction, -1, keepdims=True)]
    add x12 -> x0, local copies, waits for them, and re-layouts: 14.8 us -> none  [the longest x8 9.01 us: modulate(): return layer_norm(values) * (1.0 + scale[None, :]) + shift[None, :]]
    convert_element_type x9 -> x6, local copies, waits for them, and re-layouts: 11 us -> 1.11 us  [the longest x1 0.63 us: shards(): silu_rows = silu_wide[:, :batch].reshape(images, rows).astype(jnp.bfloat16)]
    unnamed x483 -> x364, local copies, waits for them, and re-layouts: 44.7 us -> 36.2 us
    dot_general x31 -> x24, matrix products: 73.6 us -> 66.3 us  [low_dot(): return jnp.einsum(spec, left, right, preferred_element_type=jnp.float32)]
where the time goes in v3:
time: 723 us; the launch traced here: 715 us
  Pallas kernels  458 us (63%)
  matrix products  101 us (14%)
  local copies, waits for them, and re-layouts  71.9 us (10%)
  other arithmetic  70.7 us (10%)
  between operations  13.2 us (2%)
    pallas_call x16, Pallas kernels, travel(): pl.pallas_call(partial(kernel, parts), out_shape=[shape for part in parts...  458 us
    dot_general x24, matrix products, low_dot(): return jnp.einsum(spec, left, right, preferred_element_type=jnp.float32)  66.3 us
    unnamed x364, local copies, waits for them, and re-layouts  36.2 us
    add x7, other arithmetic, adam(): average = average_decay * average + (1.0 - average_decay) * fresh  21.3 us

profile of v3, /device:TPU:0, one launch (start us, length us, event | category | flops | bytes accessed | tf_op | source)
XLA Modules:
  0.0 714.8 jit_solution(16276488217801484812)
XLA Ops:
  5.3 15.0 %shard_map.562 = (f32[8,8,144]{2,1,0:T(8,128)S(1)}, bf16[2,2,2,144,864]{4,3,2,1,0:T(8,128)(2,1)}, bf16[2,2,2,144,288]{4,3,2,1,0:T(8,128)(2,1)}) custom-call(f32[2,8,144]{2,1,0:T(8,128)S(1)} %pad.21.refs_0_, bf16[144,864]{1,0:T(8,128)(2,1)S(1)} %convert_element_type.1142.refs_1_, bf16[144,288]{1,0:T(8,128)(2,1)S(1)} %get-tuple-element.343.refs_2_), custom_call_target="tpu_custom_call" | custom-call | flops 20000000000 | bytes 1024 | tf_op jit(solution)/shard_map/pallas_call | solution.py:999
  20.9 2.3 multiply_cosine_fusion
  25.4 1.9 fusion.48
  27.3 1.9 convert_bitcast_fusion
  29.2 1.6 copy.132
  30.8 3.1 reshape.1313
  34.4 27.4 %shard_map.563 = (f32[8,4,3456]{2,1,0:T(4,128)S(1)}, bf16[2,2,2,144,864]{4,3,2,1,0:T(8,128)(2,1)}, bf16[2,2,2,144,288]{4,3,2,1,0:T(8,128)(2,1)}, bf16[2,2,2,144,1152]{4,3,2,1,0:T(8,128)(2,1)}) custom-call(f32[8,4,3456]{2,1,0:T(4,128)S(1)} %fusion.181.refs_0_, ...), custom_call_target="tpu_custom_call", output_to_operand_aliasing={{1}: (1, {}), {2}: (2, {})} | custom-call | flops 20000000000 | bytes 1024 | tf_op jit(solution)/shard_map/pallas_call | solution.py:999
  62.6 25.8 %shard_map.564 = (f32[4,12,288]{2,1,0:T(8,128)S(1)}, f32[8,24,288]{2,1,0:T(8,128)S(1)}, bf16[4,48,288]{2,1,0:T(8,128)(2,1)S(1)}, bf16[2,2,2,144,864]{4,3,2,1,0:T...) custom-call(f32[4,12,288]{2,1,0:T(8,128)S(1)} %reshape.1224.refs_0_,, ...), custom_call_target="tpu_custom_call", output_to_operand_aliasing={{3}: (3, {}), {4}: (4, {})} | custom-call | flops 20000000000 | bytes 1024 | tf_op jit(solution)/shard_map/pallas_call | solution.py:999
  91.6 31.4 %shard_map.565 = (bf16[4,160,1152]{2,1,0:T(8,128)(2,1)S(1)}, bf16[2,2,2,144,1152]{4,3,2,1,0:T(8,128)(2,1)}, bf16[2,2,2,144,864]{4,3,2,1,0:T(8,128)(2,1)}, bf16[2,2,2,144,288]{4,3,2,1,0:T(8,128)(2,1)}) custom-call(f32[160,1152]{1,0:T(8,128)S(1)} %convolution_add_fusion.refs_0_.refs_1_, ...), custom_call_target="tpu_custom_call", output_to_operand_aliasing={{1}: (2, {})} | custom-call | flops 20000000000 | bytes 1024 | tf_op jit(solution)/shard_map/pallas_call | solution.py:999
  123.0 1.8 convolution_convert_fusion.9
  130.5 1.9 fusion.180
  135.8 28.9 %shard_map.566 = (bf16[4,160,1152]{2,1,0:T(8,128)(2,1)S(1)}, f32[160,1152]{1,0:T(8,128)S(1)}, f32[160,1152]{1,0:T(8,128)S(1)}, bf16[2,2,2,144,1152]{4,3,2,1,0:T(8,128)(2,1)}, bf16[2,2,2,144,1152]{4,3,2,1,0:T(8,128)(2,1)}) custom-call(bf16[4,160,1152]{2,1,0:T(8,128)(2,1)S(1)} %convolution_convert_fusion.6.refs_0_, ...), custom_call_target="tpu_custom_call", output_to_operand_aliasing={{3}: (3, {})} | custom-call | flops 20000000000 | bytes 1024 | tf_op jit(solution)/shard_map/pallas_call | solution.py:999
  164.7 2.2 fusion.183
  167.5 4.0 convolution_convert_fusion.5.refs_0_
  173.4 35.1 %shard_map.567 = (bf16[4,256,1152]{2,1,0:T(8,128)(2,1)S(1)}, f32[160,1152]{1,0:T(8,128)S(1)}, f32[160,1152]{1,0:T(8,128)S(1)}, f32[256,1152]{1,0:T(8,128)S(1)}, ...) custom-call(bf16[4,160,1152]{2,1,0:T(8,128)(2,1)S(1)} %copy-done.45,, ...), custom_call_target="tpu_custom_call", output_to_operand_aliasing={{4}: (6, {}), {5}: (7, {}), {6}: (8, {})} | custom-call | flops 20000000000 | bytes 1024 | tf_op jit(solution)/shard_map/pallas_call | solution.py:999
  208.6 5.6 convolution_convert_fusion.8
  219.5 42.2 %shard_map.568 = (bf16[4,256,1152]{2,1,0:T(8,128)(2,1)S(1)}, f32[256,1152]{1,0:T(8,128)S(1)}, f32[256,1152]{1,0:T(8,128)S(1)}, bf16[2,2,2,144,1152]{4,3,2,1,0:T(8,128)(2,1)}, bf16[2,2,2,144,1152]{4,3,2,1,0:T(8,128)(2,1)}) custom-call(bf16[4,256,1152]{2,1,0:T(8,128)(2,1)S(1)} %convolution_convert_fusion.1.refs_0_, ...), custom_call_target="tpu_custom_call", output_to_operand_aliasing={{3}: (3, {}), {4}: (4, {})} | custom-call | flops 20000000000 | bytes 1024 | tf_op jit(solution)/shard_map/pallas_call | solution.py:999
  261.7 7.0 fusion.184
  268.7 5.4 convolution_convert_fusion.3.refs_0_
  274.4 1.7 copy-done.46
  277.4 30.8 %shard_map.569 = (bf16[4,256,1152]{2,1,0:T(8,128)(2,1)S(1)}, f32[256,1152]{1,0:T(8,128)S(1)}, f32[1,1152]{1,0:T(1,128)S(1)}, f32[16,1152]{1,0:T(8,128)S(1)}, f32[1,1]{1,0:T(1,128)}) custom-call(bf16[4,256,1152]{2,1,0:T(8,128)(2,1)S(1)} %copy-done.46, f32[256,1152]{1,0:T(8,128)S(1)} %copy-done.50, f32[6,1152]{1,0:T(8,128)S(1)} %slice.223.refs_3_.refs_2_.refs_4_, ...), custom_call_target="tpu_custom_call" | custom-call | flops 20000000000 | bytes 1024 | tf_op jit(solution)/shard_map/pallas_call | solution.py:999
  308.2 5.1 fusion.10
  313.3 3.9 convolution_convert_fusion.2.refs_0_
  317.2 3.3 fusion
  320.5 3.4 fusion.1
  324.0 32.2 %shard_map.570 = (bf16[4,256,1152]{2,1,0:T(8,128)(2,1)S(1)}, f32[256,1152]{1,0:T(8,128)S(1)}, f32[3,1152]{1,0:T(4,128)S(1)}, bf16[1,1,144,1152]{3,2,1,0:T(8,128)...) custom-call(bf16[4,256,1152]{2,1,0:T(8,128)(2,1)S(1)} %convolution_c, ...), custom_call_target="tpu_custom_call" | custom-call | flops 20000000000 | bytes 1024 | tf_op jit(solution)/shard_map/pallas_call | solution.py:999
  357.2 2.4 copy-done.62
  361.7 3.5 multiply_reduce_fusion
  368.2 2.2 copy.163
  370.4 2.4 fusion.36
  372.8 2.2 copy.162
  375.0 2.6 pad_maximum_fusion.refs_10_
  377.7 4.1 convolution_convert_fusion.refs_0_
  395.4 1.7 copy-done.40
  397.0 1.7 copy-done.42
  401.2 29.7 %shard_map.571 = (bf16[4,160,1152]{2,1,0:T(8,128)(2,1)S(1)}, f32[160,1152]{1,0:T(8,128)S(1)}, f32[4,1152]{1,0:T(4,128)S(1)}, bf16[1152,864]{1,0:T(8,128)(2,1)S(1...) custom-call(bf16[4,256,1152]{2,1,0:T(8,128)(2,1)S(1)} %copy-done.40,, ...), custom_call_target="tpu_custom_call" | custom-call | flops 20000000000 | bytes 1024 | tf_op jit(solution)/shard_map/pallas_call | solution.py:999
  431.0 3.1 fusion.18
  434.1 2.3 convolution_convert_fusion.4.refs_0_
  436.4 2.4 fusion.2
  439.0 2.5 fusion.3
  441.6 3.6 fusion.62
  445.3 34.6 %shard_map.572 = (bf16[4,160,1152]{2,1,0:T(8,128)(2,1)S(1)}, f32[160,1152]{1,0:T(8,128)S(1)}, f32[3,1152]{1,0:T(4,128)S(1)}, bf16[1,1,144,1152]{3,2,1,0:T(8,128)...) custom-call(bf16[4,160,1152]{2,1,0:T(8,128)(2,1)S(1)} %convolution_c, ...), custom_call_target="tpu_custom_call" | custom-call | flops 20000000000 | bytes 1024 | tf_op jit(solution)/shard_map/pallas_call | solution.py:999
  482.4 2.4 convolution_convert_fusion.10
  485.8 2.6 multiply_reduce_fusion.3
  490.9 2.1 copy.175
  495.6 1.8 pad_maximum_fusion.2.refs_11_
  497.4 3.0 convolution_convert_fusion.7.refs_0_
  502.0 1.6 fusion.65
  503.6 1.6 fusion.63
  511.7 40.5 %shard_map.573 = (f32[4,48,288]{2,1,0:T(8,128)S(1)}, bf16[1152,864]{1,0:T(8,128)(2,1)S(1)}, bf16[1152,288]{1,0:T(8,128)(2,1)S(1)}, bf16[1,144,1152]{2,1,0:T(8,12...) custom-call(bf16[4,160,1152]{2,1,0:T(8,128)(2,1)S(1)} %copy-done.35,, ...), custom_call_target="tpu_custom_call" | custom-call | flops 20000000000 | bytes 1024 | tf_op jit(solution)/shard_map/pallas_call | solution.py:999
  554.7 1.8 fusion.58
  558.5 29.7 %shard_map.574 = (f32[8,4,3456]{2,1,0:T(4,128)S(1)}, bf16[8,48,288]{2,1,0:T(8,128)(2,1)S(1)}, bf16[1,1,144,864]{3,2,1,0:T(8,128)(2,1)}, bf16[1,1,144,864]{3,2,1,...) custom-call(f32[4,3456]{1,0:T(4,128)S(1)} %reshape.1258.refs_0_, ...), custom_call_target="tpu_custom_call" | custom-call | flops 20000000000 | bytes 1024 | tf_op jit(solution)/shard_map/pallas_call | solution.py:999
  589.7 4.5 multiply_reduce_fusion.2
  595.5 3.4 fusion.45.refs_0_
  602.9 24.2 %shard_map.575 = (f32[4,32,144]{2,1,0:T(8,128)S(1)}, bf16[1,144,864]{2,1,0:T(8,128)(2,1)}, bf16[1,144,864]{2,1,0:T(8,128)(2,1)}, bf16[1,144,288]{2,1,0:T(8,128)(...) custom-call(f32[32,144]{1,0:T(8,128)S(1)} %fusion.45.refs_0_, ...), custom_call_target="tpu_custom_call" | custom-call | flops 20000000000 | bytes 1024 | tf_op jit(solution)/shard_map/pallas_call | solution.py:999
  629.1 20.1 %shard_map.576 = (f32[8,32,144]{2,1,0:T(8,128)S(1)}, bf16[2,144,864]{2,1,0:T(8,128)(2,1)}, bf16[2,144,288]{2,1,0:T(8,128)(2,1)}) custom-call(f32[32,144]{1,0:T(8,128)S(1)} %reduce_sum.246.refs_0_, bf16[2,144,864]{2,1,0:T(8,128)(2,1)S(1)} %pad_maximum_fusion.9.refs_1_, bf16[2,144,288]{2,1,0:T(8,128)(2,1)S(1)} %pad_maximum_fusion.11.refs_2_), custom_call_target="tpu_custom_call" | custom-call | flops 20000000000 | bytes 1024 | tf_op jit(solution)/shard_map/pallas_call | solution.py:999
  650.1 1.7 reshape.1262
  652.5 4.0 multiply_reduce_fusion.4
  664.1 11.0 %shard_map.577 = f32[32,8,128]{2,1,0:T(8,128)S(1)} custom-call(f32[8,128]{1,0:T(8,128)S(1)} %pad.25.refs_0_, bf16[2,144,864]{2,1,0:T(8,128)(2,1)S(1)} %copy-done.21, bf16[2,144,288]{2,1,0:T(8,128)(2,1)S(1)} %copy-done.29, bf16[2,144,1152]{2,1,0:T(8,128)(2,1)S(1)} %copy-done.14, bf16[2,144,1152]{2,1,0:T(8,128)(2,1)S(1)} %copy-done.13, ...), custom_call_target="tpu_custom_call" | custom-call | flops 20000000000 | bytes 1024 | tf_op jit(solution)/shard_map/pallas_call | solution.py:999
  682.1 3.2 multiply_add_fusion.5
  690.8 3.2 multiply_add_fusion.4
  696.6 3.3 multiply_add_fusion.3
  702.8 5.8 multiply_add_fusion
  709.8 3.5 multiply_add_fusion.1
  (542 shorter events, 100.6 us)
Async XLA Ops:
  0.7 273.6 %copy-start = (f32[4,256,16]{1,2,0:T(8,128)S(1)}, f32[4,256,16]{1,2,0:T(8,128)}, u32[]{:S(2)}) copy-start(f32[4,256,16]{1,2,0:T(8,128)} %param.36) | copy-start | bytes 196612
  5.3 18.1 %copy-start.165 = (s32[4]{0:T(128)S(1)}, s32[4]{0:T(128)}, u32[]{:S(2)}) copy-start(s32[4]{0:T(128)} %param.38) | copy-start | bytes 52
  23.3 5.9 copy-start.70
  23.3 5.9 copy-start.72
  24.7 147.1 %copy-start.155 = (f32[160]{0:T(256)}, f32[160]{0:T(256)S(1)}, u32[]{:S(2)}) copy-start(f32[160]{0:T(256)S(1)} %compare_convert_fusion) | copy-start | bytes 1924
  34.3 27.6 %copy-start.157 = (f32[4,1152]{1,0:T(4,128)S(1)}, f32[4,1152]{1,0:T(4,128)}, u32[]{:S(2)}) copy-start(f32[4,1152]{1,0:T(4,128)} %param.41) | copy-start | bytes 55300
  34.3 27.7 %copy-start.163 = (s32[4]{0:T(128)S(1)}, s32[4]{0:T(128)}, u32[]{:S(2)}) copy-start(s32[4]{0:T(128)} %param.40) | copy-start | bytes 52
  34.3 28.1 %copy-start.131 = (f32[33,288]{1,0:T(8,128)S(1)}, f32[33,288]{1,0:T(8,128)}, u32[]{:S(2)}) copy-start(f32[33,288]{1,0:T(8,128)} %param.47) | copy-start | bytes 114052
  34.4 28.1 %copy-start.77 = (f32[2,1152,144]{1,2,0:T(8,128)S(1)}, f32[2,1152,144]{1,2,0:T(8,128)}, u32[]{:S(2)}) copy-start(f32[2,1152,144]{1,2,0:T(8,128)} %param.45) | copy-start | bytes 3981316
  62.6 26.9 %copy-start.85 = (f32[160,1152]{1,0:T(8,128)S(1)}, f32[160,1152]{1,0:T(8,128)}, u32[]{:S(2)}) copy-start(f32[160,1152]{1,0:T(8,128)} %fusion.48) | copy-start | bytes 2211844
  88.4 41.1 %copy-start.2 = (f32[8,24,288]{2,1,0:T(8,128)}, f32[8,24,288]{2,1,0:T(8,128)S(1)}, u32[]{:S(2)}) copy-start(f32[8,24,288]{2,1,0:T(8,128)S(1)} %get-tuple-element.155) | copy-start | bytes 663556
  89.8 45.9 %copy-start.4 = (f32[160,1152]{1,0:T(8,128)}, f32[160,1152]{1,0:T(8,128)S(1)}, u32[]{:S(2)}) copy-start(f32[160,1152]{1,0:T(8,128)S(1)} %convolution_add_fusion.refs_0_.refs_1_) | copy-start | bytes 2211844
  91.6 31.4 %copy-start.174 = (bf16[2,2,2,144,864]{4,3,2,1,0:T(8,128)(2,1)S(1)}, bf16[2,2,2,144,864]{4,3,2,1,0:T(8,128)(2,1)}, u32[]{:S(2)}) copy-start(bf16[2,2,2,144,864]{4,3,2,1,0:T(8,128)(2,1)} %get-tuple-element.154) | copy-start | bytes 5971972
  135.8 28.9 %copy-start.168 = (bf16[2,2,2,144,1152]{4,3,2,1,0:T(8,128)(2,1)S(1)}, bf16[2,2,2,144,1152]{4,3,2,1,0:T(8,128)(2,1)}, u32[]{:S(2)}) copy-start(bf16[2,2,2,144,1152]{4,3,2,1,0:T(8,128)(2,1)} %get-tuple-element.159) | copy-start | bytes 7962628
  171.9 36.6 %copy-start.159 = (f32[256]{0:T(256)}, f32[256]{0:T(256)S(1)}, u32[]{:S(2)}) copy-start(f32[256]{0:T(256)S(1)} %broadcast_subtract_fusion) | copy-start | bytes 3076
  208.5 5.7 copy-start.41
  208.6 5.6 copy-start.59
  208.6 10.9 %copy-start.52 = (f32[256,1152]{1,0:T(8,128)}, f32[256,1152]{1,0:T(8,128)S(1)}, u32[]{:S(2)}) copy-start(f32[256,1152]{1,0:T(8,128)S(1)} %get-tuple-element.168.refs_1_) | copy-start | bytes 3538948
  261.7 7.0 copy-start.43
  261.7 7.0 copy-start.49
  261.7 7.0 copy-start.171
  268.7 5.5 copy-start.180
  277.4 30.8 %copy-start.172 = (bf16[2,2,2,144,1152]{4,3,2,1,0:T(8,128)(2,1)S(1)}, bf16[2,2,2,144,1152]{4,3,2,1,0:T(8,128)(2,1)}, u32[]{:S(2)}) copy-start(bf16[2,2,2,144,1152]{4,3,2,1,0:T(8,128)(2,1)} %get-tuple-element.173) | copy-start | bytes 7962628
  277.4 30.8 %copy-start.181 = (f32[4,256,1152]{2,1,0:T(8,128)S(1)}, f32[4,256,1152]{2,1,0:T(8,128)}, u32[]{:S(2)}) copy-start(f32[4,256,1152]{2,1,0:T(8,128)} %copy-done.180) | copy-start | bytes 14155780
  308.1 5.1 copy-start.170
  323.9 32.2 %copy-start.16 = (bf16[1152,1152]{1,0:T(8,128)(2,1)}, bf16[1152,1152]{1,0:T(8,128)(2,1)S(1)}, u32[]{:S(2)}) copy-start(bf16[1152,1152]{1,0:T(8,128)(2,1)S(1)} %fusion.1) | copy-start | bytes 7962628
  324.0 32.2 %copy-start.177 = (bf16[2,2,2,144,288]{4,3,2,1,0:T(8,128)(2,1)S(1)}, bf16[2,2,2,144,288]{4,3,2,1,0:T(8,128)(2,1)}, u32[]{:S(2)}) copy-start(bf16[2,2,2,144,288]{4,3,2,1,0:T(8,128)(2,1)} %get-tuple-element.167) | copy-start | bytes 1990660
  401.2 29.7 %copy-start.167 = (bf16[2,2,2,144,1152]{4,3,2,1,0:T(8,128)(2,1)S(1)}, bf16[2,2,2,144,1152]{4,3,2,1,0:T(8,128)(2,1)}, u32[]{:S(2)}) copy-start(bf16[2,2,2,144,1152]{4,3,2,1,0:T(8,128)(2,1)} %get-tuple-element.160) | copy-start | bytes 7962628
  401.2 29.7 %copy-start.179 = (f32[4,160,1152]{2,1,0:T(8,128)S(1)}, f32[4,160,1152]{2,1,0:T(8,128)}, u32[]{:S(2)}) copy-start(f32[4,160,1152]{2,1,0:T(8,128)} %copy-done.178) | copy-start | bytes 8847364
  430.9 14.3 %copy-start.17 = (bf16[1152,864]{1,0:T(8,128)(2,1)}, bf16[1152,864]{1,0:T(8,128)(2,1)S(1)}, u32[]{:S(2)}) copy-start(bf16[1152,864]{1,0:T(8,128)(2,1)S(1)} %get-tuple-element.190) | copy-start | bytes 5971972
  430.9 14.3 %copy-start.23 = (bf16[1152,288]{1,0:T(8,128)(2,1)}, bf16[1152,288]{1,0:T(8,128)(2,1)S(1)}, u32[]{:S(2)}) copy-start(bf16[1152,288]{1,0:T(8,128)(2,1)S(1)} %get-tuple-element.191) | copy-start | bytes 1990660
  438.9 6.4 copy-start.9
  445.3 34.7 %copy-start.107 = (bf16[2,2,2,144,288]{4,3,2,1,0:T(8,128)(2,1)S(1)}, bf16[2,2,2,144,288]{4,3,2,1,0:T(8,128)(2,1)}, u32[]{:S(2)}) copy-start(bf16[2,2,2,144,288]{4,3,2,1,0:T(8,128)(2,1)} %get-tuple-element.156) | copy-start | bytes 1990660
  500.5 6.2 copy-start.139
  500.5 6.2 copy-start.140
  502.0 6.9 copy-start.10
  503.6 5.3 copy-start.5
  503.6 5.3 copy-start.8
  503.6 5.3 copy-start.34
  558.5 31.2 %copy-start.147 = (bf16[32,144,1,1]{1,0,2,3:T(8,128)(2,1)S(1)}, bf16[32,144,1,1]{1,0,2,3:T(8,128)(2,1)}, u32[]{:S(2)}) copy-start(bf16[32,144,1,1]{1,0,2,3:T(8,128)(2,1)} %reshape.1330) | copy-start | bytes 27652
  595.5 4.9 copy-start.126
  595.5 4.9 copy-start.127
  595.5 4.9 copy-start.128
  595.5 4.9 copy-start.129
  629.1 23.2 %copy-start.158 = (f32[8,4]{1,0:T(8,128)S(1)}, f32[8,4]{1,0:T(8,128)}, u32[]{:S(2)}) copy-start(f32[8,4]{1,0:T(8,128)} %get-tuple-element.338) | copy-start | bytes 388
  629.1 23.3 %copy-start.162 = (f32[128]{0:T(128)S(1)}, f32[128]{0:T(128)}, u32[]{:S(2)}) copy-start(f32[128]{0:T(128)} %copy-done.161) | copy-start | bytes 1540
  629.1 32.0 %copy-start.20 = (bf16[2,144,864]{2,1,0:T(8,128)(2,1)S(1)}, bf16[2,144,864]{2,1,0:T(8,128)(2,1)}, u32[]{:S(2)}) copy-start(bf16[2,144,864]{2,1,0:T(8,128)(2,1)} %get-tuple-element.254.refs_5_) | copy-start | bytes 1492996
  649.2 12.0 %copy-start.11 = (bf16[2,144,1152]{2,1,0:T(8,128)(2,1)S(1)}, bf16[2,144,1152]{2,1,0:T(8,128)(2,1)}, u32[]{:S(2)}) copy-start(bf16[2,144,1152]{2,1,0:T(8,128)(2,1)} %get-tuple-element.256.refs_7_) | copy-start | bytes 1990660
  649.2 12.0 %copy-start.12 = (bf16[2,144,1152]{2,1,0:T(8,128)(2,1)S(1)}, bf16[2,144,1152]{2,1,0:T(8,128)(2,1)}, u32[]{:S(2)}) copy-start(bf16[2,144,1152]{2,1,0:T(8,128)(2,1)} %get-tuple-element.257.refs_8_) | copy-start | bytes 1990660
  649.2 12.0 %copy-start.13 = (bf16[2,144,1152]{2,1,0:T(8,128)(2,1)S(1)}, bf16[2,144,1152]{2,1,0:T(8,128)(2,1)}, u32[]{:S(2)}) copy-start(bf16[2,144,1152]{2,1,0:T(8,128)(2,1)} %get-tuple-element.253.refs_4_) | copy-start | bytes 1990660
  649.2 12.0 %copy-start.14 = (bf16[2,144,1152]{2,1,0:T(8,128)(2,1)S(1)}, bf16[2,144,1152]{2,1,0:T(8,128)(2,1)}, u32[]{:S(2)}) copy-start(bf16[2,144,1152]{2,1,0:T(8,128)(2,1)} %get-tuple-element.252.refs_3_) | copy-start | bytes 1990660
  694.3 5.6 copy-start.88
  696.6 5.4 copy-start.86
  696.6 6.1 copy-start.87
  702.8 5.9 copy-start.110
  702.8 5.9 copy-start.132
  702.8 5.9 copy-start.152
  702.8 5.9 copy-start.153
  702.8 5.9 copy-start.154
  702.8 6.7 copy-start.68
  702.8 6.6 copy-start.69
  702.8 6.6 copy-start.94
  702.8 6.6 copy-start.95
  702.8 7.0 copy-start.96
  (118 other events, 282.0 us)

commit v4 on v3

--- a/solution.py
+++ b/solution.py
@@ -331,12 +331,22 @@
         if self.sums:
             self.take(terms, pltpu.VMEM)
             self.first = 1
+        self.fetched = []
         for array in more:
-            self.take(array, pltpu.VMEM)
+            large = array.size * array.dtype.itemsize >= 2**18
+            if large:
+                array = pltpu.with_memory_space_constraint(array, pltpu.HBM)
+            self.fetched.append(large)
+            self.take(array, pltpu.HBM if large else pltpu.VMEM)
         if self.sends_on:
             self.give((4, length_out, width), jnp.bfloat16, pltpu.VMEM)
         self.peers = [lambda: {CORE: other(CORE)}, lambda: {ZL: other(ZL)}]
-        self.scratch = []
+        self.scratch = [
+            pltpu.VMEM(array.shape, array.dtype)
+            for array, large in zip(more, self.fetched)
+            if large
+        ]
+        self.scratch.append(pltpu.SemaphoreType.DMA((len(more),)))
         if self.sums:
             self.scratch += [pltpu.VMEM((length_in, width), jnp.bfloat16)] * 4
             self.scratch += self.sems(length_in)
@@ -370,8 +380,17 @@
 
     def begin(self, ins, outs, scratch, halfway):
         me, mate, away, away_mate = self.ranks()
-        given = ins[self.first :]
+        given = list(ins[self.first :])
         made = outs[1:] if self.sends_on else outs
+        fetches = []
+        held, scratch = scratch[: sum(self.fetched)], scratch[sum(self.fetched) :]
+        for i, large in enumerate(self.fetched):
+            if large:
+                place = held[len(fetches)]
+                fetches.append(pltpu.make_async_copy(given[i], place, scratch[0].at[i]))
+                fetches[-1].start()
+                given[i] = place
+        scratch = scratch[1:]
         state = self.start(given, made)
         sends = []
         rows_in, rows_out = self.rows(self.length_in), self.rows(self.length_out)
@@ -423,6 +442,8 @@
                     each.start()
                     sends.append(each)
 
+        for each in fetches:
+            each.wait()
         if self.whole:
             for s, r in enumerate(rows_in):
                 self.collect(r, total(s, r), given, made, state)
@@ -517,12 +538,15 @@
 class Decode(Bridge):
     whole = True
 
-    def __init__(self, terms, middle, mod, mod_next, place, base):
+    def __init__(self, terms, middle, mod, mod_next, place, base, contrast):
         (length, width), (length_next, _) = middle.shape, base.shape
-        super().__init__(terms, [middle, mod, mod_next, place, base], width, length, length_next)
+        more = [middle, mod, mod_next, place, base, *contrast]
+        super().__init__(terms, more, width, length, length_next)
         self.result((length, width))
         self.result((length, width))
         self.result((length_next, width))
+        self.result((1, width))
+        self.result((1, 1))
 
     def collect(self, r, total, given, made, state):
         middle, mod = given[:2]
@@ -531,7 +555,7 @@
         encoded[r] = middle[r] + mod[GATE_M : GATE_M + 1] * total
 
     def turn(self, given, made, state):
-        place, base = given[3:]
+        place, base = given[3:5]
         made[2][...] = full_dot(place[...], made[1][...]) + base[...]
 
     def work(self, r, total, given, made, state):
@@ -540,6 +564,23 @@
         return (unit * (1.0 + mod[SCALE_A : SCALE_A + 1]) + mod[SHIFT_A : SHIFT_A + 1]).astype(
             jnp.bfloat16
         )
+
+
+    def aside(self, given, made):
+        valid, count, teachers, positive = given[5:]
+        pooled = fold(made[1][...] * valid[...]) / count[...]
+        scale = lax.rsqrt(jnp.sum(pooled * pooled, -1, keepdims=True) + 1e-06)
+        others = teachers[...]
+        others = others * lax.rsqrt(jnp.sum(others * others, -1, keepdims=True) + 1e-06)
+        logits = jnp.sum(pooled * scale * others, -1, keepdims=True) / contrast_sharpness_divisor
+        peak = jnp.max(logits, 0, keepdims=True)
+        expo = jnp.exp(logits - peak)
+        total = fold(expo)
+        made[4][...] = peak + jnp.log(total) - fold(logits * positive[...])
+        weight = (expo / total - positive[...]) * (nce_weight / others.shape[0])
+        grad = fold(weight * others) / contrast_sharpness_divisor
+        along = jnp.sum(pooled * grad, -1, keepdims=True)
+        made[3][...] = scale * (grad - pooled * (scale * scale * along)) / count[...]
 
 
 class Turn(Bridge):
@@ -609,11 +650,12 @@
 class Encode(Bridge):
     whole = True
 
-    def __init__(self, terms, values, grad, mod, open_place, select, pool, branch, mod_next, pairs):
+    def __init__(self, terms, values, grad, mod, more, pairs):
+        branch = more[4]
         (length, width), (length_next, _) = values.shape, branch.shape
         super().__init__(
             terms,
-            [values, grad, mod, open_place, select, pool, branch, mod_next, *pairs],
+            [values, grad, mod, *more, *pairs],
             width,
             length,
             length_next,
@@ -639,11 +681,11 @@
         self.add(state, TERM_MASK, fold(open_place[r] * fresh))
 
     def turn(self, given, made, state):
-        select, pool = given[4:6]
-        made[0][...] = full_dot(select[...], self.held[...]) + pool[...]
+        select, (valid, pool) = given[4], given[5:7]
+        made[0][...] = full_dot(select[...], self.held[...]) + valid[...] * pool[...]
 
     def work(self, r, total, given, made, state):
-        branch, mod_next = given[6:8]
+        branch, mod_next = given[7:9]
         fresh = made[0][r]
         self.add(state, TERM_GATE, fold(fresh * branch[r]))
         return (mod_next[GATE_M : GATE_M + 1] * fresh).astype(jnp.bfloat16)
@@ -655,8 +697,8 @@
         made[1][3:4] = state[TERM_MASK]
 
     def aside(self, given, made):
-        outer(given[8], given[9], made[2])
-        outer(given[10], given[11], made[3])
+        outer(given[9], given[10], made[2])
+        outer(given[11], given[12], made[3])
 
 
 class Leave(Bridge):
@@ -1084,60 +1126,97 @@
         return self.got[LEAVE][kind, block][0]
 
 
-def scores_of(query, key, key_valid):
+ROWS_BY_ROWS = (((1,), (1,)), ((), ()))
+COLUMNS_BY_COLUMNS = (((0,), (0,)), ((), ()))
+
+
+def head_of(array, which, head, local):
+    first = which * local + head * HEAD_DIM
+    return array[0, :, first : first + HEAD_DIM]
+
+
+def soft(query, key, valid):
+    scores = lax.dot_general(query, key, ROWS_BY_ROWS, preferred_element_type=jnp.float32)
+    scores = jnp.where(valid > 0, scores * (1.0 / math.sqrt(HEAD_DIM)), -1e30)
+    expo = jnp.exp(scores - jnp.max(scores, -1, keepdims=True))
+    return expo / jnp.sum(expo, -1, keepdims=True)
+
+
+def attend_kernel(normed, valid, weight_in, weight_out, triple, context, terms):
+    local = context.shape[2]
+    triple[0] = jnp.dot(normed[0], weight_in[...], preferred_element_type=jnp.float32).astype(
+        jnp.bfloat16
+    )
+    parts = []
+    for head in range(local // HEAD_DIM):
+        query, key, value = [head_of(triple, which, head, local) for which in range(3)]
+        probs = soft(query, key, valid[0]).astype(jnp.bfloat16)
+        parts.append(jnp.dot(probs, value, preferred_element_type=jnp.float32))
+    flat = jnp.concatenate(parts, 1).astype(jnp.bfloat16)
+    context[0] = flat
+    terms[0] = lax.dot_general(
+        flat, weight_out[...], ROWS_BY_ROWS, preferred_element_type=jnp.float32
+    ).astype(jnp.bfloat16)
+
+
+def attend_back_kernel(
+    triple, valid, grad_attn, weight_in, weight_out, grad_triple, terms, grad_context
+):
+    local = weight_out.shape[1]
     scale = 1.0 / math.sqrt(HEAD_DIM)
-    scores = jnp.einsum("bqhe,bkhe->bhqk", query, key, preferred_element_type=jnp.float32) * scale
-    if key_valid is None:
-        return scores
-    return jnp.where(key_valid[:, None, None, :] > 0, scores, -1e30)
-
-
-def attend_forward(query, key, value, key_valid):
-    scores = scores_of(query, key, key_valid)
-    peak = jnp.max(scores, -1, keepdims=True)
-    expo = jnp.exp(scores - peak)
-    total = jnp.sum(expo, -1, keepdims=True)
-    probs = (expo / total).astype(jnp.bfloat16)
-    context = jnp.einsum(
-        "bhqk,bkhe->bqhe", probs, value, preferred_element_type=jnp.float32
+    grad_context[0] = jnp.dot(
+        grad_attn[0], weight_out[...], preferred_element_type=jnp.float32
     ).astype(jnp.bfloat16)
-    return (context, peak + jnp.log(total))
-
-
-def attend_backward(query, key, value, log_total, grad_context, key_valid):
-    scale = 1.0 / math.sqrt(HEAD_DIM)
-    probs = jnp.exp(scores_of(query, key, key_valid) - log_total)
-    grad_value = jnp.einsum(
-        "bhqk,bqhe->bkhe",
-        probs.astype(jnp.bfloat16),
-        grad_context,
-        preferred_element_type=jnp.float32,
+    queries, keys, values = [], [], []
+    for head in range(local // HEAD_DIM):
+        query, key, value = [head_of(triple, which, head, local) for which in range(3)]
+        grad = head_of(grad_context, 0, head, local)
+        probs = soft(query, key, valid[0])
+        values.append(
+            lax.dot_general(
+                probs.astype(jnp.bfloat16),
+                grad,
+                COLUMNS_BY_COLUMNS,
+                preferred_element_type=jnp.float32,
+            )
+        )
+        grad_probs = lax.dot_general(
+            grad, value, ROWS_BY_ROWS, preferred_element_type=jnp.float32
+        )
+        tilt = jnp.sum(grad_probs * probs, -1, keepdims=True)
+        grad_scores = (probs * (grad_probs - tilt)).astype(jnp.bfloat16)
+        queries.append(jnp.dot(grad_scores, key, preferred_element_type=jnp.float32) * scale)
+        keys.append(
+            lax.dot_general(
+                grad_scores, query, COLUMNS_BY_COLUMNS, preferred_element_type=jnp.float32
+            )
+            * scale
+        )
+    fresh = jnp.concatenate(queries + keys + values, 1).astype(jnp.bfloat16)
+    grad_triple[0] = fresh
+    terms[0] = lax.dot_general(
+        fresh, weight_in[...], ROWS_BY_ROWS, preferred_element_type=jnp.float32
     ).astype(jnp.bfloat16)
-    grad_probs = jnp.einsum(
-        "bqhe,bkhe->bhqk", grad_context, value, preferred_element_type=jnp.float32
-    )
-    grad_scores = (probs * (grad_probs - jnp.sum(grad_probs * probs, -1, keepdims=True))).astype(
-        jnp.bfloat16
-    )
-    grad_query = (
-        jnp.einsum("bhqk,bkhe->bqhe", grad_scores, key, preferred_element_type=jnp.float32) * scale
-    ).astype(jnp.bfloat16)
-    grad_key = (
-        jnp.einsum("bhqk,bqhe->bkhe", grad_scores, query, preferred_element_type=jnp.float32)
-        * scale
-    ).astype(jnp.bfloat16)
-    return (grad_query, grad_key, grad_value)
-
-
-def split_heads(triple):
-    batch, length, three = triple.shape
-    local = three // 3
-    return [
-        triple[:, :, i * local : (i + 1) * local].reshape(
-            batch, length, local // HEAD_DIM, HEAD_DIM
-        )
-        for i in range(3)
-    ]
+
+
+def by_image(body, arrays, weights, columns, scratch=()):
+    images, length = arrays[0].shape[:2]
+
+    def block(array):
+        return pl.BlockSpec((1,) + array.shape[1:], lambda i: (i, 0, 0))
+
+    made = [jax.ShapeDtypeStruct((images, length, each), jnp.bfloat16) for each in columns]
+    return pl.pallas_call(
+        body,
+        grid=(images,),
+        out_shape=made,
+        in_specs=[block(array) for array in arrays]
+        + [pl.BlockSpec(weight.shape, lambda i: (0, 0)) for weight in weights],
+        out_specs=[block(each) for each in made],
+        scratch_shapes=[pltpu.VMEM((1, length, each), jnp.bfloat16) for each in scratch],
+        compiler_params=pltpu.CompilerParams(vmem_limit_bytes=24 * 2**20),
+        cost_estimate=pl.CostEstimate(flops=5 * 10**9, bytes_accessed=1024, transcendentals=0),
+    )(*arrays, *weights)
 
 
 def low_dot(spec, left, right):
@@ -1145,11 +1224,12 @@
 
 
 def attend(normed, key_valid, block, route):
-    triple = low_dot("bld,dc->blc", normed, route.weight(IN, block)).astype(jnp.bfloat16)
-    context, log_total = attend_forward(*split_heads(triple), key_valid)
-    flat_context = context.reshape(triple.shape[0], triple.shape[1], triple.shape[2] // 3)
-    terms = low_dot("ble,de->bld", flat_context, route.weight(OUT, block)).astype(jnp.bfloat16)
-    return terms, (triple, flat_context, log_total)
+    weights = [route.weight(IN, block), route.weight(OUT, block)]
+    width, local = weights[1].shape
+    triple, flat_context, terms = by_image(
+        attend_kernel, [normed, key_valid], weights, (3 * local, local, width)
+    )
+    return terms, (triple, flat_context)
 
 
 def feed(normed, block, route):
@@ -1171,13 +1251,16 @@
 
 
 def attend_back(grad_attn, normed, saved, key_valid, block, route):
-    triple, flat_context, log_total = saved
-    grad_flat = low_dot("bld,de->ble", grad_attn, route.weight(OUT, block)).astype(jnp.bfloat16)
-    query, key, value = split_heads(triple)
-    grad_context = grad_flat.reshape(query.shape)
-    grad_parts = attend_backward(query, key, value, log_total, grad_context, key_valid)
-    grad_triple = jnp.concatenate([g.reshape(flat_context.shape) for g in grad_parts], 2)
-    terms = low_dot("blc,dc->bld", grad_triple, route.weight(IN, block)).astype(jnp.bfloat16)
+    triple, flat_context = saved
+    weights = [route.weight(IN, block), route.weight(OUT, block)]
+    width, local = weights[1].shape
+    grad_triple, terms = by_image(
+        attend_back_kernel,
+        [triple, key_valid, grad_attn],
+        weights,
+        (3 * local, width),
+        (local,),
+    )
     return terms, (normed, grad_triple, grad_attn, flat_context)
 
 
@@ -1206,9 +1289,9 @@
         feed(1, FAR) + feed(1, NEAR),
         feed(1, PASS),
         feed(0, FAR) + attend(1, FAR) + attend(1, NEAR) + expand(1, LEAVE),
-        feed(0, NEAR) + feed(0, PASS) + attend(1, PASS) + contract(1, LEAVE),
-        attend(0, FAR) + feed(0, LEAVE),
-        attend(0, NEAR) + attend(0, PASS) + attend(1, LEAVE),
+        contract(0, NEAR) + feed(0, PASS) + attend(1, PASS) + contract(1, LEAVE),
+        attend(0, FAR) + expand(0, NEAR) + contract(0, LEAVE) + attend(1, LEAVE),
+        attend(0, NEAR) + attend(0, PASS) + expand(0, LEAVE),
         attend(0, LEAVE),
         [],
     ]
@@ -1307,7 +1390,10 @@
         (flat_place((PY, PX)) * 2, lax.axis_index(ZH) * 2),
         (2, 2),
     ).reshape(4)
-    group_valid = (jnp.arange(capacity)[None, :] < group_counts[:, None]).astype(jnp.float32)
+    group_valid = (jnp.arange(capacity)[None, None, :] < group_counts[:, None, None]).astype(
+        jnp.float32
+    )
+    all_valid = jnp.ones((4, 1, length), jnp.float32)
     kept_patches = low_dot("cl,lp->cp", select.astype(jnp.bfloat16), own(patches))
     embed = low_dot("cp,pd->cd", kept_patches.astype(jnp.bfloat16), patch_full[:PATCH_IN])
     embed = embed + jnp.dot(select, places, precision=highest_float_accuracy)
@@ -1320,49 +1406,26 @@
     terms, saved_a0 = attend(normed_a0, group_valid, 0, route)
     normed_m0, attn0, middle0 = route.step(Middle(terms, embed, mod_enc))
     terms, saved_m0 = feed(normed_m0, 0, route)
-    normed_a1, branch0, encoded, decode_in = route.step(
-        Decode(terms, middle0, mod_enc, mod_dec, select.T, base)
-    )
-    terms, saved_a1 = attend(normed_a1, None, 1, route)
+    positive = ((wide_index * batch + narrow_index) == jnp.arange(images)).astype(jnp.float32)
+    contrast = (slot_valid, count_own.reshape(1, 1), negatives, positive[:, None])
+    normed_a1, branch0, _, decode_in, grad_pool, nce = route.step(
+        Decode(terms, middle0, mod_enc, mod_dec, select.T, base, contrast)
+    )
+    terms, saved_a1 = attend(normed_a1, all_valid, 1, route)
     normed_m1, attn1, middle1 = route.step(Middle(terms, decode_in, mod_dec))
     terms, saved_m1 = feed(normed_m1, 1, route)
     grad_branch, grad_decoded, gate_m1, grad_head, square = route.step(
         Turn(terms, middle1, mod_dec, head, own(target_noise), count_all)
     )
 
-    def pool_unit(values):
-        pooled = jnp.sum(values * slot_valid, 0, keepdims=True) / count_own
-        return pooled * lax.rsqrt(jnp.sum(pooled * pooled, -1, keepdims=True) + 1e-06)
-
-    normalised_direction, pool_back = jax.vjp(pool_unit, encoded)
-    frozen_target_direction = negatives * lax.rsqrt(
-        jnp.sum(negatives * negatives, -1, keepdims=True) + 1e-06
-    )
-    cosine_match_scores = (
-        jnp.sum(normalised_direction * frozen_target_direction, -1, keepdims=True)
-        / contrast_sharpness_divisor
-    )
-    peak = jnp.max(cosine_match_scores)
-    expo = jnp.exp(cosine_match_scores - peak)
-    total = jnp.sum(expo)
-    positive = ((wide_index * batch + narrow_index) == jnp.arange(images)).astype(jnp.float32)
-    positive = positive[:, None]
-    nce_local = peak + jnp.log(total) - jnp.sum(cosine_match_scores * positive)
-    derivative_of_raw_scores = (expo / total - positive) * (nce_weight / images)
-    unit_vector_gradient = (
-        jnp.sum(derivative_of_raw_scores * frozen_target_direction, 0, keepdims=True)
-        / contrast_sharpness_divisor
-    )
-    grad_pool = pool_back(unit_vector_gradient)[0]
-
     terms = feed_back(grad_branch, normed_m1, saved_m1, 1, route)
     grad_attn, grad_mid, sums_m1 = route.step(
         MiddleBack(terms, middle1, attn1, grad_decoded, mod_dec)
     )
-    terms, pairs = attend_back(grad_attn, normed_a1, saved_a1, None, 1, route)
-    back_to = (open_place, select, grad_pool, branch0, mod_enc)
+    terms, pairs = attend_back(grad_attn, normed_a1, saved_a1, all_valid, 1, route)
+    back_to = (open_place, select, slot_valid, grad_pool, branch0, mod_enc)
     grad_branch, grad_encoded, sums_a1, grad_in, grad_out = route.step(
-        Encode(terms, decode_in, grad_mid, mod_dec, *back_to, pairs)
+        Encode(terms, decode_in, grad_mid, mod_dec, back_to, pairs)
     )
     route.give_grad(IN, 1, grad_in)
     route.give_grad(OUT, 1, grad_out)
@@ -1430,7 +1493,7 @@
     )
     square_local = jnp.sum(grad_modulation * grad_modulation)
     square_local = square_local + (wide_index == 0).astype(jnp.float32) * square_small
-    scalars = jnp.stack([square[0, 0], nce_local, square_local])
+    scalars = jnp.stack([square[0, 0], nce[0, 0], square_local])
     scalars = jnp.pad(scalars[None, :], ((0, 7), (0, 125)))
     mets = [route.met(kind, i) for i in range(2) for kind in (IN, OUT, EXPAND, CONTRACT)]
     (scalars_all,) = route.step(Norm(scalars, mets))

time: 723 us -> 692 us (0.957)
  Pallas kernels: 458 us -> 501 us
  matrix products: 101 us -> 61.7 us
  local copies, waits for them, and re-layouts: 71.9 us -> 51 us
  other arithmetic: 70.7 us -> 59.1 us
    pallas_call x0 -> x4, Pallas kernels: none -> 46.9 us  [by_image(): pl.pallas_call(body, grid=(images,), out_shape=made, in_specs=[block(arra...]
    dot_general x12 -> x0, matrix products: 20.2 us -> none  [the longest x2 6.18 us: attend_backward(): jnp.einsum('bqhe,bkhe->bhqk', grad_context, value, preferred_element_type...]
    dot_general x24 -> x16, matrix products: 66.3 us -> 47.6 us  [low_dot(): return jnp.einsum(spec, left, right, preferred_element_type=jnp.float32)]
    reshape x8 -> x0, local copies, waits for them, and re-layouts: 13 us -> none  [the longest x6 10.1 us: attend_back(): g.reshape(flat_context.shape)]
    unnamed x364 -> x318, local copies, waits for them, and re-layouts: 36.2 us -> 35.9 us
where the time goes in v4:
time: 692 us; the launch traced here: 682 us
  Pallas kernels  501 us (72%)
  matrix products  61.7 us (9%)
  other arithmetic  59.1 us (9%)
  local copies, waits for them, and re-layouts  51 us (7%)
  between operations  9.36 us (1%)
    pallas_call x16, Pallas kernels, travel(): pl.pallas_call(partial(kernel, parts), out_shape=[shape for part in parts...  454 us
    dot_general x16, matrix products, low_dot(): return jnp.einsum(spec, left, right, preferred_element_type=jnp.float32)  47.6 us
    pallas_call x4, Pallas kernels, by_image(): pl.pallas_call(body, grid=(images,), out_shape=made, in_specs=[block(arra...  46.9 us
    unnamed x318, local copies, waits for them, and re-layouts  35.9 us
    add x7, other arithmetic, adam(): average = average_decay * average + (1.0 - average_decay) * fresh  21.3 us

profile of v4, /device:TPU:0, one launch (start us, length us, event | category | flops | bytes accessed | tf_op | source)
XLA Modules:
  0.0 682.4 jit_solution(16436804075414884393)
XLA Ops:
  0.7 1.6 convert_element_type.1054
  4.6 15.0 %shard_map.562 = (f32[8,8,144]{2,1,0:T(8,128)S(1)}, bf16[2,2,2,144,864]{4,3,2,1,0:T(8,128)(2,1)}, bf16[2,2,2,144,288]{4,3,2,1,0:T(8,128)(2,1)}) custom-call(f32[2,8,144]{2,1,0:T(8,128)S(1)} %pad.21.refs_0_, bf16[144,864]{1,0:T(8,128)(2,1)S(1)} %convert_element_type.1055.refs_1_, bf16[144,288]{1,0:T(8,128)(2,1)S(1)} %get-tuple-element.355.refs_2_), custom_call_target="tpu_custom_call" | custom-call | flops 20000000000 | bytes 1024 | tf_op jit(solution)/shard_map/pallas_call | solution.py:1041
  20.3 2.3 multiply_cosine_fusion
  24.7 1.9 fusion.29
  26.6 1.9 convert_bitcast_fusion
  28.9 2.2 reshape.1189
  31.2 1.6 fusion.154.refs_0_
  32.9 27.4 %shard_map.563 = (f32[8,4,3456]{2,1,0:T(4,128)S(1)}, bf16[2,2,2,144,864]{4,3,2,1,0:T(8,128)(2,1)}, bf16[2,2,2,144,288]{4,3,2,1,0:T(8,128)(2,1)}, bf16[2,2,2,144,1152]{4,3,2,1,0:T(8,128)(2,1)}) custom-call(f32[8,4,3456]{2,1,0:T(4,128)S(1)} %fusion.154.refs_0_, ...), custom_call_target="tpu_custom_call", output_to_operand_aliasing={{1}: (1, {}), {2}: (2, {})} | custom-call | flops 20000000000 | bytes 1024 | tf_op jit(solution)/shard_map/pallas_call | solution.py:1041
  61.2 25.6 %shard_map.564 = (f32[4,12,288]{2,1,0:T(8,128)S(1)}, f32[8,24,288]{2,1,0:T(8,128)S(1)}, bf16[4,48,288]{2,1,0:T(8,128)(2,1)S(1)}, bf16[2,2,2,144,864]{4,3,2,1,0:T...) custom-call(f32[4,12,288]{2,1,0:T(8,128)S(1)} %reshape.1116.refs_0_,, ...), custom_call_target="tpu_custom_call", output_to_operand_aliasing={{3}: (3, {}), {4}: (4, {})} | custom-call | flops 20000000000 | bytes 1024 | tf_op jit(solution)/shard_map/pallas_call | solution.py:1041
  89.7 32.5 %shard_map.565 = (bf16[4,160,1152]{2,1,0:T(8,128)(2,1)S(1)}, bf16[2,2,2,144,1152]{4,3,2,1,0:T(8,128)(2,1)}, bf16[2,2,2,144,864]{4,3,2,1,0:T(8,128)(2,1)}, bf16[2,2,2,144,288]{4,3,2,1,0:T(8,128)(2,1)}) custom-call(f32[160,1152]{1,0:T(8,128)} %convolution_add_fusion.refs_0_.refs_1_, ...), custom_call_target="tpu_custom_call", output_to_operand_aliasing={{1}: (2, {})} | custom-call | flops 20000000000 | bytes 1024 | tf_op jit(solution)/shard_map/pallas_call | solution.py:1041
  124.4 1.6 copy-done.29
  125.9 1.4 copy-done.51
  127.3 7.7 %shard_map.566 = (bf16[4,160,864]{2,1,0:T(8,128)(2,1)S(1)}, bf16[4,160,288]{2,1,0:T(8,128)(2,1)S(1)}, bf16[4,160,1152]{2,1,0:T(8,128)(2,1)S(1)}) custom-call(bf16[4,160,1152]{2,1,0:T(8,128)(2,1)S(1)} %copy-done.51, f32[4,1,160]{2,1,0:T(1,128)S(1)} %compare_convert_fusion.valid, bf16[1152,864]{1,0:T(8,128)(2,1)S(1)} %bitcast.356, bf16[1152,288]{1,0:T(8,128)(2,1)S(1)} %bitcast.360), custom_call_target="tpu_custom_call" | custom-call | flops 5000000000 | bytes 1024 | tf_op jit(solution)/shard_map/pallas_call | solution.py:1209
  136.1 28.8 %shard_map.567 = (bf16[4,160,1152]{2,1,0:T(8,128)(2,1)S(1)}, f32[160,1152]{1,0:T(8,128)S(1)}, f32[160,1152]{1,0:T(8,128)S(1)}, bf16[2,2,2,144,1152]{4,3,2,1,0:T(8,128)(2,1)}, bf16[2,2,2,144,1152]{4,3,2,1,0:T(8,128)(2,1)}) custom-call(bf16[4,160,1152]{2,1,0:T(8,128)(2,1)S(1)} %get-tuple-element.168.refs_0_, ...), custom_call_target="tpu_custom_call", output_to_operand_aliasing={{3}: (3, {})} | custom-call | flops 20000000000 | bytes 1024 | tf_op jit(solution)/shard_map/pallas_call | solution.py:1041
  164.9 2.2 fusion.156
  167.7 3.8 convolution_convert_fusion.3.refs_0_
  171.9 2.7 multiply_add_fusion.9.refs_5_
  176.1 36.1 %shard_map.568 = (bf16[4,256,1152]{2,1,0:T(8,128)(2,1)S(1)}, f32[160,1152]{1,0:T(8,128)S(1)}, f32[160,1152]{1,0:T(8,128)}, f32[256,1152]{1,0:T(8,128)S(1)}, f32[...) custom-call(bf16[4,160,1152]{2,1,0:T(8,128)(2,1)S(1)} %copy-done.39,, ...), custom_call_target="tpu_custom_call", output_to_operand_aliasing={{6}: (10, {}), {7}: (11, {}), {8}: (12, {})} | custom-call | flops 20000000000 | bytes 1024 | tf_op jit(solution)/shard_map/pallas_call | solution.py:1041
  213.0 2.9 copy-done.27
  217.1 11.4 %shard_map.569 = (bf16[4,256,864]{2,1,0:T(8,128)(2,1)S(1)}, bf16[4,256,288]{2,1,0:T(8,128)(2,1)S(1)}, bf16[4,256,1152]{2,1,0:T(8,128)(2,1)S(1)}) custom-call(bf16[4,256,1152]{2,1,0:T(8,128)(2,1)S(1)} %get-tuple-element.177.normed.refs_10_, f32[4,1,256]{2,1,0:T(1,128)S(1)} %broadcast_in_dim.7.valid, bf16[1152,864]{1,0:T(8,128)(2,1)S(1)} %bitcast.354, ...), custom_call_target="tpu_custom_call" | custom-call | flops 5000000000 | bytes 1024 | tf_op jit(solution)/shard_map/pallas_call | solution.py:1209
  229.7 42.3 %shard_map.570 = (bf16[4,256,1152]{2,1,0:T(8,128)(2,1)S(1)}, f32[256,1152]{1,0:T(8,128)S(1)}, f32[256,1152]{1,0:T(8,128)S(1)}, bf16[2,2,2,144,1152]{4,3,2,1,0:T(8,128)(2,1)}, bf16[2,2,2,144,1152]{4,3,2,1,0:T(8,128)(2,1)}) custom-call(bf16[4,256,1152]{2,1,0:T(8,128)(2,1)S(1)} %get-tuple-element.180.refs_0_, ...), custom_call_target="tpu_custom_call", output_to_operand_aliasing={{3}: (3, {}), {4}: (4, {})} | custom-call | flops 20000000000 | bytes 1024 | tf_op jit(solution)/shard_map/pallas_call | solution.py:1041
  272.1 7.0 %fusion.157 = f32[4,256,1152]{2,1,0:T(8,128)S(1)} fusion(bf16[4,256,1152]{2,1,0:T(8,128)(2,1)S(1)} %get-tuple-element.184, bf16[1152,1152,1]{1,0,2:T(8,128)(2,1)} %bitcast.375), kind=kOutput, calls=%fused_computation.297 | convolution fusion | flops 2717908992 | bytes 9732096 | tf_op jit(solution)/shard_map/bld,df->blf/dot_general | solution.py:1223
  279.1 4.5 convolution_convert_fusion.1.refs_0_
  283.9 30.8 %shard_map.571 = (bf16[4,256,1152]{2,1,0:T(8,128)(2,1)S(1)}, f32[256,1152]{1,0:T(8,128)S(1)}, f32[1,1152]{1,0:T(1,128)S(1)}, f32[16,1152]{1,0:T(8,128)S(1)}, f32[1,1]{1,0:T(1,128)}) custom-call(bf16[4,256,1152]{2,1,0:T(8,128)(2,1)S(1)} %convolution_convert_fusion.1.refs_0_, f32[256,1152]{1,0:T(8,128)} %copy-done.59, ...), custom_call_target="tpu_custom_call" | custom-call | flops 20000000000 | bytes 1024 | tf_op jit(solution)/shard_map/pallas_call | solution.py:1041
  315.8 5.1 fusion.10
  320.9 4.0 convolution_convert_fusion.refs_0_
  324.9 3.3 fusion
  328.2 3.4 fusion.1
  331.7 32.2 %shard_map.572 = (bf16[4,256,1152]{2,1,0:T(8,128)(2,1)S(1)}, f32[256,1152]{1,0:T(8,128)S(1)}, f32[3,1152]{1,0:T(4,128)S(1)}, bf16[1,1,144,1152]{3,2,1,0:T(8,128)...) custom-call(bf16[4,256,1152]{2,1,0:T(8,128)(2,1)S(1)} %convolution_c, ...), custom_call_target="tpu_custom_call" | custom-call | flops 20000000000 | bytes 1024 | tf_op jit(solution)/shard_map/pallas_call | solution.py:1041
  364.9 14.6 %shard_map.573 = (bf16[4,256,864]{2,1,0:T(8,128)(2,1)S(1)}, bf16[4,256,1152]{2,1,0:T(8,128)(2,1)S(1)}) custom-call(bf16[4,256,864]{2,1,0:T(8,128)(2,1)S(1)} %copy-done.45, f32[4,1,256]{2,1,0:T(1,128)S(1)} %broadcast_in_dim.7.valid, bf16[4,256,1152]{2,1,0:T(8,128)(2,1)S(1)} %get-tuple-element.195.grad_attn.refs_12_, bf16[1152,864]{1,0:T(8,128)(2,1)S(1)} %bitcast.355, ...), custom_call_target="tpu_custom_call" | custom-call | flops 5000000000 | bytes 1024 | tf_op jit(solution)/shard_map/pallas_call | solution.py:1209
  379.5 1.4 copy-done.41
  382.4 1.4 fusion.54
  383.8 1.4 fusion.52
  385.2 29.9 %shard_map.574 = (bf16[4,160,1152]{2,1,0:T(8,128)(2,1)S(1)}, f32[160,1152]{1,0:T(8,128)S(1)}, f32[4,1152]{1,0:T(4,128)S(1)}, bf16[1152,864]{1,0:T(8,128)(2,1)S(1...) custom-call(bf16[4,256,1152]{2,1,0:T(8,128)(2,1)S(1)} %copy-done.42,, ...), custom_call_target="tpu_custom_call" | custom-call | flops 20000000000 | bytes 1024 | tf_op jit(solution)/shard_map/pallas_call | solution.py:1041
  415.2 3.1 fusion.17
  418.4 2.3 convolution_convert_fusion.2.refs_0_
  420.7 2.4 fusion.2
  423.2 2.5 fusion.3
  425.8 3.5 fusion.43
  429.5 34.4 %shard_map.575 = (bf16[4,160,1152]{2,1,0:T(8,128)(2,1)S(1)}, f32[160,1152]{1,0:T(8,128)S(1)}, f32[3,1152]{1,0:T(4,128)S(1)}, bf16[1,1,144,1152]{3,2,1,0:T(8,128)...) custom-call(bf16[4,160,1152]{2,1,0:T(8,128)(2,1)S(1)} %convolution_c, ...), custom_call_target="tpu_custom_call" | custom-call | flops 20000000000 | bytes 1024 | tf_op jit(solution)/shard_map/pallas_call | solution.py:1041
  464.8 13.3 %shard_map.576 = (bf16[4,160,864]{2,1,0:T(8,128)(2,1)S(1)}, bf16[4,160,1152]{2,1,0:T(8,128)(2,1)S(1)}) custom-call(bf16[4,160,864]{2,1,0:T(8,128)(2,1)S(1)} %copy-done.53, f32[4,1,160]{2,1,0:T(1,128)S(1)} %copy-done.26, bf16[4,160,1152]{2,1,0:T(8,128)(2,1)S(1)} %get-tuple-element.215.grad_attn.refs_12_, bf16[1152,864]{1,0:T(8,128)(2,1)S(1)} %bitcast.357, ...), custom_call_target="tpu_custom_call" | custom-call | flops 5000000000 | bytes 1024 | tf_op jit(solution)/shard_map/pallas_call | solution.py:1209
  480.3 1.4 fusion.46
  481.8 1.6 fusion.44
  483.4 1.4 fusion.73
  485.9 34.0 %shard_map.577 = (f32[4,48,288]{2,1,0:T(8,128)S(1)}, bf16[1152,864]{1,0:T(8,128)(2,1)S(1)}, bf16[1152,288]{1,0:T(8,128)(2,1)S(1)}, bf16[1,144,1152]{2,1,0:T(8,12...) custom-call(bf16[4,160,1152]{2,1,0:T(8,128)(2,1)S(1)} %copy-done.49,, ...), custom_call_target="tpu_custom_call" | custom-call | flops 20000000000 | bytes 1024 | tf_op jit(solution)/shard_map/pallas_call | solution.py:1041
  522.4 1.8 fusion.39
  524.4 1.4 fusion.72
  527.1 34.1 %shard_map.578 = (f32[8,4,3456]{2,1,0:T(4,128)S(1)}, bf16[8,48,288]{2,1,0:T(8,128)(2,1)S(1)}, bf16[1,1,144,864]{3,2,1,0:T(8,128)(2,1)}, bf16[1,1,144,864]{3,2,1,...) custom-call(f32[4,3456]{1,0:T(4,128)S(1)} %reshape.1134.refs_0_, ...), custom_call_target="tpu_custom_call" | custom-call | flops 20000000000 | bytes 1024 | tf_op jit(solution)/shard_map/pallas_call | solution.py:1041
  561.1 1.4 reshape.1137
  562.6 4.5 multiply_reduce_fusion
  569.3 3.4 fusion.26.refs_0_
  574.5 20.5 %shard_map.579 = (f32[4,32,144]{2,1,0:T(8,128)S(1)}, bf16[1,144,864]{2,1,0:T(8,128)(2,1)}, bf16[1,144,864]{2,1,0:T(8,128)(2,1)}, bf16[1,144,288]{2,1,0:T(8,128)(...) custom-call(f32[32,144]{1,0:T(8,128)S(1)} %fusion.26.refs_0_, ...), custom_call_target="tpu_custom_call" | custom-call | flops 20000000000 | bytes 1024 | tf_op jit(solution)/shard_map/pallas_call | solution.py:1041
  595.0 1.8 fusion.66
  598.0 20.0 %shard_map.580 = (f32[8,32,144]{2,1,0:T(8,128)S(1)}, bf16[2,144,864]{2,1,0:T(8,128)(2,1)}, bf16[2,144,288]{2,1,0:T(8,128)(2,1)}) custom-call(f32[32,144]{1,0:T(8,128)S(1)} %reduce_sum.90.refs_0_, bf16[2,144,864]{2,1,0:T(8,128)(2,1)S(1)} %pad_maximum_fusion.7.refs_1_, bf16[2,144,288]{2,1,0:T(8,128)(2,1)S(1)} %pad_maximum_fusion.9.refs_2_), custom_call_target="tpu_custom_call" | custom-call | flops 20000000000 | bytes 1024 | tf_op jit(solution)/shard_map/pallas_call | solution.py:1041
  619.0 1.8 reshape.1138
  622.9 4.1 multiply_reduce_fusion.1
  632.1 10.7 %shard_map.581 = f32[32,8,128]{2,1,0:T(8,128)S(1)} custom-call(f32[8,128]{1,0:T(8,128)S(1)} %pad.25.refs_0_, bf16[2,144,864]{2,1,0:T(8,128)(2,1)S(1)} %copy-done.15, bf16[2,144,288]{2,1,0:T(8,128)(2,1)S(1)} %copy-done.23, bf16[2,144,1152]{2,1,0:T(8,128)(2,1)S(1)} %copy-done.7, bf16[2,144,1152]{2,1,0:T(8,128)(2,1)S(1)} %copy-done.6, ...), custom_call_target="tpu_custom_call" | custom-call | flops 20000000000 | bytes 1024 | tf_op jit(solution)/shard_map/pallas_call | solution.py:1041
  649.8 3.2 multiply_add_fusion.5
  654.4 1.5 multiply_add_fusion.10
  658.6 3.2 multiply_add_fusion.4
  664.3 3.3 multiply_add_fusion.3
  667.7 1.3 copy-done.68
  670.6 5.8 multiply_add_fusion
  677.4 3.5 multiply_add_fusion.1
  (438 shorter events, 54.0 us)
Async XLA Ops:
  0.7 283.1 %copy-start = (f32[4,256,16]{1,2,0:T(8,128)S(1)}, f32[4,256,16]{1,2,0:T(8,128)}, u32[]{:S(2)}) copy-start(f32[4,256,16]{1,2,0:T(8,128)} %param.36) | copy-start | bytes 196612
  4.6 18.1 %copy-start.147 = (s32[4]{0:T(128)S(1)}, s32[4]{0:T(128)}, u32[]{:S(2)}) copy-start(s32[4]{0:T(128)} %param.38) | copy-start | bytes 52
  22.7 10.1 %copy-start.71 = (f32[256,576]{1,0:T(8,128)}, f32[256,576]{1,0:T(8,128)S(1)}, u32[]{:S(2)}) copy-start(f32[256,576]{1,0:T(8,128)S(1)} %get-tuple-element.360) | copy-start | bytes 1769476
  32.9 27.6 %copy-start.141 = (f32[4,1152]{1,0:T(4,128)S(1)}, f32[4,1152]{1,0:T(4,128)}, u32[]{:S(2)}) copy-start(f32[4,1152]{1,0:T(4,128)} %param.41) | copy-start | bytes 55300
  32.9 28.1 %copy-start.121 = (f32[33,288]{1,0:T(8,128)S(1)}, f32[33,288]{1,0:T(8,128)}, u32[]{:S(2)}) copy-start(f32[33,288]{1,0:T(8,128)} %param.47) | copy-start | bytes 114052
  32.9 28.1 %copy-start.77 = (f32[2,1152,144]{1,2,0:T(8,128)S(1)}, f32[2,1152,144]{1,2,0:T(8,128)}, u32[]{:S(2)}) copy-start(f32[2,1152,144]{1,2,0:T(8,128)} %param.45) | copy-start | bytes 3981316
  61.2 26.8 %copy-start.79 = (f32[160,1152]{1,0:T(8,128)S(1)}, f32[160,1152]{1,0:T(8,128)}, u32[]{:S(2)}) copy-start(f32[160,1152]{1,0:T(8,128)} %fusion.29) | copy-start | bytes 2211844
  86.8 89.0 %copy-start.17 = (f32[8,24,288]{2,1,0:T(8,128)}, f32[8,24,288]{2,1,0:T(8,128)S(1)}, u32[]{:S(2)}) copy-start(f32[8,24,288]{2,1,0:T(8,128)S(1)} %get-tuple-element.165) | copy-start | bytes 663556
  89.7 34.6 %copy-start.33 = (bf16[2,2,2,144,288]{4,3,2,1,0:T(8,128)(2,1)S(1)}, bf16[2,2,2,144,288]{4,3,2,1,0:T(8,128)(2,1)}, u32[]{:S(2)}) copy-start(bf16[2,2,2,144,288]{4,3,2,1,0:T(8,128)(2,1)} %get-tuple-element.167) | copy-start | bytes 1990660
  124.4 10.7 %copy-start.25 = (f32[4,1,160]{2,1,0:T(1,128)}, f32[4,1,160]{2,1,0:T(1,128)S(1)}, u32[]{:S(2)}) copy-start(f32[4,1,160]{2,1,0:T(1,128)S(1)} %compare_convert_fusion.valid) | copy-start | bytes 7684
  136.0 28.8 %copy-start.56 = (bf16[4,160,288]{2,1,0:T(8,128)(2,1)}, bf16[4,160,288]{2,1,0:T(8,128)(2,1)S(1)}, u32[]{:S(2)}) copy-start(bf16[4,160,288]{2,1,0:T(8,128)(2,1)S(1)} %get-tuple-element.224.refs_13_) | copy-start | bytes 1105924
  136.0 28.8 %copy-start.150 = (bf16[2,2,2,144,1152]{4,3,2,1,0:T(8,128)(2,1)S(1)}, bf16[2,2,2,144,1152]{4,3,2,1,0:T(8,128)(2,1)}, u32[]{:S(2)}) copy-start(bf16[2,2,2,144,1152]{4,3,2,1,0:T(8,128)(2,1)} %get-tuple-element.171) | copy-start | bytes 7962628
  213.0 15.4 %copy-start.46 = (bf16[4,256,1152]{2,1,0:T(8,128)(2,1)}, bf16[4,256,1152]{2,1,0:T(8,128)(2,1)S(1)}, u32[]{:S(2)}) copy-start(bf16[4,256,1152]{2,1,0:T(8,128)(2,1)S(1)} %get-tuple-element.177.normed.refs_10_) | copy-start | bytes 7077892
  213.0 15.4 %copy-start.61 = (f32[256,1152]{1,0:T(8,128)}, f32[256,1152]{1,0:T(8,128)S(1)}, u32[]{:S(2)}) copy-start(f32[256,1152]{1,0:T(8,128)S(1)} %get-tuple-element.181.refs_1_) | copy-start | bytes 3538948
  229.7 42.3 %copy-start.55 = (bf16[4,256,288]{2,1,0:T(8,128)(2,1)}, bf16[4,256,288]{2,1,0:T(8,128)(2,1)S(1)}, u32[]{:S(2)}) copy-start(bf16[4,256,288]{2,1,0:T(8,128)(2,1)S(1)} %get-tuple-element.201.refs_13_) | copy-start | bytes 1769476
  272.0 7.0 %copy-start.37 = (bf16[4,256,1152]{2,1,0:T(8,128)(2,1)}, bf16[4,256,1152]{2,1,0:T(8,128)(2,1)S(1)}, u32[]{:S(2)}) copy-start(bf16[4,256,1152]{2,1,0:T(8,128)(2,1)S(1)} %get-tuple-element.184) | copy-start | bytes 7077892
  272.1 7.0 %copy-start.58 = (f32[256,1152]{1,0:T(8,128)}, f32[256,1152]{1,0:T(8,128)S(1)}, u32[]{:S(2)}) copy-start(f32[256,1152]{1,0:T(8,128)S(1)} %get-tuple-element.193.refs_2_) | copy-start | bytes 3538948
  272.1 7.0 %copy-start.59 = (f32[256,1152]{1,0:T(8,128)}, f32[256,1152]{1,0:T(8,128)S(1)}, u32[]{:S(2)}) copy-start(f32[256,1152]{1,0:T(8,128)S(1)} %get-tuple-element.187.refs_1_) | copy-start | bytes 3538948
  272.1 7.0 %copy-start.153 = (bf16[2,2,2,144,1152]{4,3,2,1,0:T(8,128)(2,1)S(1)}, bf16[2,2,2,144,1152]{4,3,2,1,0:T(8,128)(2,1)}, u32[]{:S(2)}) copy-start(bf16[2,2,2,144,1152]{4,3,2,1,0:T(8,128)(2,1)} %get-tuple-element.186) | copy-start | bytes 7962628
  283.9 31.9 %copy-start.154 = (bf16[2,2,2,144,1152]{4,3,2,1,0:T(8,128)(2,1)S(1)}, bf16[2,2,2,144,1152]{4,3,2,1,0:T(8,128)(2,1)}, u32[]{:S(2)}) copy-start(bf16[2,2,2,144,1152]{4,3,2,1,0:T(8,128)(2,1)} %get-tuple-element.186) | copy-start | bytes 7962628
  283.9 31.9 %copy-start.158 = (f32[4,256,1152]{2,1,0:T(8,128)S(1)}, f32[4,256,1152]{2,1,0:T(8,128)}, u32[]{:S(2)}) copy-start(f32[4,256,1152]{2,1,0:T(8,128)} %copy-done.157) | copy-start | bytes 14155780
  315.8 5.1 copy-start.152
  328.2 54.1 %copy-start.8 = (bf16[1152,1152]{1,0:T(8,128)(2,1)}, bf16[1152,1152]{1,0:T(8,128)(2,1)S(1)}, u32[]{:S(2)}) copy-start(bf16[1152,1152]{1,0:T(8,128)(2,1)S(1)} %fusion) | copy-start | bytes 7962628
  331.6 32.3 %copy-start.9 = (bf16[1152,1152]{1,0:T(8,128)(2,1)}, bf16[1152,1152]{1,0:T(8,128)(2,1)S(1)}, u32[]{:S(2)}) copy-start(bf16[1152,1152]{1,0:T(8,128)(2,1)S(1)} %fusion.1) | copy-start | bytes 7962628
  331.6 33.3 %copy-start.28 = (bf16[2,2,2,144,864]{4,3,2,1,0:T(8,128)(2,1)S(1)}, bf16[2,2,2,144,864]{4,3,2,1,0:T(8,128)(2,1)}, u32[]{:S(2)}) copy-start(bf16[2,2,2,144,864]{4,3,2,1,0:T(8,128)(2,1)} %get-tuple-element.178) | copy-start | bytes 5971972
  331.6 33.3 %copy-start.32 = (bf16[2,2,2,144,288]{4,3,2,1,0:T(8,128)(2,1)S(1)}, bf16[2,2,2,144,288]{4,3,2,1,0:T(8,128)(2,1)}, u32[]{:S(2)}) copy-start(bf16[2,2,2,144,288]{4,3,2,1,0:T(8,128)(2,1)} %get-tuple-element.179) | copy-start | bytes 1990660
  331.6 33.3 %copy-start.45 = (bf16[4,256,864]{2,1,0:T(8,128)(2,1)S(1)}, bf16[4,256,864]{2,1,0:T(8,128)(2,1)}, u32[]{:S(2)}) copy-start(bf16[4,256,864]{2,1,0:T(8,128)(2,1)} %copy-done.44) | copy-start | bytes 5308420
  364.9 14.6 %copy-start.40 = (bf16[4,256,1152]{2,1,0:T(8,128)(2,1)}, bf16[4,256,1152]{2,1,0:T(8,128)(2,1)S(1)}, u32[]{:S(2)}) copy-start(bf16[4,256,1152]{2,1,0:T(8,128)(2,1)S(1)} %get-tuple-element.195.grad_attn.refs_12_) | copy-start | bytes 7077892
  385.2 29.9 %copy-start.149 = (bf16[2,2,2,144,1152]{4,3,2,1,0:T(8,128)(2,1)S(1)}, bf16[2,2,2,144,1152]{4,3,2,1,0:T(8,128)(2,1)}, u32[]{:S(2)}) copy-start(bf16[2,2,2,144,1152]{4,3,2,1,0:T(8,128)(2,1)} %get-tuple-element.172) | copy-start | bytes 7962628
  385.2 29.9 %copy-start.156 = (f32[4,160,1152]{2,1,0:T(8,128)S(1)}, f32[4,160,1152]{2,1,0:T(8,128)}, u32[]{:S(2)}) copy-start(f32[4,160,1152]{2,1,0:T(8,128)} %copy-done.155) | copy-start | bytes 8847364
  415.1 14.3 %copy-start.10 = (bf16[1152,864]{1,0:T(8,128)(2,1)}, bf16[1152,864]{1,0:T(8,128)(2,1)S(1)}, u32[]{:S(2)}) copy-start(bf16[1152,864]{1,0:T(8,128)(2,1)S(1)} %get-tuple-element.209) | copy-start | bytes 5971972
  415.1 14.3 %copy-start.18 = (bf16[1152,288]{1,0:T(8,128)(2,1)}, bf16[1152,288]{1,0:T(8,128)(2,1)S(1)}, u32[]{:S(2)}) copy-start(bf16[1152,288]{1,0:T(8,128)(2,1)S(1)} %get-tuple-element.210) | copy-start | bytes 1990660
  429.4 35.3 %copy-start.26 = (f32[4,1,160]{2,1,0:T(1,128)S(1)}, f32[4,1,160]{2,1,0:T(1,128)}, u32[]{:S(2)}) copy-start(f32[4,1,160]{2,1,0:T(1,128)} %copy-done.25) | copy-start | bytes 7684
  429.4 35.3 %copy-start.30 = (bf16[2,2,2,144,864]{4,3,2,1,0:T(8,128)(2,1)S(1)}, bf16[2,2,2,144,864]{4,3,2,1,0:T(8,128)(2,1)}, u32[]{:S(2)}) copy-start(bf16[2,2,2,144,864]{4,3,2,1,0:T(8,128)(2,1)} %get-tuple-element.166) | copy-start | bytes 5971972
  429.5 35.3 %copy-start.34 = (bf16[2,2,2,144,288]{4,3,2,1,0:T(8,128)(2,1)S(1)}, bf16[2,2,2,144,288]{4,3,2,1,0:T(8,128)(2,1)}, u32[]{:S(2)}) copy-start(bf16[2,2,2,144,288]{4,3,2,1,0:T(8,128)(2,1)} %get-tuple-element.167) | copy-start | bytes 1990660
  429.5 35.3 %copy-start.53 = (bf16[4,160,864]{2,1,0:T(8,128)(2,1)S(1)}, bf16[4,160,864]{2,1,0:T(8,128)(2,1)}, u32[]{:S(2)}) copy-start(bf16[4,160,864]{2,1,0:T(8,128)(2,1)} %copy-done.52) | copy-start | bytes 3317764
  464.8 13.3 %copy-start.47 = (bf16[4,160,1152]{2,1,0:T(8,128)(2,1)}, bf16[4,160,1152]{2,1,0:T(8,128)(2,1)S(1)}, u32[]{:S(2)}) copy-start(bf16[4,160,1152]{2,1,0:T(8,128)(2,1)S(1)} %get-tuple-element.215.grad_attn.refs_12_) | copy-start | bytes 4423684
  464.8 15.4 %copy-start.137 = (f32[160,16]{0,1:T(8,128)S(1)}, f32[160,16]{0,1:T(8,128)}, u32[]{:S(2)}) copy-start(f32[160,16]{0,1:T(8,128)} %copy-done.136) | copy-start | bytes 30724
  527.1 35.5 %copy-start.135 = (bf16[32,144,1,1]{1,0,2,3:T(8,128)(2,1)S(1)}, bf16[32,144,1,1]{1,0,2,3:T(8,128)(2,1)}, u32[]{:S(2)}) copy-start(bf16[32,144,1,1]{1,0,2,3:T(8,128)(2,1)} %reshape.1198) | copy-start | bytes 27652
  569.2 4.7 copy-start.130
  569.2 4.8 copy-start.103
  569.3 4.8 copy-start.104
  569.3 4.8 copy-start.105
  569.3 4.8 copy-start.106
  598.0 24.6 %copy-start.142 = (f32[8,4]{1,0:T(8,128)S(1)}, f32[8,4]{1,0:T(8,128)}, u32[]{:S(2)}) copy-start(f32[8,4]{1,0:T(8,128)} %get-tuple-element.352) | copy-start | bytes 388
  598.0 24.7 %copy-start.144 = (f32[128]{0:T(128)S(1)}, f32[128]{0:T(128)}, u32[]{:S(2)}) copy-start(f32[128]{0:T(128)} %copy-done.143) | copy-start | bytes 1540
  598.0 32.0 %copy-start.14 = (bf16[2,144,864]{2,1,0:T(8,128)(2,1)S(1)}, bf16[2,144,864]{2,1,0:T(8,128)(2,1)}, u32[]{:S(2)}) copy-start(bf16[2,144,864]{2,1,0:T(8,128)(2,1)} %get-tuple-element.276.refs_5_) | copy-start | bytes 1492996
  618.0 12.0 %copy-start.4 = (bf16[2,144,1152]{2,1,0:T(8,128)(2,1)S(1)}, bf16[2,144,1152]{2,1,0:T(8,128)(2,1)}, u32[]{:S(2)}) copy-start(bf16[2,144,1152]{2,1,0:T(8,128)(2,1)} %get-tuple-element.278.refs_7_) | copy-start | bytes 1990660
  618.1 12.0 %copy-start.5 = (bf16[2,144,1152]{2,1,0:T(8,128)(2,1)S(1)}, bf16[2,144,1152]{2,1,0:T(8,128)(2,1)}, u32[]{:S(2)}) copy-start(bf16[2,144,1152]{2,1,0:T(8,128)(2,1)} %get-tuple-element.279.refs_8_) | copy-start | bytes 1990660
  618.1 12.0 %copy-start.6 = (bf16[2,144,1152]{2,1,0:T(8,128)(2,1)S(1)}, bf16[2,144,1152]{2,1,0:T(8,128)(2,1)}, u32[]{:S(2)}) copy-start(bf16[2,144,1152]{2,1,0:T(8,128)(2,1)} %get-tuple-element.275.refs_4_) | copy-start | bytes 1990660
  618.1 12.0 %copy-start.7 = (bf16[2,144,1152]{2,1,0:T(8,128)(2,1)S(1)}, bf16[2,144,1152]{2,1,0:T(8,128)(2,1)}, u32[]{:S(2)}) copy-start(bf16[2,144,1152]{2,1,0:T(8,128)(2,1)} %get-tuple-element.274.refs_3_) | copy-start | bytes 1990660
  618.1 12.0 %copy-start.22 = (bf16[2,144,288]{2,1,0:T(8,128)(2,1)S(1)}, bf16[2,144,288]{2,1,0:T(8,128)(2,1)}, u32[]{:S(2)}) copy-start(bf16[2,144,288]{2,1,0:T(8,128)(2,1)} %get-tuple-element.277.refs_6_) | copy-start | bytes 497668
  662.1 5.6 copy-start.82
  664.3 5.4 copy-start.80
  664.3 6.1 copy-start.81
  670.5 5.9 copy-start.122
  670.5 5.9 copy-start.138
  670.5 5.9 copy-start.139
  670.5 5.9 copy-start.140
  670.5 6.6 copy-start.69
  670.5 6.6 copy-start.70
  670.5 6.6 copy-start.85
  670.5 6.6 copy-start.86
  670.5 6.9 %copy-start.87 = (f32[1256,288]{0,1:T(8,128)S(1)}, f32[1256,288]{0,1:T(8,128)}, u32[]{:S(2)}) copy-start(f32[1256,288]{0,1:T(8,128)} %param.62) | copy-start | bytes 4340740
  (95 other events, 214.4 us)

commit v5 on v4

--- a/solution.py
+++ b/solution.py
@@ -1280,11 +1280,11 @@
     return [
         attend(0, ENTER),
         attend(0, STRAIGHT) + expand(0, ENTER),
-        attend(0, CROSS, RELAY) + contract(0, ENTER),
-        expand(0, STRAIGHT, CROSS, RELAY) + attend(1, ENTER),
-        contract(0, STRAIGHT, CROSS, RELAY) + expand(1, ENTER),
-        attend(1, STRAIGHT, CROSS, RELAY) + expand(1, STRAIGHT) + contract(1, ENTER),
-        contract(1, STRAIGHT, CROSS, RELAY) + expand(1, CROSS, RELAY),
+        attend(0, CROSS, RELAY) + contract(0, ENTER) + expand(0, STRAIGHT),
+        expand(0, CROSS, RELAY) + contract(0, STRAIGHT) + attend(1, ENTER),
+        contract(0, CROSS, RELAY) + attend(1, STRAIGHT) + expand(1, ENTER),
+        attend(1, CROSS, RELAY) + expand(1, STRAIGHT, CROSS) + contract(1, ENTER),
+        contract(1, STRAIGHT, CROSS, RELAY) + expand(1, RELAY),
         [],
         feed(1, FAR) + feed(1, NEAR),
         feed(1, PASS),

time: 692 us -> 684 us (0.988)
  Pallas kernels: 501 us -> 494 us
    pallas_call x16, Pallas kernels: 454 us -> 447 us  [travel(): pl.pallas_call(partial(kernel, parts), out_shape=[shape for part in parts...]
where the time goes in v5:
time: 684 us; the launch traced here: 675 us
  Pallas kernels  494 us (72%)
  matrix products  61.7 us (9%)
  other arithmetic  59.1 us (9%)
  local copies, waits for them, and re-layouts  51 us (7%)
  between operations  9.36 us (1%)
    pallas_call x16, Pallas kernels, travel(): pl.pallas_call(partial(kernel, parts), out_shape=[shape for part in parts...  447 us
    dot_general x16, matrix products, low_dot(): return jnp.einsum(spec, left, right, preferred_element_type=jnp.float32)  47.6 us
    pallas_call x4, Pallas kernels, by_image(): pl.pallas_call(body, grid=(images,), out_shape=made, in_specs=[block(arra...  46.9 us
    unnamed x318, local copies, waits for them, and re-layouts  35.9 us
    add x7, other arithmetic, adam(): average = average_decay * average + (1.0 - average_decay) * fresh  21.3 us

profile of v5, /device:TPU:0, one launch (start us, length us, event | category | flops | bytes accessed | tf_op | source)
XLA Modules:
  0.0 674.8 jit_solution(14954264181754495462)
XLA Ops:
  0.7 1.6 convert_element_type.1054
  4.6 15.0 %shard_map.562 = (f32[8,8,144]{2,1,0:T(8,128)S(1)}, bf16[2,2,2,144,864]{4,3,2,1,0:T(8,128)(2,1)}, bf16[2,2,2,144,288]{4,3,2,1,0:T(8,128)(2,1)}) custom-call(f32[2,8,144]{2,1,0:T(8,128)S(1)} %pad.21.refs_0_, bf16[144,864]{1,0:T(8,128)(2,1)S(1)} %convert_element_type.1055.refs_1_, bf16[144,288]{1,0:T(8,128)(2,1)S(1)} %get-tuple-element.363.refs_2_), custom_call_target="tpu_custom_call" | custom-call | flops 20000000000 | bytes 1024 | tf_op jit(solution)/shard_map/pallas_call | solution.py:1041
  20.3 2.3 multiply_cosine_fusion
  24.7 1.9 fusion.29
  26.6 1.9 convert_bitcast_fusion
  28.9 2.2 reshape.1189
  31.2 1.6 fusion.154.refs_0_
  32.9 27.4 %shard_map.563 = (f32[8,4,3456]{2,1,0:T(4,128)S(1)}, bf16[2,2,2,144,864]{4,3,2,1,0:T(8,128)(2,1)}, bf16[2,2,2,144,288]{4,3,2,1,0:T(8,128)(2,1)}, bf16[2,2,2,144,1152]{4,3,2,1,0:T(8,128)(2,1)}) custom-call(f32[8,4,3456]{2,1,0:T(4,128)S(1)} %fusion.154.refs_0_, ...), custom_call_target="tpu_custom_call", output_to_operand_aliasing={{1}: (1, {}), {2}: (2, {})} | custom-call | flops 20000000000 | bytes 1024 | tf_op jit(solution)/shard_map/pallas_call | solution.py:1041
  61.2 32.8 %shard_map.564 = (f32[4,12,288]{2,1,0:T(8,128)S(1)}, f32[8,24,288]{2,1,0:T(8,128)S(1)}, bf16[4,48,288]{2,1,0:T(8,128)(2,1)S(1)}, bf16[2,2,2,144,864]{4,3,2,1,0:T...) custom-call(f32[4,12,288]{2,1,0:T(8,128)S(1)} %reshape.1116.refs_0_,, ...), custom_call_target="tpu_custom_call", output_to_operand_aliasing={{3}: (3, {}), {4}: (4, {}), {6}: (6, {})} | custom-call | flops 20000000000 | bytes 1024 | tf_op jit(solution)/shard_map/pallas_call | solution.py:1041
  96.9 25.9 %shard_map.565 = (bf16[4,160,1152]{2,1,0:T(8,128)(2,1)S(1)}, bf16[2,2,2,144,1152]{4,3,2,1,0:T(8,128)(2,1)}, bf16[2,2,2,144,1152]{4,3,2,1,0:T(8,128)(2,1)}, bf16[...) custom-call(f32[160,1152]{1,0:T(8,128)} %convolution_add_fusion.refs_0_.r, ...), custom_call_target="tpu_custom_call", output_to_operand_aliasing={{1}: (2, {}), {2}: (3, {})} | custom-call | flops 20000000000 | bytes 1024 | tf_op jit(solution)/shard_map/pallas_call | solution.py:1041
  124.9 1.6 copy-done.29
  126.5 1.4 copy-done.51
  127.9 7.7 %shard_map.566 = (bf16[4,160,864]{2,1,0:T(8,128)(2,1)S(1)}, bf16[4,160,288]{2,1,0:T(8,128)(2,1)S(1)}, bf16[4,160,1152]{2,1,0:T(8,128)(2,1)S(1)}) custom-call(bf16[4,160,1152]{2,1,0:T(8,128)(2,1)S(1)} %copy-done.51, f32[4,1,160]{2,1,0:T(1,128)S(1)} %compare_convert_fusion.valid, bf16[1152,864]{1,0:T(8,128)(2,1)S(1)} %bitcast.356, bf16[1152,288]{1,0:T(8,128)(2,1)S(1)} %bitcast.360), custom_call_target="tpu_custom_call" | custom-call | flops 5000000000 | bytes 1024 | tf_op jit(solution)/shard_map/pallas_call | solution.py:1209
  136.6 28.5 %shard_map.567 = (bf16[4,160,1152]{2,1,0:T(8,128)(2,1)S(1)}, f32[160,1152]{1,0:T(8,128)S(1)}, f32[160,1152]{1,0:T(8,128)S(1)}, bf16[2,2,2,144,1152]{4,3,2,1,0:T(...) custom-call(bf16[4,160,1152]{2,1,0:T(8,128)(2,1)S(1)} %get-tuple-ele, ...), custom_call_target="tpu_custom_call", output_to_operand_aliasing={{3}: (3, {}), {4}: (4, {}), {5}: (5, {})} | custom-call | flops 20000000000 | bytes 1024 | tf_op jit(solution)/shard_map/pallas_call | solution.py:1041
  165.2 2.2 fusion.156
  168.0 3.8 convolution_convert_fusion.3.refs_0_
  172.2 2.7 multiply_add_fusion.9.refs_5_
  176.4 36.8 %shard_map.568 = (bf16[4,256,1152]{2,1,0:T(8,128)(2,1)S(1)}, f32[160,1152]{1,0:T(8,128)S(1)}, f32[160,1152]{1,0:T(8,128)}, f32[256,1152]{1,0:T(8,128)S(1)}, f32[...) custom-call(bf16[4,160,1152]{2,1,0:T(8,128)(2,1)S(1)} %copy-done.39,, ...), custom_call_target="tpu_custom_call", output_to_operand_aliasing={{6}: (10, {}), {7}: (11, {}), {8}: (12, {})} | custom-call | flops 20000000000 | bytes 1024 | tf_op jit(solution)/shard_map/pallas_call | solution.py:1041
  214.1 2.9 copy-done.27
  218.1 11.4 %shard_map.569 = (bf16[4,256,864]{2,1,0:T(8,128)(2,1)S(1)}, bf16[4,256,288]{2,1,0:T(8,128)(2,1)S(1)}, bf16[4,256,1152]{2,1,0:T(8,128)(2,1)S(1)}) custom-call(bf16[4,256,1152]{2,1,0:T(8,128)(2,1)S(1)} %get-tuple-element.185.normed.refs_10_, f32[4,1,256]{2,1,0:T(1,128)S(1)} %broadcast_in_dim.7.valid, bf16[1152,864]{1,0:T(8,128)(2,1)S(1)} %bitcast.354, ...), custom_call_target="tpu_custom_call" | custom-call | flops 5000000000 | bytes 1024 | tf_op jit(solution)/shard_map/pallas_call | solution.py:1209
  230.8 33.6 %shard_map.570 = (bf16[4,256,1152]{2,1,0:T(8,128)(2,1)S(1)}, f32[256,1152]{1,0:T(8,128)S(1)}, f32[256,1152]{1,0:T(8,128)S(1)}, bf16[2,2,2,144,1152]{4,3,2,1,0:T(8,128)(2,1)}, bf16[2,2,2,144,1152]{4,3,2,1,0:T(8,128)(2,1)}) custom-call(bf16[4,256,1152]{2,1,0:T(8,128)(2,1)S(1)} %get-tuple-element.188.refs_0_, ...), custom_call_target="tpu_custom_call", output_to_operand_aliasing={{3}: (3, {}), {4}: (4, {})} | custom-call | flops 20000000000 | bytes 1024 | tf_op jit(solution)/shard_map/pallas_call | solution.py:1041
  264.4 7.0 %fusion.157 = f32[4,256,1152]{2,1,0:T(8,128)S(1)} fusion(bf16[4,256,1152]{2,1,0:T(8,128)(2,1)S(1)} %get-tuple-element.192, bf16[1152,1152,1]{1,0,2:T(8,128)(2,1)} %bitcast.371), kind=kOutput, calls=%fused_computation.297 | convolution fusion | flops 2717908992 | bytes 9732096 | tf_op jit(solution)/shard_map/bld,df->blf/dot_general | solution.py:1223
  271.4 4.5 convolution_convert_fusion.1.refs_0_
  276.2 31.1 %shard_map.571 = (bf16[4,256,1152]{2,1,0:T(8,128)(2,1)S(1)}, f32[256,1152]{1,0:T(8,128)S(1)}, f32[1,1152]{1,0:T(1,128)S(1)}, f32[16,1152]{1,0:T(8,128)S(1)}, f32[1,1]{1,0:T(1,128)}) custom-call(bf16[4,256,1152]{2,1,0:T(8,128)(2,1)S(1)} %convolution_convert_fusion.1.refs_0_, f32[256,1152]{1,0:T(8,128)} %copy-done.59, ...), custom_call_target="tpu_custom_call" | custom-call | flops 20000000000 | bytes 1024 | tf_op jit(solution)/shard_map/pallas_call | solution.py:1041
  308.4 5.1 fusion.10
  313.5 4.0 convolution_convert_fusion.refs_0_
  317.5 3.3 fusion
  320.8 3.4 fusion.1
  324.3 32.4 %shard_map.572 = (bf16[4,256,1152]{2,1,0:T(8,128)(2,1)S(1)}, f32[256,1152]{1,0:T(8,128)S(1)}, f32[3,1152]{1,0:T(4,128)S(1)}, bf16[1,1,144,1152]{3,2,1,0:T(8,128)...) custom-call(bf16[4,256,1152]{2,1,0:T(8,128)(2,1)S(1)} %convolution_c, ...), custom_call_target="tpu_custom_call" | custom-call | flops 20000000000 | bytes 1024 | tf_op jit(solution)/shard_map/pallas_call | solution.py:1041
  357.7 14.6 %shard_map.573 = (bf16[4,256,864]{2,1,0:T(8,128)(2,1)S(1)}, bf16[4,256,1152]{2,1,0:T(8,128)(2,1)S(1)}) custom-call(bf16[4,256,864]{2,1,0:T(8,128)(2,1)S(1)} %copy-done.45, f32[4,1,256]{2,1,0:T(1,128)S(1)} %broadcast_in_dim.7.valid, bf16[4,256,1152]{2,1,0:T(8,128)(2,1)S(1)} %get-tuple-element.203.grad_attn.refs_12_, bf16[1152,864]{1,0:T(8,128)(2,1)S(1)} %bitcast.355, ...), custom_call_target="tpu_custom_call" | custom-call | flops 5000000000 | bytes 1024 | tf_op jit(solution)/shard_map/pallas_call | solution.py:1209
  372.3 1.4 copy-done.41
  375.1 1.4 fusion.54
  376.5 1.4 fusion.52
  378.0 29.3 %shard_map.574 = (bf16[4,160,1152]{2,1,0:T(8,128)(2,1)S(1)}, f32[160,1152]{1,0:T(8,128)S(1)}, f32[4,1152]{1,0:T(4,128)S(1)}, bf16[1152,864]{1,0:T(8,128)(2,1)S(1...) custom-call(bf16[4,256,1152]{2,1,0:T(8,128)(2,1)S(1)} %copy-done.42,, ...), custom_call_target="tpu_custom_call" | custom-call | flops 20000000000 | bytes 1024 | tf_op jit(solution)/shard_map/pallas_call | solution.py:1041
  407.3 3.1 fusion.17
  410.5 2.3 convolution_convert_fusion.2.refs_0_
  412.8 2.4 fusion.2
  415.4 2.5 fusion.3
  418.0 3.5 fusion.43
  421.6 34.5 %shard_map.575 = (bf16[4,160,1152]{2,1,0:T(8,128)(2,1)S(1)}, f32[160,1152]{1,0:T(8,128)S(1)}, f32[3,1152]{1,0:T(4,128)S(1)}, bf16[1,1,144,1152]{3,2,1,0:T(8,128)...) custom-call(bf16[4,160,1152]{2,1,0:T(8,128)(2,1)S(1)} %convolution_c, ...), custom_call_target="tpu_custom_call" | custom-call | flops 20000000000 | bytes 1024 | tf_op jit(solution)/shard_map/pallas_call | solution.py:1041
  457.1 13.3 %shard_map.576 = (bf16[4,160,864]{2,1,0:T(8,128)(2,1)S(1)}, bf16[4,160,1152]{2,1,0:T(8,128)(2,1)S(1)}) custom-call(bf16[4,160,864]{2,1,0:T(8,128)(2,1)S(1)} %copy-done.53, f32[4,1,160]{2,1,0:T(1,128)S(1)} %copy-done.26, bf16[4,160,1152]{2,1,0:T(8,128)(2,1)S(1)} %get-tuple-element.223.grad_attn.refs_12_, bf16[1152,864]{1,0:T(8,128)(2,1)S(1)} %bitcast.357, ...), custom_call_target="tpu_custom_call" | custom-call | flops 5000000000 | bytes 1024 | tf_op jit(solution)/shard_map/pallas_call | solution.py:1209
  472.6 1.4 fusion.46
  474.1 1.6 fusion.44
  475.7 1.4 fusion.73
  478.2 33.9 %shard_map.577 = (f32[4,48,288]{2,1,0:T(8,128)S(1)}, bf16[1152,864]{1,0:T(8,128)(2,1)S(1)}, bf16[1152,288]{1,0:T(8,128)(2,1)S(1)}, bf16[1,144,1152]{2,1,0:T(8,12...) custom-call(bf16[4,160,1152]{2,1,0:T(8,128)(2,1)S(1)} %copy-done.49,, ...), custom_call_target="tpu_custom_call" | custom-call | flops 20000000000 | bytes 1024 | tf_op jit(solution)/shard_map/pallas_call | solution.py:1041
  514.5 1.8 fusion.39
  516.5 1.4 fusion.72
  519.2 34.1 %shard_map.578 = (f32[8,4,3456]{2,1,0:T(4,128)S(1)}, bf16[8,48,288]{2,1,0:T(8,128)(2,1)S(1)}, bf16[1,1,144,864]{3,2,1,0:T(8,128)(2,1)}, bf16[1,1,144,864]{3,2,1,...) custom-call(f32[4,3456]{1,0:T(4,128)S(1)} %reshape.1134.refs_0_, ...), custom_call_target="tpu_custom_call" | custom-call | flops 20000000000 | bytes 1024 | tf_op jit(solution)/shard_map/pallas_call | solution.py:1041
  553.3 1.4 reshape.1137
  554.7 4.5 multiply_reduce_fusion
  561.5 3.4 fusion.26.refs_0_
  566.6 20.5 %shard_map.579 = (f32[4,32,144]{2,1,0:T(8,128)S(1)}, bf16[1,144,864]{2,1,0:T(8,128)(2,1)}, bf16[1,144,864]{2,1,0:T(8,128)(2,1)}, bf16[1,144,288]{2,1,0:T(8,128)(...) custom-call(f32[32,144]{1,0:T(8,128)S(1)} %fusion.26.refs_0_, ...), custom_call_target="tpu_custom_call" | custom-call | flops 20000000000 | bytes 1024 | tf_op jit(solution)/shard_map/pallas_call | solution.py:1041
  587.2 1.8 fusion.66
  590.2 20.0 %shard_map.580 = (f32[8,32,144]{2,1,0:T(8,128)S(1)}, bf16[2,144,864]{2,1,0:T(8,128)(2,1)}, bf16[2,144,288]{2,1,0:T(8,128)(2,1)}) custom-call(f32[32,144]{1,0:T(8,128)S(1)} %reduce_sum.90.refs_0_, bf16[2,144,864]{2,1,0:T(8,128)(2,1)S(1)} %pad_maximum_fusion.7.refs_1_, bf16[2,144,288]{2,1,0:T(8,128)(2,1)S(1)} %pad_maximum_fusion.9.refs_2_), custom_call_target="tpu_custom_call" | custom-call | flops 20000000000 | bytes 1024 | tf_op jit(solution)/shard_map/pallas_call | solution.py:1041
  611.1 1.8 reshape.1138
  615.0 4.1 multiply_reduce_fusion.1
  624.3 11.0 %shard_map.581 = f32[32,8,128]{2,1,0:T(8,128)S(1)} custom-call(f32[8,128]{1,0:T(8,128)S(1)} %pad.25.refs_0_, bf16[2,144,864]{2,1,0:T(8,128)(2,1)S(1)} %copy-done.15, bf16[2,144,288]{2,1,0:T(8,128)(2,1)S(1)} %copy-done.23, bf16[2,144,1152]{2,1,0:T(8,128)(2,1)S(1)} %copy-done.7, bf16[2,144,1152]{2,1,0:T(8,128)(2,1)S(1)} %copy-done.6, ...), custom_call_target="tpu_custom_call" | custom-call | flops 20000000000 | bytes 1024 | tf_op jit(solution)/shard_map/pallas_call | solution.py:1041
  642.2 3.2 multiply_add_fusion.5
  646.8 1.5 multiply_add_fusion.10
  650.9 3.2 multiply_add_fusion.4
  656.7 3.3 multiply_add_fusion.3
  660.0 1.3 copy-done.68
  662.9 5.8 multiply_add_fusion
  669.8 3.5 multiply_add_fusion.1
  (438 shorter events, 54.0 us)
Async XLA Ops:
  0.7 275.4 %copy-start = (f32[4,256,16]{1,2,0:T(8,128)S(1)}, f32[4,256,16]{1,2,0:T(8,128)}, u32[]{:S(2)}) copy-start(f32[4,256,16]{1,2,0:T(8,128)} %param.36) | copy-start | bytes 196612
  4.6 18.1 %copy-start.147 = (s32[4]{0:T(128)S(1)}, s32[4]{0:T(128)}, u32[]{:S(2)}) copy-start(s32[4]{0:T(128)} %param.38) | copy-start | bytes 52
  22.7 10.1 %copy-start.71 = (f32[256,576]{1,0:T(8,128)}, f32[256,576]{1,0:T(8,128)S(1)}, u32[]{:S(2)}) copy-start(f32[256,576]{1,0:T(8,128)S(1)} %get-tuple-element.368) | copy-start | bytes 1769476
  32.9 27.6 %copy-start.141 = (f32[4,1152]{1,0:T(4,128)S(1)}, f32[4,1152]{1,0:T(4,128)}, u32[]{:S(2)}) copy-start(f32[4,1152]{1,0:T(4,128)} %param.41) | copy-start | bytes 55300
  32.9 28.1 %copy-start.121 = (f32[33,288]{1,0:T(8,128)S(1)}, f32[33,288]{1,0:T(8,128)}, u32[]{:S(2)}) copy-start(f32[33,288]{1,0:T(8,128)} %param.47) | copy-start | bytes 114052
  32.9 28.1 %copy-start.77 = (f32[2,1152,144]{1,2,0:T(8,128)S(1)}, f32[2,1152,144]{1,2,0:T(8,128)}, u32[]{:S(2)}) copy-start(f32[2,1152,144]{1,2,0:T(8,128)} %param.45) | copy-start | bytes 3981316
  61.2 34.0 %copy-start.79 = (f32[160,1152]{1,0:T(8,128)S(1)}, f32[160,1152]{1,0:T(8,128)}, u32[]{:S(2)}) copy-start(f32[160,1152]{1,0:T(8,128)} %fusion.29) | copy-start | bytes 2211844
  94.0 82.2 %copy-start.17 = (f32[8,24,288]{2,1,0:T(8,128)}, f32[8,24,288]{2,1,0:T(8,128)S(1)}, u32[]{:S(2)}) copy-start(f32[8,24,288]{2,1,0:T(8,128)S(1)} %get-tuple-element.171) | copy-start | bytes 663556
  96.9 28.0 %copy-start.33 = (bf16[2,2,2,144,288]{4,3,2,1,0:T(8,128)(2,1)S(1)}, bf16[2,2,2,144,288]{4,3,2,1,0:T(8,128)(2,1)}, u32[]{:S(2)}) copy-start(bf16[2,2,2,144,288]{4,3,2,1,0:T(8,128)(2,1)} %get-tuple-element.173) | copy-start | bytes 1990660
  124.9 10.7 %copy-start.25 = (f32[4,1,160]{2,1,0:T(1,128)}, f32[4,1,160]{2,1,0:T(1,128)S(1)}, u32[]{:S(2)}) copy-start(f32[4,1,160]{2,1,0:T(1,128)S(1)} %compare_convert_fusion.valid) | copy-start | bytes 7684
  136.6 28.6 %copy-start.56 = (bf16[4,160,288]{2,1,0:T(8,128)(2,1)}, bf16[4,160,288]{2,1,0:T(8,128)(2,1)S(1)}, u32[]{:S(2)}) copy-start(bf16[4,160,288]{2,1,0:T(8,128)(2,1)S(1)} %get-tuple-element.232.refs_13_) | copy-start | bytes 1105924
  136.6 28.6 %copy-start.151 = (bf16[2,2,2,144,1152]{4,3,2,1,0:T(8,128)(2,1)S(1)}, bf16[2,2,2,144,1152]{4,3,2,1,0:T(8,128)(2,1)}, u32[]{:S(2)}) copy-start(bf16[2,2,2,144,1152]{4,3,2,1,0:T(8,128)(2,1)} %get-tuple-element.179) | copy-start | bytes 7962628
  214.1 15.4 %copy-start.46 = (bf16[4,256,1152]{2,1,0:T(8,128)(2,1)}, bf16[4,256,1152]{2,1,0:T(8,128)(2,1)S(1)}, u32[]{:S(2)}) copy-start(bf16[4,256,1152]{2,1,0:T(8,128)(2,1)S(1)} %get-tuple-element.185.normed.refs_10_) | copy-start | bytes 7077892
  214.1 15.4 %copy-start.61 = (f32[256,1152]{1,0:T(8,128)}, f32[256,1152]{1,0:T(8,128)S(1)}, u32[]{:S(2)}) copy-start(f32[256,1152]{1,0:T(8,128)S(1)} %get-tuple-element.189.refs_1_) | copy-start | bytes 3538948
  230.8 33.6 %copy-start.55 = (bf16[4,256,288]{2,1,0:T(8,128)(2,1)}, bf16[4,256,288]{2,1,0:T(8,128)(2,1)S(1)}, u32[]{:S(2)}) copy-start(bf16[4,256,288]{2,1,0:T(8,128)(2,1)S(1)} %get-tuple-element.209.refs_13_) | copy-start | bytes 1769476
  264.4 7.0 %copy-start.37 = (bf16[4,256,1152]{2,1,0:T(8,128)(2,1)}, bf16[4,256,1152]{2,1,0:T(8,128)(2,1)S(1)}, u32[]{:S(2)}) copy-start(bf16[4,256,1152]{2,1,0:T(8,128)(2,1)S(1)} %get-tuple-element.192) | copy-start | bytes 7077892
  264.4 7.0 %copy-start.58 = (f32[256,1152]{1,0:T(8,128)}, f32[256,1152]{1,0:T(8,128)S(1)}, u32[]{:S(2)}) copy-start(f32[256,1152]{1,0:T(8,128)S(1)} %get-tuple-element.201.refs_2_) | copy-start | bytes 3538948
  264.4 7.0 %copy-start.59 = (f32[256,1152]{1,0:T(8,128)}, f32[256,1152]{1,0:T(8,128)S(1)}, u32[]{:S(2)}) copy-start(f32[256,1152]{1,0:T(8,128)S(1)} %get-tuple-element.195.refs_1_) | copy-start | bytes 3538948
  264.4 7.0 %copy-start.153 = (bf16[2,2,2,144,1152]{4,3,2,1,0:T(8,128)(2,1)S(1)}, bf16[2,2,2,144,1152]{4,3,2,1,0:T(8,128)(2,1)}, u32[]{:S(2)}) copy-start(bf16[2,2,2,144,1152]{4,3,2,1,0:T(8,128)(2,1)} %get-tuple-element.194) | copy-start | bytes 7962628
  276.2 32.2 %copy-start.154 = (bf16[2,2,2,144,1152]{4,3,2,1,0:T(8,128)(2,1)S(1)}, bf16[2,2,2,144,1152]{4,3,2,1,0:T(8,128)(2,1)}, u32[]{:S(2)}) copy-start(bf16[2,2,2,144,1152]{4,3,2,1,0:T(8,128)(2,1)} %get-tuple-element.194) | copy-start | bytes 7962628
  276.2 32.2 %copy-start.158 = (f32[4,256,1152]{2,1,0:T(8,128)S(1)}, f32[4,256,1152]{2,1,0:T(8,128)}, u32[]{:S(2)}) copy-start(f32[4,256,1152]{2,1,0:T(8,128)} %copy-done.157) | copy-start | bytes 14155780
  308.4 5.1 copy-start.148
  320.8 54.3 %copy-start.8 = (bf16[1152,1152]{1,0:T(8,128)(2,1)}, bf16[1152,1152]{1,0:T(8,128)(2,1)S(1)}, u32[]{:S(2)}) copy-start(bf16[1152,1152]{1,0:T(8,128)(2,1)S(1)} %fusion) | copy-start | bytes 7962628
  324.2 32.4 %copy-start.9 = (bf16[1152,1152]{1,0:T(8,128)(2,1)}, bf16[1152,1152]{1,0:T(8,128)(2,1)S(1)}, u32[]{:S(2)}) copy-start(bf16[1152,1152]{1,0:T(8,128)(2,1)S(1)} %fusion.1) | copy-start | bytes 7962628
  324.2 33.5 %copy-start.28 = (bf16[2,2,2,144,864]{4,3,2,1,0:T(8,128)(2,1)S(1)}, bf16[2,2,2,144,864]{4,3,2,1,0:T(8,128)(2,1)}, u32[]{:S(2)}) copy-start(bf16[2,2,2,144,864]{4,3,2,1,0:T(8,128)(2,1)} %get-tuple-element.186) | copy-start | bytes 5971972
  324.2 33.4 %copy-start.32 = (bf16[2,2,2,144,288]{4,3,2,1,0:T(8,128)(2,1)S(1)}, bf16[2,2,2,144,288]{4,3,2,1,0:T(8,128)(2,1)}, u32[]{:S(2)}) copy-start(bf16[2,2,2,144,288]{4,3,2,1,0:T(8,128)(2,1)} %get-tuple-element.187) | copy-start | bytes 1990660
  324.2 33.4 %copy-start.45 = (bf16[4,256,864]{2,1,0:T(8,128)(2,1)S(1)}, bf16[4,256,864]{2,1,0:T(8,128)(2,1)}, u32[]{:S(2)}) copy-start(bf16[4,256,864]{2,1,0:T(8,128)(2,1)} %copy-done.44) | copy-start | bytes 5308420
  357.7 14.6 %copy-start.40 = (bf16[4,256,1152]{2,1,0:T(8,128)(2,1)}, bf16[4,256,1152]{2,1,0:T(8,128)(2,1)S(1)}, u32[]{:S(2)}) copy-start(bf16[4,256,1152]{2,1,0:T(8,128)(2,1)S(1)} %get-tuple-element.203.grad_attn.refs_12_) | copy-start | bytes 7077892
  378.0 29.3 %copy-start.150 = (bf16[2,2,2,144,1152]{4,3,2,1,0:T(8,128)(2,1)S(1)}, bf16[2,2,2,144,1152]{4,3,2,1,0:T(8,128)(2,1)}, u32[]{:S(2)}) copy-start(bf16[2,2,2,144,1152]{4,3,2,1,0:T(8,128)(2,1)} %get-tuple-element.180) | copy-start | bytes 7962628
  378.0 29.3 %copy-start.156 = (f32[4,160,1152]{2,1,0:T(8,128)S(1)}, f32[4,160,1152]{2,1,0:T(8,128)}, u32[]{:S(2)}) copy-start(f32[4,160,1152]{2,1,0:T(8,128)} %copy-done.155) | copy-start | bytes 8847364
  407.3 14.3 %copy-start.10 = (bf16[1152,864]{1,0:T(8,128)(2,1)}, bf16[1152,864]{1,0:T(8,128)(2,1)S(1)}, u32[]{:S(2)}) copy-start(bf16[1152,864]{1,0:T(8,128)(2,1)S(1)} %get-tuple-element.217) | copy-start | bytes 5971972
  407.3 14.3 %copy-start.18 = (bf16[1152,288]{1,0:T(8,128)(2,1)}, bf16[1152,288]{1,0:T(8,128)(2,1)S(1)}, u32[]{:S(2)}) copy-start(bf16[1152,288]{1,0:T(8,128)(2,1)S(1)} %get-tuple-element.218) | copy-start | bytes 1990660
  421.6 35.5 %copy-start.26 = (f32[4,1,160]{2,1,0:T(1,128)S(1)}, f32[4,1,160]{2,1,0:T(1,128)}, u32[]{:S(2)}) copy-start(f32[4,1,160]{2,1,0:T(1,128)} %copy-done.25) | copy-start | bytes 7684
  421.6 35.5 %copy-start.30 = (bf16[2,2,2,144,864]{4,3,2,1,0:T(8,128)(2,1)S(1)}, bf16[2,2,2,144,864]{4,3,2,1,0:T(8,128)(2,1)}, u32[]{:S(2)}) copy-start(bf16[2,2,2,144,864]{4,3,2,1,0:T(8,128)(2,1)} %get-tuple-element.172) | copy-start | bytes 5971972
  421.6 35.5 %copy-start.34 = (bf16[2,2,2,144,288]{4,3,2,1,0:T(8,128)(2,1)S(1)}, bf16[2,2,2,144,288]{4,3,2,1,0:T(8,128)(2,1)}, u32[]{:S(2)}) copy-start(bf16[2,2,2,144,288]{4,3,2,1,0:T(8,128)(2,1)} %get-tuple-element.173) | copy-start | bytes 1990660
  421.6 35.4 %copy-start.53 = (bf16[4,160,864]{2,1,0:T(8,128)(2,1)S(1)}, bf16[4,160,864]{2,1,0:T(8,128)(2,1)}, u32[]{:S(2)}) copy-start(bf16[4,160,864]{2,1,0:T(8,128)(2,1)} %copy-done.52) | copy-start | bytes 3317764
  457.1 13.3 %copy-start.47 = (bf16[4,160,1152]{2,1,0:T(8,128)(2,1)}, bf16[4,160,1152]{2,1,0:T(8,128)(2,1)S(1)}, u32[]{:S(2)}) copy-start(bf16[4,160,1152]{2,1,0:T(8,128)(2,1)S(1)} %get-tuple-element.223.grad_attn.refs_12_) | copy-start | bytes 4423684
  457.1 15.4 %copy-start.137 = (f32[160,16]{0,1:T(8,128)S(1)}, f32[160,16]{0,1:T(8,128)}, u32[]{:S(2)}) copy-start(f32[160,16]{0,1:T(8,128)} %copy-done.136) | copy-start | bytes 30724
  519.2 35.5 %copy-start.135 = (bf16[32,144,1,1]{1,0,2,3:T(8,128)(2,1)S(1)}, bf16[32,144,1,1]{1,0,2,3:T(8,128)(2,1)}, u32[]{:S(2)}) copy-start(bf16[32,144,1,1]{1,0,2,3:T(8,128)(2,1)} %reshape.1198) | copy-start | bytes 27652
  561.4 4.7 copy-start.130
  561.4 4.8 copy-start.103
  561.4 4.8 copy-start.104
  561.4 4.8 copy-start.105
  561.4 4.8 copy-start.106
  590.2 24.6 %copy-start.142 = (f32[8,4]{1,0:T(8,128)S(1)}, f32[8,4]{1,0:T(8,128)}, u32[]{:S(2)}) copy-start(f32[8,4]{1,0:T(8,128)} %get-tuple-element.360) | copy-start | bytes 388
  590.2 24.7 %copy-start.144 = (f32[128]{0:T(128)S(1)}, f32[128]{0:T(128)}, u32[]{:S(2)}) copy-start(f32[128]{0:T(128)} %copy-done.143) | copy-start | bytes 1540
  590.2 32.0 %copy-start.14 = (bf16[2,144,864]{2,1,0:T(8,128)(2,1)S(1)}, bf16[2,144,864]{2,1,0:T(8,128)(2,1)}, u32[]{:S(2)}) copy-start(bf16[2,144,864]{2,1,0:T(8,128)(2,1)} %get-tuple-element.284.refs_5_) | copy-start | bytes 1492996
  610.2 12.0 %copy-start.4 = (bf16[2,144,1152]{2,1,0:T(8,128)(2,1)S(1)}, bf16[2,144,1152]{2,1,0:T(8,128)(2,1)}, u32[]{:S(2)}) copy-start(bf16[2,144,1152]{2,1,0:T(8,128)(2,1)} %get-tuple-element.286.refs_7_) | copy-start | bytes 1990660
  610.2 12.0 %copy-start.5 = (bf16[2,144,1152]{2,1,0:T(8,128)(2,1)S(1)}, bf16[2,144,1152]{2,1,0:T(8,128)(2,1)}, u32[]{:S(2)}) copy-start(bf16[2,144,1152]{2,1,0:T(8,128)(2,1)} %get-tuple-element.287.refs_8_) | copy-start | bytes 1990660
  610.2 12.0 %copy-start.6 = (bf16[2,144,1152]{2,1,0:T(8,128)(2,1)S(1)}, bf16[2,144,1152]{2,1,0:T(8,128)(2,1)}, u32[]{:S(2)}) copy-start(bf16[2,144,1152]{2,1,0:T(8,128)(2,1)} %get-tuple-element.283.refs_4_) | copy-start | bytes 1990660
  610.2 12.0 %copy-start.7 = (bf16[2,144,1152]{2,1,0:T(8,128)(2,1)S(1)}, bf16[2,144,1152]{2,1,0:T(8,128)(2,1)}, u32[]{:S(2)}) copy-start(bf16[2,144,1152]{2,1,0:T(8,128)(2,1)} %get-tuple-element.282.refs_3_) | copy-start | bytes 1990660
  610.3 12.0 %copy-start.22 = (bf16[2,144,288]{2,1,0:T(8,128)(2,1)S(1)}, bf16[2,144,288]{2,1,0:T(8,128)(2,1)}, u32[]{:S(2)}) copy-start(bf16[2,144,288]{2,1,0:T(8,128)(2,1)} %get-tuple-element.285.refs_6_) | copy-start | bytes 497668
  654.5 5.6 copy-start.82
  656.7 5.4 copy-start.80
  656.7 6.1 copy-start.81
  662.9 5.9 copy-start.122
  662.9 5.9 copy-start.138
  662.9 5.9 copy-start.139
  662.9 5.9 copy-start.140
  662.9 6.6 copy-start.69
  662.9 6.6 copy-start.70
  662.9 6.6 copy-start.85
  662.9 6.6 copy-start.86
  662.9 6.9 %copy-start.87 = (f32[1256,288]{0,1:T(8,128)S(1)}, f32[1256,288]{0,1:T(8,128)}, u32[]{:S(2)}) copy-start(f32[1256,288]{0,1:T(8,128)} %param.62) | copy-start | bytes 4340740
  (95 other events, 214.4 us)

commit v6 on v5

--- a/solution.py
+++ b/solution.py
@@ -291,7 +291,7 @@
 
 
 def chunk_of(length):
-    return 64 if length % 64 == 0 else 32
+    return 32 if length % 32 == 0 else 16
 
 
 def normal(values):

time: 684 us -> 685 us (level)
  no operation moved by 1% of the time
where the time goes in v6:
time: 685 us; the launch traced here: 676 us
  Pallas kernels  495 us (72%)
  matrix products  61.7 us (9%)
  other arithmetic  59.1 us (9%)
  local copies, waits for them, and re-layouts  51 us (7%)
  between operations  9.36 us (1%)
    pallas_call x16, Pallas kernels, travel(): pl.pallas_call(partial(kernel, parts), out_shape=[shape for part in parts...  448 us
    dot_general x16, matrix products, low_dot(): return jnp.einsum(spec, left, right, preferred_element_type=jnp.float32)  47.6 us
    pallas_call x4, Pallas kernels, by_image(): pl.pallas_call(body, grid=(images,), out_shape=made, in_specs=[block(arra...  47.1 us
    unnamed x318, local copies, waits for them, and re-layouts  35.9 us
    add x7, other arithmetic, adam(): average = average_decay * average + (1.0 - average_decay) * fresh  21.3 us

profile of v6, /device:TPU:0, one launch (start us, length us, event | category | flops | bytes accessed | tf_op | source)
XLA Modules:
  0.0 676.3 jit_solution(14389716234105026005)
XLA Ops:
  0.7 1.6 convert_element_type.1054
  4.6 15.0 %shard_map.562 = (f32[8,8,144]{2,1,0:T(8,128)S(1)}, bf16[2,2,2,144,864]{4,3,2,1,0:T(8,128)(2,1)}, bf16[2,2,2,144,288]{4,3,2,1,0:T(8,128)(2,1)}) custom-call(f32[2,8,144]{2,1,0:T(8,128)S(1)} %pad.21.refs_0_, bf16[144,864]{1,0:T(8,128)(2,1)S(1)} %convert_element_type.1055.refs_1_, bf16[144,288]{1,0:T(8,128)(2,1)S(1)} %get-tuple-element.363.refs_2_), custom_call_target="tpu_custom_call" | custom-call | flops 20000000000 | bytes 1024 | tf_op jit(solution)/shard_map/pallas_call | solution.py:1041
  20.3 2.3 multiply_cosine_fusion
  24.7 1.9 fusion.29
  26.6 1.9 convert_bitcast_fusion
  28.9 2.2 reshape.1189
  31.2 1.6 fusion.154.refs_0_
  32.9 27.4 %shard_map.563 = (f32[8,4,3456]{2,1,0:T(4,128)S(1)}, bf16[2,2,2,144,864]{4,3,2,1,0:T(8,128)(2,1)}, bf16[2,2,2,144,288]{4,3,2,1,0:T(8,128)(2,1)}, bf16[2,2,2,144,1152]{4,3,2,1,0:T(8,128)(2,1)}) custom-call(f32[8,4,3456]{2,1,0:T(4,128)S(1)} %fusion.154.refs_0_, ...), custom_call_target="tpu_custom_call", output_to_operand_aliasing={{1}: (1, {}), {2}: (2, {})} | custom-call | flops 20000000000 | bytes 1024 | tf_op jit(solution)/shard_map/pallas_call | solution.py:1041
  61.2 32.8 %shard_map.564 = (f32[4,12,288]{2,1,0:T(8,128)S(1)}, f32[8,24,288]{2,1,0:T(8,128)S(1)}, bf16[4,48,288]{2,1,0:T(8,128)(2,1)S(1)}, bf16[2,2,2,144,864]{4,3,2,1,0:T...) custom-call(f32[4,12,288]{2,1,0:T(8,128)S(1)} %reshape.1116.refs_0_,, ...), custom_call_target="tpu_custom_call", output_to_operand_aliasing={{3}: (3, {}), {4}: (4, {}), {6}: (6, {})} | custom-call | flops 20000000000 | bytes 1024 | tf_op jit(solution)/shard_map/pallas_call | solution.py:1041
  96.9 25.9 %shard_map.565 = (bf16[4,160,1152]{2,1,0:T(8,128)(2,1)S(1)}, bf16[2,2,2,144,1152]{4,3,2,1,0:T(8,128)(2,1)}, bf16[2,2,2,144,1152]{4,3,2,1,0:T(8,128)(2,1)}, bf16[...) custom-call(f32[160,1152]{1,0:T(8,128)} %convolution_add_fusion.refs_0_.r, ...), custom_call_target="tpu_custom_call", output_to_operand_aliasing={{1}: (2, {}), {2}: (3, {})} | custom-call | flops 20000000000 | bytes 1024 | tf_op jit(solution)/shard_map/pallas_call | solution.py:1041
  124.9 1.6 copy-done.29
  126.5 1.4 copy-done.51
  127.9 7.7 %shard_map.566 = (bf16[4,160,864]{2,1,0:T(8,128)(2,1)S(1)}, bf16[4,160,288]{2,1,0:T(8,128)(2,1)S(1)}, bf16[4,160,1152]{2,1,0:T(8,128)(2,1)S(1)}) custom-call(bf16[4,160,1152]{2,1,0:T(8,128)(2,1)S(1)} %copy-done.51, f32[4,1,160]{2,1,0:T(1,128)S(1)} %compare_convert_fusion.valid, bf16[1152,864]{1,0:T(8,128)(2,1)S(1)} %bitcast.356, bf16[1152,288]{1,0:T(8,128)(2,1)S(1)} %bitcast.360), custom_call_target="tpu_custom_call" | custom-call | flops 5000000000 | bytes 1024 | tf_op jit(solution)/shard_map/pallas_call | solution.py:1209
  136.6 28.5 %shard_map.567 = (bf16[4,160,1152]{2,1,0:T(8,128)(2,1)S(1)}, f32[160,1152]{1,0:T(8,128)S(1)}, f32[160,1152]{1,0:T(8,128)S(1)}, bf16[2,2,2,144,1152]{4,3,2,1,0:T(...) custom-call(bf16[4,160,1152]{2,1,0:T(8,128)(2,1)S(1)} %get-tuple-ele, ...), custom_call_target="tpu_custom_call", output_to_operand_aliasing={{3}: (3, {}), {4}: (4, {}), {5}: (5, {})} | custom-call | flops 20000000000 | bytes 1024 | tf_op jit(solution)/shard_map/pallas_call | solution.py:1041
  165.2 2.2 fusion.156
  168.0 3.8 convolution_convert_fusion.3.refs_0_
  172.2 2.7 multiply_add_fusion.9.refs_5_
  176.4 36.9 %shard_map.568 = (bf16[4,256,1152]{2,1,0:T(8,128)(2,1)S(1)}, f32[160,1152]{1,0:T(8,128)S(1)}, f32[160,1152]{1,0:T(8,128)}, f32[256,1152]{1,0:T(8,128)S(1)}, f32[...) custom-call(bf16[4,160,1152]{2,1,0:T(8,128)(2,1)S(1)} %copy-done.39,, ...), custom_call_target="tpu_custom_call", output_to_operand_aliasing={{6}: (10, {}), {7}: (11, {}), {8}: (12, {})} | custom-call | flops 20000000000 | bytes 1024 | tf_op jit(solution)/shard_map/pallas_call | solution.py:1041
  214.2 2.9 copy-done.27
  218.2 11.3 %shard_map.569 = (bf16[4,256,864]{2,1,0:T(8,128)(2,1)S(1)}, bf16[4,256,288]{2,1,0:T(8,128)(2,1)S(1)}, bf16[4,256,1152]{2,1,0:T(8,128)(2,1)S(1)}) custom-call(bf16[4,256,1152]{2,1,0:T(8,128)(2,1)S(1)} %get-tuple-element.185.normed.refs_10_, f32[4,1,256]{2,1,0:T(1,128)S(1)} %broadcast_in_dim.7.valid, bf16[1152,864]{1,0:T(8,128)(2,1)S(1)} %bitcast.354, ...), custom_call_target="tpu_custom_call" | custom-call | flops 5000000000 | bytes 1024 | tf_op jit(solution)/shard_map/pallas_call | solution.py:1209
  230.8 34.0 %shard_map.570 = (bf16[4,256,1152]{2,1,0:T(8,128)(2,1)S(1)}, f32[256,1152]{1,0:T(8,128)S(1)}, f32[256,1152]{1,0:T(8,128)S(1)}, bf16[2,2,2,144,1152]{4,3,2,1,0:T(8,128)(2,1)}, bf16[2,2,2,144,1152]{4,3,2,1,0:T(8,128)(2,1)}) custom-call(bf16[4,256,1152]{2,1,0:T(8,128)(2,1)S(1)} %get-tuple-element.188.refs_0_, ...), custom_call_target="tpu_custom_call", output_to_operand_aliasing={{3}: (3, {}), {4}: (4, {})} | custom-call | flops 20000000000 | bytes 1024 | tf_op jit(solution)/shard_map/pallas_call | solution.py:1041
  264.9 7.0 %fusion.157 = f32[4,256,1152]{2,1,0:T(8,128)S(1)} fusion(bf16[4,256,1152]{2,1,0:T(8,128)(2,1)S(1)} %get-tuple-element.192, bf16[1152,1152,1]{1,0,2:T(8,128)(2,1)} %bitcast.371), kind=kOutput, calls=%fused_computation.297 | convolution fusion | flops 2717908992 | bytes 9732096 | tf_op jit(solution)/shard_map/bld,df->blf/dot_general | solution.py:1223
  271.9 4.5 convolution_convert_fusion.1.refs_0_
  276.7 31.4 %shard_map.571 = (bf16[4,256,1152]{2,1,0:T(8,128)(2,1)S(1)}, f32[256,1152]{1,0:T(8,128)S(1)}, f32[1,1152]{1,0:T(1,128)S(1)}, f32[16,1152]{1,0:T(8,128)S(1)}, f32[1,1]{1,0:T(1,128)}) custom-call(bf16[4,256,1152]{2,1,0:T(8,128)(2,1)S(1)} %convolution_convert_fusion.1.refs_0_, f32[256,1152]{1,0:T(8,128)} %copy-done.59, ...), custom_call_target="tpu_custom_call" | custom-call | flops 20000000000 | bytes 1024 | tf_op jit(solution)/shard_map/pallas_call | solution.py:1041
  309.1 5.1 fusion.10
  314.2 4.0 convolution_convert_fusion.refs_0_
  318.2 3.3 fusion
  321.5 3.4 fusion.1
  325.0 32.8 %shard_map.572 = (bf16[4,256,1152]{2,1,0:T(8,128)(2,1)S(1)}, f32[256,1152]{1,0:T(8,128)S(1)}, f32[3,1152]{1,0:T(4,128)S(1)}, bf16[1,1,144,1152]{3,2,1,0:T(8,128)...) custom-call(bf16[4,256,1152]{2,1,0:T(8,128)(2,1)S(1)} %convolution_c, ...), custom_call_target="tpu_custom_call" | custom-call | flops 20000000000 | bytes 1024 | tf_op jit(solution)/shard_map/pallas_call | solution.py:1041
  358.8 14.8 %shard_map.573 = (bf16[4,256,864]{2,1,0:T(8,128)(2,1)S(1)}, bf16[4,256,1152]{2,1,0:T(8,128)(2,1)S(1)}) custom-call(bf16[4,256,864]{2,1,0:T(8,128)(2,1)S(1)} %copy-done.45, f32[4,1,256]{2,1,0:T(1,128)S(1)} %broadcast_in_dim.7.valid, bf16[4,256,1152]{2,1,0:T(8,128)(2,1)S(1)} %get-tuple-element.203.grad_attn.refs_12_, bf16[1152,864]{1,0:T(8,128)(2,1)S(1)} %bitcast.355, ...), custom_call_target="tpu_custom_call" | custom-call | flops 5000000000 | bytes 1024 | tf_op jit(solution)/shard_map/pallas_call | solution.py:1209
  373.6 1.4 copy-done.41
  376.5 1.4 fusion.54
  377.9 1.4 fusion.52
  379.4 29.4 %shard_map.574 = (bf16[4,160,1152]{2,1,0:T(8,128)(2,1)S(1)}, f32[160,1152]{1,0:T(8,128)S(1)}, f32[4,1152]{1,0:T(4,128)S(1)}, bf16[1152,864]{1,0:T(8,128)(2,1)S(1...) custom-call(bf16[4,256,1152]{2,1,0:T(8,128)(2,1)S(1)} %copy-done.42,, ...), custom_call_target="tpu_custom_call" | custom-call | flops 20000000000 | bytes 1024 | tf_op jit(solution)/shard_map/pallas_call | solution.py:1041
  408.9 3.1 fusion.17
  412.0 2.3 convolution_convert_fusion.2.refs_0_
  414.3 2.4 fusion.2
  416.9 2.5 fusion.3
  419.5 3.5 fusion.43
  423.1 34.4 %shard_map.575 = (bf16[4,160,1152]{2,1,0:T(8,128)(2,1)S(1)}, f32[160,1152]{1,0:T(8,128)S(1)}, f32[3,1152]{1,0:T(4,128)S(1)}, bf16[1,1,144,1152]{3,2,1,0:T(8,128)...) custom-call(bf16[4,160,1152]{2,1,0:T(8,128)(2,1)S(1)} %convolution_c, ...), custom_call_target="tpu_custom_call" | custom-call | flops 20000000000 | bytes 1024 | tf_op jit(solution)/shard_map/pallas_call | solution.py:1041
  458.5 13.3 %shard_map.576 = (bf16[4,160,864]{2,1,0:T(8,128)(2,1)S(1)}, bf16[4,160,1152]{2,1,0:T(8,128)(2,1)S(1)}) custom-call(bf16[4,160,864]{2,1,0:T(8,128)(2,1)S(1)} %copy-done.53, f32[4,1,160]{2,1,0:T(1,128)S(1)} %copy-done.26, bf16[4,160,1152]{2,1,0:T(8,128)(2,1)S(1)} %get-tuple-element.223.grad_attn.refs_12_, bf16[1152,864]{1,0:T(8,128)(2,1)S(1)} %bitcast.357, ...), custom_call_target="tpu_custom_call" | custom-call | flops 5000000000 | bytes 1024 | tf_op jit(solution)/shard_map/pallas_call | solution.py:1209
  474.0 1.4 fusion.46
  475.4 1.6 fusion.44
  477.1 1.4 fusion.73
  479.6 34.0 %shard_map.577 = (f32[4,48,288]{2,1,0:T(8,128)S(1)}, bf16[1152,864]{1,0:T(8,128)(2,1)S(1)}, bf16[1152,288]{1,0:T(8,128)(2,1)S(1)}, bf16[1,144,1152]{2,1,0:T(8,12...) custom-call(bf16[4,160,1152]{2,1,0:T(8,128)(2,1)S(1)} %copy-done.49,, ...), custom_call_target="tpu_custom_call" | custom-call | flops 20000000000 | bytes 1024 | tf_op jit(solution)/shard_map/pallas_call | solution.py:1041
  516.0 1.8 fusion.39
  518.0 1.4 fusion.72
  520.7 34.1 %shard_map.578 = (f32[8,4,3456]{2,1,0:T(4,128)S(1)}, bf16[8,48,288]{2,1,0:T(8,128)(2,1)S(1)}, bf16[1,1,144,864]{3,2,1,0:T(8,128)(2,1)}, bf16[1,1,144,864]{3,2,1,...) custom-call(f32[4,3456]{1,0:T(4,128)S(1)} %reshape.1134.refs_0_, ...), custom_call_target="tpu_custom_call" | custom-call | flops 20000000000 | bytes 1024 | tf_op jit(solution)/shard_map/pallas_call | solution.py:1041
  554.8 1.4 reshape.1137
  556.2 4.5 multiply_reduce_fusion
  562.9 3.4 fusion.26.refs_0_
  568.1 20.4 %shard_map.579 = (f32[4,32,144]{2,1,0:T(8,128)S(1)}, bf16[1,144,864]{2,1,0:T(8,128)(2,1)}, bf16[1,144,864]{2,1,0:T(8,128)(2,1)}, bf16[1,144,288]{2,1,0:T(8,128)(...) custom-call(f32[32,144]{1,0:T(8,128)S(1)} %fusion.26.refs_0_, ...), custom_call_target="tpu_custom_call" | custom-call | flops 20000000000 | bytes 1024 | tf_op jit(solution)/shard_map/pallas_call | solution.py:1041
  588.6 1.8 fusion.66
  591.6 20.1 %shard_map.580 = (f32[8,32,144]{2,1,0:T(8,128)S(1)}, bf16[2,144,864]{2,1,0:T(8,128)(2,1)}, bf16[2,144,288]{2,1,0:T(8,128)(2,1)}) custom-call(f32[32,144]{1,0:T(8,128)S(1)} %reduce_sum.90.refs_0_, bf16[2,144,864]{2,1,0:T(8,128)(2,1)S(1)} %pad_maximum_fusion.7.refs_1_, bf16[2,144,288]{2,1,0:T(8,128)(2,1)S(1)} %pad_maximum_fusion.9.refs_2_), custom_call_target="tpu_custom_call" | custom-call | flops 20000000000 | bytes 1024 | tf_op jit(solution)/shard_map/pallas_call | solution.py:1041
  612.6 1.8 reshape.1138
  616.5 4.1 multiply_reduce_fusion.1
  625.8 10.9 %shard_map.581 = f32[32,8,128]{2,1,0:T(8,128)S(1)} custom-call(f32[8,128]{1,0:T(8,128)S(1)} %pad.25.refs_0_, bf16[2,144,864]{2,1,0:T(8,128)(2,1)S(1)} %copy-done.15, bf16[2,144,288]{2,1,0:T(8,128)(2,1)S(1)} %copy-done.23, bf16[2,144,1152]{2,1,0:T(8,128)(2,1)S(1)} %copy-done.7, bf16[2,144,1152]{2,1,0:T(8,128)(2,1)S(1)} %copy-done.6, ...), custom_call_target="tpu_custom_call" | custom-call | flops 20000000000 | bytes 1024 | tf_op jit(solution)/shard_map/pallas_call | solution.py:1041
  643.6 3.2 multiply_add_fusion.5
  648.3 1.5 multiply_add_fusion.10
  652.4 3.2 multiply_add_fusion.4
  658.2 3.3 multiply_add_fusion.3
  661.5 1.3 copy-done.68
  664.4 5.8 multiply_add_fusion
  671.3 3.5 multiply_add_fusion.1
  (438 shorter events, 54.0 us)
Async XLA Ops:
  0.7 275.9 %copy-start = (f32[4,256,16]{1,2,0:T(8,128)S(1)}, f32[4,256,16]{1,2,0:T(8,128)}, u32[]{:S(2)}) copy-start(f32[4,256,16]{1,2,0:T(8,128)} %param.36) | copy-start | bytes 196612
  4.6 18.1 %copy-start.147 = (s32[4]{0:T(128)S(1)}, s32[4]{0:T(128)}, u32[]{:S(2)}) copy-start(s32[4]{0:T(128)} %param.38) | copy-start | bytes 52
  22.7 10.1 %copy-start.71 = (f32[256,576]{1,0:T(8,128)}, f32[256,576]{1,0:T(8,128)S(1)}, u32[]{:S(2)}) copy-start(f32[256,576]{1,0:T(8,128)S(1)} %get-tuple-element.368) | copy-start | bytes 1769476
  32.9 27.6 %copy-start.141 = (f32[4,1152]{1,0:T(4,128)S(1)}, f32[4,1152]{1,0:T(4,128)}, u32[]{:S(2)}) copy-start(f32[4,1152]{1,0:T(4,128)} %param.41) | copy-start | bytes 55300
  32.9 28.1 %copy-start.121 = (f32[33,288]{1,0:T(8,128)S(1)}, f32[33,288]{1,0:T(8,128)}, u32[]{:S(2)}) copy-start(f32[33,288]{1,0:T(8,128)} %param.47) | copy-start | bytes 114052
  32.9 28.1 %copy-start.77 = (f32[2,1152,144]{1,2,0:T(8,128)S(1)}, f32[2,1152,144]{1,2,0:T(8,128)}, u32[]{:S(2)}) copy-start(f32[2,1152,144]{1,2,0:T(8,128)} %param.45) | copy-start | bytes 3981316
  61.2 34.0 %copy-start.79 = (f32[160,1152]{1,0:T(8,128)S(1)}, f32[160,1152]{1,0:T(8,128)}, u32[]{:S(2)}) copy-start(f32[160,1152]{1,0:T(8,128)} %fusion.29) | copy-start | bytes 2211844
  94.0 82.2 %copy-start.17 = (f32[8,24,288]{2,1,0:T(8,128)}, f32[8,24,288]{2,1,0:T(8,128)S(1)}, u32[]{:S(2)}) copy-start(f32[8,24,288]{2,1,0:T(8,128)S(1)} %get-tuple-element.171) | copy-start | bytes 663556
  96.9 28.0 %copy-start.33 = (bf16[2,2,2,144,288]{4,3,2,1,0:T(8,128)(2,1)S(1)}, bf16[2,2,2,144,288]{4,3,2,1,0:T(8,128)(2,1)}, u32[]{:S(2)}) copy-start(bf16[2,2,2,144,288]{4,3,2,1,0:T(8,128)(2,1)} %get-tuple-element.173) | copy-start | bytes 1990660
  124.9 10.7 %copy-start.25 = (f32[4,1,160]{2,1,0:T(1,128)}, f32[4,1,160]{2,1,0:T(1,128)S(1)}, u32[]{:S(2)}) copy-start(f32[4,1,160]{2,1,0:T(1,128)S(1)} %compare_convert_fusion.valid) | copy-start | bytes 7684
  136.6 28.6 %copy-start.56 = (bf16[4,160,288]{2,1,0:T(8,128)(2,1)}, bf16[4,160,288]{2,1,0:T(8,128)(2,1)S(1)}, u32[]{:S(2)}) copy-start(bf16[4,160,288]{2,1,0:T(8,128)(2,1)S(1)} %get-tuple-element.232.refs_13_) | copy-start | bytes 1105924
  136.6 28.6 %copy-start.151 = (bf16[2,2,2,144,1152]{4,3,2,1,0:T(8,128)(2,1)S(1)}, bf16[2,2,2,144,1152]{4,3,2,1,0:T(8,128)(2,1)}, u32[]{:S(2)}) copy-start(bf16[2,2,2,144,1152]{4,3,2,1,0:T(8,128)(2,1)} %get-tuple-element.179) | copy-start | bytes 7962628
  214.2 15.4 %copy-start.46 = (bf16[4,256,1152]{2,1,0:T(8,128)(2,1)}, bf16[4,256,1152]{2,1,0:T(8,128)(2,1)S(1)}, u32[]{:S(2)}) copy-start(bf16[4,256,1152]{2,1,0:T(8,128)(2,1)S(1)} %get-tuple-element.185.normed.refs_10_) | copy-start | bytes 7077892
  214.2 15.4 %copy-start.61 = (f32[256,1152]{1,0:T(8,128)}, f32[256,1152]{1,0:T(8,128)S(1)}, u32[]{:S(2)}) copy-start(f32[256,1152]{1,0:T(8,128)S(1)} %get-tuple-element.189.refs_1_) | copy-start | bytes 3538948
  230.8 34.0 %copy-start.55 = (bf16[4,256,288]{2,1,0:T(8,128)(2,1)}, bf16[4,256,288]{2,1,0:T(8,128)(2,1)S(1)}, u32[]{:S(2)}) copy-start(bf16[4,256,288]{2,1,0:T(8,128)(2,1)S(1)} %get-tuple-element.209.refs_13_) | copy-start | bytes 1769476
  264.8 7.0 %copy-start.37 = (bf16[4,256,1152]{2,1,0:T(8,128)(2,1)}, bf16[4,256,1152]{2,1,0:T(8,128)(2,1)S(1)}, u32[]{:S(2)}) copy-start(bf16[4,256,1152]{2,1,0:T(8,128)(2,1)S(1)} %get-tuple-element.192) | copy-start | bytes 7077892
  264.8 7.0 %copy-start.58 = (f32[256,1152]{1,0:T(8,128)}, f32[256,1152]{1,0:T(8,128)S(1)}, u32[]{:S(2)}) copy-start(f32[256,1152]{1,0:T(8,128)S(1)} %get-tuple-element.201.refs_2_) | copy-start | bytes 3538948
  264.8 7.0 %copy-start.59 = (f32[256,1152]{1,0:T(8,128)}, f32[256,1152]{1,0:T(8,128)S(1)}, u32[]{:S(2)}) copy-start(f32[256,1152]{1,0:T(8,128)S(1)} %get-tuple-element.195.refs_1_) | copy-start | bytes 3538948
  264.8 7.0 %copy-start.153 = (bf16[2,2,2,144,1152]{4,3,2,1,0:T(8,128)(2,1)S(1)}, bf16[2,2,2,144,1152]{4,3,2,1,0:T(8,128)(2,1)}, u32[]{:S(2)}) copy-start(bf16[2,2,2,144,1152]{4,3,2,1,0:T(8,128)(2,1)} %get-tuple-element.194) | copy-start | bytes 7962628
  276.6 32.5 %copy-start.154 = (bf16[2,2,2,144,1152]{4,3,2,1,0:T(8,128)(2,1)S(1)}, bf16[2,2,2,144,1152]{4,3,2,1,0:T(8,128)(2,1)}, u32[]{:S(2)}) copy-start(bf16[2,2,2,144,1152]{4,3,2,1,0:T(8,128)(2,1)} %get-tuple-element.194) | copy-start | bytes 7962628
  276.7 32.4 %copy-start.158 = (f32[4,256,1152]{2,1,0:T(8,128)S(1)}, f32[4,256,1152]{2,1,0:T(8,128)}, u32[]{:S(2)}) copy-start(f32[4,256,1152]{2,1,0:T(8,128)} %copy-done.157) | copy-start | bytes 14155780
  309.1 5.1 copy-start.148
  321.5 54.9 %copy-start.8 = (bf16[1152,1152]{1,0:T(8,128)(2,1)}, bf16[1152,1152]{1,0:T(8,128)(2,1)S(1)}, u32[]{:S(2)}) copy-start(bf16[1152,1152]{1,0:T(8,128)(2,1)S(1)} %fusion) | copy-start | bytes 7962628
  324.9 32.9 %copy-start.9 = (bf16[1152,1152]{1,0:T(8,128)(2,1)}, bf16[1152,1152]{1,0:T(8,128)(2,1)S(1)}, u32[]{:S(2)}) copy-start(bf16[1152,1152]{1,0:T(8,128)(2,1)S(1)} %fusion.1) | copy-start | bytes 7962628
  324.9 33.9 %copy-start.28 = (bf16[2,2,2,144,864]{4,3,2,1,0:T(8,128)(2,1)S(1)}, bf16[2,2,2,144,864]{4,3,2,1,0:T(8,128)(2,1)}, u32[]{:S(2)}) copy-start(bf16[2,2,2,144,864]{4,3,2,1,0:T(8,128)(2,1)} %get-tuple-element.186) | copy-start | bytes 5971972
  324.9 33.9 %copy-start.32 = (bf16[2,2,2,144,288]{4,3,2,1,0:T(8,128)(2,1)S(1)}, bf16[2,2,2,144,288]{4,3,2,1,0:T(8,128)(2,1)}, u32[]{:S(2)}) copy-start(bf16[2,2,2,144,288]{4,3,2,1,0:T(8,128)(2,1)} %get-tuple-element.187) | copy-start | bytes 1990660
  325.0 33.9 %copy-start.45 = (bf16[4,256,864]{2,1,0:T(8,128)(2,1)S(1)}, bf16[4,256,864]{2,1,0:T(8,128)(2,1)}, u32[]{:S(2)}) copy-start(bf16[4,256,864]{2,1,0:T(8,128)(2,1)} %copy-done.44) | copy-start | bytes 5308420
  358.8 14.8 %copy-start.40 = (bf16[4,256,1152]{2,1,0:T(8,128)(2,1)}, bf16[4,256,1152]{2,1,0:T(8,128)(2,1)S(1)}, u32[]{:S(2)}) copy-start(bf16[4,256,1152]{2,1,0:T(8,128)(2,1)S(1)} %get-tuple-element.203.grad_attn.refs_12_) | copy-start | bytes 7077892
  379.4 29.5 %copy-start.150 = (bf16[2,2,2,144,1152]{4,3,2,1,0:T(8,128)(2,1)S(1)}, bf16[2,2,2,144,1152]{4,3,2,1,0:T(8,128)(2,1)}, u32[]{:S(2)}) copy-start(bf16[2,2,2,144,1152]{4,3,2,1,0:T(8,128)(2,1)} %get-tuple-element.180) | copy-start | bytes 7962628
  379.4 29.5 %copy-start.156 = (f32[4,160,1152]{2,1,0:T(8,128)S(1)}, f32[4,160,1152]{2,1,0:T(8,128)}, u32[]{:S(2)}) copy-start(f32[4,160,1152]{2,1,0:T(8,128)} %copy-done.155) | copy-start | bytes 8847364
  408.8 14.3 %copy-start.10 = (bf16[1152,864]{1,0:T(8,128)(2,1)}, bf16[1152,864]{1,0:T(8,128)(2,1)S(1)}, u32[]{:S(2)}) copy-start(bf16[1152,864]{1,0:T(8,128)(2,1)S(1)} %get-tuple-element.217) | copy-start | bytes 5971972
  408.8 14.3 %copy-start.18 = (bf16[1152,288]{1,0:T(8,128)(2,1)}, bf16[1152,288]{1,0:T(8,128)(2,1)S(1)}, u32[]{:S(2)}) copy-start(bf16[1152,288]{1,0:T(8,128)(2,1)S(1)} %get-tuple-element.218) | copy-start | bytes 1990660
  423.1 35.3 %copy-start.26 = (f32[4,1,160]{2,1,0:T(1,128)S(1)}, f32[4,1,160]{2,1,0:T(1,128)}, u32[]{:S(2)}) copy-start(f32[4,1,160]{2,1,0:T(1,128)} %copy-done.25) | copy-start | bytes 7684
  423.1 35.3 %copy-start.30 = (bf16[2,2,2,144,864]{4,3,2,1,0:T(8,128)(2,1)S(1)}, bf16[2,2,2,144,864]{4,3,2,1,0:T(8,128)(2,1)}, u32[]{:S(2)}) copy-start(bf16[2,2,2,144,864]{4,3,2,1,0:T(8,128)(2,1)} %get-tuple-element.172) | copy-start | bytes 5971972
  423.1 35.3 %copy-start.34 = (bf16[2,2,2,144,288]{4,3,2,1,0:T(8,128)(2,1)S(1)}, bf16[2,2,2,144,288]{4,3,2,1,0:T(8,128)(2,1)}, u32[]{:S(2)}) copy-start(bf16[2,2,2,144,288]{4,3,2,1,0:T(8,128)(2,1)} %get-tuple-element.173) | copy-start | bytes 1990660
  423.1 35.3 %copy-start.53 = (bf16[4,160,864]{2,1,0:T(8,128)(2,1)S(1)}, bf16[4,160,864]{2,1,0:T(8,128)(2,1)}, u32[]{:S(2)}) copy-start(bf16[4,160,864]{2,1,0:T(8,128)(2,1)} %copy-done.52) | copy-start | bytes 3317764
  458.4 13.3 %copy-start.47 = (bf16[4,160,1152]{2,1,0:T(8,128)(2,1)}, bf16[4,160,1152]{2,1,0:T(8,128)(2,1)S(1)}, u32[]{:S(2)}) copy-start(bf16[4,160,1152]{2,1,0:T(8,128)(2,1)S(1)} %get-tuple-element.223.grad_attn.refs_12_) | copy-start | bytes 4423684
  458.5 15.4 %copy-start.137 = (f32[160,16]{0,1:T(8,128)S(1)}, f32[160,16]{0,1:T(8,128)}, u32[]{:S(2)}) copy-start(f32[160,16]{0,1:T(8,128)} %copy-done.136) | copy-start | bytes 30724
  520.7 35.5 %copy-start.135 = (bf16[32,144,1,1]{1,0,2,3:T(8,128)(2,1)S(1)}, bf16[32,144,1,1]{1,0,2,3:T(8,128)(2,1)}, u32[]{:S(2)}) copy-start(bf16[32,144,1,1]{1,0,2,3:T(8,128)(2,1)} %reshape.1198) | copy-start | bytes 27652
  562.9 4.7 copy-start.130
  562.9 4.8 copy-start.103
  562.9 4.8 copy-start.104
  562.9 4.8 copy-start.105
  562.9 4.8 copy-start.106
  591.6 24.7 %copy-start.142 = (f32[8,4]{1,0:T(8,128)S(1)}, f32[8,4]{1,0:T(8,128)}, u32[]{:S(2)}) copy-start(f32[8,4]{1,0:T(8,128)} %get-tuple-element.360) | copy-start | bytes 388
  591.6 24.8 %copy-start.144 = (f32[128]{0:T(128)S(1)}, f32[128]{0:T(128)}, u32[]{:S(2)}) copy-start(f32[128]{0:T(128)} %copy-done.143) | copy-start | bytes 1540
  591.6 32.1 %copy-start.14 = (bf16[2,144,864]{2,1,0:T(8,128)(2,1)S(1)}, bf16[2,144,864]{2,1,0:T(8,128)(2,1)}, u32[]{:S(2)}) copy-start(bf16[2,144,864]{2,1,0:T(8,128)(2,1)} %get-tuple-element.284.refs_5_) | copy-start | bytes 1492996
  611.7 12.0 %copy-start.4 = (bf16[2,144,1152]{2,1,0:T(8,128)(2,1)S(1)}, bf16[2,144,1152]{2,1,0:T(8,128)(2,1)}, u32[]{:S(2)}) copy-start(bf16[2,144,1152]{2,1,0:T(8,128)(2,1)} %get-tuple-element.286.refs_7_) | copy-start | bytes 1990660
  611.7 12.0 %copy-start.5 = (bf16[2,144,1152]{2,1,0:T(8,128)(2,1)S(1)}, bf16[2,144,1152]{2,1,0:T(8,128)(2,1)}, u32[]{:S(2)}) copy-start(bf16[2,144,1152]{2,1,0:T(8,128)(2,1)} %get-tuple-element.287.refs_8_) | copy-start | bytes 1990660
  611.7 12.0 %copy-start.6 = (bf16[2,144,1152]{2,1,0:T(8,128)(2,1)S(1)}, bf16[2,144,1152]{2,1,0:T(8,128)(2,1)}, u32[]{:S(2)}) copy-start(bf16[2,144,1152]{2,1,0:T(8,128)(2,1)} %get-tuple-element.283.refs_4_) | copy-start | bytes 1990660
  611.7 12.0 %copy-start.7 = (bf16[2,144,1152]{2,1,0:T(8,128)(2,1)S(1)}, bf16[2,144,1152]{2,1,0:T(8,128)(2,1)}, u32[]{:S(2)}) copy-start(bf16[2,144,1152]{2,1,0:T(8,128)(2,1)} %get-tuple-element.282.refs_3_) | copy-start | bytes 1990660
  611.7 12.0 %copy-start.22 = (bf16[2,144,288]{2,1,0:T(8,128)(2,1)S(1)}, bf16[2,144,288]{2,1,0:T(8,128)(2,1)}, u32[]{:S(2)}) copy-start(bf16[2,144,288]{2,1,0:T(8,128)(2,1)} %get-tuple-element.285.refs_6_) | copy-start | bytes 497668
  655.9 5.6 copy-start.82
  658.2 5.4 copy-start.80
  658.2 6.1 copy-start.81
  664.3 5.9 copy-start.122
  664.3 5.9 copy-start.138
  664.3 5.9 copy-start.139
  664.3 5.9 copy-start.140
  664.3 6.6 copy-start.69
  664.3 6.6 copy-start.70
  664.4 6.6 copy-start.85
  664.4 6.6 copy-start.86
  664.4 6.9 %copy-start.87 = (f32[1256,288]{0,1:T(8,128)S(1)}, f32[1256,288]{0,1:T(8,128)}, u32[]{:S(2)}) copy-start(f32[1256,288]{0,1:T(8,128)} %param.62) | copy-start | bytes 4340740
  (95 other events, 214.4 us)
